TPU v7x, 32 devices: a whole 2x2x4 slice. The times are simulated.
32 devices in a mesh: groups: 2 (over x), tm: 16 (over z, y, core).
Axes of the slice: x: 2, y: 2, z: 4, core: 2. Of those that a mesh axis runs over, the one named last changes fastest.
Arguments:
- links: float32 [4, 2, 3, 3, 2, 64, 512], P(None, None, None, None, 'groups', 'tm'), parts along dimension 4, may hold values from -1 to 1, as said below
- cotangent: bfloat16 [4, 2, 3, 3, 2, 64, 512], P(None, None, None, None, 'groups', 'tm'), parts along dimension 4, may hold values from -0.078125 to 0.078125
- parity: int32 [2, 64], P('groups', 'tm'), parts along dimension 0, may hold values from 0 to 1
- link_subset: int32 [2, 64], P('groups', 'tm'), parts along dimension 0, may hold values from 1 to 15
- w_first: bfloat16 [3456], P('tm'), may hold values from -0.75 to 0.75
- w_second: bfloat16 [20736], P('tm'), may hold values from -0.3125 to 0.3125
- w_third: bfloat16 [20736], P('tm'), may hold values from -0.3125 to 0.3125
- w_last: bfloat16 [1728], P('tm'), may hold values from -0.3125 to 0.3125
Outputs:
- new_links: float32 [4, 2, 3, 3, 2, 64, 512], P(None, None, None, None, 'groups', 'tm'), parts along dimension 4
- grad_first: float32 [2, 3456], P('groups', 'tm'), parts along dimension 0
- grad_second: float32 [2, 20736], P('groups', 'tm'), parts along dimension 0
- grad_third: float32 [2, 20736], P('groups', 'tm'), parts along dimension 0
- grad_last: float32 [2, 1728], P('groups', 'tm'), parts along dimension 0
There are 2 independent parts, one for each index of `groups`. A program takes and returns all parts, laid end to end along the dimension named above; an argument that names none is the same for every part. Nothing has to cross between parts.
Inputs may be any that keep to these rules, and one draw needn't show every extreme that they name: `links`: each link is a special unitary 3 x 3 matrix.
All inputs are finite; a program needn't handle non-finite values.
Results may differ from a plain program's by a relative error of at most 0.028.
Values may be sent and summed in bfloat16 or wider, within the bound.
No kernel may reach another device: no remote copies, remote signals or barrier semaphores. Data moves between devices by JAX's collectives and lax.ppermute only.
A program may use at most 128 MiB of HBM per device.

v0:
```python
import jax
import jax.numpy as jnp
from jax import lax
from jax.sharding import PartitionSpec as P

LS = 8


OFFSETS = (
    (0, 0, 0, 0),
    (1, 0, 0, 0),
    (-1, 0, 0, 0),
    (0, 1, 0, 0),
    (0, -1, 0, 0),
    (0, 0, 1, 0),
    (0, 0, -1, 0),
    (0, 0, 0, 1),
    (0, 0, 0, -1),
)
PLANES = ((0, 1), (0, 2), (0, 3), (1, 2), (1, 3), (2, 3))


def extended_2(block, sides, width):
    for axis, dim in sides:
        count = lax.axis_size(axis)
        forward = [(i, i + 1) for i in range(count - 1)]
        forward.append((count - 1, 0))
        backward = [(target, source) for source, target in forward]
        low = lax.ppermute(
            lax.slice_in_dim(block, block.shape[dim] - width, None, axis=dim), axis, forward
        )
        high = lax.ppermute(lax.slice_in_dim(block, 0, width, axis=dim), axis, backward)
        block = jnp.concatenate([low, block, high], axis=dim)
    return block


def real_product(left, right):
    return jnp.sum(left[:, :, None] * right[None], axis=1)


def complex_mul(left, right):
    real_part = real_product(left[0], right[0]) - real_product(left[1], right[1])
    imag_part = real_product(left[0], right[1]) + real_product(left[1], right[0])
    return jnp.stack([real_part, imag_part])


def dagger(matrix):
    return jnp.stack([jnp.swapaxes(matrix[0], 0, 1), -jnp.swapaxes(matrix[1], 0, 1)])


def trace_of(matrix):
    return matrix[:, 0, 0] + matrix[:, 1, 1] + matrix[:, 2, 2]


def unit_step(direction, amount):
    return tuple((amount if index == direction else 0 for index in range(4)))


def step_sum(first, second):
    return tuple((first[index] + second[index] for index in range(4)))


def space_roll(flat, space_axis, amount):
    stride = LS ** (2 - space_axis)
    site_ids = jnp.arange(flat.shape[-1], dtype=jnp.int32)
    coord = site_ids // stride % LS
    inner = jnp.roll(flat, -amount * stride, axis=flat.ndim - 1)
    if amount > 0:
        wrapped = jnp.roll(flat, -(amount - LS) * stride, axis=flat.ndim - 1)
        edge = coord >= LS - amount
    else:
        wrapped = jnp.roll(flat, -(amount + LS) * stride, axis=flat.ndim - 1)
        edge = coord < -amount
    return jnp.where(edge, wrapped, inner)


def shifted(extended, disp):
    slab_len = extended.shape[-2] - 2
    window = lax.slice_in_dim(extended, 1 + disp[3], 1 + disp[3] + slab_len, axis=extended.ndim - 2)
    for space_axis in range(3):
        if disp[space_axis] != 0:
            window = space_roll(window, space_axis, disp[space_axis])
    return window


def gauge_terms(fields, locate):
    anchor = (0, 0, 0, 0)

    def link(direction, disp):
        return locate(fields[direction], disp)

    plaquettes = []
    for first_dir, second_dir in PLANES:
        loop = complex_mul(
            complex_mul(link(first_dir, anchor), link(second_dir, unit_step(first_dir, 1))),
            complex_mul(
                dagger(link(first_dir, unit_step(second_dir, 1))), dagger(link(second_dir, anchor))
            ),
        )
        plaquettes.append(trace_of(loop)[0] / 3.0)
    forces = []
    for direction in range(4):
        staple = None
        for other in range(4):
            if other == direction:
                continue
            upper = complex_mul(
                complex_mul(
                    link(other, unit_step(direction, 1)),
                    dagger(link(direction, unit_step(other, 1))),
                ),
                dagger(link(other, anchor)),
            )
            lower = complex_mul(
                complex_mul(
                    dagger(link(other, step_sum(unit_step(direction, 1), unit_step(other, -1)))),
                    dagger(link(direction, unit_step(other, -1))),
                ),
                link(other, unit_step(other, -1)),
            )
            staple = upper + lower if staple is None else staple + upper + lower
        current = link(direction, anchor)
        omega = complex_mul(current, staple)
        anti = 0.5 * (omega - dagger(omega))
        diag_mean = trace_of(anti) / 3.0
        eye_three = jnp.eye(3, dtype=anti.dtype)
        generator = (
            anti - diag_mean[:, None, None] * eye_three[None, :, :, None, None, None]
        ) / 6.0
        applied = complex_mul(generator, current)
        twice = complex_mul(generator, applied)
        forces.append((current, applied, twice))
    return (plaquettes, forces)


def identity_like(sample):
    eye_three = jnp.eye(3, dtype=sample.dtype)[:, :, None, None]
    real_part = jnp.broadcast_to(eye_three, sample.shape[1:])
    return jnp.stack([real_part, jnp.zeros_like(real_part)])


def activity(parity, link_subset, times, sites):
    site_ids = jnp.arange(sites, dtype=jnp.int32)
    coord_sum = site_ids // (LS * LS) + site_ids // LS % LS + site_ids % LS
    colour = (times[:, None] + coord_sum[None, :]) % 2
    on_site = colour[None] == parity[:, :, None]
    masks = []
    for direction in range(4):
        chosen = (jnp.right_shift(link_subset, direction) % 2 == 1)[:, :, None]
        masks.append(jnp.logical_and(on_site, chosen))
    return jnp.stack(masks)


def time_faces(values):
    return extended_2(values, (("tm", 2),), 1)


def stacked(extended, sign):
    columns = [shifted(extended, tuple((sign * value for value in offset))) for offset in OFFSETS]
    joined = jnp.concatenate(columns, axis=0)
    return joined.reshape(joined.shape[0], -1)


def conv_forward(weight, extended, outputs):
    inputs = extended.shape[0]
    panel = weight.reshape(len(OFFSETS), outputs, inputs).transpose(1, 0, 2).reshape(outputs, -1)
    result = jnp.dot(panel, stacked(extended, 1), preferred_element_type=jnp.float32)
    return result.reshape((outputs, extended.shape[1], extended.shape[2] - 2, extended.shape[3]))


def conv_back(weight, grad, inputs):
    outputs = grad.shape[0]
    panel = weight.reshape(len(OFFSETS), outputs, inputs).transpose(2, 0, 1).reshape(inputs, -1)
    result = jnp.dot(panel, stacked(time_faces(grad), -1), preferred_element_type=jnp.float32)
    return result.reshape((inputs,) + grad.shape[1:])


def weight_grad(grad, extended):
    outputs = grad.shape[0]
    inputs = extended.shape[0]
    product = lax.dot_general(
        grad.reshape(outputs, -1),
        stacked(extended, 1),
        (((1,), (1,)), ((), ())),
        preferred_element_type=jnp.float32,
    )
    return product.reshape(outputs, len(OFFSETS), inputs).transpose(1, 0, 2).reshape(1, -1)


def on_device(links, cotangent, parity, link_subset, w_first, w_second, w_third, w_last):
    panels = (
        lax.all_gather(w_first, "tm", axis=0, tiled=True),
        lax.all_gather(w_second, "tm", axis=0, tiled=True),
        lax.all_gather(w_third, "tm", axis=0, tiled=True),
        lax.all_gather(w_last, "tm", axis=0, tiled=True),
    )
    ext_links = extended_2(links.astype(jnp.bfloat16), (("tm", 5),), 1).astype(links.dtype)
    fields = [ext_links[index] for index in range(4)]
    plaquettes, forces = gauge_terms(fields, shifted)
    time_links = links[3]
    slab_len = time_links.shape[4]
    conf_count = links.shape[4]
    sites = links.shape[6]
    identity = identity_like(time_links[:, :, :, :, 0])

    def advance(index, product):
        return complex_mul(
            product, lax.dynamic_index_in_dim(time_links, index, axis=4, keepdims=False)
        )

    slab = lax.fori_loop(0, slab_len, advance, identity)
    pieces = lax.all_gather(slab[None].astype(jnp.bfloat16), "tm", axis=0, tiled=True).astype(
        jnp.float32
    )

    def chain(index, product):
        return complex_mul(product, pieces[index])

    whole = lax.fori_loop(0, pieces.shape[0], chain, identity)
    loop_trace = trace_of(whole) / 3.0
    polyakov = jnp.broadcast_to(loop_trace[:, :, None, :], (2, conf_count, slab_len, sites))
    features = jnp.concatenate([jnp.stack(plaquettes), polyakov], axis=0).astype(jnp.bfloat16)
    hidden = panels[0].shape[0] // (len(OFFSETS) * features.shape[0])
    ext_features = time_faces(features)
    hidden_one = jnp.tanh(conv_forward(panels[0], ext_features, hidden)).astype(jnp.bfloat16)
    ext_one = time_faces(hidden_one)
    hidden_two = jnp.tanh(conv_forward(panels[1], ext_one, hidden)).astype(jnp.bfloat16)
    ext_two = time_faces(hidden_two)
    hidden_three = jnp.tanh(conv_forward(panels[2], ext_two, hidden)).astype(jnp.bfloat16)
    ext_three = time_faces(hidden_three)
    coeff = jnp.tanh(conv_forward(panels[3], ext_three, 4))
    times = lax.axis_index("tm") * slab_len + jnp.arange(slab_len, dtype=jnp.int32)
    masks = activity(parity, link_subset, times, sites).astype(jnp.float32)
    new_fields = []
    coeff_grads = []
    for direction in range(4):
        current, applied, twice = forces[direction]
        factor = coeff[direction]
        gate = masks[direction]
        new_fields.append(current + gate * (factor * applied + 0.5 * factor * factor * twice))
        incoming = cotangent[direction].astype(jnp.float32)
        slope = applied + factor * twice
        coeff_grads.append(gate * jnp.sum(incoming * slope, axis=(0, 1, 2)))
    new_links = jnp.stack(new_fields)
    coeff_grad = jnp.stack(coeff_grads)
    last_pre = (coeff_grad * (1.0 - coeff * coeff)).astype(jnp.bfloat16)
    three = hidden_three.astype(jnp.float32)
    third_pre = (conv_back(panels[3], last_pre, hidden) * (1.0 - three * three)).astype(
        jnp.bfloat16
    )
    two = hidden_two.astype(jnp.float32)
    second_pre = (conv_back(panels[2], third_pre, hidden) * (1.0 - two * two)).astype(jnp.bfloat16)
    one = hidden_one.astype(jnp.float32)
    first_pre = (conv_back(panels[1], second_pre, hidden) * (1.0 - one * one)).astype(jnp.bfloat16)
    part_last = weight_grad(last_pre, ext_three)
    part_third = weight_grad(third_pre, ext_two)
    part_second = weight_grad(second_pre, ext_one)
    part_first = weight_grad(first_pre, ext_features)
    grad_first, grad_second, grad_third, grad_last = (
        lax.psum_scatter(
            part_first.astype(jnp.bfloat16), "tm", scatter_dimension=1, tiled=True
        ).astype(jnp.float32),
        lax.psum_scatter(
            part_second.astype(jnp.bfloat16), "tm", scatter_dimension=1, tiled=True
        ).astype(jnp.float32),
        lax.psum_scatter(
            part_third.astype(jnp.bfloat16), "tm", scatter_dimension=1, tiled=True
        ).astype(jnp.float32),
        lax.psum_scatter(
            part_last.astype(jnp.bfloat16), "tm", scatter_dimension=1, tiled=True
        ).astype(jnp.float32),
    )
    return (new_links, grad_first, grad_second, grad_third, grad_last)


def solution(mesh):
    placed = (
        P(None, None, None, None, "groups", "tm", None),
        P(None, None, None, None, "groups", "tm", None),
        P("groups", "tm"),
        P("groups", "tm"),
        P("tm"),
        P("tm"),
        P("tm"),
        P("tm"),
    )
    return jax.shard_map(
        on_device,
        mesh=mesh,
        in_specs=placed,
        out_specs=(
            P(None, None, None, None, "groups", "tm", None),
            P("groups", "tm"),
            P("groups", "tm"),
            P("groups", "tm"),
            P("groups", "tm"),
        ),
        check_vma=False,
    )
```

profile of v0, /device:TPU:0, one launch (start us, length us, event | category | flops | bytes accessed | tf_op | source)
XLA Modules:
  0.0 440.1 jit_solution(11352301790095417479)
XLA Ops:
  8.6 5.5 %collective-permute-start.1 = (bf16[4,2,3,3,1,1,512]{6,5,3,2,1,4,0:T(2,128)(2,1)S(1)}, bf16[4,2,3,3,1,1,512]{6,5,3,2,1,4,0:T(2,128)(2,1)S(1)}, u32[]{:S(2)}, u32[]{:S(2)}) collective-permute-start(bf16[4,2,3,3,1,1,512]{6,5,3,2,1,4,0:T(2,128)(2,1)S(1)} %get-tuple-element.645), channel_id=1, source_target_pairs={{1,0},{2,1},{3,2},{4,3},{5,4},{6,5},{7,6},{8,7},{9,8},{10,9},{11,1... | collective-permute-start | bytes 221192 | tf_op jit(solution)/shard_map/ppermute | solution.py:32
  24.2 19.4 %all-gather = bf16[32,3,3,1,512]{4,2,3,1,0:T(4,128)(2,1)S(1)} all-gather(bf16[2,3,3,1,512]{4,2,3,1,0:T(4,128)(2,1)S(1)} %convert_bitcast_fusion), channel_id=2, replica_groups=mesh['groups'=2,'tm'=16] {'tm'}, dimensions={0}, use_global_device_ids=true | all-gather | bytes 313344 | tf_op jit(solution)/shard_map/all_gather | solution.py:212
  43.9 6.8 %while.27 = (s32[]{:T(128)}, f32[2,3,3,1,512]{4,2,1,3,0:T(4,128)S(1)}, f32[16,2,3,3,1,512]{5,3,2,4,1,0:T(4,128)S(1)}, s32[]{:T(128)}, s32[]{:T(128)}, /*index=5*/s32[]{}) while((s32[]{:T(128)}, f32[2,3,3,1,512]{4,2,1,3,0:T(4,128)S(1)}, f32[16,2,3,3,1,512]{5,3,2,4,1,0:T(4,128)S(1)}, s32[]{:T(128)}, s32[]{:T(128)}, /*index=5*/s32[]{}) %tuple.641), condition=%wide.region_83.84_spmd, body=%wide.region_78.83_spmd.sunk | while | flops 110595 | bytes 479329 | solution.py:219
  53.6 57.4 %all-reduce.11.cloned.1.call-done = (bf16[3456]{0:T(1024)(128)(2,1)}, bf16[20736]{0:T(1024)(128)(2,1)}, bf16[20736]{0:T(1024)(128)(2,1)}, bf16[1728]{0:T(1024)(128)(2,1)}) async-done(((bf16[3456]{0:T(1024)(128)(2,1)}, bf16[20736]{0:T(1024)(128)(2,1)}, bf16[20736]{0:T(1024)(128)(2,1)}, bf16[1728]{0:T(1024)(128)(2,1)}), (bf16[3456]{0:T(1024)(128)(2,1)}, bf16[20736]{0:T(1024)(128)(2,1)}, ...) | async-done | bytes 93328
  137.2 2.1 multiply_reduce_fusion.210
  144.3 1.7 multiply_reduce_fusion.226
  158.5 4.4 %collective-permute-start.2 = (bf16[8,1,1,512]{3,0,2,1:T(8,128)(2,1)S(1)}, bf16[8,1,1,512]{3,0,2,1:T(8,128)(2,1)S(1)}, u32[]{:S(2)}, u32[]{:S(2)}) collective-permute-start(bf16[8,1,1,512]{3,0,2,1:T(8,128)(2,1)S(1)} %get-tuple-element.894), channel_id=1, source_target_pairs={{1,0},{2,1},{3,2},{4,3},{5,4},{6,5},{7,6},{8,7},{9,8},{10,9},{11,1... | collective-permute-start | bytes 24584 | tf_op jit(solution)/shard_map/ppermute | solution.py:32
  176.2 4.4 %collective-permute-start.4 = (bf16[48,1,1,512]{3,2,0,1:T(2,128)(2,1)S(1)}, bf16[48,1,1,512]{3,2,0,1:T(2,128)(2,1)S(1)}, u32[]{:S(2)}, u32[]{:S(2)}) collective-permute-start(bf16[48,1,1,512]{3,2,0,1:T(2,128)(2,1)S(1)} %get-tuple-element.745), channel_id=1, source_target_pairs={{1,0},{2,1},{3,2},{4,3},{5,4},{6,5},{7,6},{8,7},{9,8},{10,9},{11,1... | collective-permute-start | bytes 147464 | tf_op jit(solution)/shard_map/ppermute | solution.py:32
  181.0 2.0 collective-permute-done.5
  188.8 4.7 %collective-permute-start.6 = (bf16[48,1,1,512]{3,2,0,1:T(2,128)(2,1)S(1)}, bf16[48,1,1,512]{3,2,0,1:T(2,128)(2,1)S(1)}, u32[]{:S(2)}, u32[]{:S(2)}) collective-permute-start(bf16[48,1,1,512]{3,2,0,1:T(2,128)(2,1)S(1)} %get-tuple-element.721), channel_id=1, source_target_pairs={{1,0},{2,1},{3,2},{4,3},{5,4},{6,5},{7,6},{8,7},{9,8},{10,9},{11,1... | collective-permute-start | bytes 147464 | tf_op jit(solution)/shard_map/ppermute | solution.py:32
  193.9 1.7 collective-permute-done.7
  201.8 4.6 %collective-permute-start.8 = (bf16[48,1,1,512]{3,2,0,1:T(2,128)(2,1)S(1)}, bf16[48,1,1,512]{3,2,0,1:T(2,128)(2,1)S(1)}, u32[]{:S(2)}, u32[]{:S(2)}) collective-permute-start(bf16[48,1,1,512]{3,2,0,1:T(2,128)(2,1)S(1)} %get-tuple-element.697), channel_id=1, source_target_pairs={{1,0},{2,1},{3,2},{4,3},{5,4},{6,5},{7,6},{8,7},{9,8},{10,9},{11,1... | collective-permute-start | bytes 147464 | tf_op jit(solution)/shard_map/ppermute | solution.py:32
  206.7 1.9 collective-permute-done.9
  222.4 1.9 fusion.58
  228.7 4.6 %collective-permute-start.11 = (bf16[4,1,1,512]{3,2,0,1:T(2,128)(2,1)}, bf16[4,1,1,512]{3,2,0,1:T(2,128)(2,1)S(1)}, u32[]{:S(2)}, u32[]{:S(2)}) collective-permute-start(bf16[4,1,1,512]{3,2,0,1:T(2,128)(2,1)} %get-tuple-element.917), channel_id=1, source_target_pairs={{1,0},{2,1},{3,2},{4,3},{5,4},{6,5},{7,6},{8,7},{9,8},{10,9},{11,1... | collective-permute-start | bytes 12296 | tf_op jit(solution)/shard_map/ppermute | solution.py:32
  254.6 4.4 %collective-permute-start.13 = (bf16[48,1,1,512]{3,2,0,1:T(2,128)(2,1)}, bf16[48,1,1,512]{3,2,0,1:T(2,128)(2,1)}, u32[]{:S(2)}, u32[]{:S(2)}) collective-permute-start(bf16[48,1,1,512]{3,2,0,1:T(2,128)(2,1)} %get-tuple-element.672), channel_id=1, source_target_pairs={{1,0},{2,1},{3,2},{4,3},{5,4},{6,5},{7,6},{8,7},{9,8},{10,9},{11,1... | collective-permute-start | bytes 147464 | tf_op jit(solution)/shard_map/ppermute | solution.py:32
  260.1 7.0 %convert_element_type.423 = bf16[1,20736]{0,1:T(8,128)(2,1)} reshape(bf16[9,48,48]{2,1,0:T(8,128)(2,1)S(1)} %fusion.9) | data formatting | bytes 82944 | tf_op jit(solution)/shard_map/convert_element_type | solution.py:267
  274.7 2.8 constant_dynamic-update-slice_fusion.24
  284.9 4.4 %collective-permute-start.15 = (bf16[48,1,1,512]{3,2,0,1:T(2,128)(2,1)}, bf16[48,1,1,512]{3,2,0,1:T(2,128)(2,1)}, u32[]{:S(2)}, u32[]{:S(2)}) collective-permute-start(bf16[48,1,1,512]{3,2,0,1:T(2,128)(2,1)} %get-tuple-element.648), channel_id=1, source_target_pairs={{1,0},{2,1},{3,2},{4,3},{5,4},{6,5},{7,6},{8,7},{9,8},{10,9},{11,1... | collective-permute-start | bytes 147464 | tf_op jit(solution)/shard_map/ppermute | solution.py:32
  292.0 7.1 %convert_element_type.422 = bf16[1,20736]{0,1:T(8,128)(2,1)} reshape(bf16[9,48,48]{2,1,0:T(8,128)(2,1)S(1)} %fusion.8) | data formatting | bytes 82944 | tf_op jit(solution)/shard_map/convert_element_type | solution.py:264
  302.1 46.0 %reduce-scatter.11.cloned.1.call-done = bf16[1296,1]{1,0:T(8,128)(2,1)} async-done(((bf16[20736,1]{1,0:T(8,128)(2,1)}), bf16[1296,1]{1,0:T(8,128)(2,1)}) %reduce-scatter.11.cloned.1.call-update) | async-done | bytes 2608
  352.7 2.3 fusion.10
  355.3 60.2 %all-reduce.7 = (bf16[1,3456]{1,0:T(2,128)(2,1)S(1)}, bf16[1,1728]{1,0:T(2,128)(2,1)S(1)}) all-reduce(bf16[1,3456]{1,0:T(2,128)(2,1)S(1)} %convert_element_type.403, bf16[1,1728]{1,0:T(2,128)(2,1)S(1)} %copy-done.84), channel_id=3, replica_groups=mesh['groups'=2,'tm'=16] {'tm'}, use_global_device_ids=true, to_apply=%region_328.329.clone | all-reduce | flops 5184 | bytes 20736
  416.7 15.0 %reduce-scatter.9.cloned.1.call-done = bf16[1296,1]{1,0:T(8,128)(2,1)} async-done(((bf16[20736,1]{1,0:T(8,128)(2,1)}), bf16[1296,1]{1,0:T(8,128)(2,1)}) %reduce-scatter.9.cloned.1.call-update) | async-done | bytes 2608
  (1049 shorter events, 154.0 us)
Async XLA Ops:
  7.2 103.9 %all-reduce.11.cloned.1.call-start = ((), (), s32[]{:S(2)}) async-start(), calls=%async_computation.4 | async-start | bytes 196608
  8.6 108.8 %collective-permute-start.1 = (bf16[4,2,3,3,1,1,512]{6,5,3,2,1,4,0:T(2,128)(2,1)S(1)}, bf16[4,2,3,3,1,1,512]{6,5,3,2,1,4,0:T(2,128)(2,1)S(1)}, u32[]{:S(2)}, u32[]{:S(2)}) collective-permute-start(bf16[4,2,3,3,1,1,512]{6,5,3,2,1,4,0:T(2,128)(2,1)S(1)} %get-tuple-element.645), channel_id=1, source_target_pairs={{1,0},{2,1},{3,2},{4,3},{5,4},{6,5},{7,6},{8,7},{9,8},{10,9},{11,1... | collective-permute-start | bytes 221192 | tf_op jit(solution)/shard_map/ppermute | solution.py:32
  14.1 103.4 %collective-permute-start = (bf16[4,2,3,3,1,1,512]{6,5,3,2,1,4,0:T(2,128)(2,1)S(1)}, bf16[4,2,3,3,1,1,512]{6,5,3,2,1,4,0:T(2,128)(2,1)S(1)}, u32[]{:S(2)}, u32[]{:S(2)}) collective-permute-start(bf16[4,2,3,3,1,1,512]{6,5,3,2,1,4,0:T(2,128)(2,1)S(1)} %get-tuple-element.644), channel_id=1, source_target_pairs={{0,1},{1,2},{2,3},{3,4},{4,5},{5,6},{6,7},{7,8},{8,9},{9,10},{10,1... | collective-permute-start | bytes 221192 | tf_op jit(solution)/shard_map/ppermute | solution.py:29
  21.6 326.4 %reduce-scatter.11.cloned.1.call-start = ((), (), s32[]{:S(2)}) async-start(), calls=%async_computation.3 | async-start | bytes 5640192
  21.7 98.8 %copy-start.95 = (pred[512]{0:T(512)(128)(4,1)}, pred[512]{0:T(512)(128)(4,1)S(1)}, u32[]{:S(2)}) copy-start(pred[512]{0:T(512)(128)(4,1)S(1)} %broadcast_compare_fusion.2) | copy-start | bytes 1540
  50.8 66.7 %copy-start.85 = (bf16[2,1,1,1,512]{4,0,1,3,2:T(2,128)(2,1)}, bf16[2,1,1,1,512]{4,0,1,3,2:T(2,128)(2,1)S(1)}, u32[]{:S(2)}) copy-start(bf16[2,1,1,1,512]{4,0,1,3,2:T(2,128)(2,1)S(1)} %copy.1116) | copy-start | bytes 6148
  52.3 118.2 %copy-start.55 = (pred[1,4,4,128]{3,1,2,0:T(4,128)(4,1)}, pred[1,4,4,128]{3,1,2,0:T(4,128)(4,1)S(1)}, u32[]{:S(2)}) copy-start(pred[1,4,4,128]{3,1,2,0:T(4,128)(4,1)S(1)} %copy.774) | copy-start | bytes 6148
  52.3 118.2 %copy-start.63 = (pred[1,4,4,128]{3,1,2,0:T(4,128)(4,1)}, pred[1,4,4,128]{3,1,2,0:T(4,128)(4,1)S(1)}, u32[]{:S(2)}) copy-start(pred[1,4,4,128]{3,1,2,0:T(4,128)(4,1)S(1)} %copy.775) | copy-start | bytes 6148
  52.4 118.2 %copy-start.59 = (pred[1,4,4,128]{3,1,2,0:T(4,128)(4,1)}, pred[1,4,4,128]{3,1,2,0:T(4,128)(4,1)S(1)}, u32[]{:S(2)}) copy-start(pred[1,4,4,128]{3,1,2,0:T(4,128)(4,1)S(1)} %copy.777) | copy-start | bytes 6148
  158.4 12.4 %collective-permute-start.3 = (bf16[8,1,1,512]{3,0,2,1:T(8,128)(2,1)S(1)}, bf16[8,1,1,512]{3,0,2,1:T(8,128)(2,1)S(1)}, u32[]{:S(2)}, u32[]{:S(2)}) collective-permute-start(bf16[8,1,1,512]{3,0,2,1:T(8,128)(2,1)S(1)} %get-tuple-element.893), channel_id=1, source_target_pairs={{0,1},{1,2},{2,3},{3,4},{4,5},{5,6},{6,7},{7,8},{8,9},{9,10},{10,1... | collective-permute-start | bytes 24584 | tf_op jit(solution)/shard_map/ppermute | solution.py:29
  158.5 12.4 %collective-permute-start.2 = (bf16[8,1,1,512]{3,0,2,1:T(8,128)(2,1)S(1)}, bf16[8,1,1,512]{3,0,2,1:T(8,128)(2,1)S(1)}, u32[]{:S(2)}, u32[]{:S(2)}) collective-permute-start(bf16[8,1,1,512]{3,0,2,1:T(8,128)(2,1)S(1)} %get-tuple-element.894), channel_id=1, source_target_pairs={{1,0},{2,1},{3,2},{4,3},{5,4},{6,5},{7,6},{8,7},{9,8},{10,9},{11,1... | collective-permute-start | bytes 24584 | tf_op jit(solution)/shard_map/ppermute | solution.py:32
  176.2 6.8 %collective-permute-start.5 = (bf16[48,1,1,512]{3,2,0,1:T(2,128)(2,1)S(1)}, bf16[48,1,1,512]{3,2,0,1:T(2,128)(2,1)S(1)}, u32[]{:S(2)}, u32[]{:S(2)}) collective-permute-start(bf16[48,1,1,512]{3,2,0,1:T(2,128)(2,1)S(1)} %get-tuple-element.744), channel_id=1, source_target_pairs={{0,1},{1,2},{2,3},{3,4},{4,5},{5,6},{6,7},{7,8},{8,9},{9,10},{10,1... | collective-permute-start | bytes 147464 | tf_op jit(solution)/shard_map/ppermute | solution.py:29
  176.2 6.7 %collective-permute-start.4 = (bf16[48,1,1,512]{3,2,0,1:T(2,128)(2,1)S(1)}, bf16[48,1,1,512]{3,2,0,1:T(2,128)(2,1)S(1)}, u32[]{:S(2)}, u32[]{:S(2)}) collective-permute-start(bf16[48,1,1,512]{3,2,0,1:T(2,128)(2,1)S(1)} %get-tuple-element.745), channel_id=1, source_target_pairs={{1,0},{2,1},{3,2},{4,3},{5,4},{6,5},{7,6},{8,7},{9,8},{10,9},{11,1... | collective-permute-start | bytes 147464 | tf_op jit(solution)/shard_map/ppermute | solution.py:32
  188.8 6.8 %collective-permute-start.7 = (bf16[48,1,1,512]{3,2,0,1:T(2,128)(2,1)S(1)}, bf16[48,1,1,512]{3,2,0,1:T(2,128)(2,1)S(1)}, u32[]{:S(2)}, u32[]{:S(2)}) collective-permute-start(bf16[48,1,1,512]{3,2,0,1:T(2,128)(2,1)S(1)} %get-tuple-element.720), channel_id=1, source_target_pairs={{0,1},{1,2},{2,3},{3,4},{4,5},{5,6},{6,7},{7,8},{8,9},{9,10},{10,1... | collective-permute-start | bytes 147464 | tf_op jit(solution)/shard_map/ppermute | solution.py:29
  188.8 6.9 %collective-permute-start.6 = (bf16[48,1,1,512]{3,2,0,1:T(2,128)(2,1)S(1)}, bf16[48,1,1,512]{3,2,0,1:T(2,128)(2,1)S(1)}, u32[]{:S(2)}, u32[]{:S(2)}) collective-permute-start(bf16[48,1,1,512]{3,2,0,1:T(2,128)(2,1)S(1)} %get-tuple-element.721), channel_id=1, source_target_pairs={{1,0},{2,1},{3,2},{4,3},{5,4},{6,5},{7,6},{8,7},{9,8},{10,9},{11,1... | collective-permute-start | bytes 147464 | tf_op jit(solution)/shard_map/ppermute | solution.py:32
  201.7 6.9 %collective-permute-start.9 = (bf16[48,1,1,512]{3,2,0,1:T(2,128)(2,1)S(1)}, bf16[48,1,1,512]{3,2,0,1:T(2,128)(2,1)S(1)}, u32[]{:S(2)}, u32[]{:S(2)}) collective-permute-start(bf16[48,1,1,512]{3,2,0,1:T(2,128)(2,1)S(1)} %get-tuple-element.696), channel_id=1, source_target_pairs={{0,1},{1,2},{2,3},{3,4},{4,5},{5,6},{6,7},{7,8},{8,9},{9,10},{10,1... | collective-permute-start | bytes 147464 | tf_op jit(solution)/shard_map/ppermute | solution.py:29
  201.8 6.8 %collective-permute-start.8 = (bf16[48,1,1,512]{3,2,0,1:T(2,128)(2,1)S(1)}, bf16[48,1,1,512]{3,2,0,1:T(2,128)(2,1)S(1)}, u32[]{:S(2)}, u32[]{:S(2)}) collective-permute-start(bf16[48,1,1,512]{3,2,0,1:T(2,128)(2,1)S(1)} %get-tuple-element.697), channel_id=1, source_target_pairs={{1,0},{2,1},{3,2},{4,3},{5,4},{6,5},{7,6},{8,7},{9,8},{10,9},{11,1... | collective-permute-start | bytes 147464 | tf_op jit(solution)/shard_map/ppermute | solution.py:32
  228.7 12.3 %collective-permute-start.11 = (bf16[4,1,1,512]{3,2,0,1:T(2,128)(2,1)}, bf16[4,1,1,512]{3,2,0,1:T(2,128)(2,1)S(1)}, u32[]{:S(2)}, u32[]{:S(2)}) collective-permute-start(bf16[4,1,1,512]{3,2,0,1:T(2,128)(2,1)} %get-tuple-element.917), channel_id=1, source_target_pairs={{1,0},{2,1},{3,2},{4,3},{5,4},{6,5},{7,6},{8,7},{9,8},{10,9},{11,1... | collective-permute-start | bytes 12296 | tf_op jit(solution)/shard_map/ppermute | solution.py:32
  233.3 7.7 %collective-permute-start.10 = (bf16[4,1,1,512]{3,2,0,1:T(2,128)(2,1)}, bf16[4,1,1,512]{3,2,0,1:T(2,128)(2,1)}, u32[]{:S(2)}, u32[]{:S(2)}) collective-permute-start(bf16[4,1,1,512]{3,2,0,1:T(2,128)(2,1)} %get-tuple-element.918), channel_id=1, source_target_pairs={{0,1},{1,2},{2,3},{3,4},{4,5},{5,6},{6,7},{7,8},{8,9},{9,10},{10,1... | collective-permute-start | bytes 12296 | tf_op jit(solution)/shard_map/ppermute | solution.py:29
  254.6 17.2 %collective-permute-start.13 = (bf16[48,1,1,512]{3,2,0,1:T(2,128)(2,1)}, bf16[48,1,1,512]{3,2,0,1:T(2,128)(2,1)}, u32[]{:S(2)}, u32[]{:S(2)}) collective-permute-start(bf16[48,1,1,512]{3,2,0,1:T(2,128)(2,1)} %get-tuple-element.672), channel_id=1, source_target_pairs={{1,0},{2,1},{3,2},{4,3},{5,4},{6,5},{7,6},{8,7},{9,8},{10,9},{11,1... | collective-permute-start | bytes 147464 | tf_op jit(solution)/shard_map/ppermute | solution.py:32
  259.1 12.8 %collective-permute-start.12 = (bf16[48,1,1,512]{3,2,0,1:T(2,128)(2,1)}, bf16[48,1,1,512]{3,2,0,1:T(2,128)(2,1)}, u32[]{:S(2)}, u32[]{:S(2)}) collective-permute-start(bf16[48,1,1,512]{3,2,0,1:T(2,128)(2,1)} %get-tuple-element.673), channel_id=1, source_target_pairs={{0,1},{1,2},{2,3},{3,4},{4,5},{5,6},{6,7},{7,8},{8,9},{9,10},{10,1... | collective-permute-start | bytes 147464 | tf_op jit(solution)/shard_map/ppermute | solution.py:29
  267.2 164.5 %reduce-scatter.9.cloned.1.call-start = ((), (), s32[]{:S(2)}) async-start(), calls=%async_computation.2 | async-start | bytes 5640192
  284.9 64.9 %collective-permute-start.15 = (bf16[48,1,1,512]{3,2,0,1:T(2,128)(2,1)}, bf16[48,1,1,512]{3,2,0,1:T(2,128)(2,1)}, u32[]{:S(2)}, u32[]{:S(2)}) collective-permute-start(bf16[48,1,1,512]{3,2,0,1:T(2,128)(2,1)} %get-tuple-element.648), channel_id=1, source_target_pairs={{1,0},{2,1},{3,2},{4,3},{5,4},{6,5},{7,6},{8,7},{9,8},{10,9},{11,1... | collective-permute-start | bytes 147464 | tf_op jit(solution)/shard_map/ppermute | solution.py:32
  289.3 60.5 %collective-permute-start.14 = (bf16[48,1,1,512]{3,2,0,1:T(2,128)(2,1)}, bf16[48,1,1,512]{3,2,0,1:T(2,128)(2,1)}, u32[]{:S(2)}, u32[]{:S(2)}) collective-permute-start(bf16[48,1,1,512]{3,2,0,1:T(2,128)(2,1)} %get-tuple-element.649), channel_id=1, source_target_pairs={{0,1},{1,2},{2,3},{3,4},{4,5},{5,6},{6,7},{7,8},{8,9},{9,10},{10,1... | collective-permute-start | bytes 147464 | tf_op jit(solution)/shard_map/ppermute | solution.py:29
  (97 other events, 741.6 us)
Sparse Core Ops, SparseCore 0:
  21.7 89.2 all-reduce.10
  267.3 80.6 reduce-scatter.10
  352.6 79.0 reduce-scatter.8
where the time goes:
time: 445 us; the launch traced here: 440 us
  waiting for transfers between devices  124 us (28%)
  other arithmetic  84.9 us (19%)
  blocking collectives  79.6 us (18%)
  local copies, waits for them, and re-layouts  77 us (17%)
  starting transfers between devices  38 us (9%)
  between operations  21.3 us (5%)
  matrix products  14.1 us (3%)
    unnamed x6, waiting for transfers between devices  118 us
    unnamed x1, blocking collectives  60.2 us
    ppermute x8, starting transfers between devices, extended_2(): lax.ppermute(lax.slice_in_dim(block, 0, width, axis=dim), axis, backward)  37 us
    reduce_sum x76, other arithmetic, real_product(): return jnp.sum(left[:, :, None] * right[None], axis=1)  27.1 us
    unnamed x323, local copies, waits for them, and re-layouts  25.7 us
    all_gather x1, blocking collectives, on_device(): lax.all_gather(slab[None].astype(jnp.bfloat16), 'tm', axis=0, tiled=True)  19.4 us
  transfers between devices with their start and end apart: 19, of which 7 were waited for; matrix products, arithmetic and copies ran while one was open for 19% of the time, Pallas kernels for 0%

commit v1 on v0

v1 whole, which is shorter than its diff:
```python
import functools

import jax
import jax.numpy as jnp
from jax import lax
from jax.experimental import pallas as pl
from jax.experimental.pallas import tpu as pltpu
from jax.sharding import PartitionSpec as P

F32 = jnp.float32
BF16 = jnp.bfloat16
TAPS = 9
H = 48
LANES = 128
SITES = 512
PAIRS = ((0, 1), (0, 2), (0, 3), (1, 2), (1, 3), (2, 3))
SWAP = (0, 2, 1, 4, 3, 6, 5, 8, 7)
ENTRIES = tuple((c, i, j) for c in range(2) for i in range(3) for j in range(3))
SLABROWS = 80
BLOCKROWS = 112
LIMIT = 40 * 1024 * 1024


def lane_iota(rows):
    return lax.broadcasted_iota(jnp.int32, (rows, LANES), 1)


def row_iota():
    return lax.broadcasted_iota(jnp.int32, (8, LANES), 0)


def roll_lanes(value, amount):
    return pltpu.roll(value, amount % LANES, 1)


def shift_z(chunk, sign, lanes):
    z = lanes % 8
    if sign > 0:
        return jnp.where(z == 7, roll_lanes(chunk, 7), roll_lanes(chunk, -1))
    return jnp.where(z == 0, roll_lanes(chunk, -7), roll_lanes(chunk, 1))


def shift_y(chunk, sign, lanes):
    y = lanes // 8 % 8
    if sign > 0:
        return jnp.where(y == 7, roll_lanes(chunk, 56), roll_lanes(chunk, -8))
    return jnp.where(y == 0, roll_lanes(chunk, -56), roll_lanes(chunk, 8))


def dense_shift(pair, axis, sign):
    lanes = lane_iota(8)
    if axis == 2:
        return [shift_z(chunk, sign, lanes) for chunk in pair]
    if axis == 1:
        return [shift_y(chunk, sign, lanes) for chunk in pair]
    low = lanes < 64
    first, second = [roll_lanes(chunk, 64) for chunk in pair]
    if sign > 0:
        return [jnp.where(low, first, second), jnp.where(low, second, pltpu.roll(first, 4, 0))]
    return [jnp.where(low, pltpu.roll(second, 4, 0), first), jnp.where(low, first, second)]


def pack_pair(value):
    return [
        jnp.concatenate([value[:, c * 128:c * 128 + 128], value[:, 256 + c * 128:384 + c * 128]], axis=0)
        for c in range(2)
    ]


def halo_pair(ref, index):
    top = row_iota() < 4
    pair = []
    for c in range(2):
        low = jnp.broadcast_to(ref[index, c:c + 1, :], (8, LANES))
        high = jnp.broadcast_to(ref[index, 2 + c:3 + c, :], (8, LANES))
        pair.append(jnp.where(top, low, high))
    return pair


def load_matrix(read):
    real = [[read(3 * i + j) for j in range(3)] for i in range(3)]
    imag = [[read(9 + 3 * i + j) for j in range(3)] for i in range(3)]
    return (real, imag, 1)


def dagger(matrix):
    real, imag, sign = matrix
    return (
        [[real[j][i] for j in range(3)] for i in range(3)],
        [[imag[j][i] for j in range(3)] for i in range(3)],
        -sign,
    )


def total(terms, signs):
    value = None
    for term, sign in zip(terms, signs):
        if value is None:
            value = term if sign > 0 else -term
        else:
            value = value + term if sign > 0 else value - term
    return value


def mat_mul(left, right):
    lr, li, ls = left
    rr, ri, rs = right
    same = ls == rs
    real = [[None] * 3 for _ in range(3)]
    imag = [[None] * 3 for _ in range(3)]
    for i in range(3):
        for j in range(3):
            real[i][j] = total(
                [lr[i][k] * rr[k][j] for k in range(3)] + [li[i][k] * ri[k][j] for k in range(3)],
                [1, 1, 1] + [-1 if same else 1] * 3,
            )
            imag[i][j] = total(
                [lr[i][k] * ri[k][j] for k in range(3)] + [li[i][k] * rr[k][j] for k in range(3)],
                [1, 1, 1] + [1 if same else -1] * 3,
            )
    return (real, imag, ls if same else rs)


def imag_of(matrix, i, j):
    return matrix[1][i][j] if matrix[2] > 0 else -matrix[1][i][j]


def store_matrix(matrix, write):
    for i in range(3):
        for j in range(3):
            write(3 * i + j, matrix[0][i][j])
            write(9 + 3 * i + j, imag_of(matrix, i, j))


def anti_parts(matrix):
    parts = [2.0 * imag_of(matrix, i, i) for i in range(3)]
    for i, j in ((0, 1), (0, 2), (1, 2)):
        parts.append(matrix[0][i][j] - matrix[0][j][i])
        parts.append(imag_of(matrix, i, j) + imag_of(matrix, j, i))
    return parts


def anti_matrix(parts):
    zero = jnp.zeros_like(parts[0])
    real = [[zero, parts[3], parts[5]], [-parts[3], zero, parts[7]], [-parts[5], -parts[7], zero]]
    imag = [[parts[0], parts[4], parts[6]], [parts[4], parts[1], parts[8]], [parts[6], parts[8], parts[2]]]
    return real, imag


def anti_mul(parts, right):
    real, imag = anti_matrix(parts)
    rr, ri, _ = right
    out_r = [[None] * 3 for _ in range(3)]
    out_i = [[None] * 3 for _ in range(3)]
    for i in range(3):
        for j in range(3):
            value_r = -(imag[i][i] * ri[i][j])
            value_i = imag[i][i] * rr[i][j]
            for k in range(3):
                if k != i:
                    value_r = value_r + real[i][k] * rr[k][j] - imag[i][k] * ri[k][j]
                    value_i = value_i + real[i][k] * ri[k][j] + imag[i][k] * rr[k][j]
            out_r[i][j] = value_r
            out_i[i][j] = value_i
    return (out_r, out_i, 1)


def pack_links(links_ref, dense):
    def body(mu, carry):
        for e, (c, i, j) in enumerate(ENTRIES):
            low, high = pack_pair(links_ref[mu, c, i, j, 0].astype(F32))
            dense[mu, e, 0] = low
            dense[mu, e, 1] = high
        return carry

    lax.fori_loop(0, 4, body, 0)


def first_kernel(widths, links_ref, w1_ref, w2_ref, w3_ref, w4_ref, up_ref, down_ref, block_ref, dense, moved, rows, block):
    pack_links(links_ref, dense)

    def shift_body(e, carry):
        pair = [dense[3, e, 0], dense[3, e, 1]]
        for mu in range(3):
            low, high = dense_shift(pair, mu, 1)
            moved[mu, e, 0] = low
            moved[mu, e, 1] = high
        return carry

    lax.fori_loop(0, 18, shift_body, 0)

    for mu in range(3):
        def staple_body(c, carry):
            u_mu = load_matrix(lambda e: dense[mu, e, c])
            u_t = load_matrix(lambda e: dense[3, e, c])
            edge = mat_mul(u_mu, load_matrix(lambda e: moved[mu, e, c]))
            staple = mat_mul(dagger(edge), u_t)

            def write(e, value):
                rows[mu * 18 + e, pl.ds(c, 1)] = value[3:4]
                rows[mu * 18 + e, pl.ds(2 + c, 1)] = value[7:8]

            store_matrix(staple, write)
            return carry

        lax.fori_loop(0, 2, staple_body, 0)
    for q in range(4):
        up_ref[:, q * 128:q * 128 + 128] = rows[:, q, :].astype(BF16)
    for mu in range(3):
        for e in range(18):
            for c in range(2):
                value = dense[mu, e, c]
                rows[mu * 18 + e, c:c + 1] = value[0:1]
                rows[mu * 18 + e, 2 + c:3 + c] = value[4:5]
    for q in range(4):
        down_ref[:, q * 128:q * 128 + 128] = rows[:, q, :].astype(BF16)

    block[...] = jnp.zeros_like(block)

    def slab_body(c, carry):
        u_t = load_matrix(lambda e: dense[3, e, c])
        ahead = load_matrix(lambda e: pltpu.roll(dense[3, e, c], 7, 0))
        two = mat_mul(u_t, ahead)
        later = tuple(
            [[pltpu.roll(part[i][j], 6, 0) for j in range(3)] for i in range(3)] for part in two[:2]
        ) + (two[2],)
        four = mat_mul(two, later)

        def write(e, value):
            block[pl.ds(4 * e + c, 1), :] = value[0:1]
            block[pl.ds(4 * e + 2 + c, 1), :] = value[4:5]

        store_matrix(four, write)
        return carry

    lax.fori_loop(0, 2, slab_body, 0)
    offset = 0
    for ref, width in zip((w2_ref, w3_ref, w1_ref, w4_ref), widths):
        flat = ref[...].astype(F32)
        for r in range(27):
            block[SLABROWS + r:SLABROWS + r + 1, offset:offset + width] = flat[:, width * r:width * r + width]
        offset += width
    block_ref[...] = block[...].astype(BF16)


def gauge_kernel(
    links_ref, cot_ref, up_ref, down_ref, parity_ref, subset_ref,
    fm_ref, fup_ref, fdown_ref, w1_ref, w2_ref,
    dense, cots, moved, staples, sums, halo_up, halo_down, forces, rows,
):
    pack_links(links_ref, dense)
    pack_links(cot_ref, cots)
    for q in range(4):
        halo_up[:, q, :] = up_ref[:, q * 128:q * 128 + 128].astype(F32)
        halo_down[:, q, :] = down_ref[:, q * 128:q * 128 + 128].astype(F32)
    rows[...] = jnp.zeros_like(rows)
    forces[...] = jnp.zeros_like(forces)
    steps = row_iota() % 4
    lanes = lane_iota(8)

    def shift_body(e, carry):
        for nu in range(4):
            pair = [dense[nu, e, 0], dense[nu, e, 1]]
            for mu in range(3):
                if mu != nu:
                    low, high = dense_shift(pair, mu, 1)
                    moved[mu, nu, e, 0] = low
                    moved[mu, nu, e, 1] = high
            if nu < 3:
                halo = halo_pair(halo_down, nu * 18 + e)
                for c in range(2):
                    moved[3, nu, e, c] = jnp.where(steps == 3, halo[c], pltpu.roll(pair[c], 7, 0))
        return carry

    lax.fori_loop(0, 18, shift_body, 0)

    def put_row(channel, c, value):
        for t in range(4):
            rows[t, c, pl.ds(channel, 1), :] = value[t:t + 1]
            rows[t, 2 + c, pl.ds(channel, 1), :] = value[4 + t:5 + t]

    def plane_body(step, carry):
        plane = step // 2
        c = step % 2
        mu = jnp.where(plane < 3, 0, jnp.where(plane < 5, 1, 2))
        nu = jnp.where(plane < 3, plane + 1, jnp.where(plane < 5, plane - 1, 3))
        u_mu = load_matrix(lambda e: dense[mu, e, c])
        u_nu = load_matrix(lambda e: dense[nu, e, c])
        one = mat_mul(u_mu, load_matrix(lambda e: moved[mu, nu, e, c]))
        two = mat_mul(u_nu, load_matrix(lambda e: moved[nu, mu, e, c]))
        loop = mat_mul(one, dagger(two))
        put_row(plane, c, (loop[0][0][0] + loop[0][1][1] + loop[0][2][2]) / 3.0)
        for e, part in enumerate(anti_parts(loop)):
            forces[mu, e, c] += part
            forces[nu, e, c] -= part

        def write_mu(e, value):
            staples[mu, nu, e, c] = value

        def write_nu(e, value):
            staples[nu, mu, e, c] = value

        store_matrix(mat_mul(dagger(one), u_nu), write_mu)
        store_matrix(mat_mul(dagger(two), u_mu), write_nu)
        return carry

    lax.fori_loop(0, 12, plane_body, 0)

    def lower_body(e, carry):
        for mu in range(4):
            acc = [None, None]
            for nu in range(4):
                if nu == mu:
                    continue
                pair = [staples[mu, nu, e, 0], staples[mu, nu, e, 1]]
                if nu < 3:
                    pair = dense_shift(pair, nu, -1)
                else:
                    halo = halo_pair(halo_up, mu * 18 + e)
                    pair = [jnp.where(steps == 0, halo[c], pltpu.roll(pair[c], 1, 0)) for c in range(2)]
                acc = [pair[c] if acc[c] is None else acc[c] + pair[c] for c in range(2)]
            sums[mu, e, 0] = acc[0]
            sums[mu, e, 1] = acc[1]
        return carry

    lax.fori_loop(0, 18, lower_body, 0)

    colour = (lanes // 64 + lanes // 8 % 8 + lanes % 8 + steps) % 2
    parity = jnp.zeros_like(steps)
    subset = jnp.zeros_like(steps)
    for t in range(4):
        parity = jnp.where(steps == t, parity_ref[0, t], parity)
        subset = jnp.where(steps == t, subset_ref[0, t], subset)
    on_site = colour == parity

    def force_body(step, carry):
        mu = step // 2
        c = step % 2
        current = load_matrix(lambda e: dense[mu, e, c])
        omega = mat_mul(current, load_matrix(lambda e: sums[mu, e, c]))
        parts = [part + forces[mu, e, c] for e, part in enumerate(anti_parts(omega))]
        mean = (parts[0] + parts[1] + parts[2]) * (1.0 / 3.0)
        parts = [parts[e] - mean if e < 3 else parts[e] for e in range(9)]
        parts = [part * (1.0 / 12.0) for part in parts]
        applied = anti_mul(parts, current)
        twice = anti_mul(parts, applied)
        gate = jnp.where(jnp.logical_and(on_site, jnp.right_shift(subset, mu) % 2 == 1), 1.0, 0.0)
        slope = jnp.zeros_like(gate)
        curve = jnp.zeros_like(gate)
        for e, (part, i, j) in enumerate(ENTRIES):
            weight = cots[mu, e, c]
            slope = slope + weight * applied[part][i][j]
            curve = curve + weight * twice[part][i][j]
            w1_ref[mu, e, c] = gate * applied[part][i][j]
            w2_ref[mu, e, c] = gate * twice[part][i][j]
        put_row(8 + mu, c, gate * slope)
        put_row(12 + mu, c, gate * curve)
        return carry

    lax.fori_loop(0, 8, force_body, 0)
    for t in range(4):
        for q in range(4):
            value = rows[t, q]
            fm_ref[t, :, q * 128:q * 128 + 128] = value.astype(BF16)
            if t > 0:
                fup_ref[t - 1, :, q * 128:q * 128 + 128] = value[0:8].astype(BF16)
            if t < 3:
                fdown_ref[t, :, q * 128:q * 128 + 128] = value[0:8].astype(BF16)


def selectors():
    row = lax.broadcasted_iota(jnp.int32, (432, 72), 0)
    col = lax.broadcasted_iota(jnp.int32, (432, 72), 1)
    group = row // 12
    spread = (group // 4 * 8 + group % 4 == col).astype(F32).astype(BF16)
    keep = (
        lax.broadcasted_iota(jnp.int32, (432, H), 1) // 4 == lax.broadcasted_iota(jnp.int32, (432, H), 0) % 12
    )
    return spread, keep


def panel_kernel(gathered_ref, weights_ref, loops_ref, p1_ref, p2_ref, p3_ref, p4_ref, b2_ref, b3_ref, b4_ref, weights):
    count = gathered_ref.shape[0]

    def read(d):
        return load_matrix(lambda e: slabs[4 * e:4 * e + 4, :])

    slabs = gathered_ref[0, 0:SLABROWS, :].astype(F32)
    product = read(0)
    state = tuple(product[0][i][j] for i in range(3) for j in range(3)) + tuple(
        product[1][i][j] for i in range(3) for j in range(3)
    )

    def chain(d, state):
        slab = gathered_ref[d, 0:SLABROWS, :].astype(F32)
        left = load_matrix(lambda e: state[e])
        product = mat_mul(left, load_matrix(lambda e: slab[4 * e:4 * e + 4, :]))
        out = []
        store_matrix(product, lambda e, value: out.append((e, value)))
        return tuple(value for _, value in sorted(out, key=lambda item: item[0]))

    state = lax.fori_loop(1, count, chain, state)
    loops_ref[0] = (state[0] + state[4] + state[8]) / 3.0
    loops_ref[1] = (state[9] + state[13] + state[17]) / 3.0

    if weights_ref is None:
        for d in range(count):
            block = gathered_ref[d, SLABROWS:BLOCKROWS, :].astype(F32)
            weights[27 * d:27 * d + 27, :] = block[0:27]
    else:
        weights[...] = weights_ref[...].astype(F32)
    for k in range(TAPS):
        rows = slice(H * k, H * k + H)
        back = slice(H * SWAP[k], H * SWAP[k] + H)
        p2_ref[:, rows] = weights[rows, 0:48].astype(BF16)
        p3_ref[:, rows] = weights[rows, 48:96].astype(BF16)
        p1_ref[:, 8 * k:8 * k + 8] = weights[rows, 96:104].astype(BF16)
        turned = weights[back, :].T
        b2_ref[:, rows] = turned[0:48].astype(BF16)
        b3_ref[:, rows] = turned[48:96].astype(BF16)
    spread, keep = selectors()
    place = (
        lax.broadcasted_iota(jnp.int32, (LANES, H), 0) == 104 + lax.broadcasted_iota(jnp.int32, (LANES, H), 1) % 4
    ).astype(F32).astype(BF16)
    wide = jnp.dot(weights[...].astype(BF16), place, preferred_element_type=F32)
    wide = jnp.where(keep, wide, 0.0).astype(BF16)
    last = lax.dot_general(spread, wide, (((0,), (0,)), ((), ())), preferred_element_type=F32)
    p4_ref[...] = last.astype(BF16)
    for k in range(TAPS):
        b4_ref[:, 8 * k:8 * k + 8] = last[8 * SWAP[k]:8 * SWAP[k] + 8, :].T.astype(BF16)


def panel_kernel_plain(gathered_ref, *rest):
    panel_kernel(gathered_ref, None, *rest)


def chunks_of(value):
    return [value[:, q * 128:q * 128 + 128] for q in range(4)]


def one_shift(chunks, position):
    if position == 0:
        return chunks
    lanes = lane_iota(chunks[0].shape[0])
    sign = 1 if position % 2 == 1 else -1
    if position > 4:
        return [shift_z(chunk, sign, lanes) for chunk in chunks]
    if position > 2:
        return [shift_y(chunk, sign, lanes) for chunk in chunks]
    low = lanes < 64
    rolled = [roll_lanes(chunk, 64) for chunk in chunks]
    if sign > 0:
        return [jnp.where(low, rolled[q], rolled[(q + 1) % 4]) for q in range(4)]
    return [jnp.where(low, rolled[(q + 3) % 4], rolled[q]) for q in range(4)]


def span(slice_index, count=1):
    if isinstance(slice_index, int):
        return slice(slice_index * SITES, (slice_index + count) * SITES)
    return pl.ds(pl.multiple_of(slice_index * SITES, SITES), count * SITES)


def stack_wide(source, target, first, count):
    for s in range(count):
        chunks = chunks_of(source[:, span(first + s)])
        for position in range(7):
            shifted = one_shift(chunks, position)
            for q in range(4):
                lanes = slice(s * SITES + q * 128, s * SITES + q * 128 + 128)
                target[H * position:H * position + H, lanes] = shifted[q]
    width = slice(0, count * SITES)
    target[7 * H:8 * H, width] = source[:, span(first + 1, count)]
    target[8 * H:9 * H, width] = source[:, span(first - 1, count)]


def stack_thin(source, target, first, count):
    for s in range(count):
        chunks = chunks_of(source[:, span(first + s)])
        ahead = chunks_of(source[:, span(first + s + 1)])
        behind = chunks_of(source[:, span(first + s - 1)])
        columns = [one_shift(chunks, position) for position in range(7)] + [ahead, behind]
        for q in range(4):
            lanes = slice(s * SITES + q * 128, s * SITES + q * 128 + 128)
            target[0:72, lanes] = jnp.concatenate([column[q] for column in columns], axis=0).astype(BF16)


def one_minus_square(value):
    value = value.astype(F32)
    return 1.0 - value * value


def conv_kernel(
    split, fm_ref, below_ref, above_ref, fbelow_ref, fabove_ref, loops_ref,
    p1_ref, p2_ref, p3_ref, p4_ref, b2_ref, b3_ref, b4_ref,
    coeff_ref, grads_ref,
    feats, mixed, h1, h2, h3, parts, lasts, g3, g2, wide, thin, packed,
):
    row8 = lax.broadcasted_iota(jnp.int32, (8, SITES), 0)
    loop_re = jnp.concatenate([loops_ref[0, q:q + 1, :] for q in range(4)], axis=1)
    loop_im = jnp.concatenate([loops_ref[1, q:q + 1, :] for q in range(4)], axis=1)
    loops = jnp.where(row8 == 6, loop_re, jnp.where(row8 == 7, loop_im, 0.0))
    loops = loops.astype(BF16).astype(F32)
    for j in range(3):
        feats[:, span(j)] = fbelow_ref[j].astype(F32) + loops
        feats[:, span(15 + j)] = fabove_ref[j].astype(F32) + loops
    for base, ref in ((3, below_ref), (7, fm_ref), (11, above_ref)):
        for j in range(4):
            value = ref[j].astype(F32)
            feats[:, span(base + j)] = value[0:8] + loops
            mixed[:, span(base + j)] = value[8:16]

    def layer_one(step, carry):
        first = 1 + 4 * step
        stack_thin(feats, thin, first, 4)
        out = jnp.dot(p1_ref[...], thin[...], preferred_element_type=F32)
        h1[:, span(first, 4)] = jnp.tanh(out).astype(BF16)
        return carry

    lax.fori_loop(0, 4, layer_one, 0)

    def layer_two(step, carry):
        first = 2 + 2 * step
        stack_wide(h1, wide, first, 2)
        out = jnp.dot(p2_ref[...], wide[:, 0:1024], preferred_element_type=F32)
        h2[:, span(first, 2)] = jnp.tanh(out).astype(BF16)
        return carry

    lax.fori_loop(0, 7, layer_two, 0)

    def layer_three(step, carry):
        first = 3 + 2 * step
        stack_wide(h2, wide, first, 2)
        out = jnp.dot(p3_ref[...], wide[:, 0:1024], preferred_element_type=F32)
        out = jnp.tanh(out).astype(BF16)
        h3[:, span(first, 2)] = out
        taps = jnp.dot(p4_ref[...], out, preferred_element_type=F32)
        for s in range(2):
            acc = None
            for position in range(7):
                shifted = one_shift(
                    chunks_of(taps[8 * position:8 * position + 8, s * SITES:(s + 1) * SITES]), position
                )
                acc = shifted if acc is None else [a + b for a, b in zip(acc, shifted)]
            parts[0, :, span(first + s)] = jnp.concatenate(acc, axis=1)
            parts[1, :, span(first + s)] = taps[56:64, s * SITES:(s + 1) * SITES]
            parts[2, :, span(first + s)] = taps[64:72, s * SITES:(s + 1) * SITES]
        return carry

    lax.fori_loop(0, 6, layer_three, 0)

    def last_layer(step, carry):
        for s in range(2):
            index = 4 + 2 * step + s
            coeff = jnp.tanh(parts[0, :, span(index)] + parts[1, :, span(index + 1)] + parts[2, :, span(index - 1)])
            blend = mixed[:, span(index)]
            value = (blend + coeff * pltpu.roll(blend, 4, 0)) * (1.0 - coeff * coeff)
            lasts[:, span(index)] = jnp.where(row8 < 4, value, 0.0).astype(BF16).astype(F32)
            parts[0, :, span(index)] = coeff
        return carry

    lax.fori_loop(0, 5, last_layer, 0)
    for t in range(4):
        coeff_ref[t] = parts[0, :, span(7 + t)]

    def back_three(first, count):
        stack_thin(lasts, thin, first, count)
        out = jnp.dot(b4_ref[...], thin[:, 0:count * SITES], preferred_element_type=F32)
        g3[:, span(first, count)] = (out * one_minus_square(h3[:, span(first, count)])).astype(BF16)

    back_three(5, 2)
    back_three(11, 2)
    back_three(7, 4)
    own = span(7, 4)
    contract = (((1,), (1,)), ((), ()))
    grad_last = lax.dot_general(thin[...], h3[:, own], contract, preferred_element_type=F32)

    stack_wide(g3, wide, 6, 1)
    out = jnp.dot(b3_ref[...], wide[:, 0:SITES], preferred_element_type=F32)
    g2[:, span(6)] = (out * one_minus_square(h2[:, span(6)])).astype(BF16)
    stack_wide(g3, wide, 11, 1)
    out = jnp.dot(b3_ref[...], wide[:, 0:SITES], preferred_element_type=F32)
    g2[:, span(11)] = (out * one_minus_square(h2[:, span(11)])).astype(BF16)
    stack_wide(g3, wide, 7, 4)
    out = jnp.dot(b3_ref[...], wide[...], preferred_element_type=F32)
    g2[:, own] = (out * one_minus_square(h2[:, own])).astype(BF16)
    grad_third = lax.dot_general(wide[...], h2[:, own], contract, preferred_element_type=F32)

    stack_wide(g2, wide, 7, 4)
    out = jnp.dot(b2_ref[...], wide[...], preferred_element_type=F32)
    g1 = (out * one_minus_square(h1[:, own])).astype(BF16)
    grad_second = lax.dot_general(wide[...], h1[:, own], contract, preferred_element_type=F32)

    stack_thin(feats, thin, 7, 4)
    grad_first = lax.dot_general(g1, thin[...], contract, preferred_element_type=F32)

    spread, keep = selectors()
    ordered = jnp.concatenate([grad_last[8 * SWAP[k]:8 * SWAP[k] + 8] for k in range(TAPS)], axis=0)
    broad = jnp.dot(spread, ordered.astype(BF16), preferred_element_type=F32)
    broad = jnp.where(keep, broad, 0.0).astype(BF16)
    place = (
        lax.broadcasted_iota(jnp.int32, (H, LANES), 1) == 104 + lax.broadcasted_iota(jnp.int32, (H, LANES), 0) % 4
    ).astype(F32).astype(BF16)
    packed[...] = jnp.dot(broad, place, preferred_element_type=F32)
    for k in range(TAPS):
        rows = slice(H * k, H * k + H)
        back = slice(H * SWAP[k], H * SWAP[k] + H)
        packed[rows, 0:48] = grad_second[back]
        packed[rows, 48:96] = grad_third[back]
        packed[rows, 96:104] = grad_first[:, 8 * k:8 * k + 8]
    if split:
        for d in range(16):
            grads_ref[d] = packed[27 * d:27 * d + 27, :].astype(BF16)
    else:
        grads_ref[...] = packed[...].astype(BF16)


def update_kernel(links_ref, w1_ref, w2_ref, coeff_ref, out_ref, factors):
    for mu in range(4):
        for t in range(4):
            for c in range(2):
                factors[mu, c, t:t + 1, :] = coeff_ref[t, mu:mu + 1, c * 128:c * 128 + 128]
                factors[mu, c, 4 + t:5 + t, :] = coeff_ref[t, mu:mu + 1, 256 + c * 128:384 + c * 128]

    def body(mu, carry):
        factor = [factors[mu, c] for c in range(2)]
        half = [0.5 * value * value for value in factor]
        for e, (part, i, j) in enumerate(ENTRIES):
            pair = pack_pair(links_ref[mu, part, i, j, 0])
            new = [pair[c] + factor[c] * w1_ref[mu, e, c] + half[c] * w2_ref[mu, e, c] for c in range(2)]
            out_ref[mu, part, i, j, 0] = jnp.concatenate(
                [new[0][0:4], new[1][0:4], new[0][4:8], new[1][4:8]], axis=1
            )
        return carry

    lax.fori_loop(0, 4, body, 0)


def sum_kernel(widths, parts_ref, first_ref, second_ref, third_ref, last_ref):
    value = parts_ref[0].astype(F32)
    for d in range(1, parts_ref.shape[0]):
        value = value + parts_ref[d].astype(F32)
    offset = 0
    for ref, width in zip((second_ref, third_ref, first_ref, last_ref), widths):
        for r in range(27):
            ref[:, width * r:width * r + width] = value[r:r + 1, offset:offset + width]
        offset += width


def call(body, outs, scratch, smem=(), count=0):
    specs = {}
    if smem:
        specs["in_specs"] = [
            pl.BlockSpec(memory_space=pltpu.SMEM if i in smem else pltpu.VMEM) for i in range(count)
        ]
    return pl.pallas_call(
        body,
        out_shape=[jax.ShapeDtypeStruct(shape, dtype) for shape, dtype in outs],
        scratch_shapes=[pltpu.VMEM(shape, dtype) for shape, dtype in scratch],
        compiler_params=pltpu.CompilerParams(vmem_limit_bytes=LIMIT),
        **specs,
    )


def on_device(links, cotangent, parity, link_subset, w_first, w_second, w_third, w_last):
    count = lax.axis_size("tm")

    def send(value, distance):
        return lax.ppermute(value, "tm", [(i, (i + distance) % count) for i in range(count)])

    widths = (768 // count, 768 // count, 128 // count, 64 // count)
    up, down, block = call(
        functools.partial(first_kernel, widths),
        [((54, SITES), BF16), ((54, SITES), BF16), ((BLOCKROWS, LANES), BF16)],
        [((4, 18, 2, 8, LANES), F32), ((3, 18, 2, 8, LANES), F32), ((54, 4, LANES), F32), ((BLOCKROWS, LANES), F32)],
    )(links, w_first[None], w_second[None], w_third[None], w_last[None])
    up = send(up, 1)
    down = send(down, -1)
    gathered = lax.all_to_all(
        jnp.broadcast_to(block[None], (count,) + block.shape), "tm", split_axis=0, concat_axis=0, tiled=True
    )
    fm, fup, fdown, applied, twice = call(
        gauge_kernel,
        [
            ((4, 16, SITES), BF16), ((3, 8, SITES), BF16), ((3, 8, SITES), BF16),
            ((4, 18, 2, 8, LANES), F32), ((4, 18, 2, 8, LANES), F32),
        ],
        [
            ((4, 18, 2, 8, LANES), F32), ((4, 18, 2, 8, LANES), F32), ((4, 4, 18, 2, 8, LANES), F32),
            ((4, 4, 18, 2, 8, LANES), F32), ((4, 18, 2, 8, LANES), F32), ((54, 4, LANES), F32), ((54, 4, LANES), F32),
            ((4, 9, 2, 8, LANES), F32), ((4, 4, 16, LANES), F32),
        ],
        smem=(4, 5), count=6,
    )(links, cotangent, up, down, parity, link_subset)
    below = send(fm, 1)
    above = send(fm, -1)
    fbelow = send(fup, 2)
    fabove = send(fdown, -2)

    panel_outs = [
        ((2, 4, LANES), F32), ((H, 72), BF16), ((H, 432), BF16), ((H, 432), BF16), ((72, H), BF16),
        ((H, 432), BF16), ((H, 432), BF16), ((H, 72), BF16),
    ]
    panel_scratch = [((432, LANES), F32)]
    if count == 16:
        loops, p1, p2, p3, p4, b2, b3, b4 = call(panel_kernel_plain, panel_outs, panel_scratch)(gathered)
    else:
        pieces = []
        offset = 0
        for width, full in zip(widths, (48, 48, 8, 4)):
            piece = gathered[:, SLABROWS:SLABROWS + 27, offset:offset + width]
            pieces.append(piece.reshape(432, full))
            offset += width
        pieces.append(jnp.zeros((432, 20), BF16))
        loops, p1, p2, p3, p4, b2, b3, b4 = call(panel_kernel, panel_outs, panel_scratch)(
            gathered, jnp.concatenate(pieces, axis=1)
        )

    window = 18 * SITES
    coeff, grads = call(
        functools.partial(conv_kernel, count == 16),
        [((4, 8, SITES), F32), ((16, 27, LANES) if count == 16 else (432, LANES), BF16)],
        [
            ((8, window), F32), ((8, window), F32), ((H, window), BF16), ((H, window), BF16), ((H, window), BF16),
            ((3, 8, window), F32), ((8, window), F32), ((H, window), BF16), ((H, window), BF16),
            ((432, 4 * SITES), BF16), ((72, 4 * SITES), BF16), ((432, LANES), F32),
        ],
    )(fm, below, above, fbelow, fabove, loops, p1, p2, p3, p4, b2, b3, b4)
    if count != 16:
        offset = 0
        pieces = []
        for width, full in zip(widths, (48, 48, 8, 4)):
            pieces.append(grads[:, offset:offset + full].reshape(count, 27, width))
            offset += full
        grads = jnp.concatenate(pieces, axis=2)
    grads = lax.all_to_all(grads, "tm", split_axis=0, concat_axis=0, tiled=True)
    (new_links,) = call(
        update_kernel, [(links.shape, F32)], [((4, 2, 8, LANES), F32)]
    )(links, applied, twice, coeff)
    grad_first, grad_second, grad_third, grad_last = call(
        functools.partial(sum_kernel, widths),
        [((1, 27 * width), F32) for width in (widths[2], widths[0], widths[1], widths[3])],
        [],
    )(grads)
    return (new_links, grad_first, grad_second, grad_third, grad_last)


def solution(mesh):
    placed = (
        P(None, None, None, None, "groups", "tm", None),
        P(None, None, None, None, "groups", "tm", None),
        P("groups", "tm"),
        P("groups", "tm"),
        P("tm"),
        P("tm"),
        P("tm"),
        P("tm"),
    )
    return jax.shard_map(
        on_device,
        mesh=mesh,
        in_specs=placed,
        out_specs=(
            P(None, None, None, None, "groups", "tm", None),
            P("groups", "tm"),
            P("groups", "tm"),
            P("groups", "tm"),
            P("groups", "tm"),
        ),
        check_vma=False,
    )
```

time: 445 us -> 72.2 us (0.16)
  waiting for transfers between devices: 124 us -> 16.5 us
  other arithmetic: 84.9 us -> 0 us
  blocking collectives: 79.6 us -> 0 us
  local copies, waits for them, and re-layouts: 77 us -> 3.94 us
  Pallas kernels: 0 us -> 27.2 us
  between operations: 21.3 us -> 0.74 us
  starting transfers between devices: 38 us -> 23.4 us
  matrix products: 14.1 us -> 0 us
    unnamed x6 -> x0, waiting for transfers between devices: 118 us -> none
    unnamed x1 -> x0, blocking collectives: 60.2 us -> none
    reduce_sum x78 -> x0, other arithmetic: 30.6 us -> none  [the longest x76 27.1 us: real_product(): return jnp.sum(left[:, :, None] * right[None], axis=1)]
    ppermute x16 -> x6, starting transfers between devices: 37.7 us -> 9.77 us  [send(): lax.ppermute(value, 'tm', [(i, (i + distance) % count) for i in range(cou...]
    pallas_call x0 -> x6, Pallas kernels: none -> 27.2 us  [the longest x1 14 us: on_device(): call(functools.partial(conv_kernel, count == 16), [((4, 8, SITES), F32),...]
    unnamed x323 -> x14, local copies, waits for them, and re-layouts: 25.7 us -> 1.74 us
    all_gather x1 -> x0, blocking collectives: 19.4 us -> none  [on_device(): lax.all_gather(slab[None].astype(jnp.bfloat16), 'tm', axis=0, tiled=True)]
    slice x127 -> x0, local copies, waits for them, and re-layouts: 18.1 us -> none  [the longest x47 5.91 us: space_roll(): inner = jnp.roll(flat, -amount * stride, axis=flat.ndim - 1)]
  transfers between devices with their start and end apart: 19 -> 8, of which waited for: 7 -> 3; matrix products, arithmetic and copies ran while one was open for 19% -> 0% of each run, Pallas kernels for 0% -> 14%
where the time goes in v1:
time: 72.2 us; the launch traced here: 71.8 us
  Pallas kernels  27.2 us (38%)
  starting transfers between devices  23.4 us (32%)
  waiting for transfers between devices  16.5 us (23%)
  local copies, waits for them, and re-layouts  3.94 us (5%)
  between operations  0.74 us (1%)
    pallas_call x1, Pallas kernels, on_device(): call(functools.partial(conv_kernel, count == 16), [((4, 8, SITES), F32),...  14 us
    ppermute x6, starting transfers between devices, send(): lax.ppermute(value, 'tm', [(i, (i + distance) % count) for i in range(cou...  9.77 us
    ppermute x6, waiting for transfers between devices, send(): lax.ppermute(value, 'tm', [(i, (i + distance) % count) for i in range(cou...  9.62 us
    all_to_all x1, starting transfers between devices, on_device(): lax.all_to_all(jnp.broadcast_to(block[None], (count,) + block.shape), 'tm...  7.52 us
    pallas_call x1, Pallas kernels, on_device(): call(gauge_kernel, [((4, 16, SITES), BF16), ((3, 8, SITES), BF16), ((3, 8...  7.38 us
    all_to_all x1, waiting for transfers between devices, on_device(): grads = lax.all_to_all(grads, 'tm', split_axis=0, concat_axis=0, tiled=True)  6.91 us
    all_to_all x1, starting transfers between devices, on_device(): grads = lax.all_to_all(grads, 'tm', split_axis=0, concat_axis=0, tiled=True)  6.1 us
    pallas_call x1, Pallas kernels, on_device(): call(functools.partial(first_kernel, widths), [((54, SITES), BF16), ((54,...  2.48 us
  transfers between devices with their start and end apart: 8, of which 3 were waited for; matrix products, arithmetic and copies ran while one was open for 0% of the time, Pallas kernels for 14%

profile of v1, /device:TPU:0, one launch (start us, length us, event | category | flops | bytes accessed | tf_op | source)
XLA Modules:
  0.0 71.8 jit_solution(14573151067336865229)
XLA Ops:
  0.6 0.7 broadcast_in_dim.18.w1_ref
  1.3 0.7 broadcast_in_dim.19.w2_ref
  2.0 0.0 copy-start.5
  2.0 0.6 copy-done.5
  2.7 1.1 %copy-done = f32[4,2,3,3,1,4,512]{6,5,4,3,2,1,0:T(4,128)S(1)} copy-done((f32[4,2,3,3,1,4,512]{6,5,4,3,2,1,0:T(4,128)S(1)}, f32[4,2,3,3,1,4,512]{6,5,4,3,2,1,0:T(4,128)}, u32[]{:S(2)}) %copy-start) | copy-done | bytes 589848
  3.7 2.5 %shard_map.119 = (bf16[54,512]{1,0:T(8,128)(2,1)S(1)}, bf16[54,512]{1,0:T(8,128)(2,1)S(1)}, bf16[112,128]{1,0:T(8,128)(2,1)S(1)}) custom-call(f32[4,2,3,3,1,4,512]{6,5,4,3,2,1,0:T(4,128)S(1)} %copy-done, bf16[1,216]{1,0:T(2,128)(2,1)S(1)} %broadcast_in_dim.18.w1_ref, bf16[1,1296]{1,0:T(2,128)(2,1)S(1)} %broadcast_in_dim.19.w2_ref, ...), custom_call_target="tpu_custom_call" | custom-call | tf_op jit(solution)/shard_map/pallas_call | solution.py:671
  6.2 0.8 %broadcast_in_dim.22 = bf16[16,112,128]{2,1,0:T(8,128)(2,1)} broadcast(bf16[112,128]{1,0:T(8,128)(2,1)S(1)} %get-tuple-element.34), dimensions={1,2} | broadcast | bytes 487424 | tf_op jit(solution)/shard_map/broadcast_in_dim | solution.py:679
  7.1 7.5 %all-to-all-start = ((bf16[16,112,128]{2,1,0:T(8,128)(2,1)}), bf16[16,112,128]{2,1,0:T(8,128)(2,1)S(1)}, u32[]{:S(2)}, u32[]{:S(2)}) async-start(bf16[16,112,128]{2,1,0:T(8,128)(2,1)} %broadcast_in_dim.22), calls=%async_computation | async-start | bytes 917504 | tf_op jit(solution)/shard_map/all_to_all | solution.py:678
  14.6 0.0 copy-start.3
  14.6 0.0 copy-start.4
  14.6 0.5 collective-permute-start
  15.1 4.0 %collective-permute-start.1 = (bf16[54,512]{1,0:T(8,128)(2,1)S(1)}, bf16[54,512]{1,0:T(8,128)(2,1)S(1)}, u32[]{:S(2)}, u32[]{:S(2)}) collective-permute-start(bf16[54,512]{1,0:T(8,128)(2,1)S(1)} %get-tuple-element.28), channel_id=1, source_target_pairs={{0,15},{1,0},{2,1},{3,2},{4,3},{5,4},{6,5},{7,6},{8,7},{9,8},{10,9... | collective-permute-start | bytes 165896 | tf_op jit(solution)/shard_map/ppermute | solution.py:668
  19.1 9.3 %collective-permute-done.up_ref = bf16[54,512]{1,0:T(8,128)(2,1)S(1)} collective-permute-done((bf16[54,512]{1,0:T(8,128)(2,1)S(1)}, bf16[54,512]{1,0:T(8,128)(2,1)S(1)}, u32[]{:S(2)}, u32[]{:S(2)}) %collective-permute-start) | collective-permute-done | bytes 55328 | tf_op jit(solution)/shard_map/ppermute | solution.py:668
  28.5 7.4 %shard_map.120 = (bf16[4,16,512]{2,1,0:T(8,128)(2,1)S(1)}, bf16[3,8,512]{2,1,0:T(8,128)(2,1)S(1)}, bf16[3,8,512]{2,1,0:T(8,128)(2,1)S(1)}, f32[4,18,2,8,128]{4,3,2,1,0:T(8,128)S(1)}, f32[4,18,2,8,128]{4,3,2,1,0:T(8,128)S(1)}) custom-call(f32[4,2,3,3,1,4,512]{6,5,4,3,2,1,0:T(4,128)S(1)} %copy-done.1, bf16[4,2,3,3,1,4,512]{6,5,4,3,2,1,0:T(4,128)(2,1)S(1)} %copy-done.2, ...), custom_call_target="tpu_custom_call" | custom-call | tf_op jit(solution)/shard_map/pallas_call | solution.py:681
  35.9 0.1 collective-permute-start.3
  35.9 0.5 collective-permute-start.2
  36.4 4.7 %collective-permute-start.5 = (bf16[3,8,512]{2,1,0:T(8,128)(2,1)S(1)}, bf16[3,8,512]{2,1,0:T(8,128)(2,1)S(1)}, u32[]{:S(2)}, u32[]{:S(2)}) collective-permute-start(bf16[3,8,512]{2,1,0:T(8,128)(2,1)S(1)} %get-tuple-element.33), channel_id=1, source_target_pairs={{0,14},{1,15},{2,0},{3,1},{4,2},{5,3},{6,4},{7,5},{8,6},{9,7},{10,... | collective-permute-start | bytes 73736 | tf_op jit(solution)/shard_map/ppermute | solution.py:668
  41.1 1.5 %shard_map.121 = (f32[2,4,128]{2,1,0:T(4,128)S(1)}, bf16[48,72]{1,0:T(8,128)(2,1)S(1)}, bf16[48,432]{1,0:T(8,128)(2,1)S(1)}, bf16[48,432]{1,0:T(8,128)(2,1)S(1)}...) custom-call(bf16[16,112,128]{2,1,0:T(8,128)(2,1)S(1)} %all-to-all-do, ...), custom_call_target="tpu_custom_call" | custom-call | tf_op jit(solution)/shard_map/pallas_call | solution.py:705
  42.7 0.3 collective-permute-done.4.fbelow_ref
  43.0 14.0 %shard_map.122 = (f32[4,8,512]{2,1,0:T(8,128)S(1)}, bf16[16,27,128]{2,1,0:T(8,128)(2,1)}) custom-call(bf16[4,16,512]{2,1,0:T(8,128)(2,1)S(1)} %get-tuple-element.31.fm_ref, bf16[4,16,512]{2,1,0:T(8,128)(2,1)S(1)} %collective-permute-done.2.below_ref, bf16[4,16,512]{2,1,0:T(8,128)(2,1)S(1)} %collective-permute-done.3.above_ref, ...), custom_call_target="tpu_custom_call" | custom-call | tf_op jit(solution)/shard_map/pallas_call | solution.py:719
  57.0 6.1 %all-to-all-start.1 = ((bf16[16,27,128]{2,1,0:T(8,128)(2,1)}), bf16[16,27,128]{2,1,0:T(8,128)(2,1)S(1)}, u32[]{:S(2)}, u32[]{:S(2)}) async-start(bf16[16,27,128]{2,1,0:T(8,128)(2,1)} %get-tuple-element.44), calls=%async_computation.1 | async-start | bytes 262144 | tf_op jit(solution)/shard_map/all_to_all | solution.py:735
  63.1 1.0 %shard_map.123 = f32[4,2,3,3,1,4,512]{6,5,4,3,2,1,0:T(4,128)} custom-call(f32[4,2,3,3,1,4,512]{6,5,4,3,2,1,0:T(4,128)S(1)} %copy-done.1, f32[4,18,2,8,128]{4,3,2,1,0:T(8,128)S(1)} %get-tuple-element.29.w1_ref, f32[4,18,2,8,128]{4,3,2,1,0:T(8,128)S(1)} %get-tuple-element.30.w2_ref, f32[4,8,512]{2,1,0:T(8,128)S(1)} %get-tuple-element.43.coeff_ref), custom_call_target="tpu_custom_call" | custom-call | tf_op jit(solution)/shard_map/pallas_call | solution.py:736
  64.1 6.9 %all-to-all-done.1.parts_ref = bf16[16,27,128]{2,1,0:T(8,128)(2,1)S(1)} async-done(((bf16[16,27,128]{2,1,0:T(8,128)(2,1)}), bf16[16,27,128]{2,1,0:T(8,128)(2,1)S(1)}, u32[]{:S(2)}, u32[]{:S(2)}) %all-to-all-start.1) | async-done | bytes 110624 | tf_op jit(solution)/shard_map/all_to_all | solution.py:735
  71.0 0.8 %shard_map.124 = (f32[1,216]{1,0:T(1,128)}, f32[1,1296]{1,0:T(1,128)}, f32[1,1296]{1,0:T(1,128)}, f32[1,108]{1,0:T(1,128)}) custom-call(bf16[16,27,128]{2,1,0:T(8,128)(2,1)S(1)} %all-to-all-done.1.parts_ref), custom_call_target="tpu_custom_call" | custom-call | tf_op jit(solution)/shard_map/pallas_call | solution.py:739
  (16 shorter events, 0.0 us)
Async XLA Ops:
  1.3 0.7 copy-start.6
  2.0 0.7 copy-start.5
  2.7 1.1 %copy-start = (f32[4,2,3,3,1,4,512]{6,5,4,3,2,1,0:T(4,128)S(1)}, f32[4,2,3,3,1,4,512]{6,5,4,3,2,1,0:T(4,128)}, u32[]{:S(2)}) copy-start(f32[4,2,3,3,1,4,512]{6,5,4,3,2,1,0:T(4,128)} %links_ref.5) | copy-start | bytes 1769476
  6.2 22.2 %copy-start.1 = (f32[4,2,3,3,1,4,512]{6,5,4,3,2,1,0:T(4,128)S(1)}, f32[4,2,3,3,1,4,512]{6,5,4,3,2,1,0:T(4,128)}, u32[]{:S(2)}) copy-start(f32[4,2,3,3,1,4,512]{6,5,4,3,2,1,0:T(4,128)} %links_ref.5) | copy-start | bytes 1769476
  7.0 21.4 %copy-start.2 = (bf16[4,2,3,3,1,4,512]{6,5,4,3,2,1,0:T(4,128)(2,1)S(1)}, bf16[4,2,3,3,1,4,512]{6,5,4,3,2,1,0:T(4,128)(2,1)}, u32[]{:S(2)}) copy-start(bf16[4,2,3,3,1,4,512]{6,5,4,3,2,1,0:T(4,128)(2,1)} %cot_ref.1) | copy-start | bytes 884740
  7.1 34.1 %all-to-all-start = ((bf16[16,112,128]{2,1,0:T(8,128)(2,1)}), bf16[16,112,128]{2,1,0:T(8,128)(2,1)S(1)}, u32[]{:S(2)}, u32[]{:S(2)}) async-start(bf16[16,112,128]{2,1,0:T(8,128)(2,1)} %broadcast_in_dim.22), calls=%async_computation | async-start | bytes 917504 | tf_op jit(solution)/shard_map/all_to_all | solution.py:678
  14.6 13.9 %copy-start.3 = (s32[1,4]{1,0:T(1,128)S(1)}, s32[1,4]{1,0:T(1,128)}, u32[]{:S(2)}) copy-start(s32[1,4]{1,0:T(1,128)} %parity_ref.1) | copy-start | bytes 52
  14.6 13.9 %copy-start.4 = (s32[1,4]{1,0:T(1,128)S(1)}, s32[1,4]{1,0:T(1,128)}, u32[]{:S(2)}) copy-start(s32[1,4]{1,0:T(1,128)} %subset_ref.1) | copy-start | bytes 52
  14.6 13.8 %collective-permute-start = (bf16[54,512]{1,0:T(8,128)(2,1)S(1)}, bf16[54,512]{1,0:T(8,128)(2,1)S(1)}, u32[]{:S(2)}, u32[]{:S(2)}) collective-permute-start(bf16[54,512]{1,0:T(8,128)(2,1)S(1)} %get-tuple-element.27), channel_id=1, source_target_pairs={{0,1},{1,2},{2,3},{3,4},{4,5},{5,6},{6,7},{7,8},{8,9},{9,10},{10,1... | collective-permute-start | bytes 165896 | tf_op jit(solution)/shard_map/ppermute | solution.py:668
  15.1 13.4 %collective-permute-start.1 = (bf16[54,512]{1,0:T(8,128)(2,1)S(1)}, bf16[54,512]{1,0:T(8,128)(2,1)S(1)}, u32[]{:S(2)}, u32[]{:S(2)}) collective-permute-start(bf16[54,512]{1,0:T(8,128)(2,1)S(1)} %get-tuple-element.28), channel_id=1, source_target_pairs={{0,15},{1,0},{2,1},{3,2},{4,3},{5,4},{6,5},{7,6},{8,7},{9,8},{10,9... | collective-permute-start | bytes 165896 | tf_op jit(solution)/shard_map/ppermute | solution.py:668
  35.9 7.1 %collective-permute-start.3 = (bf16[4,16,512]{2,1,0:T(8,128)(2,1)S(1)}, bf16[4,16,512]{2,1,0:T(8,128)(2,1)S(1)}, u32[]{:S(2)}, u32[]{:S(2)}) collective-permute-start(bf16[4,16,512]{2,1,0:T(8,128)(2,1)S(1)} %get-tuple-element.31.fm_ref), channel_id=1, source_target_pairs={{0,15},{1,0},{2,1},{3,2},{4,3},{5,4},{6,5},{7,6},{8,7},{9,8},{10,9... | collective-permute-start | bytes 196616 | tf_op jit(solution)/shard_map/ppermute | solution.py:668
  35.9 7.0 %collective-permute-start.2 = (bf16[4,16,512]{2,1,0:T(8,128)(2,1)S(1)}, bf16[4,16,512]{2,1,0:T(8,128)(2,1)S(1)}, u32[]{:S(2)}, u32[]{:S(2)}) collective-permute-start(bf16[4,16,512]{2,1,0:T(8,128)(2,1)S(1)} %get-tuple-element.31.fm_ref), channel_id=1, source_target_pairs={{0,1},{1,2},{2,3},{3,4},{4,5},{5,6},{6,7},{7,8},{8,9},{9,10},{10,1... | collective-permute-start | bytes 196616 | tf_op jit(solution)/shard_map/ppermute | solution.py:668
  36.4 6.5 %collective-permute-start.4 = (bf16[3,8,512]{2,1,0:T(8,128)(2,1)S(1)}, bf16[3,8,512]{2,1,0:T(8,128)(2,1)S(1)}, u32[]{:S(2)}, u32[]{:S(2)}) collective-permute-start(bf16[3,8,512]{2,1,0:T(8,128)(2,1)S(1)} %get-tuple-element.32), channel_id=1, source_target_pairs={{0,2},{1,3},{2,4},{3,5},{4,6},{5,7},{6,8},{7,9},{8,10},{9,11},{10,... | collective-permute-start | bytes 73736 | tf_op jit(solution)/shard_map/ppermute | solution.py:668
  36.4 6.5 %collective-permute-start.5 = (bf16[3,8,512]{2,1,0:T(8,128)(2,1)S(1)}, bf16[3,8,512]{2,1,0:T(8,128)(2,1)S(1)}, u32[]{:S(2)}, u32[]{:S(2)}) collective-permute-start(bf16[3,8,512]{2,1,0:T(8,128)(2,1)S(1)} %get-tuple-element.33), channel_id=1, source_target_pairs={{0,14},{1,15},{2,0},{3,1},{4,2},{5,3},{6,4},{7,5},{8,6},{9,7},{10,... | collective-permute-start | bytes 73736 | tf_op jit(solution)/shard_map/ppermute | solution.py:668
  57.0 14.0 %all-to-all-start.1 = ((bf16[16,27,128]{2,1,0:T(8,128)(2,1)}), bf16[16,27,128]{2,1,0:T(8,128)(2,1)S(1)}, u32[]{:S(2)}, u32[]{:S(2)}) async-start(bf16[16,27,128]{2,1,0:T(8,128)(2,1)} %get-tuple-element.44), calls=%async_computation.1 | async-start | bytes 262144 | tf_op jit(solution)/shard_map/all_to_all | solution.py:735

commit v2 on v1

--- a/solution.py
+++ b/solution.py
@@ -16,8 +16,8 @@
 PAIRS = ((0, 1), (0, 2), (0, 3), (1, 2), (1, 3), (2, 3))
 SWAP = (0, 2, 1, 4, 3, 6, 5, 8, 7)
 ENTRIES = tuple((c, i, j) for c in range(2) for i in range(3) for j in range(3))
-SLABROWS = 80
-BLOCKROWS = 112
+SLABROWS = 48
+BLOCKROWS = 80
 LIMIT = 40 * 1024 * 1024
 
 
@@ -176,7 +176,7 @@
     lax.fori_loop(0, 4, body, 0)
 
 
-def first_kernel(widths, links_ref, w1_ref, w2_ref, w3_ref, w4_ref, up_ref, down_ref, block_ref, dense, moved, rows, block):
+def face_kernel(links_ref, up_ref, down_ref, dense, moved, rows):
     pack_links(links_ref, dense)
 
     def shift_body(e, carry):
@@ -189,37 +189,46 @@
 
     lax.fori_loop(0, 18, shift_body, 0)
 
-    for mu in range(3):
-        def staple_body(c, carry):
-            u_mu = load_matrix(lambda e: dense[mu, e, c])
-            u_t = load_matrix(lambda e: dense[3, e, c])
-            edge = mat_mul(u_mu, load_matrix(lambda e: moved[mu, e, c]))
-            staple = mat_mul(dagger(edge), u_t)
-
-            def write(e, value):
-                rows[mu * 18 + e, pl.ds(c, 1)] = value[3:4]
-                rows[mu * 18 + e, pl.ds(2 + c, 1)] = value[7:8]
-
-            store_matrix(staple, write)
-            return carry
-
-        lax.fori_loop(0, 2, staple_body, 0)
+    def staple_body(step, carry):
+        mu = step // 2
+        c = step % 2
+        u_mu = load_matrix(lambda e: dense[mu, e, c])
+        u_t = load_matrix(lambda e: dense[3, e, c])
+        edge = mat_mul(u_mu, load_matrix(lambda e: moved[mu, e, c]))
+        staple = mat_mul(dagger(edge), u_t)
+
+        def write(e, value):
+            rows[mu * 18 + e, pl.ds(c, 1)] = value[3:4]
+            rows[mu * 18 + e, pl.ds(2 + c, 1)] = value[7:8]
+
+        store_matrix(staple, write)
+        return carry
+
+    lax.fori_loop(0, 6, staple_body, 0)
     for q in range(4):
         up_ref[:, q * 128:q * 128 + 128] = rows[:, q, :].astype(BF16)
-    for mu in range(3):
-        for e in range(18):
+
+    def down_body(e, carry):
+        for mu in range(3):
             for c in range(2):
                 value = dense[mu, e, c]
                 rows[mu * 18 + e, c:c + 1] = value[0:1]
                 rows[mu * 18 + e, 2 + c:3 + c] = value[4:5]
+        return carry
+
+    lax.fori_loop(0, 18, down_body, 0)
     for q in range(4):
         down_ref[:, q * 128:q * 128 + 128] = rows[:, q, :].astype(BF16)
 
+
+def block_kernel(widths, links_ref, w1_ref, w2_ref, w3_ref, w4_ref, block_ref, dense, block):
+    for e, (part, i, j) in enumerate(ENTRIES):
+        dense[e, 0], dense[e, 1] = pack_pair(links_ref[3, part, i, j, 0])
     block[...] = jnp.zeros_like(block)
 
     def slab_body(c, carry):
-        u_t = load_matrix(lambda e: dense[3, e, c])
-        ahead = load_matrix(lambda e: pltpu.roll(dense[3, e, c], 7, 0))
+        u_t = load_matrix(lambda e: dense[e, c])
+        ahead = load_matrix(lambda e: pltpu.roll(dense[e, c], 7, 0))
         two = mat_mul(u_t, ahead)
         later = tuple(
             [[pltpu.roll(part[i][j], 6, 0) for j in range(3)] for i in range(3)] for part in two[:2]
@@ -227,8 +236,10 @@
         four = mat_mul(two, later)
 
         def write(e, value):
-            block[pl.ds(4 * e + c, 1), :] = value[0:1]
-            block[pl.ds(4 * e + 2 + c, 1), :] = value[4:5]
+            if e % 9 < 6:
+                row = 4 * (e // 9 * 6 + e % 9)
+                block[pl.ds(row + c, 1), :] = value[0:1]
+                block[pl.ds(row + 2 + c, 1), :] = value[4:5]
 
         store_matrix(four, write)
         return carry
@@ -383,23 +394,32 @@
     count = gathered_ref.shape[0]
 
     def read(d):
-        return load_matrix(lambda e: slabs[4 * e:4 * e + 4, :])
-
-    slabs = gathered_ref[0, 0:SLABROWS, :].astype(F32)
-    product = read(0)
-    state = tuple(product[0][i][j] for i in range(3) for j in range(3)) + tuple(
-        product[1][i][j] for i in range(3) for j in range(3)
-    )
+        slab = gathered_ref[d, 0:SLABROWS, :].astype(F32)
+        real = [[slab[4 * (3 * i + j):4 * (3 * i + j) + 4, :] for j in range(3)] for i in range(2)]
+        imag = [[slab[24 + 4 * (3 * i + j):28 + 4 * (3 * i + j), :] for j in range(3)] for i in range(2)]
+        real.append([])
+        imag.append([])
+        for k in range(3):
+            i, j = (k + 1) % 3, (k + 2) % 3
+            real[2].append(
+                (real[0][i] * real[1][j] - imag[0][i] * imag[1][j])
+                - (real[0][j] * real[1][i] - imag[0][j] * imag[1][i])
+            )
+            imag[2].append(
+                (real[0][j] * imag[1][i] + imag[0][j] * real[1][i])
+                - (real[0][i] * imag[1][j] + imag[0][i] * real[1][j])
+            )
+        return (real, imag, 1)
+
+    def flat(matrix):
+        return tuple(matrix[0][i][j] for i in range(3) for j in range(3)) + tuple(
+            imag_of(matrix, i, j) for i in range(3) for j in range(3)
+        )
 
     def chain(d, state):
-        slab = gathered_ref[d, 0:SLABROWS, :].astype(F32)
-        left = load_matrix(lambda e: state[e])
-        product = mat_mul(left, load_matrix(lambda e: slab[4 * e:4 * e + 4, :]))
-        out = []
-        store_matrix(product, lambda e, value: out.append((e, value)))
-        return tuple(value for _, value in sorted(out, key=lambda item: item[0]))
-
-    state = lax.fori_loop(1, count, chain, state)
+        return flat(mat_mul(load_matrix(lambda e: state[e]), read(d)))
+
+    state = lax.fori_loop(1, count, chain, flat(read(0)))
     loops_ref[0] = (state[0] + state[4] + state[8]) / 3.0
     loops_ref[1] = (state[9] + state[13] + state[17]) / 3.0
 
@@ -609,7 +629,7 @@
         packed[rows, 96:104] = grad_first[:, 8 * k:8 * k + 8]
     if split:
         for d in range(16):
-            grads_ref[d] = packed[27 * d:27 * d + 27, :].astype(BF16)
+            grads_ref[d % 4 * 4 + d // 4] = packed[27 * d:27 * d + 27, :].astype(BF16)
     else:
         grads_ref[...] = packed[...].astype(BF16)
 
@@ -633,6 +653,15 @@
         return carry
 
     lax.fori_loop(0, 4, body, 0)
+
+
+def half_kernel(inner, parts_ref, out_ref):
+    outer = out_ref.shape[0]
+    for z in range(outer):
+        value = parts_ref[z].astype(F32)
+        for c in range(1, inner):
+            value = value + parts_ref[c * outer + z].astype(F32)
+        out_ref[z] = value.astype(BF16)
 
 
 def sum_kernel(widths, parts_ref, first_ref, second_ref, third_ref, last_ref):
@@ -668,13 +697,18 @@
         return lax.ppermute(value, "tm", [(i, (i + distance) % count) for i in range(count)])
 
     widths = (768 // count, 768 // count, 128 // count, 64 // count)
-    up, down, block = call(
-        functools.partial(first_kernel, widths),
-        [((54, SITES), BF16), ((54, SITES), BF16), ((BLOCKROWS, LANES), BF16)],
-        [((4, 18, 2, 8, LANES), F32), ((3, 18, 2, 8, LANES), F32), ((54, 4, LANES), F32), ((BLOCKROWS, LANES), F32)],
-    )(links, w_first[None], w_second[None], w_third[None], w_last[None])
+    up, down = call(
+        face_kernel,
+        [((54, SITES), BF16), ((54, SITES), BF16)],
+        [((4, 18, 2, 8, LANES), F32), ((3, 18, 2, 8, LANES), F32), ((54, 4, LANES), F32)],
+    )(links)
     up = send(up, 1)
     down = send(down, -1)
+    (block,) = call(
+        functools.partial(block_kernel, widths),
+        [((BLOCKROWS, LANES), BF16)],
+        [((18, 2, 8, LANES), F32), ((BLOCKROWS, LANES), F32)],
+    )(links, w_first[None], w_second[None], w_third[None], w_last[None])
     gathered = lax.all_to_all(
         jnp.broadcast_to(block[None], (count,) + block.shape), "tm", split_axis=0, concat_axis=0, tiled=True
     )
@@ -732,7 +766,21 @@
             pieces.append(grads[:, offset:offset + full].reshape(count, 27, width))
             offset += full
         grads = jnp.concatenate(pieces, axis=2)
-    grads = lax.all_to_all(grads, "tm", split_axis=0, concat_axis=0, tiled=True)
+        grads = grads.reshape(count // 4, 4, 27, grads.shape[2]).swapaxes(0, 1)
+        grads = grads.reshape(count, 27, grads.shape[3])
+    inner = 4
+    outer = count // inner
+    near = [[inner * z + c for c in range(inner)] for z in range(outer)]
+    far = [[inner * z + c for z in range(outer)] for c in range(inner)]
+    grads = lax.all_to_all(
+        grads, "tm", split_axis=0, concat_axis=0, axis_index_groups=near, tiled=True
+    )
+    (grads,) = call(
+        functools.partial(half_kernel, inner), [((outer,) + grads.shape[1:], BF16)], []
+    )(grads)
+    grads = lax.all_to_all(
+        grads, "tm", split_axis=0, concat_axis=0, axis_index_groups=far, tiled=True
+    )
     (new_links,) = call(
         update_kernel, [(links.shape, F32)], [((4, 2, 8, LANES), F32)]
     )(links, applied, twice, coeff)

time: 72.2 us -> 72.5 us (level)
  blocking collectives: 0 us -> 7.02 us
  waiting for transfers between devices: 16.5 us -> 9.9 us
    all_to_all x0 -> x1, blocking collectives: none -> 7.02 us  [on_device(): lax.all_to_all(grads, 'tm', split_axis=0, concat_axis=0, axis_index_group...]
    ppermute x6, waiting for transfers between devices: 9.62 us -> 5.26 us  [send(): lax.ppermute(value, 'tm', [(i, (i + distance) % count) for i in range(cou...]
    all_to_all x1, waiting for transfers between devices: 6.91 us -> 4.64 us  [on_device(): lax.all_to_all(grads, 'tm', split_axis=0, concat_axis=0, axis_index_group...]
    all_to_all x1, starting transfers between devices: 6.1 us -> 5.03 us  [on_device(): lax.all_to_all(grads, 'tm', split_axis=0, concat_axis=0, axis_index_group...]
    ppermute x6, starting transfers between devices: 9.77 us -> 10.8 us  [send(): lax.ppermute(value, 'tm', [(i, (i + distance) % count) for i in range(cou...]
    pallas_call x1 -> x3, Pallas kernels: 2.48 us -> 3.19 us  [the longest x1 2.26 us: on_device(): call(face_kernel, [((54, SITES), BF16), ((54, SITES), BF16)], [((4, 18, 2...]
  transfers between devices with their start and end apart: 8 -> 8, of which waited for: 3 -> 3; matrix products, arithmetic and copies ran while one was open for 0% -> 0% of each run, Pallas kernels for 14% -> 17%
where the time goes in v2:
time: 72.5 us; the launch traced here: 72.1 us
  Pallas kernels  27.3 us (38%)
  starting transfers between devices  23.2 us (32%)
  waiting for transfers between devices  9.9 us (14%)
  blocking collectives  7.02 us (10%)
  local copies, waits for them, and re-layouts  3.88 us (5%)
  between operations  0.74 us (1%)
    pallas_call x1, Pallas kernels, on_device(): call(functools.partial(conv_kernel, count == 16), [((4, 8, SITES), F32),...  13.4 us
    ppermute x6, starting transfers between devices, send(): lax.ppermute(value, 'tm', [(i, (i + distance) % count) for i in range(cou...  10.8 us
    all_to_all x1, starting transfers between devices, on_device(): lax.all_to_all(jnp.broadcast_to(block[None], (count,) + block.shape), 'tm...  7.39 us
    pallas_call x1, Pallas kernels, on_device(): call(gauge_kernel, [((4, 16, SITES), BF16), ((3, 8, SITES), BF16), ((3, 8...  7.38 us
    all_to_all x1, blocking collectives, on_device(): lax.all_to_all(grads, 'tm', split_axis=0, concat_axis=0, axis_index_group...  7.02 us
    ppermute x6, waiting for transfers between devices, send(): lax.ppermute(value, 'tm', [(i, (i + distance) % count) for i in range(cou...  5.26 us
    all_to_all x1, starting transfers between devices, on_device(): lax.all_to_all(grads, 'tm', split_axis=0, concat_axis=0, axis_index_group...  5.03 us
    all_to_all x1, waiting for transfers between devices, on_device(): lax.all_to_all(grads, 'tm', split_axis=0, concat_axis=0, axis_index_group...  4.64 us
  transfers between devices with their start and end apart: 8, of which 3 were waited for; matrix products, arithmetic and copies ran while one was open for 0% of the time, Pallas kernels for 17%

profile of v2, /device:TPU:0, one launch (start us, length us, event | category | flops | bytes accessed | tf_op | source)
XLA Modules:
  0.0 72.1 jit_solution(9198984136045163486)
XLA Ops:
  0.6 0.7 broadcast_in_dim.18.w1_ref
  1.3 0.7 broadcast_in_dim.19.w2_ref
  2.0 0.6 copy-done.5
  2.7 1.1 %copy-done = f32[4,2,3,3,1,4,512]{6,5,4,3,2,1,0:T(4,128)S(1)} copy-done((f32[4,2,3,3,1,4,512]{6,5,4,3,2,1,0:T(4,128)S(1)}, f32[4,2,3,3,1,4,512]{6,5,4,3,2,1,0:T(4,128)}, u32[]{:S(2)}) %copy-start) | copy-done | bytes 589848
  3.7 0.3 shard_map.121
  4.1 0.8 %broadcast_in_dim.22 = bf16[16,80,128]{2,1,0:T(8,128)(2,1)} broadcast(bf16[80,128]{1,0:T(8,128)(2,1)S(1)} %shard_map.121), dimensions={1,2} | broadcast | bytes 348160 | tf_op jit(solution)/shard_map/broadcast_in_dim | solution.py:713
  4.8 7.4 %all-to-all-start = ((bf16[16,80,128]{2,1,0:T(8,128)(2,1)}), bf16[16,80,128]{2,1,0:T(8,128)(2,1)S(1)}, u32[]{:S(2)}, u32[]{:S(2)}) async-start(bf16[16,80,128]{2,1,0:T(8,128)(2,1)} %broadcast_in_dim.22), calls=%async_computation | async-start | bytes 655360 | tf_op jit(solution)/shard_map/all_to_all | solution.py:712
  12.2 0.0 copy-start.2
  12.2 2.3 %shard_map.119 = (bf16[54,512]{1,0:T(8,128)(2,1)S(1)}, bf16[54,512]{1,0:T(8,128)(2,1)S(1)}) custom-call(f32[4,2,3,3,1,4,512]{6,5,4,3,2,1,0:T(4,128)S(1)} %copy-done.1), custom_call_target="tpu_custom_call" | custom-call | tf_op jit(solution)/shard_map/pallas_call | solution.py:700
  14.5 0.5 collective-permute-start
  15.0 4.0 %collective-permute-start.1 = (bf16[54,512]{1,0:T(8,128)(2,1)S(1)}, bf16[54,512]{1,0:T(8,128)(2,1)S(1)}, u32[]{:S(2)}, u32[]{:S(2)}) collective-permute-start(bf16[54,512]{1,0:T(8,128)(2,1)S(1)} %get-tuple-element.27), channel_id=1, source_target_pairs={{0,15},{1,0},{2,1},{3,2},{4,3},{5,4},{6,5},{7,6},{8,7},{9,8},{10,9... | collective-permute-start | bytes 165896 | tf_op jit(solution)/shard_map/ppermute | solution.py:697
  19.0 4.9 %collective-permute-done.up_ref = bf16[54,512]{1,0:T(8,128)(2,1)S(1)} collective-permute-done((bf16[54,512]{1,0:T(8,128)(2,1)S(1)}, bf16[54,512]{1,0:T(8,128)(2,1)S(1)}, u32[]{:S(2)}, u32[]{:S(2)}) %collective-permute-start) | collective-permute-done | bytes 55328 | tf_op jit(solution)/shard_map/ppermute | solution.py:697
  24.0 7.4 %shard_map.120 = (bf16[4,16,512]{2,1,0:T(8,128)(2,1)S(1)}, bf16[3,8,512]{2,1,0:T(8,128)(2,1)S(1)}, bf16[3,8,512]{2,1,0:T(8,128)(2,1)S(1)}, f32[4,18,2,8,128]{4,3,2,1,0:T(8,128)S(1)}, f32[4,18,2,8,128]{4,3,2,1,0:T(8,128)S(1)}) custom-call(f32[4,2,3,3,1,4,512]{6,5,4,3,2,1,0:T(4,128)S(1)} %copy-done.1, bf16[4,2,3,3,1,4,512]{6,5,4,3,2,1,0:T(4,128)(2,1)S(1)} %copy-done.2, ...), custom_call_target="tpu_custom_call" | custom-call | tf_op jit(solution)/shard_map/pallas_call | solution.py:715
  31.3 1.5 %collective-permute-start.3 = (bf16[4,16,512]{2,1,0:T(8,128)(2,1)S(1)}, bf16[4,16,512]{2,1,0:T(8,128)(2,1)S(1)}, u32[]{:S(2)}, u32[]{:S(2)}) collective-permute-start(bf16[4,16,512]{2,1,0:T(8,128)(2,1)S(1)} %get-tuple-element.30.fm_ref), channel_id=1, source_target_pairs={{0,15},{1,0},{2,1},{3,2},{4,3},{5,4},{6,5},{7,6},{8,7},{9,8},{10,9... | collective-permute-start | bytes 196616 | tf_op jit(solution)/shard_map/ppermute | solution.py:697
  32.9 4.8 %collective-permute-start.5 = (bf16[3,8,512]{2,1,0:T(8,128)(2,1)S(1)}, bf16[3,8,512]{2,1,0:T(8,128)(2,1)S(1)}, u32[]{:S(2)}, u32[]{:S(2)}) collective-permute-start(bf16[3,8,512]{2,1,0:T(8,128)(2,1)S(1)} %get-tuple-element.32), channel_id=1, source_target_pairs={{0,14},{1,15},{2,0},{3,1},{4,2},{5,3},{6,4},{7,5},{8,6},{9,7},{10,... | collective-permute-start | bytes 73736 | tf_op jit(solution)/shard_map/ppermute | solution.py:697
  37.6 1.6 %shard_map.122 = (f32[2,4,128]{2,1,0:T(4,128)S(1)}, bf16[48,72]{1,0:T(8,128)(2,1)S(1)}, bf16[48,432]{1,0:T(8,128)(2,1)S(1)}, bf16[48,432]{1,0:T(8,128)(2,1)S(1)}...) custom-call(bf16[16,80,128]{2,1,0:T(8,128)(2,1)S(1)} %all-to-all-don, ...), custom_call_target="tpu_custom_call" | custom-call | tf_op jit(solution)/shard_map/pallas_call | solution.py:739
  39.3 0.3 collective-permute-done.4.fbelow_ref
  39.6 13.4 %shard_map.123 = (f32[4,8,512]{2,1,0:T(8,128)S(1)}, bf16[16,27,128]{2,1,0:T(8,128)(2,1)S(1)}) custom-call(bf16[4,16,512]{2,1,0:T(8,128)(2,1)S(1)} %get-tuple-element.30.fm_ref, bf16[4,16,512]{2,1,0:T(8,128)(2,1)S(1)} %collective-permute-done.2.below_ref, bf16[4,16,512]{2,1,0:T(8,128)(2,1)S(1)} %collective-permute-done.3.above_ref, ...), custom_call_target="tpu_custom_call" | custom-call | tf_op jit(solution)/shard_map/pallas_call | solution.py:753
  53.0 7.0 %all_to_all.15.parts_ref = bf16[16,27,128]{2,1,0:T(8,128)(2,1)S(1)} all-to-all(bf16[16,27,128]{2,1,0:T(8,128)(2,1)S(1)} %get-tuple-element.42), channel_id=1, replica_groups={{0,1,2,3},{4,5,6,7},{8,9,10,11},{12,13,14,15},{16,17,18,19},{20,21,22,2..., dimensions={0} | all-to-all | bytes 221184 | tf_op jit(solution)/shard_map/all_to_all | solution.py:775
  60.0 0.6 shard_map.125
  60.7 5.0 %all-to-all-start.2 = ((bf16[4,27,128]{2,1,0:T(8,128)(2,1)}), bf16[4,27,128]{2,1,0:T(8,128)(2,1)S(1)}, u32[]{:S(2)}, u32[]{:S(2)}) async-start(bf16[4,27,128]{2,1,0:T(8,128)(2,1)} %shard_map.125), calls=%async_computation.2 | async-start | bytes 65536 | tf_op jit(solution)/shard_map/all_to_all | solution.py:781
  65.7 1.0 %shard_map.124 = f32[4,2,3,3,1,4,512]{6,5,4,3,2,1,0:T(4,128)} custom-call(f32[4,2,3,3,1,4,512]{6,5,4,3,2,1,0:T(4,128)S(1)} %copy-done.1, f32[4,18,2,8,128]{4,3,2,1,0:T(8,128)S(1)} %get-tuple-element.28.w1_ref, f32[4,18,2,8,128]{4,3,2,1,0:T(8,128)S(1)} %get-tuple-element.29.w2_ref, f32[4,8,512]{2,1,0:T(8,128)S(1)} %get-tuple-element.41.coeff_ref), custom_call_target="tpu_custom_call" | custom-call | tf_op jit(solution)/shard_map/pallas_call | solution.py:784
  66.7 4.6 %all-to-all-done.2.parts_ref = bf16[4,27,128]{2,1,0:T(8,128)(2,1)S(1)} async-done(((bf16[4,27,128]{2,1,0:T(8,128)(2,1)}), bf16[4,27,128]{2,1,0:T(8,128)(2,1)S(1)}, u32[]{:S(2)}, u32[]{:S(2)}) %all-to-all-start.2) | async-done | bytes 27680 | tf_op jit(solution)/shard_map/all_to_all | solution.py:781
  71.3 0.7 %shard_map.126 = (f32[1,216]{1,0:T(1,128)}, f32[1,1296]{1,0:T(1,128)}, f32[1,1296]{1,0:T(1,128)}, f32[1,108]{1,0:T(1,128)}) custom-call(bf16[4,27,128]{2,1,0:T(8,128)(2,1)S(1)} %all-to-all-done.2.parts_ref), custom_call_target="tpu_custom_call" | custom-call | tf_op jit(solution)/shard_map/pallas_call | solution.py:787
  (19 shorter events, 0.1 us)
Async XLA Ops:
  1.3 0.7 copy-start.6
  2.0 0.7 copy-start.5
  2.7 1.1 %copy-start = (f32[4,2,3,3,1,4,512]{6,5,4,3,2,1,0:T(4,128)S(1)}, f32[4,2,3,3,1,4,512]{6,5,4,3,2,1,0:T(4,128)}, u32[]{:S(2)}) copy-start(f32[4,2,3,3,1,4,512]{6,5,4,3,2,1,0:T(4,128)} %links_ref.7) | copy-start | bytes 1769476
  4.0 8.2 %copy-start.1 = (f32[4,2,3,3,1,4,512]{6,5,4,3,2,1,0:T(4,128)S(1)}, f32[4,2,3,3,1,4,512]{6,5,4,3,2,1,0:T(4,128)}, u32[]{:S(2)}) copy-start(f32[4,2,3,3,1,4,512]{6,5,4,3,2,1,0:T(4,128)} %links_ref.7) | copy-start | bytes 1769476
  4.8 32.8 %all-to-all-start = ((bf16[16,80,128]{2,1,0:T(8,128)(2,1)}), bf16[16,80,128]{2,1,0:T(8,128)(2,1)S(1)}, u32[]{:S(2)}, u32[]{:S(2)}) async-start(bf16[16,80,128]{2,1,0:T(8,128)(2,1)} %broadcast_in_dim.22), calls=%async_computation | async-start | bytes 655360 | tf_op jit(solution)/shard_map/all_to_all | solution.py:712
  12.2 11.7 %copy-start.2 = (bf16[4,2,3,3,1,4,512]{6,5,4,3,2,1,0:T(4,128)(2,1)S(1)}, bf16[4,2,3,3,1,4,512]{6,5,4,3,2,1,0:T(4,128)(2,1)}, u32[]{:S(2)}) copy-start(bf16[4,2,3,3,1,4,512]{6,5,4,3,2,1,0:T(4,128)(2,1)} %cot_ref.1) | copy-start | bytes 884740
  14.5 9.4 %copy-start.3 = (s32[1,4]{1,0:T(1,128)S(1)}, s32[1,4]{1,0:T(1,128)}, u32[]{:S(2)}) copy-start(s32[1,4]{1,0:T(1,128)} %parity_ref.1) | copy-start | bytes 52
  14.5 9.4 %copy-start.4 = (s32[1,4]{1,0:T(1,128)S(1)}, s32[1,4]{1,0:T(1,128)}, u32[]{:S(2)}) copy-start(s32[1,4]{1,0:T(1,128)} %subset_ref.1) | copy-start | bytes 52
  14.5 9.4 %collective-permute-start = (bf16[54,512]{1,0:T(8,128)(2,1)S(1)}, bf16[54,512]{1,0:T(8,128)(2,1)S(1)}, u32[]{:S(2)}, u32[]{:S(2)}) collective-permute-start(bf16[54,512]{1,0:T(8,128)(2,1)S(1)} %get-tuple-element.26), channel_id=1, source_target_pairs={{0,1},{1,2},{2,3},{3,4},{4,5},{5,6},{6,7},{7,8},{8,9},{9,10},{10,1... | collective-permute-start | bytes 165896 | tf_op jit(solution)/shard_map/ppermute | solution.py:697
  15.0 9.0 %collective-permute-start.1 = (bf16[54,512]{1,0:T(8,128)(2,1)S(1)}, bf16[54,512]{1,0:T(8,128)(2,1)S(1)}, u32[]{:S(2)}, u32[]{:S(2)}) collective-permute-start(bf16[54,512]{1,0:T(8,128)(2,1)S(1)} %get-tuple-element.27), channel_id=1, source_target_pairs={{0,15},{1,0},{2,1},{3,2},{4,3},{5,4},{6,5},{7,6},{8,7},{9,8},{10,9... | collective-permute-start | bytes 165896 | tf_op jit(solution)/shard_map/ppermute | solution.py:697
  31.3 8.3 %collective-permute-start.3 = (bf16[4,16,512]{2,1,0:T(8,128)(2,1)S(1)}, bf16[4,16,512]{2,1,0:T(8,128)(2,1)S(1)}, u32[]{:S(2)}, u32[]{:S(2)}) collective-permute-start(bf16[4,16,512]{2,1,0:T(8,128)(2,1)S(1)} %get-tuple-element.30.fm_ref), channel_id=1, source_target_pairs={{0,15},{1,0},{2,1},{3,2},{4,3},{5,4},{6,5},{7,6},{8,7},{9,8},{10,9... | collective-permute-start | bytes 196616 | tf_op jit(solution)/shard_map/ppermute | solution.py:697
  32.9 6.8 %collective-permute-start.2 = (bf16[4,16,512]{2,1,0:T(8,128)(2,1)S(1)}, bf16[4,16,512]{2,1,0:T(8,128)(2,1)S(1)}, u32[]{:S(2)}, u32[]{:S(2)}) collective-permute-start(bf16[4,16,512]{2,1,0:T(8,128)(2,1)S(1)} %get-tuple-element.30.fm_ref), channel_id=1, source_target_pairs={{0,1},{1,2},{2,3},{3,4},{4,5},{5,6},{6,7},{7,8},{8,9},{9,10},{10,1... | collective-permute-start | bytes 196616 | tf_op jit(solution)/shard_map/ppermute | solution.py:697
  32.9 6.8 %collective-permute-start.4 = (bf16[3,8,512]{2,1,0:T(8,128)(2,1)S(1)}, bf16[3,8,512]{2,1,0:T(8,128)(2,1)S(1)}, u32[]{:S(2)}, u32[]{:S(2)}) collective-permute-start(bf16[3,8,512]{2,1,0:T(8,128)(2,1)S(1)} %get-tuple-element.31), channel_id=1, source_target_pairs={{0,2},{1,3},{2,4},{3,5},{4,6},{5,7},{6,8},{7,9},{8,10},{9,11},{10,... | collective-permute-start | bytes 73736 | tf_op jit(solution)/shard_map/ppermute | solution.py:697
  32.9 6.8 %collective-permute-start.5 = (bf16[3,8,512]{2,1,0:T(8,128)(2,1)S(1)}, bf16[3,8,512]{2,1,0:T(8,128)(2,1)S(1)}, u32[]{:S(2)}, u32[]{:S(2)}) collective-permute-start(bf16[3,8,512]{2,1,0:T(8,128)(2,1)S(1)} %get-tuple-element.32), channel_id=1, source_target_pairs={{0,14},{1,15},{2,0},{3,1},{4,2},{5,3},{6,4},{7,5},{8,6},{9,7},{10,... | collective-permute-start | bytes 73736 | tf_op jit(solution)/shard_map/ppermute | solution.py:697
  60.7 10.7 %all-to-all-start.2 = ((bf16[4,27,128]{2,1,0:T(8,128)(2,1)}), bf16[4,27,128]{2,1,0:T(8,128)(2,1)S(1)}, u32[]{:S(2)}, u32[]{:S(2)}) async-start(bf16[4,27,128]{2,1,0:T(8,128)(2,1)} %shard_map.125), calls=%async_computation.2 | async-start | bytes 65536 | tf_op jit(solution)/shard_map/all_to_all | solution.py:781

commit v3 on v2

--- a/solution.py
+++ b/solution.py
@@ -221,14 +221,12 @@
         down_ref[:, q * 128:q * 128 + 128] = rows[:, q, :].astype(BF16)
 
 
-def block_kernel(widths, links_ref, w1_ref, w2_ref, w3_ref, w4_ref, block_ref, dense, block):
-    for e, (part, i, j) in enumerate(ENTRIES):
-        dense[e, 0], dense[e, 1] = pack_pair(links_ref[3, part, i, j, 0])
+def block_kernel(widths, dense, w1_ref, w2_ref, w3_ref, w4_ref, block_ref, block):
     block[...] = jnp.zeros_like(block)
 
     def slab_body(c, carry):
-        u_t = load_matrix(lambda e: dense[e, c])
-        ahead = load_matrix(lambda e: pltpu.roll(dense[e, c], 7, 0))
+        u_t = load_matrix(lambda e: dense[3, e, c])
+        ahead = load_matrix(lambda e: pltpu.roll(dense[3, e, c], 7, 0))
         two = mat_mul(u_t, ahead)
         later = tuple(
             [[pltpu.roll(part[i][j], 6, 0) for j in range(3)] for i in range(3)] for part in two[:2]
@@ -255,11 +253,10 @@
 
 
 def gauge_kernel(
-    links_ref, cot_ref, up_ref, down_ref, parity_ref, subset_ref,
+    dense, cot_ref, up_ref, down_ref, parity_ref, subset_ref,
     fm_ref, fup_ref, fdown_ref, w1_ref, w2_ref,
-    dense, cots, moved, staples, sums, halo_up, halo_down, forces, rows,
+    cots, moved, staples, sums, halo_up, halo_down, forces, rows,
 ):
-    pack_links(links_ref, dense)
     pack_links(cot_ref, cots)
     for q in range(4):
         halo_up[:, q, :] = up_ref[:, q * 128:q * 128 + 128].astype(F32)
@@ -629,7 +626,7 @@
         packed[rows, 96:104] = grad_first[:, 8 * k:8 * k + 8]
     if split:
         for d in range(16):
-            grads_ref[d % 4 * 4 + d // 4] = packed[27 * d:27 * d + 27, :].astype(BF16)
+            grads_ref[d] = packed[27 * d:27 * d + 27, :].astype(BF16)
     else:
         grads_ref[...] = packed[...].astype(BF16)
 
@@ -655,15 +652,6 @@
     lax.fori_loop(0, 4, body, 0)
 
 
-def half_kernel(inner, parts_ref, out_ref):
-    outer = out_ref.shape[0]
-    for z in range(outer):
-        value = parts_ref[z].astype(F32)
-        for c in range(1, inner):
-            value = value + parts_ref[c * outer + z].astype(F32)
-        out_ref[z] = value.astype(BF16)
-
-
 def sum_kernel(widths, parts_ref, first_ref, second_ref, third_ref, last_ref):
     value = parts_ref[0].astype(F32)
     for d in range(1, parts_ref.shape[0]):
@@ -675,7 +663,7 @@
         offset += width
 
 
-def call(body, outs, scratch, smem=(), count=0):
+def call(body, outs, scratch, smem=(), count=0, cost=None):
     specs = {}
     if smem:
         specs["in_specs"] = [
@@ -686,6 +674,7 @@
         out_shape=[jax.ShapeDtypeStruct(shape, dtype) for shape, dtype in outs],
         scratch_shapes=[pltpu.VMEM(shape, dtype) for shape, dtype in scratch],
         compiler_params=pltpu.CompilerParams(vmem_limit_bytes=LIMIT),
+        cost_estimate=cost,
         **specs,
     )
 
@@ -697,18 +686,19 @@
         return lax.ppermute(value, "tm", [(i, (i + distance) % count) for i in range(count)])
 
     widths = (768 // count, 768 // count, 128 // count, 64 // count)
-    up, down = call(
+    up, down, dense = call(
         face_kernel,
-        [((54, SITES), BF16), ((54, SITES), BF16)],
-        [((4, 18, 2, 8, LANES), F32), ((3, 18, 2, 8, LANES), F32), ((54, 4, LANES), F32)],
+        [((54, SITES), BF16), ((54, SITES), BF16), ((4, 18, 2, 8, LANES), F32)],
+        [((3, 18, 2, 8, LANES), F32), ((54, 4, LANES), F32)],
     )(links)
     up = send(up, 1)
     down = send(down, -1)
     (block,) = call(
         functools.partial(block_kernel, widths),
         [((BLOCKROWS, LANES), BF16)],
-        [((18, 2, 8, LANES), F32), ((BLOCKROWS, LANES), F32)],
-    )(links, w_first[None], w_second[None], w_third[None], w_last[None])
+        [((BLOCKROWS, LANES), F32)],
+        cost=pl.CostEstimate(flops=4_000_000_000, bytes_accessed=16_000_000, transcendentals=0),
+    )(dense, w_first[None], w_second[None], w_third[None], w_last[None])
     gathered = lax.all_to_all(
         jnp.broadcast_to(block[None], (count,) + block.shape), "tm", split_axis=0, concat_axis=0, tiled=True
     )
@@ -719,12 +709,12 @@
             ((4, 18, 2, 8, LANES), F32), ((4, 18, 2, 8, LANES), F32),
         ],
         [
-            ((4, 18, 2, 8, LANES), F32), ((4, 18, 2, 8, LANES), F32), ((4, 4, 18, 2, 8, LANES), F32),
+            ((4, 18, 2, 8, LANES), F32), ((4, 4, 18, 2, 8, LANES), F32),
             ((4, 4, 18, 2, 8, LANES), F32), ((4, 18, 2, 8, LANES), F32), ((54, 4, LANES), F32), ((54, 4, LANES), F32),
             ((4, 9, 2, 8, LANES), F32), ((4, 4, 16, LANES), F32),
         ],
         smem=(4, 5), count=6,
-    )(links, cotangent, up, down, parity, link_subset)
+    )(dense, cotangent, up, down, parity, link_subset)
     below = send(fm, 1)
     above = send(fm, -1)
     fbelow = send(fup, 2)
@@ -766,21 +756,7 @@
             pieces.append(grads[:, offset:offset + full].reshape(count, 27, width))
             offset += full
         grads = jnp.concatenate(pieces, axis=2)
-        grads = grads.reshape(count // 4, 4, 27, grads.shape[2]).swapaxes(0, 1)
-        grads = grads.reshape(count, 27, grads.shape[3])
-    inner = 4
-    outer = count // inner
-    near = [[inner * z + c for c in range(inner)] for z in range(outer)]
-    far = [[inner * z + c for z in range(outer)] for c in range(inner)]
-    grads = lax.all_to_all(
-        grads, "tm", split_axis=0, concat_axis=0, axis_index_groups=near, tiled=True
-    )
-    (grads,) = call(
-        functools.partial(half_kernel, inner), [((outer,) + grads.shape[1:], BF16)], []
-    )(grads)
-    grads = lax.all_to_all(
-        grads, "tm", split_axis=0, concat_axis=0, axis_index_groups=far, tiled=True
-    )
+    grads = lax.all_to_all(grads, "tm", split_axis=0, concat_axis=0, tiled=True)
     (new_links,) = call(
         update_kernel, [(links.shape, F32)], [((4, 2, 8, LANES), F32)]
     )(links, applied, twice, coeff)

time: 72.5 us -> 73.2 us (level)
  blocking collectives: 7.02 us -> 0 us
  waiting for transfers between devices: 9.9 us -> 14.2 us
  starting transfers between devices: 23.2 us -> 27.3 us
    all_to_all x1 -> x0, blocking collectives: 7.02 us -> none  [on_device(): lax.all_to_all(grads, 'tm', split_axis=0, concat_axis=0, axis_index_group...]
    ppermute x6, starting transfers between devices: 10.8 us -> 13.7 us  [send(): lax.ppermute(value, 'tm', [(i, (i + distance) % count) for i in range(cou...]
    all_to_all x1, waiting for transfers between devices: 4.64 us -> 6.9 us  [on_device(): grads = lax.all_to_all(grads, 'tm', split_axis=0, concat_axis=0, tiled=True)]
    ppermute x6, waiting for transfers between devices: 5.26 us -> 7.34 us  [send(): lax.ppermute(value, 'tm', [(i, (i + distance) % count) for i in range(cou...]
    all_to_all x1, starting transfers between devices: 5.03 us -> 6.1 us  [on_device(): grads = lax.all_to_all(grads, 'tm', split_axis=0, concat_axis=0, tiled=True)]
    unnamed x14 -> x18, local copies, waits for them, and re-layouts: 1.74 us -> 2.41 us
    pallas_call x2 -> x1, Pallas kernels: 2.88 us -> 2.25 us  [on_device(): call(face_kernel, [((54, SITES), BF16), ((54, SITES), BF16), ((4, 18, 2,...]
  transfers between devices with their start and end apart: 8 -> 8, of which waited for: 3 -> 3; matrix products, arithmetic and copies ran while one was open for 0% -> 0% of each run, Pallas kernels for 17% -> 14%
where the time goes in v3:
time: 73.2 us; the launch traced here: 72.8 us
  Pallas kernels  27.3 us (37%)
  starting transfers between devices  27.3 us (37%)
  waiting for transfers between devices  14.2 us (19%)
  local copies, waits for them, and re-layouts  3.2 us (4%)
  between operations  0.78 us (1%)
    pallas_call x1, Pallas kernels, on_device(): call(functools.partial(conv_kernel, count == 16), [((4, 8, SITES), F32),...  14 us
    ppermute x6, starting transfers between devices, send(): lax.ppermute(value, 'tm', [(i, (i + distance) % count) for i in range(cou...  13.7 us
    all_to_all x1, starting transfers between devices, on_device(): lax.all_to_all(jnp.broadcast_to(block[None], (count,) + block.shape), 'tm...  7.52 us
    ppermute x6, waiting for transfers between devices, send(): lax.ppermute(value, 'tm', [(i, (i + distance) % count) for i in range(cou...  7.34 us
    pallas_call x1, Pallas kernels, on_device(): call(gauge_kernel, [((4, 16, SITES), BF16), ((3, 8, SITES), BF16), ((3, 8...  7.31 us
    all_to_all x1, waiting for transfers between devices, on_device(): grads = lax.all_to_all(grads, 'tm', split_axis=0, concat_axis=0, tiled=True)  6.9 us
    all_to_all x1, starting transfers between devices, on_device(): grads = lax.all_to_all(grads, 'tm', split_axis=0, concat_axis=0, tiled=True)  6.1 us
    unnamed x18, local copies, waits for them, and re-layouts  2.41 us
  transfers between devices with their start and end apart: 8, of which 3 were waited for; matrix products, arithmetic and copies ran while one was open for 0% of the time, Pallas kernels for 14%

profile of v3, /device:TPU:0, one launch (start us, length us, event | category | flops | bytes accessed | tf_op | source)
XLA Modules:
  0.0 72.8 jit_solution(7885797683498390983)
XLA Ops:
  0.6 0.0 copy-start
  0.6 1.1 %copy-done = f32[4,2,3,3,1,4,512]{6,5,4,3,2,1,0:T(4,128)S(1)} copy-done((f32[4,2,3,3,1,4,512]{6,5,4,3,2,1,0:T(4,128)S(1)}, f32[4,2,3,3,1,4,512]{6,5,4,3,2,1,0:T(4,128)}, u32[]{:S(2)}) %copy-start) | copy-done | bytes 589848
  1.7 2.2 %shard_map.119 = (bf16[54,512]{1,0:T(8,128)(2,1)S(1)}, bf16[54,512]{1,0:T(8,128)(2,1)S(1)}, f32[4,18,2,8,128]{4,3,2,1,0:T(8,128)S(1)}) custom-call(f32[4,2,3,3,1,4,512]{6,5,4,3,2,1,0:T(4,128)S(1)} %copy-done), custom_call_target="tpu_custom_call" | custom-call | tf_op jit(solution)/shard_map/pallas_call | solution.py:689
  4.0 0.0 copy-start.7
  4.0 0.7 copy-done.7
  4.7 0.7 copy-done.5
  5.3 0.3 shard_map.121
  5.6 0.8 %broadcast_in_dim.22 = bf16[16,80,128]{2,1,0:T(8,128)(2,1)} broadcast(bf16[80,128]{1,0:T(8,128)(2,1)S(1)} %shard_map.121), dimensions={1,2} | broadcast | bytes 348160 | tf_op jit(solution)/shard_map/broadcast_in_dim | solution.py:703
  6.4 7.5 %all-to-all-start = ((bf16[16,80,128]{2,1,0:T(8,128)(2,1)}), bf16[16,80,128]{2,1,0:T(8,128)(2,1)S(1)}, u32[]{:S(2)}, u32[]{:S(2)}) async-start(bf16[16,80,128]{2,1,0:T(8,128)(2,1)} %broadcast_in_dim.22), calls=%async_computation | async-start | bytes 655360 | tf_op jit(solution)/shard_map/all_to_all | solution.py:702
  14.0 0.5 collective-permute-start
  14.4 4.0 %collective-permute-start.1 = (bf16[54,512]{1,0:T(8,128)(2,1)S(1)}, bf16[54,512]{1,0:T(8,128)(2,1)S(1)}, u32[]{:S(2)}, u32[]{:S(2)}) collective-permute-start(bf16[54,512]{1,0:T(8,128)(2,1)S(1)} %get-tuple-element.29), channel_id=1, source_target_pairs={{0,15},{1,0},{2,1},{3,2},{4,3},{5,4},{6,5},{7,6},{8,7},{9,8},{10,9... | collective-permute-start | bytes 165896 | tf_op jit(solution)/shard_map/ppermute | solution.py:686
  18.5 7.2 %collective-permute-done.up_ref = bf16[54,512]{1,0:T(8,128)(2,1)S(1)} collective-permute-done((bf16[54,512]{1,0:T(8,128)(2,1)S(1)}, bf16[54,512]{1,0:T(8,128)(2,1)S(1)}, u32[]{:S(2)}, u32[]{:S(2)}) %collective-permute-start) | collective-permute-done | bytes 55328 | tf_op jit(solution)/shard_map/ppermute | solution.py:686
  25.7 7.3 %shard_map.120 = (bf16[4,16,512]{2,1,0:T(8,128)(2,1)S(1)}, bf16[3,8,512]{2,1,0:T(8,128)(2,1)S(1)}, bf16[3,8,512]{2,1,0:T(8,128)(2,1)S(1)}, f32[4,18,2,8,128]{4,3,2,1,0:T(8,128)S(1)}, f32[4,18,2,8,128]{4,3,2,1,0:T(8,128)S(1)}) custom-call(f32[4,18,2,8,128]{4,3,2,1,0:T(8,128)S(1)} %get-tuple-element.27.dense, bf16[4,2,3,3,1,4,512]{6,5,4,3,2,1,0:T(4,128)(2,1)S(1)} %copy-done.2, ...), custom_call_target="tpu_custom_call" | custom-call | tf_op jit(solution)/shard_map/pallas_call | solution.py:705
  33.0 0.0 copy-start.1
  33.0 0.1 collective-permute-start.2
  33.1 4.4 %collective-permute-start.3 = (bf16[4,16,512]{2,1,0:T(8,128)(2,1)S(1)}, bf16[4,16,512]{2,1,0:T(8,128)(2,1)S(1)}, u32[]{:S(2)}, u32[]{:S(2)}) collective-permute-start(bf16[4,16,512]{2,1,0:T(8,128)(2,1)S(1)} %get-tuple-element.32.fm_ref), channel_id=1, source_target_pairs={{0,15},{1,0},{2,1},{3,2},{4,3},{5,4},{6,5},{7,6},{8,7},{9,8},{10,9... | collective-permute-start | bytes 196616 | tf_op jit(solution)/shard_map/ppermute | solution.py:686
  37.5 4.7 %collective-permute-start.5 = (bf16[3,8,512]{2,1,0:T(8,128)(2,1)S(1)}, bf16[3,8,512]{2,1,0:T(8,128)(2,1)S(1)}, u32[]{:S(2)}, u32[]{:S(2)}) collective-permute-start(bf16[3,8,512]{2,1,0:T(8,128)(2,1)S(1)} %get-tuple-element.34), channel_id=1, source_target_pairs={{0,14},{1,15},{2,0},{3,1},{4,2},{5,3},{6,4},{7,5},{8,6},{9,7},{10,... | collective-permute-start | bytes 73736 | tf_op jit(solution)/shard_map/ppermute | solution.py:686
  42.2 1.6 %shard_map.122 = (f32[2,4,128]{2,1,0:T(4,128)S(1)}, bf16[48,72]{1,0:T(8,128)(2,1)S(1)}, bf16[48,432]{1,0:T(8,128)(2,1)S(1)}, bf16[48,432]{1,0:T(8,128)(2,1)S(1)}...) custom-call(bf16[16,80,128]{2,1,0:T(8,128)(2,1)S(1)} %all-to-all-don, ...), custom_call_target="tpu_custom_call" | custom-call | tf_op jit(solution)/shard_map/pallas_call | solution.py:729
  43.9 0.1 collective-permute-done.4.fbelow_ref
  44.0 14.0 %shard_map.123 = (f32[4,8,512]{2,1,0:T(8,128)S(1)}, bf16[16,27,128]{2,1,0:T(8,128)(2,1)}) custom-call(bf16[4,16,512]{2,1,0:T(8,128)(2,1)S(1)} %get-tuple-element.32.fm_ref, bf16[4,16,512]{2,1,0:T(8,128)(2,1)S(1)} %collective-permute-done.2.below_ref, bf16[4,16,512]{2,1,0:T(8,128)(2,1)S(1)} %collective-permute-done.3.above_ref, ...), custom_call_target="tpu_custom_call" | custom-call | tf_op jit(solution)/shard_map/pallas_call | solution.py:743
  58.1 6.1 %all-to-all-start.1 = ((bf16[16,27,128]{2,1,0:T(8,128)(2,1)}), bf16[16,27,128]{2,1,0:T(8,128)(2,1)S(1)}, u32[]{:S(2)}, u32[]{:S(2)}) async-start(bf16[16,27,128]{2,1,0:T(8,128)(2,1)} %get-tuple-element.44), calls=%async_computation.1 | async-start | bytes 262144 | tf_op jit(solution)/shard_map/all_to_all | solution.py:759
  64.2 1.0 %shard_map.124 = f32[4,2,3,3,1,4,512]{6,5,4,3,2,1,0:T(4,128)} custom-call(f32[4,2,3,3,1,4,512]{6,5,4,3,2,1,0:T(4,128)S(1)} %copy-done.1, f32[4,18,2,8,128]{4,3,2,1,0:T(8,128)S(1)} %get-tuple-element.30.w1_ref, f32[4,18,2,8,128]{4,3,2,1,0:T(8,128)S(1)} %get-tuple-element.31.w2_ref, f32[4,8,512]{2,1,0:T(8,128)S(1)} %get-tuple-element.43.coeff_ref), custom_call_target="tpu_custom_call" | custom-call | tf_op jit(solution)/shard_map/pallas_call | solution.py:760
  65.2 6.9 %all-to-all-done.1.parts_ref = bf16[16,27,128]{2,1,0:T(8,128)(2,1)S(1)} async-done(((bf16[16,27,128]{2,1,0:T(8,128)(2,1)}), bf16[16,27,128]{2,1,0:T(8,128)(2,1)S(1)}, u32[]{:S(2)}, u32[]{:S(2)}) %all-to-all-start.1) | async-done | bytes 110624 | tf_op jit(solution)/shard_map/all_to_all | solution.py:759
  72.1 0.8 %shard_map.125 = (f32[1,216]{1,0:T(1,128)}, f32[1,1296]{1,0:T(1,128)}, f32[1,1296]{1,0:T(1,128)}, f32[1,108]{1,0:T(1,128)}) custom-call(bf16[16,27,128]{2,1,0:T(8,128)(2,1)S(1)} %all-to-all-done.1.parts_ref), custom_call_target="tpu_custom_call" | custom-call | tf_op jit(solution)/shard_map/pallas_call | solution.py:763
  (21 shorter events, 0.1 us)
Async XLA Ops:
  0.6 1.1 %copy-start = (f32[4,2,3,3,1,4,512]{6,5,4,3,2,1,0:T(4,128)S(1)}, f32[4,2,3,3,1,4,512]{6,5,4,3,2,1,0:T(4,128)}, u32[]{:S(2)}) copy-start(f32[4,2,3,3,1,4,512]{6,5,4,3,2,1,0:T(4,128)} %links_ref.3) | copy-start | bytes 1769476
  1.7 2.3 %copy-start.8 = (bf16[216]{0:T(256)(128)(2,1)S(1)}, bf16[216]{0:T(256)(128)(2,1)}, u32[]{:S(2)}) copy-start(bf16[216]{0:T(256)(128)(2,1)} %param.12) | copy-start | bytes 1300
  1.7 2.3 %copy-start.6 = (bf16[1296]{0:T(1024)(128)(2,1)S(1)}, bf16[1296]{0:T(1024)(128)(2,1)}, u32[]{:S(2)}) copy-start(bf16[1296]{0:T(1024)(128)(2,1)} %param.13) | copy-start | bytes 7780
  4.0 0.7 copy-start.7
  4.7 0.7 copy-start.5
  6.4 19.2 %copy-start.2 = (bf16[4,2,3,3,1,4,512]{6,5,4,3,2,1,0:T(4,128)(2,1)S(1)}, bf16[4,2,3,3,1,4,512]{6,5,4,3,2,1,0:T(4,128)(2,1)}, u32[]{:S(2)}) copy-start(bf16[4,2,3,3,1,4,512]{6,5,4,3,2,1,0:T(4,128)(2,1)} %cot_ref.1) | copy-start | bytes 884740
  6.4 35.8 %all-to-all-start = ((bf16[16,80,128]{2,1,0:T(8,128)(2,1)}), bf16[16,80,128]{2,1,0:T(8,128)(2,1)S(1)}, u32[]{:S(2)}, u32[]{:S(2)}) async-start(bf16[16,80,128]{2,1,0:T(8,128)(2,1)} %broadcast_in_dim.22), calls=%async_computation | async-start | bytes 655360 | tf_op jit(solution)/shard_map/all_to_all | solution.py:702
  13.9 11.7 %copy-start.3 = (s32[1,4]{1,0:T(1,128)S(1)}, s32[1,4]{1,0:T(1,128)}, u32[]{:S(2)}) copy-start(s32[1,4]{1,0:T(1,128)} %parity_ref.1) | copy-start | bytes 52
  14.0 11.7 %copy-start.4 = (s32[1,4]{1,0:T(1,128)S(1)}, s32[1,4]{1,0:T(1,128)}, u32[]{:S(2)}) copy-start(s32[1,4]{1,0:T(1,128)} %subset_ref.1) | copy-start | bytes 52
  14.0 11.7 %collective-permute-start = (bf16[54,512]{1,0:T(8,128)(2,1)S(1)}, bf16[54,512]{1,0:T(8,128)(2,1)S(1)}, u32[]{:S(2)}, u32[]{:S(2)}) collective-permute-start(bf16[54,512]{1,0:T(8,128)(2,1)S(1)} %get-tuple-element.28), channel_id=1, source_target_pairs={{0,1},{1,2},{2,3},{3,4},{4,5},{5,6},{6,7},{7,8},{8,9},{9,10},{10,1... | collective-permute-start | bytes 165896 | tf_op jit(solution)/shard_map/ppermute | solution.py:686
  14.4 11.2 %collective-permute-start.1 = (bf16[54,512]{1,0:T(8,128)(2,1)S(1)}, bf16[54,512]{1,0:T(8,128)(2,1)S(1)}, u32[]{:S(2)}, u32[]{:S(2)}) collective-permute-start(bf16[54,512]{1,0:T(8,128)(2,1)S(1)} %get-tuple-element.29), channel_id=1, source_target_pairs={{0,15},{1,0},{2,1},{3,2},{4,3},{5,4},{6,5},{7,6},{8,7},{9,8},{10,9... | collective-permute-start | bytes 165896 | tf_op jit(solution)/shard_map/ppermute | solution.py:686
  33.0 31.2 %copy-start.1 = (f32[4,2,3,3,1,4,512]{6,5,4,3,2,1,0:T(4,128)S(1)}, f32[4,2,3,3,1,4,512]{6,5,4,3,2,1,0:T(4,128)}, u32[]{:S(2)}) copy-start(f32[4,2,3,3,1,4,512]{6,5,4,3,2,1,0:T(4,128)} %links_ref.3) | copy-start | bytes 1769476
  33.0 11.0 %collective-permute-start.2 = (bf16[4,16,512]{2,1,0:T(8,128)(2,1)S(1)}, bf16[4,16,512]{2,1,0:T(8,128)(2,1)S(1)}, u32[]{:S(2)}, u32[]{:S(2)}) collective-permute-start(bf16[4,16,512]{2,1,0:T(8,128)(2,1)S(1)} %get-tuple-element.32.fm_ref), channel_id=1, source_target_pairs={{0,1},{1,2},{2,3},{3,4},{4,5},{5,6},{6,7},{7,8},{8,9},{9,10},{10,1... | collective-permute-start | bytes 196616 | tf_op jit(solution)/shard_map/ppermute | solution.py:686
  33.1 11.0 %collective-permute-start.3 = (bf16[4,16,512]{2,1,0:T(8,128)(2,1)S(1)}, bf16[4,16,512]{2,1,0:T(8,128)(2,1)S(1)}, u32[]{:S(2)}, u32[]{:S(2)}) collective-permute-start(bf16[4,16,512]{2,1,0:T(8,128)(2,1)S(1)} %get-tuple-element.32.fm_ref), channel_id=1, source_target_pairs={{0,15},{1,0},{2,1},{3,2},{4,3},{5,4},{6,5},{7,6},{8,7},{9,8},{10,9... | collective-permute-start | bytes 196616 | tf_op jit(solution)/shard_map/ppermute | solution.py:686
  37.5 6.5 %collective-permute-start.4 = (bf16[3,8,512]{2,1,0:T(8,128)(2,1)S(1)}, bf16[3,8,512]{2,1,0:T(8,128)(2,1)S(1)}, u32[]{:S(2)}, u32[]{:S(2)}) collective-permute-start(bf16[3,8,512]{2,1,0:T(8,128)(2,1)S(1)} %get-tuple-element.33), channel_id=1, source_target_pairs={{0,2},{1,3},{2,4},{3,5},{4,6},{5,7},{6,8},{7,9},{8,10},{9,11},{10,... | collective-permute-start | bytes 73736 | tf_op jit(solution)/shard_map/ppermute | solution.py:686
  37.5 6.5 %collective-permute-start.5 = (bf16[3,8,512]{2,1,0:T(8,128)(2,1)S(1)}, bf16[3,8,512]{2,1,0:T(8,128)(2,1)S(1)}, u32[]{:S(2)}, u32[]{:S(2)}) collective-permute-start(bf16[3,8,512]{2,1,0:T(8,128)(2,1)S(1)} %get-tuple-element.34), channel_id=1, source_target_pairs={{0,14},{1,15},{2,0},{3,1},{4,2},{5,3},{6,4},{7,5},{8,6},{9,7},{10,... | collective-permute-start | bytes 73736 | tf_op jit(solution)/shard_map/ppermute | solution.py:686
  58.1 14.0 %all-to-all-start.1 = ((bf16[16,27,128]{2,1,0:T(8,128)(2,1)}), bf16[16,27,128]{2,1,0:T(8,128)(2,1)S(1)}, u32[]{:S(2)}, u32[]{:S(2)}) async-start(bf16[16,27,128]{2,1,0:T(8,128)(2,1)} %get-tuple-element.44), calls=%async_computation.1 | async-start | bytes 262144 | tf_op jit(solution)/shard_map/all_to_all | solution.py:759

commit v4 on v3

--- a/solution.py
+++ b/solution.py
@@ -16,8 +16,8 @@
 PAIRS = ((0, 1), (0, 2), (0, 3), (1, 2), (1, 3), (2, 3))
 SWAP = (0, 2, 1, 4, 3, 6, 5, 8, 7)
 ENTRIES = tuple((c, i, j) for c in range(2) for i in range(3) for j in range(3))
-SLABROWS = 48
-BLOCKROWS = 80
+SLABROWS = 24
+BLOCKROWS = 64
 LIMIT = 40 * 1024 * 1024
 
 
@@ -106,9 +106,10 @@
     lr, li, ls = left
     rr, ri, rs = right
     same = ls == rs
-    real = [[None] * 3 for _ in range(3)]
-    imag = [[None] * 3 for _ in range(3)]
-    for i in range(3):
+    height = len(lr)
+    real = [[None] * 3 for _ in range(height)]
+    imag = [[None] * 3 for _ in range(height)]
+    for i in range(height):
         for j in range(3):
             real[i][j] = total(
                 [lr[i][k] * rr[k][j] for k in range(3)] + [li[i][k] * ri[k][j] for k in range(3)],
@@ -130,6 +131,35 @@
         for j in range(3):
             write(3 * i + j, matrix[0][i][j])
             write(9 + 3 * i + j, imag_of(matrix, i, j))
+
+
+def two_rows(read):
+    real = [[read(3 * i + j) for j in range(3)] for i in range(2)]
+    imag = [[read(6 + 3 * i + j) for j in range(3)] for i in range(2)]
+    return (real, imag, 1)
+
+
+def store_rows(matrix, write):
+    for i in range(2):
+        for j in range(3):
+            write(3 * i + j, matrix[0][i][j])
+            write(6 + 3 * i + j, imag_of(matrix, i, j))
+
+
+def special(matrix):
+    real, imag, _ = matrix
+    last_r, last_i = [], []
+    for k in range(3):
+        i, j = (k + 1) % 3, (k + 2) % 3
+        last_r.append(
+            (real[0][i] * real[1][j] - imag[0][i] * imag[1][j])
+            - (real[0][j] * real[1][i] - imag[0][j] * imag[1][i])
+        )
+        last_i.append(
+            (real[0][j] * imag[1][i] + imag[0][j] * real[1][i])
+            - (real[0][i] * imag[1][j] + imag[0][i] * real[1][j])
+        )
+    return (real + [last_r], imag + [last_i], 1)
 
 
 def anti_parts(matrix):
@@ -176,7 +206,7 @@
     lax.fori_loop(0, 4, body, 0)
 
 
-def face_kernel(links_ref, up_ref, down_ref, dense, moved, rows):
+def face_kernel(links_ref, up_ref, down_ref, dense, edges, staples, slab, moved, rows):
     pack_links(links_ref, dense)
 
     def shift_body(e, carry):
@@ -195,34 +225,21 @@
         u_mu = load_matrix(lambda e: dense[mu, e, c])
         u_t = load_matrix(lambda e: dense[3, e, c])
         edge = mat_mul(u_mu, load_matrix(lambda e: moved[mu, e, c]))
-        staple = mat_mul(dagger(edge), u_t)
+
+        def write_edge(e, value):
+            edges[mu, e, c] = value
+
+        store_matrix(edge, write_edge)
 
         def write(e, value):
+            staples[mu, e, c] = value
             rows[mu * 18 + e, pl.ds(c, 1)] = value[3:4]
             rows[mu * 18 + e, pl.ds(2 + c, 1)] = value[7:8]
 
-        store_matrix(staple, write)
+        store_matrix(mat_mul(dagger(edge), u_t), write)
         return carry
 
     lax.fori_loop(0, 6, staple_body, 0)
-    for q in range(4):
-        up_ref[:, q * 128:q * 128 + 128] = rows[:, q, :].astype(BF16)
-
-    def down_body(e, carry):
-        for mu in range(3):
-            for c in range(2):
-                value = dense[mu, e, c]
-                rows[mu * 18 + e, c:c + 1] = value[0:1]
-                rows[mu * 18 + e, 2 + c:3 + c] = value[4:5]
-        return carry
-
-    lax.fori_loop(0, 18, down_body, 0)
-    for q in range(4):
-        down_ref[:, q * 128:q * 128 + 128] = rows[:, q, :].astype(BF16)
-
-
-def block_kernel(widths, dense, w1_ref, w2_ref, w3_ref, w4_ref, block_ref, block):
-    block[...] = jnp.zeros_like(block)
 
     def slab_body(c, carry):
         u_t = load_matrix(lambda e: dense[3, e, c])
@@ -231,73 +248,97 @@
         later = tuple(
             [[pltpu.roll(part[i][j], 6, 0) for j in range(3)] for i in range(3)] for part in two[:2]
         ) + (two[2],)
-        four = mat_mul(two, later)
+        four = mat_mul((two[0][:2], two[1][:2], two[2]), later)
 
         def write(e, value):
-            if e % 9 < 6:
-                row = 4 * (e // 9 * 6 + e % 9)
-                block[pl.ds(row + c, 1), :] = value[0:1]
-                block[pl.ds(row + 2 + c, 1), :] = value[4:5]
-
-        store_matrix(four, write)
+            slab[e, pl.ds(c, 1)] = value[0:1]
+            slab[e, pl.ds(2 + c, 1)] = value[4:5]
+            rows[54 + e, pl.ds(c, 1)] = value[0:1]
+            rows[54 + e, pl.ds(2 + c, 1)] = value[4:5]
+
+        store_rows(four, write)
         return carry
 
     lax.fori_loop(0, 2, slab_body, 0)
+    for q in range(4):
+        up_ref[:, q * 128:q * 128 + 128] = rows[:, q, :].astype(BF16)
+
+    def down_body(e, carry):
+        for mu in range(3):
+            for c in range(2):
+                value = dense[mu, e, c]
+                rows[mu * 18 + e, c:c + 1] = value[0:1]
+                rows[mu * 18 + e, 2 + c:3 + c] = value[4:5]
+        return carry
+
+    lax.fori_loop(0, 18, down_body, 0)
+    for q in range(4):
+        down_ref[:, q * 128:q * 128 + 128] = rows[:, q, :].astype(BF16)
+
+
+def block_kernel(
+    widths, core_ref, up_ref, down_ref, slab, w1_ref, w2_ref, w3_ref, w4_ref, block_ref, other, block
+):
+    even = core_ref[0] == 0
+    up = up_ref[...].astype(F32)
+    down = down_ref[...].astype(F32)
+    for q in range(4):
+        lanes = slice(q * 128, q * 128 + 128)
+        other[:, q, :] = jnp.where(even, down[54:66, lanes], up[54:66, lanes])
+    first = two_rows(lambda e: jnp.where(even, slab[e], other[e]))
+    second = special(two_rows(lambda e: jnp.where(even, other[e], slab[e])))
+    block[...] = jnp.zeros_like(block)
+
+    def write(e, value):
+        block[2 * e:2 * e + 2, :] = jnp.where(even, value[0:2], value[2:4])
+
+    store_rows(mat_mul(first, second), write)
     offset = 0
     for ref, width in zip((w2_ref, w3_ref, w1_ref, w4_ref), widths):
         flat = ref[...].astype(F32)
         for r in range(27):
             block[SLABROWS + r:SLABROWS + r + 1, offset:offset + width] = flat[:, width * r:width * r + width]
         offset += width
-    block_ref[...] = block[...].astype(BF16)
-
-
-def gauge_kernel(
-    dense, cot_ref, up_ref, down_ref, parity_ref, subset_ref,
-    fm_ref, fup_ref, fdown_ref, w1_ref, w2_ref,
-    cots, moved, staples, sums, halo_up, halo_down, forces, rows,
-):
+    value = block[...].astype(BF16)
+    for d in range(block_ref.shape[0]):
+        block_ref[d] = value
+
+
+def put_row(rows, channel, c, value):
+    for t in range(4):
+        rows[t, c, pl.ds(channel, 1), :] = value[t:t + 1]
+        rows[t, 2 + c, pl.ds(channel, 1), :] = value[4 + t:5 + t]
+
+
+def space_kernel(dense, cot_ref, time_staples, cots, rows, forces, sums, moved, staples):
     pack_links(cot_ref, cots)
-    for q in range(4):
-        halo_up[:, q, :] = up_ref[:, q * 128:q * 128 + 128].astype(F32)
-        halo_down[:, q, :] = down_ref[:, q * 128:q * 128 + 128].astype(F32)
     rows[...] = jnp.zeros_like(rows)
     forces[...] = jnp.zeros_like(forces)
     steps = row_iota() % 4
-    lanes = lane_iota(8)
 
     def shift_body(e, carry):
-        for nu in range(4):
+        for nu in range(3):
             pair = [dense[nu, e, 0], dense[nu, e, 1]]
             for mu in range(3):
                 if mu != nu:
                     low, high = dense_shift(pair, mu, 1)
                     moved[mu, nu, e, 0] = low
                     moved[mu, nu, e, 1] = high
-            if nu < 3:
-                halo = halo_pair(halo_down, nu * 18 + e)
-                for c in range(2):
-                    moved[3, nu, e, c] = jnp.where(steps == 3, halo[c], pltpu.roll(pair[c], 7, 0))
         return carry
 
     lax.fori_loop(0, 18, shift_body, 0)
-
-    def put_row(channel, c, value):
-        for t in range(4):
-            rows[t, c, pl.ds(channel, 1), :] = value[t:t + 1]
-            rows[t, 2 + c, pl.ds(channel, 1), :] = value[4 + t:5 + t]
 
     def plane_body(step, carry):
         plane = step // 2
         c = step % 2
-        mu = jnp.where(plane < 3, 0, jnp.where(plane < 5, 1, 2))
-        nu = jnp.where(plane < 3, plane + 1, jnp.where(plane < 5, plane - 1, 3))
+        mu = jnp.where(plane == 2, 1, 0)
+        nu = jnp.where(plane == 0, 1, 2)
         u_mu = load_matrix(lambda e: dense[mu, e, c])
         u_nu = load_matrix(lambda e: dense[nu, e, c])
         one = mat_mul(u_mu, load_matrix(lambda e: moved[mu, nu, e, c]))
         two = mat_mul(u_nu, load_matrix(lambda e: moved[nu, mu, e, c]))
         loop = mat_mul(one, dagger(two))
-        put_row(plane, c, (loop[0][0][0] + loop[0][1][1] + loop[0][2][2]) / 3.0)
+        put_row(rows, jnp.where(plane == 2, 3, plane), c, (loop[0][0][0] + loop[0][1][1] + loop[0][2][2]) / 3.0)
         for e, part in enumerate(anti_parts(loop)):
             forces[mu, e, c] += part
             forces[nu, e, c] -= part
@@ -312,23 +353,72 @@
         store_matrix(mat_mul(dagger(two), u_mu), write_nu)
         return carry
 
-    lax.fori_loop(0, 12, plane_body, 0)
+    lax.fori_loop(0, 6, plane_body, 0)
 
     def lower_body(e, carry):
-        for mu in range(4):
-            acc = [None, None]
-            for nu in range(4):
-                if nu == mu:
-                    continue
-                pair = [staples[mu, nu, e, 0], staples[mu, nu, e, 1]]
-                if nu < 3:
-                    pair = dense_shift(pair, nu, -1)
-                else:
-                    halo = halo_pair(halo_up, mu * 18 + e)
-                    pair = [jnp.where(steps == 0, halo[c], pltpu.roll(pair[c], 1, 0)) for c in range(2)]
-                acc = [pair[c] if acc[c] is None else acc[c] + pair[c] for c in range(2)]
+        for mu in range(3):
+            acc = [jnp.where(steps == 0, 0.0, pltpu.roll(time_staples[mu, e, c], 1, 0)) for c in range(2)]
+            for nu in range(3):
+                if nu != mu:
+                    pair = dense_shift([staples[mu, nu, e, 0], staples[mu, nu, e, 1]], nu, -1)
+                    acc = [acc[c] + pair[c] for c in range(2)]
             sums[mu, e, 0] = acc[0]
             sums[mu, e, 1] = acc[1]
+        return carry
+
+    lax.fori_loop(0, 18, lower_body, 0)
+
+
+def time_kernel(
+    dense, cots, up_ref, down_ref, parity_ref, subset_ref, edges, rows_ref, forces_ref, sums_ref,
+    fm_ref, fup_ref, fdown_ref, w1_ref, w2_ref,
+    moved, staples, sums, halo_up, halo_down, forces, rows,
+):
+    for q in range(4):
+        halo_up[:, q, :] = up_ref[:, q * 128:q * 128 + 128].astype(F32)
+        halo_down[:, q, :] = down_ref[:, q * 128:q * 128 + 128].astype(F32)
+    rows[...] = rows_ref[...]
+    forces[...] = forces_ref[...]
+    steps = row_iota() % 4
+    lanes = lane_iota(8)
+
+    def shift_body(e, carry):
+        for nu in range(3):
+            halo = halo_pair(halo_down, nu * 18 + e)
+            below = halo_pair(halo_up, nu * 18 + e)
+            for c in range(2):
+                moved[nu, e, c] = jnp.where(steps == 3, halo[c], pltpu.roll(dense[nu, e, c], 7, 0))
+                sums[nu, e, c] = sums_ref[nu, e, c] + jnp.where(steps == 0, below[c], 0.0)
+        return carry
+
+    lax.fori_loop(0, 18, shift_body, 0)
+
+    def plane_body(step, carry):
+        mu = step // 2
+        c = step % 2
+        one = load_matrix(lambda e: edges[mu, e, c])
+        two = mat_mul(load_matrix(lambda e: dense[3, e, c]), load_matrix(lambda e: moved[mu, e, c]))
+        loop = mat_mul(one, dagger(two))
+        put_row(rows, jnp.where(mu == 0, 2, mu + 3), c, (loop[0][0][0] + loop[0][1][1] + loop[0][2][2]) / 3.0)
+        for e, part in enumerate(anti_parts(loop)):
+            forces[mu, e, c] += part
+            forces[3, e, c] -= part
+
+        def write(e, value):
+            staples[mu, e, c] = value
+
+        store_matrix(mat_mul(dagger(two), load_matrix(lambda e: dense[mu, e, c])), write)
+        return carry
+
+    lax.fori_loop(0, 6, plane_body, 0)
+
+    def lower_body(e, carry):
+        acc = None
+        for mu in range(3):
+            pair = dense_shift([staples[mu, e, 0], staples[mu, e, 1]], mu, -1)
+            acc = pair if acc is None else [acc[c] + pair[c] for c in range(2)]
+        sums[3, e, 0] = acc[0]
+        sums[3, e, 1] = acc[1]
         return carry
 
     lax.fori_loop(0, 18, lower_body, 0)
@@ -361,8 +451,8 @@
             curve = curve + weight * twice[part][i][j]
             w1_ref[mu, e, c] = gate * applied[part][i][j]
             w2_ref[mu, e, c] = gate * twice[part][i][j]
-        put_row(8 + mu, c, gate * slope)
-        put_row(12 + mu, c, gate * curve)
+        put_row(rows, 8 + mu, c, gate * slope)
+        put_row(rows, 12 + mu, c, gate * curve)
         return carry
 
     lax.fori_loop(0, 8, force_body, 0)
@@ -390,40 +480,29 @@
 def panel_kernel(gathered_ref, weights_ref, loops_ref, p1_ref, p2_ref, p3_ref, p4_ref, b2_ref, b3_ref, b4_ref, weights):
     count = gathered_ref.shape[0]
 
-    def read(d):
-        slab = gathered_ref[d, 0:SLABROWS, :].astype(F32)
-        real = [[slab[4 * (3 * i + j):4 * (3 * i + j) + 4, :] for j in range(3)] for i in range(2)]
-        imag = [[slab[24 + 4 * (3 * i + j):28 + 4 * (3 * i + j), :] for j in range(3)] for i in range(2)]
-        real.append([])
-        imag.append([])
-        for k in range(3):
-            i, j = (k + 1) % 3, (k + 2) % 3
-            real[2].append(
-                (real[0][i] * real[1][j] - imag[0][i] * imag[1][j])
-                - (real[0][j] * real[1][i] - imag[0][j] * imag[1][i])
-            )
-            imag[2].append(
-                (real[0][j] * imag[1][i] + imag[0][j] * real[1][i])
-                - (real[0][i] * imag[1][j] + imag[0][i] * real[1][j])
-            )
-        return (real, imag, 1)
+    def read(chip):
+        low = gathered_ref[2 * chip].astype(F32)
+        high = gathered_ref[2 * chip + 1].astype(F32)
+        return special(
+            two_rows(lambda e: jnp.concatenate([low[2 * e:2 * e + 2], high[2 * e:2 * e + 2]], axis=0))
+        )
 
     def flat(matrix):
         return tuple(matrix[0][i][j] for i in range(3) for j in range(3)) + tuple(
             imag_of(matrix, i, j) for i in range(3) for j in range(3)
         )
 
-    def chain(d, state):
-        return flat(mat_mul(load_matrix(lambda e: state[e]), read(d)))
-
-    state = lax.fori_loop(1, count, chain, flat(read(0)))
+    def chain(chip, state):
+        return flat(mat_mul(load_matrix(lambda e: state[e]), read(chip)))
+
+    state = lax.fori_loop(1, count // 2, chain, flat(read(0)))
     loops_ref[0] = (state[0] + state[4] + state[8]) / 3.0
     loops_ref[1] = (state[9] + state[13] + state[17]) / 3.0
 
     if weights_ref is None:
         for d in range(count):
-            block = gathered_ref[d, SLABROWS:BLOCKROWS, :].astype(F32)
-            weights[27 * d:27 * d + 27, :] = block[0:27]
+            block = gathered_ref[d].astype(F32)
+            weights[27 * d:27 * d + 27, :] = block[SLABROWS:SLABROWS + 27]
     else:
         weights[...] = weights_ref[...].astype(F32)
     for k in range(TAPS):
@@ -686,35 +765,39 @@
         return lax.ppermute(value, "tm", [(i, (i + distance) % count) for i in range(count)])
 
     widths = (768 // count, 768 // count, 128 // count, 64 // count)
-    up, down, dense = call(
+    field = ((4, 18, 2, 8, LANES), F32)
+    space = ((3, 18, 2, 8, LANES), F32)
+    edge_rows = ((66, SITES), BF16)
+    up, down, dense, edges, staples, slab = call(
         face_kernel,
-        [((54, SITES), BF16), ((54, SITES), BF16), ((4, 18, 2, 8, LANES), F32)],
-        [((3, 18, 2, 8, LANES), F32), ((54, 4, LANES), F32)],
+        [edge_rows, edge_rows, field, space, space, ((12, 4, LANES), F32)],
+        [space, ((66, 4, LANES), F32)],
     )(links)
     up = send(up, 1)
     down = send(down, -1)
+    cots, rows, forces, sums = call(
+        space_kernel,
+        [field, ((4, 4, 16, LANES), F32), ((4, 9, 2, 8, LANES), F32), space],
+        [((3, 3, 18, 2, 8, LANES), F32), ((3, 3, 18, 2, 8, LANES), F32)],
+        cost=pl.CostEstimate(flops=4_000_000_000, bytes_accessed=16_000_000, transcendentals=0),
+    )(dense, cotangent, staples)
+    core = (lax.axis_index("tm") % 2).astype(jnp.int32)[None]
     (block,) = call(
         functools.partial(block_kernel, widths),
-        [((BLOCKROWS, LANES), BF16)],
-        [((BLOCKROWS, LANES), F32)],
-        cost=pl.CostEstimate(flops=4_000_000_000, bytes_accessed=16_000_000, transcendentals=0),
-    )(dense, w_first[None], w_second[None], w_third[None], w_last[None])
-    gathered = lax.all_to_all(
-        jnp.broadcast_to(block[None], (count,) + block.shape), "tm", split_axis=0, concat_axis=0, tiled=True
-    )
+        [((count, BLOCKROWS, LANES), BF16)],
+        [((12, 4, LANES), F32), ((BLOCKROWS, LANES), F32)],
+        smem=(0,), count=8,
+    )(core, up, down, slab, w_first[None], w_second[None], w_third[None], w_last[None])
+    gathered = lax.all_to_all(block, "tm", split_axis=0, concat_axis=0, tiled=True)
     fm, fup, fdown, applied, twice = call(
-        gauge_kernel,
+        time_kernel,
+        [((4, 16, SITES), BF16), ((3, 8, SITES), BF16), ((3, 8, SITES), BF16), field, field],
         [
-            ((4, 16, SITES), BF16), ((3, 8, SITES), BF16), ((3, 8, SITES), BF16),
-            ((4, 18, 2, 8, LANES), F32), ((4, 18, 2, 8, LANES), F32),
-        ],
-        [
-            ((4, 18, 2, 8, LANES), F32), ((4, 4, 18, 2, 8, LANES), F32),
-            ((4, 4, 18, 2, 8, LANES), F32), ((4, 18, 2, 8, LANES), F32), ((54, 4, LANES), F32), ((54, 4, LANES), F32),
+            space, space, field, ((66, 4, LANES), F32), ((66, 4, LANES), F32),
             ((4, 9, 2, 8, LANES), F32), ((4, 4, 16, LANES), F32),
         ],
-        smem=(4, 5), count=6,
-    )(dense, cotangent, up, down, parity, link_subset)
+        smem=(4, 5), count=10,
+    )(dense, cots, up, down, parity, link_subset, edges, rows, forces, sums)
     below = send(fm, 1)
     above = send(fm, -1)
     fbelow = send(fup, 2)

time: 73.2 us -> 68.6 us (0.937)
  waiting for transfers between devices: 14.2 us -> 8.13 us
  Pallas kernels: 27.3 us -> 28.7 us
    ppermute x6, waiting for transfers between devices: 7.34 us -> 1.22 us  [send(): lax.ppermute(value, 'tm', [(i, (i + distance) % count) for i in range(cou...]
    pallas_call x3 -> x4, Pallas kernels: 9.86 us -> 11.7 us  [the longest x1 4.28 us: on_device(): call(space_kernel, [field, ((4, 4, 16, LANES), F32), ((4, 9, 2, 8, LANES)...]
    all_to_all x1, starting transfers between devices: 7.52 us -> 5.9 us  [on_device(): lax.all_to_all(block, 'tm', split_axis=0, concat_axis=0, tiled=True)]
    unnamed x18, local copies, waits for them, and re-layouts: 2.41 us -> 3.74 us
    ppermute x6, starting transfers between devices: 13.7 us -> 14.8 us  [send(): lax.ppermute(value, 'tm', [(i, (i + distance) % count) for i in range(cou...]
    broadcast_in_dim x1 -> x0, local copies, waits for them, and re-layouts: 0.77 us -> none  [on_device(): jnp.broadcast_to(block[None], (count,) + block.shape)]
  transfers between devices with their start and end apart: 8 -> 8, of which waited for: 3 -> 3; matrix products, arithmetic and copies ran while one was open for 0% -> 0% of each run, Pallas kernels for 14% -> 16%
where the time goes in v4:
time: 68.6 us; the launch traced here: 68.1 us
  Pallas kernels  28.7 us (42%)
  starting transfers between devices  26.8 us (39%)
  waiting for transfers between devices  8.13 us (12%)
  local copies, waits for them, and re-layouts  3.76 us (5%)
  between operations  0.74 us (1%)
    ppermute x6, starting transfers between devices, send(): lax.ppermute(value, 'tm', [(i, (i + distance) % count) for i in range(cou...  14.8 us
    pallas_call x1, Pallas kernels, on_device(): call(functools.partial(conv_kernel, count == 16), [((4, 8, SITES), F32),...  14 us
    all_to_all x1, waiting for transfers between devices, on_device(): grads = lax.all_to_all(grads, 'tm', split_axis=0, concat_axis=0, tiled=True)  6.9 us
    all_to_all x1, starting transfers between devices, on_device(): grads = lax.all_to_all(grads, 'tm', split_axis=0, concat_axis=0, tiled=True)  6.09 us
    all_to_all x1, starting transfers between devices, on_device(): lax.all_to_all(block, 'tm', split_axis=0, concat_axis=0, tiled=True)  5.9 us
    pallas_call x1, Pallas kernels, on_device(): call(space_kernel, [field, ((4, 4, 16, LANES), F32), ((4, 9, 2, 8, LANES)...  4.28 us
    pallas_call x1, Pallas kernels, on_device(): call(time_kernel, [((4, 16, SITES), BF16), ((3, 8, SITES), BF16), ((3, 8,...  4.07 us
    unnamed x18, local copies, waits for them, and re-layouts  3.74 us
  transfers between devices with their start and end apart: 8, of which 3 were waited for; matrix products, arithmetic and copies ran while one was open for 0% of the time, Pallas kernels for 16%

profile of v4, /device:TPU:0, one launch (start us, length us, event | category | flops | bytes accessed | tf_op | source)
XLA Modules:
  0.0 68.1 jit_solution(7039602466642703664)
XLA Ops:
  0.6 1.1 %copy-done = f32[4,2,3,3,1,4,512]{6,5,4,3,2,1,0:T(4,128)S(1)} copy-done((f32[4,2,3,3,1,4,512]{6,5,4,3,2,1,0:T(4,128)S(1)}, f32[4,2,3,3,1,4,512]{6,5,4,3,2,1,0:T(4,128)}, u32[]{:S(2)}) %copy-start) | copy-done | bytes 589848
  1.7 2.4 %shard_map.119 = (bf16[66,512]{1,0:T(8,128)(2,1)S(1)}, bf16[66,512]{1,0:T(8,128)(2,1)S(1)}, f32[4,18,2,8,128]{4,3,2,1,0:T(8,128)S(1)}, f32[3,18,2,8,128]{4,3,2,1...) custom-call(f32[4,2,3,3,1,4,512]{6,5,4,3,2,1,0:T(4,128)S(1)} %copy-done), custom_call_target="tpu_custom_call" | custom-call | tf_op jit(solution)/shard_map/pallas_call | solution.py:771
  4.1 0.5 collective-permute-start
  4.6 5.1 %collective-permute-start.1 = (bf16[66,512]{1,0:T(8,128)(2,1)S(1)}, bf16[66,512]{1,0:T(8,128)(2,1)S(1)}, u32[]{:S(2)}, u32[]{:S(2)}) collective-permute-start(bf16[66,512]{1,0:T(8,128)(2,1)S(1)} %get-tuple-element.38), channel_id=1, source_target_pairs={{0,15},{1,0},{2,1},{3,2},{4,3},{5,4},{6,5},{7,6},{8,7},{9,8},{10,9... | collective-permute-start | bytes 202760 | tf_op jit(solution)/shard_map/ppermute | solution.py:765
  9.7 0.7 copy-done.8
  10.4 0.7 copy-done.7
  11.1 0.7 %collective-permute-done.up_ref = bf16[66,512]{1,0:T(8,128)(2,1)S(1)} collective-permute-done((bf16[66,512]{1,0:T(8,128)(2,1)S(1)}, bf16[66,512]{1,0:T(8,128)(2,1)S(1)}, u32[]{:S(2)}, u32[]{:S(2)}) %collective-permute-start) | collective-permute-done | bytes 67616 | tf_op jit(solution)/shard_map/ppermute | solution.py:765
  11.8 0.7 copy-done.2
  12.4 0.9 %shard_map.122 = bf16[16,64,128]{2,1,0:T(8,128)(2,1)} custom-call(s32[1]{0:T(128)} %bitcast.core_ref, bf16[66,512]{1,0:T(8,128)(2,1)S(1)} %collective-permute-done.up_ref, bf16[66,512]{1,0:T(8,128)(2,1)S(1)} %collective-permute-done.1.down_ref, f32[12,4,128]{2,1,0:T(4,128)S(1)} %get-tuple-element.48.slab, bf16[1,216]{1,0:T(2,128)(2,1)S(1)} %broadcast_in_dim.16.w1_ref, ...), custom_call_target="tpu_custom_call" | custom-call | tf_op jit(solution)/shard_map/pallas_call | solution.py:785
  13.3 5.9 %all-to-all-start = ((bf16[16,64,128]{2,1,0:T(8,128)(2,1)}), bf16[16,64,128]{2,1,0:T(8,128)(2,1)S(1)}, u32[]{:S(2)}, u32[]{:S(2)}) async-start(bf16[16,64,128]{2,1,0:T(8,128)(2,1)} %shard_map.122), calls=%async_computation | async-start | bytes 524288 | tf_op jit(solution)/shard_map/all_to_all | solution.py:791
  19.3 4.3 %shard_map.120 = (f32[4,18,2,8,128]{4,3,2,1,0:T(8,128)S(1)}, f32[4,4,16,128]{3,2,1,0:T(8,128)S(1)}, f32[4,9,2,8,128]{4,3,2,1,0:T(8,128)S(1)}, f32[3,18,2,8,128]{4,3,2,1,0:T(8,128)S(1)}) custom-call(f32[4,18,2,8,128]{4,3,2,1,0:T(8,128)S(1)} %get-tuple-element.34.dense, bf16[4,2,3,3,1,4,512]{6,5,4,3,2,1,0:T(4,128)(2,1)S(1)} %copy-done.5, ...), custom_call_target="tpu_custom_call" | custom-call | flops 4000000000 | bytes 16000000 | tf_op jit(solution)/shard_map/pallas_call | solution.py:778
  23.6 0.6 copy-done.3
  24.2 0.0 copy-done.4
  24.2 4.1 %shard_map.121 = (bf16[4,16,512]{2,1,0:T(8,128)(2,1)S(1)}, bf16[3,8,512]{2,1,0:T(8,128)(2,1)S(1)}, bf16[3,8,512]{2,1,0:T(8,128)(2,1)S(1)}, f32[4,18,2,8,128]{4,3,2,1,0:T(8,128)S(1)}, f32[4,18,2,8,128]{4,3,2,1,0:T(8,128)S(1)}) custom-call(f32[4,18,2,8,128]{4,3,2,1,0:T(8,128)S(1)} %get-tuple-element.34.dense, ...), custom_call_target="tpu_custom_call" | custom-call | tf_op jit(solution)/shard_map/pallas_call | solution.py:792
  28.3 0.5 collective-permute-start.2
  28.8 4.0 %collective-permute-start.3 = (bf16[4,16,512]{2,1,0:T(8,128)(2,1)S(1)}, bf16[4,16,512]{2,1,0:T(8,128)(2,1)S(1)}, u32[]{:S(2)}, u32[]{:S(2)}) collective-permute-start(bf16[4,16,512]{2,1,0:T(8,128)(2,1)S(1)} %get-tuple-element.45.fm_ref), channel_id=1, source_target_pairs={{0,15},{1,0},{2,1},{3,2},{4,3},{5,4},{6,5},{7,6},{8,7},{9,8},{10,9... | collective-permute-start | bytes 196616 | tf_op jit(solution)/shard_map/ppermute | solution.py:765
  32.8 4.7 %collective-permute-start.5 = (bf16[3,8,512]{2,1,0:T(8,128)(2,1)S(1)}, bf16[3,8,512]{2,1,0:T(8,128)(2,1)S(1)}, u32[]{:S(2)}, u32[]{:S(2)}) collective-permute-start(bf16[3,8,512]{2,1,0:T(8,128)(2,1)S(1)} %get-tuple-element.47), channel_id=1, source_target_pairs={{0,14},{1,15},{2,0},{3,1},{4,2},{5,3},{6,4},{7,5},{8,6},{9,7},{10,... | collective-permute-start | bytes 73736 | tf_op jit(solution)/shard_map/ppermute | solution.py:765
  37.5 1.3 %shard_map.123 = (f32[2,4,128]{2,1,0:T(4,128)S(1)}, bf16[48,72]{1,0:T(8,128)(2,1)S(1)}, bf16[48,432]{1,0:T(8,128)(2,1)S(1)}, bf16[48,432]{1,0:T(8,128)(2,1)S(1)}...) custom-call(bf16[16,64,128]{2,1,0:T(8,128)(2,1)S(1)} %all-to-all-don, ...), custom_call_target="tpu_custom_call" | custom-call | tf_op jit(solution)/shard_map/pallas_call | solution.py:812
  38.8 0.5 collective-permute-done.4.fbelow_ref
  39.3 14.0 %shard_map.124 = (f32[4,8,512]{2,1,0:T(8,128)S(1)}, bf16[16,27,128]{2,1,0:T(8,128)(2,1)}) custom-call(bf16[4,16,512]{2,1,0:T(8,128)(2,1)S(1)} %get-tuple-element.45.fm_ref, bf16[4,16,512]{2,1,0:T(8,128)(2,1)S(1)} %collective-permute-done.2.below_ref, bf16[4,16,512]{2,1,0:T(8,128)(2,1)S(1)} %collective-permute-done.3.above_ref, ...), custom_call_target="tpu_custom_call" | custom-call | tf_op jit(solution)/shard_map/pallas_call | solution.py:826
  53.3 6.1 %all-to-all-start.1 = ((bf16[16,27,128]{2,1,0:T(8,128)(2,1)}), bf16[16,27,128]{2,1,0:T(8,128)(2,1)S(1)}, u32[]{:S(2)}, u32[]{:S(2)}) async-start(bf16[16,27,128]{2,1,0:T(8,128)(2,1)} %get-tuple-element.58), calls=%async_computation.1 | async-start | bytes 262144 | tf_op jit(solution)/shard_map/all_to_all | solution.py:842
  59.4 1.0 %shard_map.125 = f32[4,2,3,3,1,4,512]{6,5,4,3,2,1,0:T(4,128)} custom-call(f32[4,2,3,3,1,4,512]{6,5,4,3,2,1,0:T(4,128)S(1)} %copy-done.1, f32[4,18,2,8,128]{4,3,2,1,0:T(8,128)S(1)} %get-tuple-element.43.w1_ref, f32[4,18,2,8,128]{4,3,2,1,0:T(8,128)S(1)} %get-tuple-element.44.w2_ref, f32[4,8,512]{2,1,0:T(8,128)S(1)} %get-tuple-element.57.coeff_ref), custom_call_target="tpu_custom_call" | custom-call | tf_op jit(solution)/shard_map/pallas_call | solution.py:843
  60.5 6.9 %all-to-all-done.1.parts_ref = bf16[16,27,128]{2,1,0:T(8,128)(2,1)S(1)} async-done(((bf16[16,27,128]{2,1,0:T(8,128)(2,1)}), bf16[16,27,128]{2,1,0:T(8,128)(2,1)S(1)}, u32[]{:S(2)}, u32[]{:S(2)}) %all-to-all-start.1) | async-done | bytes 110624 | tf_op jit(solution)/shard_map/all_to_all | solution.py:842
  67.4 0.8 %shard_map.126 = (f32[1,216]{1,0:T(1,128)}, f32[1,1296]{1,0:T(1,128)}, f32[1,1296]{1,0:T(1,128)}, f32[1,108]{1,0:T(1,128)}) custom-call(bf16[16,27,128]{2,1,0:T(8,128)(2,1)S(1)} %all-to-all-done.1.parts_ref), custom_call_target="tpu_custom_call" | custom-call | tf_op jit(solution)/shard_map/pallas_call | solution.py:846
  (21 shorter events, 0.1 us)
Async XLA Ops:
  0.6 1.1 %copy-start = (f32[4,2,3,3,1,4,512]{6,5,4,3,2,1,0:T(4,128)S(1)}, f32[4,2,3,3,1,4,512]{6,5,4,3,2,1,0:T(4,128)}, u32[]{:S(2)}) copy-start(f32[4,2,3,3,1,4,512]{6,5,4,3,2,1,0:T(4,128)} %links_ref.3) | copy-start | bytes 1769476
  4.1 7.6 %collective-permute-start = (bf16[66,512]{1,0:T(8,128)(2,1)S(1)}, bf16[66,512]{1,0:T(8,128)(2,1)S(1)}, u32[]{:S(2)}, u32[]{:S(2)}) collective-permute-start(bf16[66,512]{1,0:T(8,128)(2,1)S(1)} %get-tuple-element.37), channel_id=1, source_target_pairs={{0,1},{1,2},{2,3},{3,4},{4,5},{5,6},{6,7},{7,8},{8,9},{9,10},{10,1... | collective-permute-start | bytes 202760 | tf_op jit(solution)/shard_map/ppermute | solution.py:765
  4.6 7.1 %collective-permute-start.1 = (bf16[66,512]{1,0:T(8,128)(2,1)S(1)}, bf16[66,512]{1,0:T(8,128)(2,1)S(1)}, u32[]{:S(2)}, u32[]{:S(2)}) collective-permute-start(bf16[66,512]{1,0:T(8,128)(2,1)S(1)} %get-tuple-element.38), channel_id=1, source_target_pairs={{0,15},{1,0},{2,1},{3,2},{4,3},{5,4},{6,5},{7,6},{8,7},{9,8},{10,9... | collective-permute-start | bytes 202760 | tf_op jit(solution)/shard_map/ppermute | solution.py:765
  9.7 0.7 %copy-start.6 = (bf16[1296]{0:T(1024)(128)(2,1)S(1)}, bf16[1296]{0:T(1024)(128)(2,1)}, u32[]{:S(2)}) copy-start(bf16[1296]{0:T(1024)(128)(2,1)} %param.13) | copy-start | bytes 7780
  9.7 0.7 copy-start.8
  10.4 0.7 %copy-start.7 = (bf16[1296]{0:T(1024)(128)(2,1)S(1)}, bf16[1296]{0:T(1024)(128)(2,1)}, u32[]{:S(2)}) copy-start(bf16[1296]{0:T(1024)(128)(2,1)} %param.14) | copy-start | bytes 7780
  11.8 0.7 copy-start.2
  13.3 5.9 %copy-start.5 = (bf16[4,2,3,3,1,4,512]{6,5,4,3,2,1,0:T(4,128)(2,1)S(1)}, bf16[4,2,3,3,1,4,512]{6,5,4,3,2,1,0:T(4,128)(2,1)}, u32[]{:S(2)}) copy-start(bf16[4,2,3,3,1,4,512]{6,5,4,3,2,1,0:T(4,128)(2,1)} %cot_ref.1) | copy-start | bytes 884740
  13.3 24.2 %all-to-all-start = ((bf16[16,64,128]{2,1,0:T(8,128)(2,1)}), bf16[16,64,128]{2,1,0:T(8,128)(2,1)S(1)}, u32[]{:S(2)}, u32[]{:S(2)}) async-start(bf16[16,64,128]{2,1,0:T(8,128)(2,1)} %shard_map.122), calls=%async_computation | async-start | bytes 524288 | tf_op jit(solution)/shard_map/all_to_all | solution.py:791
  23.5 0.7 copy-start.3
  23.6 0.7 copy-start.4
  28.3 31.1 %copy-start.1 = (f32[4,2,3,3,1,4,512]{6,5,4,3,2,1,0:T(4,128)S(1)}, f32[4,2,3,3,1,4,512]{6,5,4,3,2,1,0:T(4,128)}, u32[]{:S(2)}) copy-start(f32[4,2,3,3,1,4,512]{6,5,4,3,2,1,0:T(4,128)} %links_ref.3) | copy-start | bytes 1769476
  28.3 11.0 %collective-permute-start.2 = (bf16[4,16,512]{2,1,0:T(8,128)(2,1)S(1)}, bf16[4,16,512]{2,1,0:T(8,128)(2,1)S(1)}, u32[]{:S(2)}, u32[]{:S(2)}) collective-permute-start(bf16[4,16,512]{2,1,0:T(8,128)(2,1)S(1)} %get-tuple-element.45.fm_ref), channel_id=1, source_target_pairs={{0,1},{1,2},{2,3},{3,4},{4,5},{5,6},{6,7},{7,8},{8,9},{9,10},{10,1... | collective-permute-start | bytes 196616 | tf_op jit(solution)/shard_map/ppermute | solution.py:765
  28.8 10.6 %collective-permute-start.3 = (bf16[4,16,512]{2,1,0:T(8,128)(2,1)S(1)}, bf16[4,16,512]{2,1,0:T(8,128)(2,1)S(1)}, u32[]{:S(2)}, u32[]{:S(2)}) collective-permute-start(bf16[4,16,512]{2,1,0:T(8,128)(2,1)S(1)} %get-tuple-element.45.fm_ref), channel_id=1, source_target_pairs={{0,15},{1,0},{2,1},{3,2},{4,3},{5,4},{6,5},{7,6},{8,7},{9,8},{10,9... | collective-permute-start | bytes 196616 | tf_op jit(solution)/shard_map/ppermute | solution.py:765
  32.8 6.5 %collective-permute-start.4 = (bf16[3,8,512]{2,1,0:T(8,128)(2,1)S(1)}, bf16[3,8,512]{2,1,0:T(8,128)(2,1)S(1)}, u32[]{:S(2)}, u32[]{:S(2)}) collective-permute-start(bf16[3,8,512]{2,1,0:T(8,128)(2,1)S(1)} %get-tuple-element.46), channel_id=1, source_target_pairs={{0,2},{1,3},{2,4},{3,5},{4,6},{5,7},{6,8},{7,9},{8,10},{9,11},{10,... | collective-permute-start | bytes 73736 | tf_op jit(solution)/shard_map/ppermute | solution.py:765
  32.8 6.5 %collective-permute-start.5 = (bf16[3,8,512]{2,1,0:T(8,128)(2,1)S(1)}, bf16[3,8,512]{2,1,0:T(8,128)(2,1)S(1)}, u32[]{:S(2)}, u32[]{:S(2)}) collective-permute-start(bf16[3,8,512]{2,1,0:T(8,128)(2,1)S(1)} %get-tuple-element.47), channel_id=1, source_target_pairs={{0,14},{1,15},{2,0},{3,1},{4,2},{5,3},{6,4},{7,5},{8,6},{9,7},{10,... | collective-permute-start | bytes 73736 | tf_op jit(solution)/shard_map/ppermute | solution.py:765
  53.3 14.0 %all-to-all-start.1 = ((bf16[16,27,128]{2,1,0:T(8,128)(2,1)}), bf16[16,27,128]{2,1,0:T(8,128)(2,1)S(1)}, u32[]{:S(2)}, u32[]{:S(2)}) async-start(bf16[16,27,128]{2,1,0:T(8,128)(2,1)} %get-tuple-element.58), calls=%async_computation.1 | async-start | bytes 262144 | tf_op jit(solution)/shard_map/all_to_all | solution.py:842

commit v5 on v4

--- a/solution.py
+++ b/solution.py
@@ -556,28 +556,29 @@
     return pl.ds(pl.multiple_of(slice_index * SITES, SITES), count * SITES)
 
 
-def stack_wide(source, target, first, count):
-    for s in range(count):
-        chunks = chunks_of(source[:, span(first + s)])
-        for position in range(7):
-            shifted = one_shift(chunks, position)
-            for q in range(4):
-                lanes = slice(s * SITES + q * 128, s * SITES + q * 128 + 128)
-                target[H * position:H * position + H, lanes] = shifted[q]
-    width = slice(0, count * SITES)
-    target[7 * H:8 * H, width] = source[:, span(first + 1, count)]
-    target[8 * H:9 * H, width] = source[:, span(first - 1, count)]
-
-
-def stack_thin(source, target, first, count):
-    for s in range(count):
-        chunks = chunks_of(source[:, span(first + s)])
-        ahead = chunks_of(source[:, span(first + s + 1)])
-        behind = chunks_of(source[:, span(first + s - 1)])
-        columns = [one_shift(chunks, position) for position in range(7)] + [ahead, behind]
+def slot_of(slot):
+    return slice(slot * SITES, (slot + 1) * SITES)
+
+
+def stack_wide(source, target, index, slot):
+    chunks = chunks_of(source[:, span(index)])
+    for position in range(7):
+        shifted = one_shift(chunks, position)
         for q in range(4):
-            lanes = slice(s * SITES + q * 128, s * SITES + q * 128 + 128)
-            target[0:72, lanes] = jnp.concatenate([column[q] for column in columns], axis=0).astype(BF16)
+            lanes = slice(slot * SITES + q * 128, slot * SITES + q * 128 + 128)
+            target[H * position:H * position + H, lanes] = shifted[q]
+    target[7 * H:8 * H, slot_of(slot)] = source[:, span(index + 1)]
+    target[8 * H:9 * H, slot_of(slot)] = source[:, span(index - 1)]
+
+
+def stack_thin(source, target, index, slot):
+    chunks = chunks_of(source[:, span(index)])
+    ahead = chunks_of(source[:, span(index + 1)])
+    behind = chunks_of(source[:, span(index - 1)])
+    columns = [one_shift(chunks, position) for position in range(7)] + [ahead, behind]
+    for q in range(4):
+        lanes = slice(slot * SITES + q * 128, slot * SITES + q * 128 + 128)
+        target[0:72, lanes] = jnp.concatenate([column[q] for column in columns], axis=0).astype(BF16)
 
 
 def one_minus_square(value):
@@ -589,7 +590,7 @@
     split, fm_ref, below_ref, above_ref, fbelow_ref, fabove_ref, loops_ref,
     p1_ref, p2_ref, p3_ref, p4_ref, b2_ref, b3_ref, b4_ref,
     coeff_ref, grads_ref,
-    feats, mixed, h1, h2, h3, parts, lasts, g3, g2, wide, thin, packed,
+    feats, mixed, h1, h2, h3, parts, lasts, g3, g2, g1, wide, thin, packed,
 ):
     row8 = lax.broadcasted_iota(jnp.int32, (8, SITES), 0)
     loop_re = jnp.concatenate([loops_ref[0, q:q + 1, :] for q in range(4)], axis=1)
@@ -605,89 +606,55 @@
             feats[:, span(base + j)] = value[0:8] + loops
             mixed[:, span(base + j)] = value[8:16]
 
-    def layer_one(step, carry):
-        first = 1 + 4 * step
-        stack_thin(feats, thin, first, 4)
-        out = jnp.dot(p1_ref[...], thin[...], preferred_element_type=F32)
-        h1[:, span(first, 4)] = jnp.tanh(out).astype(BF16)
-        return carry
-
-    lax.fori_loop(0, 4, layer_one, 0)
-
-    def layer_two(step, carry):
-        first = 2 + 2 * step
-        stack_wide(h1, wide, first, 2)
-        out = jnp.dot(p2_ref[...], wide[:, 0:1024], preferred_element_type=F32)
-        h2[:, span(first, 2)] = jnp.tanh(out).astype(BF16)
-        return carry
-
-    lax.fori_loop(0, 7, layer_two, 0)
-
-    def layer_three(step, carry):
-        first = 3 + 2 * step
-        stack_wide(h2, wide, first, 2)
-        out = jnp.dot(p3_ref[...], wide[:, 0:1024], preferred_element_type=F32)
-        out = jnp.tanh(out).astype(BF16)
-        h3[:, span(first, 2)] = out
+    def wide_dot(source, weights, index, slot):
+        stack_wide(source, wide, index, slot)
+        return jnp.dot(weights[...], wide[:, slot_of(slot)], preferred_element_type=F32)
+
+    def thin_dot(source, weights, index, slot):
+        stack_thin(source, thin, index, slot)
+        return jnp.dot(weights[...], thin[:, slot_of(slot)], preferred_element_type=F32)
+
+    for index in range(1, 17):
+        h1[:, span(index)] = jnp.tanh(thin_dot(feats, p1_ref, index, index % 4)).astype(BF16)
+    for index in range(2, 16):
+        h2[:, span(index)] = jnp.tanh(wide_dot(h1, p2_ref, index, index % 4)).astype(BF16)
+    for index in range(3, 15):
+        out = jnp.tanh(wide_dot(h2, p3_ref, index, index % 4)).astype(BF16)
+        h3[:, span(index)] = out
         taps = jnp.dot(p4_ref[...], out, preferred_element_type=F32)
-        for s in range(2):
-            acc = None
-            for position in range(7):
-                shifted = one_shift(
-                    chunks_of(taps[8 * position:8 * position + 8, s * SITES:(s + 1) * SITES]), position
-                )
-                acc = shifted if acc is None else [a + b for a, b in zip(acc, shifted)]
-            parts[0, :, span(first + s)] = jnp.concatenate(acc, axis=1)
-            parts[1, :, span(first + s)] = taps[56:64, s * SITES:(s + 1) * SITES]
-            parts[2, :, span(first + s)] = taps[64:72, s * SITES:(s + 1) * SITES]
-        return carry
-
-    lax.fori_loop(0, 6, layer_three, 0)
-
-    def last_layer(step, carry):
-        for s in range(2):
-            index = 4 + 2 * step + s
-            coeff = jnp.tanh(parts[0, :, span(index)] + parts[1, :, span(index + 1)] + parts[2, :, span(index - 1)])
-            blend = mixed[:, span(index)]
-            value = (blend + coeff * pltpu.roll(blend, 4, 0)) * (1.0 - coeff * coeff)
-            lasts[:, span(index)] = jnp.where(row8 < 4, value, 0.0).astype(BF16).astype(F32)
-            parts[0, :, span(index)] = coeff
-        return carry
-
-    lax.fori_loop(0, 5, last_layer, 0)
-    for t in range(4):
-        coeff_ref[t] = parts[0, :, span(7 + t)]
-
-    def back_three(first, count):
-        stack_thin(lasts, thin, first, count)
-        out = jnp.dot(b4_ref[...], thin[:, 0:count * SITES], preferred_element_type=F32)
-        g3[:, span(first, count)] = (out * one_minus_square(h3[:, span(first, count)])).astype(BF16)
-
-    back_three(5, 2)
-    back_three(11, 2)
-    back_three(7, 4)
+        acc = None
+        for position in range(7):
+            shifted = one_shift(chunks_of(taps[8 * position:8 * position + 8]), position)
+            acc = shifted if acc is None else [a + b for a, b in zip(acc, shifted)]
+        parts[0, :, span(index)] = jnp.concatenate(acc, axis=1)
+        parts[1, :, span(index)] = taps[56:64]
+        parts[2, :, span(index)] = taps[64:72]
+
+    for index in range(4, 14):
+        coeff = jnp.tanh(parts[0, :, span(index)] + parts[1, :, span(index + 1)] + parts[2, :, span(index - 1)])
+        blend = mixed[:, span(index)]
+        value = (blend + coeff * pltpu.roll(blend, 4, 0)) * (1.0 - coeff * coeff)
+        lasts[:, span(index)] = jnp.where(row8 < 4, value, 0.0).astype(BF16).astype(F32)
+        if 7 <= index < 11:
+            coeff_ref[index - 7] = coeff
+
     own = span(7, 4)
     contract = (((1,), (1,)), ((), ()))
+    for index in (5, 6, 11, 12, 7, 8, 9, 10):
+        out = thin_dot(lasts, b4_ref, index, (index + 1) % 4)
+        g3[:, span(index)] = (out * one_minus_square(h3[:, span(index)])).astype(BF16)
     grad_last = lax.dot_general(thin[...], h3[:, own], contract, preferred_element_type=F32)
-
-    stack_wide(g3, wide, 6, 1)
-    out = jnp.dot(b3_ref[...], wide[:, 0:SITES], preferred_element_type=F32)
-    g2[:, span(6)] = (out * one_minus_square(h2[:, span(6)])).astype(BF16)
-    stack_wide(g3, wide, 11, 1)
-    out = jnp.dot(b3_ref[...], wide[:, 0:SITES], preferred_element_type=F32)
-    g2[:, span(11)] = (out * one_minus_square(h2[:, span(11)])).astype(BF16)
-    stack_wide(g3, wide, 7, 4)
-    out = jnp.dot(b3_ref[...], wide[...], preferred_element_type=F32)
-    g2[:, own] = (out * one_minus_square(h2[:, own])).astype(BF16)
+    for index in (6, 11, 7, 8, 9, 10):
+        out = wide_dot(g3, b3_ref, index, (index + 1) % 4)
+        g2[:, span(index)] = (out * one_minus_square(h2[:, span(index)])).astype(BF16)
     grad_third = lax.dot_general(wide[...], h2[:, own], contract, preferred_element_type=F32)
-
-    stack_wide(g2, wide, 7, 4)
-    out = jnp.dot(b2_ref[...], wide[...], preferred_element_type=F32)
-    g1 = (out * one_minus_square(h1[:, own])).astype(BF16)
+    for index in (7, 8, 9, 10):
+        out = wide_dot(g2, b2_ref, index, (index + 1) % 4)
+        g1[:, slot_of(index - 7)] = (out * one_minus_square(h1[:, span(index)])).astype(BF16)
     grad_second = lax.dot_general(wide[...], h1[:, own], contract, preferred_element_type=F32)
-
-    stack_thin(feats, thin, 7, 4)
-    grad_first = lax.dot_general(g1, thin[...], contract, preferred_element_type=F32)
+    for index in (7, 8, 9, 10):
+        stack_thin(feats, thin, index, index - 7)
+    grad_first = lax.dot_general(g1[...], thin[...], contract, preferred_element_type=F32)
 
     spread, keep = selectors()
     ordered = jnp.concatenate([grad_last[8 * SWAP[k]:8 * SWAP[k] + 8] for k in range(TAPS)], axis=0)
@@ -828,7 +795,7 @@
         [((4, 8, SITES), F32), ((16, 27, LANES) if count == 16 else (432, LANES), BF16)],
         [
             ((8, window), F32), ((8, window), F32), ((H, window), BF16), ((H, window), BF16), ((H, window), BF16),
-            ((3, 8, window), F32), ((8, window), F32), ((H, window), BF16), ((H, window), BF16),
+            ((3, 8, window), F32), ((8, window), F32), ((H, window), BF16), ((H, window), BF16), ((H, 4 * SITES), BF16),
             ((432, 4 * SITES), BF16), ((72, 4 * SITES), BF16), ((432, LANES), F32),
         ],
     )(fm, below, above, fbelow, fabove, loops, p1, p2, p3, p4, b2, b3, b4)

time: 68.6 us -> 63.6 us (0.927)
  Pallas kernels: 28.7 us -> 23.8 us
    pallas_call x1, Pallas kernels: 14 us -> 9.04 us  [on_device(): call(functools.partial(conv_kernel, count == 16), [((4, 8, SITES), F32),...]
  transfers between devices with their start and end apart: 8 -> 8, of which waited for: 3 -> 3; matrix products, arithmetic and copies ran while one was open for 0% -> 0% of each run, Pallas kernels for 16% -> 17%
where the time goes in v5:
time: 63.6 us; the launch traced here: 63.2 us
  starting transfers between devices  26.8 us (42%)
  Pallas kernels  23.8 us (37%)
  waiting for transfers between devices  8.13 us (13%)
  local copies, waits for them, and re-layouts  3.76 us (6%)
  between operations  0.74 us (1%)
    ppermute x6, starting transfers between devices, send(): lax.ppermute(value, 'tm', [(i, (i + distance) % count) for i in range(cou...  14.8 us
    pallas_call x1, Pallas kernels, on_device(): call(functools.partial(conv_kernel, count == 16), [((4, 8, SITES), F32),...  9.04 us
    all_to_all x1, waiting for transfers between devices, on_device(): grads = lax.all_to_all(grads, 'tm', split_axis=0, concat_axis=0, tiled=True)  6.9 us
    all_to_all x1, starting transfers between devices, on_device(): grads = lax.all_to_all(grads, 'tm', split_axis=0, concat_axis=0, tiled=True)  6.09 us
    all_to_all x1, starting transfers between devices, on_device(): lax.all_to_all(block, 'tm', split_axis=0, concat_axis=0, tiled=True)  5.9 us
    pallas_call x1, Pallas kernels, on_device(): call(space_kernel, [field, ((4, 4, 16, LANES), F32), ((4, 9, 2, 8, LANES)...  4.28 us
    pallas_call x1, Pallas kernels, on_device(): call(time_kernel, [((4, 16, SITES), BF16), ((3, 8, SITES), BF16), ((3, 8,...  4.07 us
    unnamed x18, local copies, waits for them, and re-layouts  3.74 us
  transfers between devices with their start and end apart: 8, of which 3 were waited for; matrix products, arithmetic and copies ran while one was open for 0% of the time, Pallas kernels for 17%

profile of v5, /device:TPU:0, one launch (start us, length us, event | category | flops | bytes accessed | tf_op | source)
XLA Modules:
  0.0 63.2 jit_solution(7440957066051740724)
XLA Ops:
  0.6 1.1 %copy-done = f32[4,2,3,3,1,4,512]{6,5,4,3,2,1,0:T(4,128)S(1)} copy-done((f32[4,2,3,3,1,4,512]{6,5,4,3,2,1,0:T(4,128)S(1)}, f32[4,2,3,3,1,4,512]{6,5,4,3,2,1,0:T(4,128)}, u32[]{:S(2)}) %copy-start) | copy-done | bytes 589848
  1.7 2.4 %shard_map.119 = (bf16[66,512]{1,0:T(8,128)(2,1)S(1)}, bf16[66,512]{1,0:T(8,128)(2,1)S(1)}, f32[4,18,2,8,128]{4,3,2,1,0:T(8,128)S(1)}, f32[3,18,2,8,128]{4,3,2,1...) custom-call(f32[4,2,3,3,1,4,512]{6,5,4,3,2,1,0:T(4,128)S(1)} %copy-done), custom_call_target="tpu_custom_call" | custom-call | tf_op jit(solution)/shard_map/pallas_call | solution.py:738
  4.1 0.5 collective-permute-start
  4.6 5.1 %collective-permute-start.1 = (bf16[66,512]{1,0:T(8,128)(2,1)S(1)}, bf16[66,512]{1,0:T(8,128)(2,1)S(1)}, u32[]{:S(2)}, u32[]{:S(2)}) collective-permute-start(bf16[66,512]{1,0:T(8,128)(2,1)S(1)} %get-tuple-element.38), channel_id=1, source_target_pairs={{0,15},{1,0},{2,1},{3,2},{4,3},{5,4},{6,5},{7,6},{8,7},{9,8},{10,9... | collective-permute-start | bytes 202760 | tf_op jit(solution)/shard_map/ppermute | solution.py:732
  9.7 0.7 %copy-done.8 = bf16[216]{0:T(256)(128)(2,1)S(1)} copy-done((bf16[216]{0:T(256)(128)(2,1)S(1)}, bf16[216]{0:T(256)(128)(2,1)}, u32[]{:S(2)}) %copy-start.8) | copy-done | bytes 456
  10.4 0.7 %copy-done.7 = bf16[1296]{0:T(1024)(128)(2,1)S(1)} copy-done((bf16[1296]{0:T(1024)(128)(2,1)S(1)}, bf16[1296]{0:T(1024)(128)(2,1)}, u32[]{:S(2)}) %copy-start.7) | copy-done | bytes 2616
  11.1 0.7 %collective-permute-done.up_ref = bf16[66,512]{1,0:T(8,128)(2,1)S(1)} collective-permute-done((bf16[66,512]{1,0:T(8,128)(2,1)S(1)}, bf16[66,512]{1,0:T(8,128)(2,1)S(1)}, u32[]{:S(2)}, u32[]{:S(2)}) %collective-permute-start) | collective-permute-done | bytes 67616 | tf_op jit(solution)/shard_map/ppermute | solution.py:732
  11.8 0.7 %copy-done.2 = bf16[108]{0:T(256)(128)(2,1)S(1)} copy-done((bf16[108]{0:T(256)(128)(2,1)S(1)}, bf16[108]{0:T(256)(128)(2,1)}, u32[]{:S(2)}) %copy-start.2) | copy-done | bytes 240
  12.4 0.9 %shard_map.122 = bf16[16,64,128]{2,1,0:T(8,128)(2,1)} custom-call(s32[1]{0:T(128)} %bitcast.core_ref, bf16[66,512]{1,0:T(8,128)(2,1)S(1)} %collective-permute-done.up_ref, bf16[66,512]{1,0:T(8,128)(2,1)S(1)} %collective-permute-done.1.down_ref, f32[12,4,128]{2,1,0:T(4,128)S(1)} %get-tuple-element.48.slab, bf16[1,216]{1,0:T(2,128)(2,1)S(1)} %broadcast_in_dim.16.w1_ref, ...), custom_call_target="tpu_custom_call" | custom-call | tf_op jit(solution)/shard_map/pallas_call | solution.py:752
  13.3 5.9 %all-to-all-start = ((bf16[16,64,128]{2,1,0:T(8,128)(2,1)}), bf16[16,64,128]{2,1,0:T(8,128)(2,1)S(1)}, u32[]{:S(2)}, u32[]{:S(2)}) async-start(bf16[16,64,128]{2,1,0:T(8,128)(2,1)} %shard_map.122), calls=%async_computation | async-start | bytes 524288 | tf_op jit(solution)/shard_map/all_to_all | solution.py:758
  19.3 4.3 %shard_map.120 = (f32[4,18,2,8,128]{4,3,2,1,0:T(8,128)S(1)}, f32[4,4,16,128]{3,2,1,0:T(8,128)S(1)}, f32[4,9,2,8,128]{4,3,2,1,0:T(8,128)S(1)}, f32[3,18,2,8,128]{4,3,2,1,0:T(8,128)S(1)}) custom-call(f32[4,18,2,8,128]{4,3,2,1,0:T(8,128)S(1)} %get-tuple-element.34.dense, bf16[4,2,3,3,1,4,512]{6,5,4,3,2,1,0:T(4,128)(2,1)S(1)} %copy-done.5, ...), custom_call_target="tpu_custom_call" | custom-call | flops 4000000000 | bytes 16000000 | tf_op jit(solution)/shard_map/pallas_call | solution.py:745
  23.6 0.6 %copy-done.3 = s32[1,4]{1,0:T(1,128)S(1)} copy-done((s32[1,4]{1,0:T(1,128)S(1)}, s32[1,4]{1,0:T(1,128)}, u32[]{:S(2)}) %copy-start.3) | copy-done | bytes 40
  24.2 0.0 copy-done.4
  24.2 4.1 %shard_map.121 = (bf16[4,16,512]{2,1,0:T(8,128)(2,1)S(1)}, bf16[3,8,512]{2,1,0:T(8,128)(2,1)S(1)}, bf16[3,8,512]{2,1,0:T(8,128)(2,1)S(1)}, f32[4,18,2,8,128]{4,3,2,1,0:T(8,128)S(1)}, f32[4,18,2,8,128]{4,3,2,1,0:T(8,128)S(1)}) custom-call(f32[4,18,2,8,128]{4,3,2,1,0:T(8,128)S(1)} %get-tuple-element.34.dense, ...), custom_call_target="tpu_custom_call" | custom-call | tf_op jit(solution)/shard_map/pallas_call | solution.py:759
  28.3 0.5 collective-permute-start.2
  28.8 4.0 %collective-permute-start.3 = (bf16[4,16,512]{2,1,0:T(8,128)(2,1)S(1)}, bf16[4,16,512]{2,1,0:T(8,128)(2,1)S(1)}, u32[]{:S(2)}, u32[]{:S(2)}) collective-permute-start(bf16[4,16,512]{2,1,0:T(8,128)(2,1)S(1)} %get-tuple-element.45.fm_ref), channel_id=1, source_target_pairs={{0,15},{1,0},{2,1},{3,2},{4,3},{5,4},{6,5},{7,6},{8,7},{9,8},{10,9... | collective-permute-start | bytes 196616 | tf_op jit(solution)/shard_map/ppermute | solution.py:732
  32.8 4.7 %collective-permute-start.5 = (bf16[3,8,512]{2,1,0:T(8,128)(2,1)S(1)}, bf16[3,8,512]{2,1,0:T(8,128)(2,1)S(1)}, u32[]{:S(2)}, u32[]{:S(2)}) collective-permute-start(bf16[3,8,512]{2,1,0:T(8,128)(2,1)S(1)} %get-tuple-element.47), channel_id=1, source_target_pairs={{0,14},{1,15},{2,0},{3,1},{4,2},{5,3},{6,4},{7,5},{8,6},{9,7},{10,... | collective-permute-start | bytes 73736 | tf_op jit(solution)/shard_map/ppermute | solution.py:732
  37.5 1.3 %shard_map.123 = (f32[2,4,128]{2,1,0:T(4,128)S(1)}, bf16[48,72]{1,0:T(8,128)(2,1)S(1)}, bf16[48,432]{1,0:T(8,128)(2,1)S(1)}, bf16[48,432]{1,0:T(8,128)(2,1)S(1)}...) custom-call(bf16[16,64,128]{2,1,0:T(8,128)(2,1)S(1)} %all-to-all-don, ...), custom_call_target="tpu_custom_call" | custom-call | tf_op jit(solution)/shard_map/pallas_call | solution.py:779
  38.8 0.5 collective-permute-done.4.fbelow_ref
  39.3 9.0 %shard_map.124 = (f32[4,8,512]{2,1,0:T(8,128)S(1)}, bf16[16,27,128]{2,1,0:T(8,128)(2,1)}) custom-call(bf16[4,16,512]{2,1,0:T(8,128)(2,1)S(1)} %get-tuple-element.45.fm_ref, bf16[4,16,512]{2,1,0:T(8,128)(2,1)S(1)} %collective-permute-done.2.below_ref, bf16[4,16,512]{2,1,0:T(8,128)(2,1)S(1)} %collective-permute-done.3.above_ref, ...), custom_call_target="tpu_custom_call" | custom-call | tf_op jit(solution)/shard_map/pallas_call | solution.py:793
  48.4 6.1 %all-to-all-start.1 = ((bf16[16,27,128]{2,1,0:T(8,128)(2,1)}), bf16[16,27,128]{2,1,0:T(8,128)(2,1)S(1)}, u32[]{:S(2)}, u32[]{:S(2)}) async-start(bf16[16,27,128]{2,1,0:T(8,128)(2,1)} %get-tuple-element.58), calls=%async_computation.1 | async-start | bytes 262144 | tf_op jit(solution)/shard_map/all_to_all | solution.py:809
  54.5 1.0 %shard_map.125 = f32[4,2,3,3,1,4,512]{6,5,4,3,2,1,0:T(4,128)} custom-call(f32[4,2,3,3,1,4,512]{6,5,4,3,2,1,0:T(4,128)S(1)} %copy-done.1, f32[4,18,2,8,128]{4,3,2,1,0:T(8,128)S(1)} %get-tuple-element.43.w1_ref, f32[4,18,2,8,128]{4,3,2,1,0:T(8,128)S(1)} %get-tuple-element.44.w2_ref, f32[4,8,512]{2,1,0:T(8,128)S(1)} %get-tuple-element.57.coeff_ref), custom_call_target="tpu_custom_call" | custom-call | tf_op jit(solution)/shard_map/pallas_call | solution.py:810
  55.5 6.9 %all-to-all-done.1.parts_ref = bf16[16,27,128]{2,1,0:T(8,128)(2,1)S(1)} async-done(((bf16[16,27,128]{2,1,0:T(8,128)(2,1)}), bf16[16,27,128]{2,1,0:T(8,128)(2,1)S(1)}, u32[]{:S(2)}, u32[]{:S(2)}) %all-to-all-start.1) | async-done | bytes 110624 | tf_op jit(solution)/shard_map/all_to_all | solution.py:809
  62.4 0.8 %shard_map.126 = (f32[1,216]{1,0:T(1,128)}, f32[1,1296]{1,0:T(1,128)}, f32[1,1296]{1,0:T(1,128)}, f32[1,108]{1,0:T(1,128)}) custom-call(bf16[16,27,128]{2,1,0:T(8,128)(2,1)S(1)} %all-to-all-done.1.parts_ref), custom_call_target="tpu_custom_call" | custom-call | tf_op jit(solution)/shard_map/pallas_call | solution.py:813
  (21 shorter events, 0.1 us)
Async XLA Ops:
  0.6 1.1 %copy-start = (f32[4,2,3,3,1,4,512]{6,5,4,3,2,1,0:T(4,128)S(1)}, f32[4,2,3,3,1,4,512]{6,5,4,3,2,1,0:T(4,128)}, u32[]{:S(2)}) copy-start(f32[4,2,3,3,1,4,512]{6,5,4,3,2,1,0:T(4,128)} %links_ref.3) | copy-start | bytes 1769476
  4.1 7.6 %collective-permute-start = (bf16[66,512]{1,0:T(8,128)(2,1)S(1)}, bf16[66,512]{1,0:T(8,128)(2,1)S(1)}, u32[]{:S(2)}, u32[]{:S(2)}) collective-permute-start(bf16[66,512]{1,0:T(8,128)(2,1)S(1)} %get-tuple-element.37), channel_id=1, source_target_pairs={{0,1},{1,2},{2,3},{3,4},{4,5},{5,6},{6,7},{7,8},{8,9},{9,10},{10,1... | collective-permute-start | bytes 202760 | tf_op jit(solution)/shard_map/ppermute | solution.py:732
  4.6 7.1 %collective-permute-start.1 = (bf16[66,512]{1,0:T(8,128)(2,1)S(1)}, bf16[66,512]{1,0:T(8,128)(2,1)S(1)}, u32[]{:S(2)}, u32[]{:S(2)}) collective-permute-start(bf16[66,512]{1,0:T(8,128)(2,1)S(1)} %get-tuple-element.38), channel_id=1, source_target_pairs={{0,15},{1,0},{2,1},{3,2},{4,3},{5,4},{6,5},{7,6},{8,7},{9,8},{10,9... | collective-permute-start | bytes 202760 | tf_op jit(solution)/shard_map/ppermute | solution.py:732
  9.7 0.7 %copy-start.6 = (bf16[1296]{0:T(1024)(128)(2,1)S(1)}, bf16[1296]{0:T(1024)(128)(2,1)}, u32[]{:S(2)}) copy-start(bf16[1296]{0:T(1024)(128)(2,1)} %param.13) | copy-start | bytes 7780
  9.7 0.7 %copy-start.8 = (bf16[216]{0:T(256)(128)(2,1)S(1)}, bf16[216]{0:T(256)(128)(2,1)}, u32[]{:S(2)}) copy-start(bf16[216]{0:T(256)(128)(2,1)} %param.12) | copy-start | bytes 1300
  10.4 0.7 %copy-start.7 = (bf16[1296]{0:T(1024)(128)(2,1)S(1)}, bf16[1296]{0:T(1024)(128)(2,1)}, u32[]{:S(2)}) copy-start(bf16[1296]{0:T(1024)(128)(2,1)} %param.14) | copy-start | bytes 7780
  11.8 0.7 %copy-start.2 = (bf16[108]{0:T(256)(128)(2,1)S(1)}, bf16[108]{0:T(256)(128)(2,1)}, u32[]{:S(2)}) copy-start(bf16[108]{0:T(256)(128)(2,1)} %param.15) | copy-start | bytes 652
  13.3 5.9 %copy-start.5 = (bf16[4,2,3,3,1,4,512]{6,5,4,3,2,1,0:T(4,128)(2,1)S(1)}, bf16[4,2,3,3,1,4,512]{6,5,4,3,2,1,0:T(4,128)(2,1)}, u32[]{:S(2)}) copy-start(bf16[4,2,3,3,1,4,512]{6,5,4,3,2,1,0:T(4,128)(2,1)} %cot_ref.1) | copy-start | bytes 884740
  13.3 24.2 %all-to-all-start = ((bf16[16,64,128]{2,1,0:T(8,128)(2,1)}), bf16[16,64,128]{2,1,0:T(8,128)(2,1)S(1)}, u32[]{:S(2)}, u32[]{:S(2)}) async-start(bf16[16,64,128]{2,1,0:T(8,128)(2,1)} %shard_map.122), calls=%async_computation | async-start | bytes 524288 | tf_op jit(solution)/shard_map/all_to_all | solution.py:758
  23.5 0.7 %copy-start.3 = (s32[1,4]{1,0:T(1,128)S(1)}, s32[1,4]{1,0:T(1,128)}, u32[]{:S(2)}) copy-start(s32[1,4]{1,0:T(1,128)} %parity_ref.1) | copy-start | bytes 52
  23.6 0.7 %copy-start.4 = (s32[1,4]{1,0:T(1,128)S(1)}, s32[1,4]{1,0:T(1,128)}, u32[]{:S(2)}) copy-start(s32[1,4]{1,0:T(1,128)} %subset_ref.1) | copy-start | bytes 52
  28.3 26.2 %copy-start.1 = (f32[4,2,3,3,1,4,512]{6,5,4,3,2,1,0:T(4,128)S(1)}, f32[4,2,3,3,1,4,512]{6,5,4,3,2,1,0:T(4,128)}, u32[]{:S(2)}) copy-start(f32[4,2,3,3,1,4,512]{6,5,4,3,2,1,0:T(4,128)} %links_ref.3) | copy-start | bytes 1769476
  28.3 11.0 %collective-permute-start.2 = (bf16[4,16,512]{2,1,0:T(8,128)(2,1)S(1)}, bf16[4,16,512]{2,1,0:T(8,128)(2,1)S(1)}, u32[]{:S(2)}, u32[]{:S(2)}) collective-permute-start(bf16[4,16,512]{2,1,0:T(8,128)(2,1)S(1)} %get-tuple-element.45.fm_ref), channel_id=1, source_target_pairs={{0,1},{1,2},{2,3},{3,4},{4,5},{5,6},{6,7},{7,8},{8,9},{9,10},{10,1... | collective-permute-start | bytes 196616 | tf_op jit(solution)/shard_map/ppermute | solution.py:732
  28.8 10.6 %collective-permute-start.3 = (bf16[4,16,512]{2,1,0:T(8,128)(2,1)S(1)}, bf16[4,16,512]{2,1,0:T(8,128)(2,1)S(1)}, u32[]{:S(2)}, u32[]{:S(2)}) collective-permute-start(bf16[4,16,512]{2,1,0:T(8,128)(2,1)S(1)} %get-tuple-element.45.fm_ref), channel_id=1, source_target_pairs={{0,15},{1,0},{2,1},{3,2},{4,3},{5,4},{6,5},{7,6},{8,7},{9,8},{10,9... | collective-permute-start | bytes 196616 | tf_op jit(solution)/shard_map/ppermute | solution.py:732
  32.8 6.5 %collective-permute-start.4 = (bf16[3,8,512]{2,1,0:T(8,128)(2,1)S(1)}, bf16[3,8,512]{2,1,0:T(8,128)(2,1)S(1)}, u32[]{:S(2)}, u32[]{:S(2)}) collective-permute-start(bf16[3,8,512]{2,1,0:T(8,128)(2,1)S(1)} %get-tuple-element.46), channel_id=1, source_target_pairs={{0,2},{1,3},{2,4},{3,5},{4,6},{5,7},{6,8},{7,9},{8,10},{9,11},{10,... | collective-permute-start | bytes 73736 | tf_op jit(solution)/shard_map/ppermute | solution.py:732
  32.8 6.5 %collective-permute-start.5 = (bf16[3,8,512]{2,1,0:T(8,128)(2,1)S(1)}, bf16[3,8,512]{2,1,0:T(8,128)(2,1)S(1)}, u32[]{:S(2)}, u32[]{:S(2)}) collective-permute-start(bf16[3,8,512]{2,1,0:T(8,128)(2,1)S(1)} %get-tuple-element.47), channel_id=1, source_target_pairs={{0,14},{1,15},{2,0},{3,1},{4,2},{5,3},{6,4},{7,5},{8,6},{9,7},{10,... | collective-permute-start | bytes 73736 | tf_op jit(solution)/shard_map/ppermute | solution.py:732
  48.4 14.0 %all-to-all-start.1 = ((bf16[16,27,128]{2,1,0:T(8,128)(2,1)}), bf16[16,27,128]{2,1,0:T(8,128)(2,1)S(1)}, u32[]{:S(2)}, u32[]{:S(2)}) async-start(bf16[16,27,128]{2,1,0:T(8,128)(2,1)} %get-tuple-element.58), calls=%async_computation.1 | async-start | bytes 262144 | tf_op jit(solution)/shard_map/all_to_all | solution.py:809

commit v6 on v5

--- a/solution.py
+++ b/solution.py
@@ -233,8 +233,8 @@
 
         def write(e, value):
             staples[mu, e, c] = value
-            rows[mu * 18 + e, pl.ds(c, 1)] = value[3:4]
-            rows[mu * 18 + e, pl.ds(2 + c, 1)] = value[7:8]
+            rows[16 + mu * 18 + e, pl.ds(c, 1)] = value[3:4]
+            rows[16 + mu * 18 + e, pl.ds(2 + c, 1)] = value[7:8]
 
         store_matrix(mat_mul(dagger(edge), u_t), write)
         return carry
@@ -253,8 +253,8 @@
         def write(e, value):
             slab[e, pl.ds(c, 1)] = value[0:1]
             slab[e, pl.ds(2 + c, 1)] = value[4:5]
-            rows[54 + e, pl.ds(c, 1)] = value[0:1]
-            rows[54 + e, pl.ds(2 + c, 1)] = value[4:5]
+            rows[e, pl.ds(c, 1)] = value[0:1]
+            rows[e, pl.ds(2 + c, 1)] = value[4:5]
 
         store_rows(four, write)
         return carry
@@ -267,8 +267,8 @@
         for mu in range(3):
             for c in range(2):
                 value = dense[mu, e, c]
-                rows[mu * 18 + e, c:c + 1] = value[0:1]
-                rows[mu * 18 + e, 2 + c:3 + c] = value[4:5]
+                rows[16 + mu * 18 + e, c:c + 1] = value[0:1]
+                rows[16 + mu * 18 + e, 2 + c:3 + c] = value[4:5]
         return carry
 
     lax.fori_loop(0, 18, down_body, 0)
@@ -277,27 +277,29 @@
 
 
 def block_kernel(
-    widths, core_ref, up_ref, down_ref, slab, w1_ref, w2_ref, w3_ref, w4_ref, block_ref, other, block
+    widths, core_ref, up_ref, down_ref, slab, w1_ref, w2_ref, w3_ref, w4_ref, rows_ref, block_ref, other, block
 ):
     even = core_ref[0] == 0
-    up = up_ref[...].astype(F32)
-    down = down_ref[...].astype(F32)
+    up = up_ref[0:16].astype(F32)
+    down = down_ref[0:16].astype(F32)
     for q in range(4):
         lanes = slice(q * 128, q * 128 + 128)
-        other[:, q, :] = jnp.where(even, down[54:66, lanes], up[54:66, lanes])
+        other[:, q, :] = jnp.where(even, down[0:12, lanes], up[0:12, lanes])
     first = two_rows(lambda e: jnp.where(even, slab[e], other[e]))
     second = special(two_rows(lambda e: jnp.where(even, other[e], slab[e])))
-    block[...] = jnp.zeros_like(block)
 
     def write(e, value):
         block[2 * e:2 * e + 2, :] = jnp.where(even, value[0:2], value[2:4])
 
     store_rows(mat_mul(first, second), write)
+    block[SLABROWS:BLOCKROWS] = jnp.zeros((BLOCKROWS - SLABROWS, LANES), F32)
     offset = 0
     for ref, width in zip((w2_ref, w3_ref, w1_ref, w4_ref), widths):
         flat = ref[...].astype(F32)
         for r in range(27):
-            block[SLABROWS + r:SLABROWS + r + 1, offset:offset + width] = flat[:, width * r:width * r + width]
+            block[SLABROWS + r:SLABROWS + r + 1, offset:offset + width] = (
+                flat[width * r:width * r + width].reshape(1, width)
+            )
         offset += width
     value = block[...].astype(BF16)
     for d in range(block_ref.shape[0]):
@@ -310,11 +312,23 @@
         rows[t, 2 + c, pl.ds(channel, 1), :] = value[4 + t:5 + t]
 
 
-def space_kernel(dense, cot_ref, time_staples, cots, rows, forces, sums, moved, staples):
+def space_kernel(
+    parity_ref, subset_ref, dense, cot_ref, time_staples, cots, rows, forces, sums, gates, moved, staples
+):
     pack_links(cot_ref, cots)
     rows[...] = jnp.zeros_like(rows)
     forces[...] = jnp.zeros_like(forces)
     steps = row_iota() % 4
+    lanes = lane_iota(8)
+    colour = (lanes // 64 + lanes // 8 % 8 + lanes % 8 + steps) % 2
+    parity = jnp.zeros_like(steps)
+    subset = jnp.zeros_like(steps)
+    for t in range(4):
+        parity = jnp.where(steps == t, parity_ref[0, t], parity)
+        subset = jnp.where(steps == t, subset_ref[0, t], subset)
+    for mu in range(4):
+        active = jnp.logical_and(colour == parity, jnp.right_shift(subset, mu) % 2 == 1)
+        gates[mu] = jnp.where(active, 1.0, 0.0)
 
     def shift_body(e, carry):
         for nu in range(3):
@@ -370,7 +384,7 @@
 
 
 def time_kernel(
-    dense, cots, up_ref, down_ref, parity_ref, subset_ref, edges, rows_ref, forces_ref, sums_ref,
+    dense, cots, up_ref, down_ref, gates, edges, rows_ref, forces_ref, sums_ref,
     fm_ref, fup_ref, fdown_ref, w1_ref, w2_ref,
     moved, staples, sums, halo_up, halo_down, forces, rows,
 ):
@@ -380,12 +394,11 @@
     rows[...] = rows_ref[...]
     forces[...] = forces_ref[...]
     steps = row_iota() % 4
-    lanes = lane_iota(8)
 
     def shift_body(e, carry):
         for nu in range(3):
-            halo = halo_pair(halo_down, nu * 18 + e)
-            below = halo_pair(halo_up, nu * 18 + e)
+            halo = halo_pair(halo_down, 16 + nu * 18 + e)
+            below = halo_pair(halo_up, 16 + nu * 18 + e)
             for c in range(2):
                 moved[nu, e, c] = jnp.where(steps == 3, halo[c], pltpu.roll(dense[nu, e, c], 7, 0))
                 sums[nu, e, c] = sums_ref[nu, e, c] + jnp.where(steps == 0, below[c], 0.0)
@@ -422,14 +435,6 @@
         return carry
 
     lax.fori_loop(0, 18, lower_body, 0)
-
-    colour = (lanes // 64 + lanes // 8 % 8 + lanes % 8 + steps) % 2
-    parity = jnp.zeros_like(steps)
-    subset = jnp.zeros_like(steps)
-    for t in range(4):
-        parity = jnp.where(steps == t, parity_ref[0, t], parity)
-        subset = jnp.where(steps == t, subset_ref[0, t], subset)
-    on_site = colour == parity
 
     def force_body(step, carry):
         mu = step // 2
@@ -442,7 +447,7 @@
         parts = [part * (1.0 / 12.0) for part in parts]
         applied = anti_mul(parts, current)
         twice = anti_mul(parts, applied)
-        gate = jnp.where(jnp.logical_and(on_site, jnp.right_shift(subset, mu) % 2 == 1), 1.0, 0.0)
+        gate = gates[mu]
         slope = jnp.zeros_like(gate)
         curve = jnp.zeros_like(gate)
         for e, (part, i, j) in enumerate(ENTRIES):
@@ -677,7 +682,7 @@
         grads_ref[...] = packed[...].astype(BF16)
 
 
-def update_kernel(links_ref, w1_ref, w2_ref, coeff_ref, out_ref, factors):
+def update_kernel(dense, w1_ref, w2_ref, coeff_ref, out_ref, factors):
     for mu in range(4):
         for t in range(4):
             for c in range(2):
@@ -688,8 +693,7 @@
         factor = [factors[mu, c] for c in range(2)]
         half = [0.5 * value * value for value in factor]
         for e, (part, i, j) in enumerate(ENTRIES):
-            pair = pack_pair(links_ref[mu, part, i, j, 0])
-            new = [pair[c] + factor[c] * w1_ref[mu, e, c] + half[c] * w2_ref[mu, e, c] for c in range(2)]
+            new = [dense[mu, e, c] + factor[c] * w1_ref[mu, e, c] + half[c] * w2_ref[mu, e, c] for c in range(2)]
             out_ref[mu, part, i, j, 0] = jnp.concatenate(
                 [new[0][0:4], new[1][0:4], new[0][4:8], new[1][4:8]], axis=1
             )
@@ -709,16 +713,14 @@
         offset += width
 
 
-def call(body, outs, scratch, smem=(), count=0, cost=None):
+def call(body, outs, scratch, places=None, cost=None):
     specs = {}
-    if smem:
-        specs["in_specs"] = [
-            pl.BlockSpec(memory_space=pltpu.SMEM if i in smem else pltpu.VMEM) for i in range(count)
-        ]
+    if places is not None:
+        specs["in_specs"] = [pl.BlockSpec(memory_space=place) for place in places]
     return pl.pallas_call(
         body,
         out_shape=[jax.ShapeDtypeStruct(shape, dtype) for shape, dtype in outs],
-        scratch_shapes=[pltpu.VMEM(shape, dtype) for shape, dtype in scratch],
+        scratch_shapes=[pltpu.VMEM(*item) if isinstance(item, tuple) else item for item in scratch],
         compiler_params=pltpu.CompilerParams(vmem_limit_bytes=LIMIT),
         cost_estimate=cost,
         **specs,
@@ -734,37 +736,38 @@
     widths = (768 // count, 768 // count, 128 // count, 64 // count)
     field = ((4, 18, 2, 8, LANES), F32)
     space = ((3, 18, 2, 8, LANES), F32)
-    edge_rows = ((66, SITES), BF16)
+    edge_rows = ((70, SITES), BF16)
+    vmem, smem = pltpu.VMEM, pltpu.SMEM
     up, down, dense, edges, staples, slab = call(
         face_kernel,
         [edge_rows, edge_rows, field, space, space, ((12, 4, LANES), F32)],
-        [space, ((66, 4, LANES), F32)],
+        [space, ((70, 4, LANES), F32)],
     )(links)
     up = send(up, 1)
     down = send(down, -1)
-    cots, rows, forces, sums = call(
+    cots, rows, forces, sums, gates = call(
         space_kernel,
-        [field, ((4, 4, 16, LANES), F32), ((4, 9, 2, 8, LANES), F32), space],
+        [field, ((4, 4, 16, LANES), F32), ((4, 9, 2, 8, LANES), F32), space, ((4, 8, LANES), F32)],
         [((3, 3, 18, 2, 8, LANES), F32), ((3, 3, 18, 2, 8, LANES), F32)],
+        places=(smem, smem, vmem, vmem, vmem),
         cost=pl.CostEstimate(flops=4_000_000_000, bytes_accessed=16_000_000, transcendentals=0),
-    )(dense, cotangent, staples)
+    )(parity, link_subset, dense, cotangent, staples)
     core = (lax.axis_index("tm") % 2).astype(jnp.int32)[None]
     (block,) = call(
         functools.partial(block_kernel, widths),
         [((count, BLOCKROWS, LANES), BF16)],
         [((12, 4, LANES), F32), ((BLOCKROWS, LANES), F32)],
-        smem=(0,), count=8,
-    )(core, up, down, slab, w_first[None], w_second[None], w_third[None], w_last[None])
+        places=(smem,) + (vmem,) * 8,
+    )(core, up, down, slab, w_first, w_second, w_third, w_last, rows)
     gathered = lax.all_to_all(block, "tm", split_axis=0, concat_axis=0, tiled=True)
     fm, fup, fdown, applied, twice = call(
         time_kernel,
         [((4, 16, SITES), BF16), ((3, 8, SITES), BF16), ((3, 8, SITES), BF16), field, field],
         [
-            space, space, field, ((66, 4, LANES), F32), ((66, 4, LANES), F32),
+            space, space, field, ((70, 4, LANES), F32), ((70, 4, LANES), F32),
             ((4, 9, 2, 8, LANES), F32), ((4, 4, 16, LANES), F32),
         ],
-        smem=(4, 5), count=10,
-    )(dense, cots, up, down, parity, link_subset, edges, rows, forces, sums)
+    )(dense, cots, up, down, gates, edges, rows, forces, sums)
     below = send(fm, 1)
     above = send(fm, -1)
     fbelow = send(fup, 2)
@@ -809,7 +812,7 @@
     grads = lax.all_to_all(grads, "tm", split_axis=0, concat_axis=0, tiled=True)
     (new_links,) = call(
         update_kernel, [(links.shape, F32)], [((4, 2, 8, LANES), F32)]
-    )(links, applied, twice, coeff)
+    )(dense, applied, twice, coeff)
     grad_first, grad_second, grad_third, grad_last = call(
         functools.partial(sum_kernel, widths),
         [((1, 27 * width), F32) for width in (widths[2], widths[0], widths[1], widths[3])],

time: 63.6 us -> 65.1 us (1.024)
  local copies, waits for them, and re-layouts: 3.76 us -> 7.29 us
  starting transfers between devices: 26.8 us -> 24.4 us
    unnamed x18 -> x32, local copies, waits for them, and re-layouts: 3.74 us -> 7.29 us
    all_to_all x1, starting transfers between devices: 5.9 us -> 3.62 us  [on_device(): lax.all_to_all(block, 'tm', split_axis=0, concat_axis=0, tiled=True)]
  transfers between devices with their start and end apart: 8 -> 8, of which waited for: 3 -> 2; matrix products, arithmetic and copies ran while one was open for 0% -> 0% of each run, Pallas kernels for 17% -> 17%
where the time goes in v6:
time: 65.1 us; the launch traced here: 64.5 us
  starting transfers between devices  24.4 us (37%)
  Pallas kernels  24.3 us (37%)
  waiting for transfers between devices  7.69 us (12%)
  local copies, waits for them, and re-layouts  7.29 us (11%)
  between operations  0.75 us (1%)
    ppermute x6, starting transfers between devices, send(): lax.ppermute(value, 'tm', [(i, (i + distance) % count) for i in range(cou...  14.7 us
    pallas_call x1, Pallas kernels, on_device(): call(functools.partial(conv_kernel, count == 16), [((4, 8, SITES), F32),...  9.05 us
    unnamed x32, local copies, waits for them, and re-layouts  7.29 us
    all_to_all x1, waiting for transfers between devices, on_device(): grads = lax.all_to_all(grads, 'tm', split_axis=0, concat_axis=0, tiled=True)  6.95 us
    all_to_all x1, starting transfers between devices, on_device(): grads = lax.all_to_all(grads, 'tm', split_axis=0, concat_axis=0, tiled=True)  6.09 us
    pallas_call x1, Pallas kernels, on_device(): call(space_kernel, [field, ((4, 4, 16, LANES), F32), ((4, 9, 2, 8, LANES)...  4.81 us
    pallas_call x1, Pallas kernels, on_device(): call(time_kernel, [((4, 16, SITES), BF16), ((3, 8, SITES), BF16), ((3, 8,...  4.13 us
    all_to_all x1, starting transfers between devices, on_device(): lax.all_to_all(block, 'tm', split_axis=0, concat_axis=0, tiled=True)  3.62 us
  transfers between devices with their start and end apart: 8, of which 2 were waited for; matrix products, arithmetic and copies ran while one was open for 0% of the time, Pallas kernels for 17%

profile of v6, /device:TPU:0, one launch (start us, length us, event | category | flops | bytes accessed | tf_op | source)
XLA Modules:
  0.0 64.5 jit_solution(548147559367137906)
XLA Ops:
  0.6 1.1 %copy-done = f32[4,2,3,3,1,4,512]{6,5,4,3,2,1,0:T(4,128)S(1)} copy-done((f32[4,2,3,3,1,4,512]{6,5,4,3,2,1,0:T(4,128)S(1)}, f32[4,2,3,3,1,4,512]{6,5,4,3,2,1,0:T(4,128)}, u32[]{:S(2)}) %copy-start) | copy-done | bytes 589848
  1.7 2.4 %shard_map.119 = (bf16[70,512]{1,0:T(8,128)(2,1)S(1)}, bf16[70,512]{1,0:T(8,128)(2,1)S(1)}, f32[4,18,2,8,128]{4,3,2,1,0:T(8,128)S(1)}, f32[3,18,2,8,128]{4,3,2,1...) custom-call(f32[4,2,3,3,1,4,512]{6,5,4,3,2,1,0:T(4,128)S(1)} %copy-done), custom_call_target="tpu_custom_call" | custom-call | tf_op jit(solution)/shard_map/pallas_call | solution.py:741
  4.7 5.1 %collective-permute-start.1 = (bf16[70,512]{1,0:T(8,128)(2,1)S(1)}, bf16[70,512]{1,0:T(8,128)(2,1)S(1)}, u32[]{:S(2)}, u32[]{:S(2)}) collective-permute-start(bf16[70,512]{1,0:T(8,128)(2,1)S(1)} %get-tuple-element.39), channel_id=1, source_target_pairs={{0,15},{1,0},{2,1},{3,2},{4,3},{5,4},{6,5},{7,6},{8,7},{9,8},{10,9... | collective-permute-start | bytes 215048 | tf_op jit(solution)/shard_map/ppermute | solution.py:734
  9.7 0.6 %copy-done.14 = s32[1,4]{1,0:T(1,128)S(1)} copy-done((s32[1,4]{1,0:T(1,128)S(1)}, s32[1,4]{1,0:T(1,128)}, u32[]{:S(2)}) %copy-start.14) | copy-done | bytes 40
  10.4 4.8 %shard_map.120 = (f32[4,18,2,8,128]{4,3,2,1,0:T(8,128)S(1)}, f32[4,4,16,128]{3,2,1,0:T(8,128)S(1)}, f32[4,9,2,8,128]{4,3,2,1,0:T(8,128)S(1)}, f32[3,18,2,8,128]{4,3,2,1,0:T(8,128)S(1)}, f32[4,8,128]{2,1,0:T(8,128)S(1)}) custom-call(s32[1,4]{1,0:T(1,128)S(1)} %copy-done.14, s32[1,4]{1,0:T(1,128)S(1)} %copy-done.15, ...), custom_call_target="tpu_custom_call" | custom-call | flops 4000000000 | bytes 16000000 | tf_op jit(solution)/shard_map/pallas_call | solution.py:748
  15.2 0.8 %copy-done.1 = f32[3,18,2,8,128]{4,3,2,1,0:T(8,128)} copy-done((f32[3,18,2,8,128]{4,3,2,1,0:T(8,128)}, f32[3,18,2,8,128]{4,3,2,1,0:T(8,128)S(1)}, u32[]{:S(2)}) %copy-start.1) | copy-done | bytes 442392
  16.0 0.6 copy-done.7
  16.6 0.6 copy-done.10
  17.3 0.9 %shard_map.122 = bf16[16,64,128]{2,1,0:T(8,128)(2,1)} custom-call(s32[1]{0:T(128)} %bitcast.core_ref, bf16[70,512]{1,0:T(8,128)(2,1)S(1)} %collective-permute-done.up_ref, bf16[70,512]{1,0:T(8,128)(2,1)S(1)} %collective-permute-done.1.down_ref, f32[12,4,128]{2,1,0:T(4,128)S(1)} %get-tuple-element.50.slab, bf16[216]{0:T(256)(128)(2,1)S(1)} %copy-done.11, ...), custom_call_target="tpu_custom_call" | custom-call | tf_op jit(solution)/shard_map/pallas_call | solution.py:756
  18.2 3.6 %all-to-all-start = ((bf16[16,64,128]{2,1,0:T(8,128)(2,1)}), bf16[16,64,128]{2,1,0:T(8,128)(2,1)S(1)}, u32[]{:S(2)}, u32[]{:S(2)}) async-start(bf16[16,64,128]{2,1,0:T(8,128)(2,1)} %shard_map.122), calls=%async_computation | async-start | bytes 524288 | tf_op jit(solution)/shard_map/all_to_all | solution.py:762
  21.8 1.0 %copy-done.2 = f32[3,18,2,8,128]{4,3,2,1,0:T(8,128)S(1)} copy-done((f32[3,18,2,8,128]{4,3,2,1,0:T(8,128)S(1)}, f32[3,18,2,8,128]{4,3,2,1,0:T(8,128)}, u32[]{:S(2)}) %copy-start.2) | copy-done | bytes 442392
  22.8 0.9 %copy-done.4 = bf16[70,512]{1,0:T(8,128)(2,1)S(1)} copy-done((bf16[70,512]{1,0:T(8,128)(2,1)S(1)}, bf16[70,512]{1,0:T(8,128)(2,1)}, u32[]{:S(2)}) %copy-start.4) | copy-done | bytes 71704
  23.7 0.9 %copy-done.6 = bf16[70,512]{1,0:T(8,128)(2,1)S(1)} copy-done((bf16[70,512]{1,0:T(8,128)(2,1)S(1)}, bf16[70,512]{1,0:T(8,128)(2,1)}, u32[]{:S(2)}) %copy-start.6) | copy-done | bytes 71704
  24.6 0.7 %copy-done.8 = f32[4,8,128]{2,1,0:T(8,128)S(1)} copy-done((f32[4,8,128]{2,1,0:T(8,128)S(1)}, f32[4,8,128]{2,1,0:T(8,128)}, u32[]{:S(2)}) %copy-start.8) | copy-done | bytes 16408
  25.3 4.1 %shard_map.121 = (bf16[4,16,512]{2,1,0:T(8,128)(2,1)S(1)}, bf16[3,8,512]{2,1,0:T(8,128)(2,1)}, bf16[3,8,512]{2,1,0:T(8,128)(2,1)}, f32[4,18,2,8,128]{4,3,2,1,0:T(8,128)S(1)}, f32[4,18,2,8,128]{4,3,2,1,0:T(8,128)S(1)}) custom-call(f32[4,18,2,8,128]{4,3,2,1,0:T(8,128)S(1)} %get-tuple-element.35.dense, f32[4,18,2,8,128]{4,3,2,1,0:T(8,128)S(1)} %get-tuple-element.37.cots, ...), custom_call_target="tpu_custom_call" | custom-call | tf_op jit(solution)/shard_map/pallas_call | solution.py:763
  29.9 4.0 %collective-permute-start.3 = (bf16[4,16,512]{2,1,0:T(8,128)(2,1)S(1)}, bf16[4,16,512]{2,1,0:T(8,128)(2,1)S(1)}, u32[]{:S(2)}, u32[]{:S(2)}) collective-permute-start(bf16[4,16,512]{2,1,0:T(8,128)(2,1)S(1)} %get-tuple-element.47.fm_ref), channel_id=1, source_target_pairs={{0,15},{1,0},{2,1},{3,2},{4,3},{5,4},{6,5},{7,6},{8,7},{9,8},{10,9... | collective-permute-start | bytes 196616 | tf_op jit(solution)/shard_map/ppermute | solution.py:734
  33.9 4.7 %collective-permute-start.5 = (bf16[3,8,512]{2,1,0:T(8,128)(2,1)}, bf16[3,8,512]{2,1,0:T(8,128)(2,1)S(1)}, u32[]{:S(2)}, u32[]{:S(2)}) collective-permute-start(bf16[3,8,512]{2,1,0:T(8,128)(2,1)} %get-tuple-element.49), channel_id=1, source_target_pairs={{0,14},{1,15},{2,0},{3,1},{4,2},{5,3},{6,4},{7,5},{8,6},{9,7},{10,... | collective-permute-start | bytes 73736 | tf_op jit(solution)/shard_map/ppermute | solution.py:734
  38.6 1.3 %shard_map.123 = (f32[2,4,128]{2,1,0:T(4,128)S(1)}, bf16[48,72]{1,0:T(8,128)(2,1)S(1)}, bf16[48,432]{1,0:T(8,128)(2,1)S(1)}, bf16[48,432]{1,0:T(8,128)(2,1)S(1)}...) custom-call(bf16[16,64,128]{2,1,0:T(8,128)(2,1)S(1)} %all-to-all-don, ...), custom_call_target="tpu_custom_call" | custom-call | tf_op jit(solution)/shard_map/pallas_call | solution.py:782
  39.9 0.7 %collective-permute-done.4.fbelow_ref = bf16[3,8,512]{2,1,0:T(8,128)(2,1)S(1)} collective-permute-done((bf16[3,8,512]{2,1,0:T(8,128)(2,1)}, bf16[3,8,512]{2,1,0:T(8,128)(2,1)S(1)}, u32[]{:S(2)}, u32[]{:S(2)}) %collective-permute-start.4) | collective-permute-done | bytes 24608 | tf_op jit(solution)/shard_map/ppermute | solution.py:734
  40.7 9.1 %shard_map.124 = (f32[4,8,512]{2,1,0:T(8,128)S(1)}, bf16[16,27,128]{2,1,0:T(8,128)(2,1)}) custom-call(bf16[4,16,512]{2,1,0:T(8,128)(2,1)S(1)} %get-tuple-element.47.fm_ref, bf16[4,16,512]{2,1,0:T(8,128)(2,1)S(1)} %collective-permute-done.2.below_ref, bf16[4,16,512]{2,1,0:T(8,128)(2,1)S(1)} %collective-permute-done.3.above_ref, ...), custom_call_target="tpu_custom_call" | custom-call | tf_op jit(solution)/shard_map/pallas_call | solution.py:796
  49.7 6.1 %all-to-all-start.1 = ((bf16[16,27,128]{2,1,0:T(8,128)(2,1)}), bf16[16,27,128]{2,1,0:T(8,128)(2,1)S(1)}, u32[]{:S(2)}, u32[]{:S(2)}) async-start(bf16[16,27,128]{2,1,0:T(8,128)(2,1)} %get-tuple-element.60), calls=%async_computation.1 | async-start | bytes 262144 | tf_op jit(solution)/shard_map/all_to_all | solution.py:812
  55.8 1.0 %shard_map.125 = f32[4,2,3,3,1,4,512]{6,5,4,3,2,1,0:T(4,128)} custom-call(f32[4,18,2,8,128]{4,3,2,1,0:T(8,128)S(1)} %get-tuple-element.35.dense, f32[4,18,2,8,128]{4,3,2,1,0:T(8,128)S(1)} %get-tuple-element.45.w1_ref, f32[4,18,2,8,128]{4,3,2,1,0:T(8,128)S(1)} %get-tuple-element.46.w2_ref, f32[4,8,512]{2,1,0:T(8,128)S(1)} %get-tuple-element.59.coeff_ref), custom_call_target="tpu_custom_call" | custom-call | tf_op jit(solution)/shard_map/pallas_call | solution.py:813
  56.8 6.9 %all-to-all-done.1.parts_ref = bf16[16,27,128]{2,1,0:T(8,128)(2,1)S(1)} async-done(((bf16[16,27,128]{2,1,0:T(8,128)(2,1)}), bf16[16,27,128]{2,1,0:T(8,128)(2,1)S(1)}, u32[]{:S(2)}, u32[]{:S(2)}) %all-to-all-start.1) | async-done | bytes 110624 | tf_op jit(solution)/shard_map/all_to_all | solution.py:812
  63.7 0.8 %shard_map.126 = (f32[1,216]{1,0:T(1,128)}, f32[1,1296]{1,0:T(1,128)}, f32[1,1296]{1,0:T(1,128)}, f32[1,108]{1,0:T(1,128)}) custom-call(bf16[16,27,128]{2,1,0:T(8,128)(2,1)S(1)} %all-to-all-done.1.parts_ref), custom_call_target="tpu_custom_call" | custom-call | tf_op jit(solution)/shard_map/pallas_call | solution.py:816
  (32 shorter events, 1.1 us)
Async XLA Ops:
  0.6 1.1 %copy-start = (f32[4,2,3,3,1,4,512]{6,5,4,3,2,1,0:T(4,128)S(1)}, f32[4,2,3,3,1,4,512]{6,5,4,3,2,1,0:T(4,128)}, u32[]{:S(2)}) copy-start(f32[4,2,3,3,1,4,512]{6,5,4,3,2,1,0:T(4,128)} %links_ref.1) | copy-start | bytes 1769476
  1.7 8.0 %copy-start.13 = (bf16[4,2,3,3,1,4,512]{6,5,4,3,2,1,0:T(4,128)(2,1)S(1)}, bf16[4,2,3,3,1,4,512]{6,5,4,3,2,1,0:T(4,128)(2,1)}, u32[]{:S(2)}) copy-start(bf16[4,2,3,3,1,4,512]{6,5,4,3,2,1,0:T(4,128)(2,1)} %cot_ref.1) | copy-start | bytes 884740
  4.2 12.4 %collective-permute-start = (bf16[70,512]{1,0:T(8,128)(2,1)S(1)}, bf16[70,512]{1,0:T(8,128)(2,1)S(1)}, u32[]{:S(2)}, u32[]{:S(2)}) collective-permute-start(bf16[70,512]{1,0:T(8,128)(2,1)S(1)} %get-tuple-element.38), channel_id=1, source_target_pairs={{0,1},{1,2},{2,3},{3,4},{4,5},{5,6},{6,7},{7,8},{8,9},{9,10},{10,1... | collective-permute-start | bytes 215048 | tf_op jit(solution)/shard_map/ppermute | solution.py:734
  4.7 11.9 %collective-permute-start.1 = (bf16[70,512]{1,0:T(8,128)(2,1)S(1)}, bf16[70,512]{1,0:T(8,128)(2,1)S(1)}, u32[]{:S(2)}, u32[]{:S(2)}) collective-permute-start(bf16[70,512]{1,0:T(8,128)(2,1)S(1)} %get-tuple-element.39), channel_id=1, source_target_pairs={{0,15},{1,0},{2,1},{3,2},{4,3},{5,4},{6,5},{7,6},{8,7},{9,8},{10,9... | collective-permute-start | bytes 215048 | tf_op jit(solution)/shard_map/ppermute | solution.py:734
  9.7 0.7 %copy-start.14 = (s32[1,4]{1,0:T(1,128)S(1)}, s32[1,4]{1,0:T(1,128)}, u32[]{:S(2)}) copy-start(s32[1,4]{1,0:T(1,128)} %parity_ref.1) | copy-start | bytes 52
  9.7 0.7 %copy-start.15 = (s32[1,4]{1,0:T(1,128)S(1)}, s32[1,4]{1,0:T(1,128)}, u32[]{:S(2)}) copy-start(s32[1,4]{1,0:T(1,128)} %subset_ref.1) | copy-start | bytes 52
  15.2 0.8 %copy-start.1 = (f32[3,18,2,8,128]{4,3,2,1,0:T(8,128)}, f32[3,18,2,8,128]{4,3,2,1,0:T(8,128)S(1)}, u32[]{:S(2)}) copy-start(f32[3,18,2,8,128]{4,3,2,1,0:T(8,128)S(1)} %get-tuple-element.44.sums_ref) | copy-start | bytes 1327108
  16.0 0.6 copy-start.7
  16.6 0.7 %copy-start.10 = (bf16[1296]{0:T(1024)(128)(2,1)S(1)}, bf16[1296]{0:T(1024)(128)(2,1)}, u32[]{:S(2)}) copy-start(bf16[1296]{0:T(1024)(128)(2,1)} %w3_ref.1) | copy-start | bytes 7780
  16.6 0.7 %copy-start.9 = (bf16[1296]{0:T(1024)(128)(2,1)S(1)}, bf16[1296]{0:T(1024)(128)(2,1)}, u32[]{:S(2)}) copy-start(bf16[1296]{0:T(1024)(128)(2,1)} %w2_ref.1) | copy-start | bytes 7780
  16.6 1.6 %copy-start.3 = (bf16[70,512]{1,0:T(8,128)(2,1)}, bf16[70,512]{1,0:T(8,128)(2,1)S(1)}, u32[]{:S(2)}) copy-start(bf16[70,512]{1,0:T(8,128)(2,1)S(1)} %collective-permute-done.up_ref) | copy-start | bytes 215044
  16.6 1.6 %copy-start.5 = (bf16[70,512]{1,0:T(8,128)(2,1)}, bf16[70,512]{1,0:T(8,128)(2,1)S(1)}, u32[]{:S(2)}) copy-start(bf16[70,512]{1,0:T(8,128)(2,1)S(1)} %collective-permute-done.1.down_ref) | copy-start | bytes 215044
  16.6 0.7 %copy-start.11 = (bf16[216]{0:T(256)(128)(2,1)S(1)}, bf16[216]{0:T(256)(128)(2,1)}, u32[]{:S(2)}) copy-start(bf16[216]{0:T(256)(128)(2,1)} %w1_ref.1) | copy-start | bytes 1300
  16.6 0.7 %copy-start.12 = (bf16[108]{0:T(256)(128)(2,1)S(1)}, bf16[108]{0:T(256)(128)(2,1)}, u32[]{:S(2)}) copy-start(bf16[108]{0:T(256)(128)(2,1)} %w4_ref.1) | copy-start | bytes 652
  18.2 20.4 %all-to-all-start = ((bf16[16,64,128]{2,1,0:T(8,128)(2,1)}), bf16[16,64,128]{2,1,0:T(8,128)(2,1)S(1)}, u32[]{:S(2)}, u32[]{:S(2)}) async-start(bf16[16,64,128]{2,1,0:T(8,128)(2,1)} %shard_map.122), calls=%async_computation | async-start | bytes 524288 | tf_op jit(solution)/shard_map/all_to_all | solution.py:762
  21.8 1.0 %copy-start.2 = (f32[3,18,2,8,128]{4,3,2,1,0:T(8,128)S(1)}, f32[3,18,2,8,128]{4,3,2,1,0:T(8,128)}, u32[]{:S(2)}) copy-start(f32[3,18,2,8,128]{4,3,2,1,0:T(8,128)} %copy-done.1) | copy-start | bytes 1327108
  22.8 0.9 %copy-start.4 = (bf16[70,512]{1,0:T(8,128)(2,1)S(1)}, bf16[70,512]{1,0:T(8,128)(2,1)}, u32[]{:S(2)}) copy-start(bf16[70,512]{1,0:T(8,128)(2,1)} %copy-done.3) | copy-start | bytes 215044
  23.7 0.9 %copy-start.6 = (bf16[70,512]{1,0:T(8,128)(2,1)S(1)}, bf16[70,512]{1,0:T(8,128)(2,1)}, u32[]{:S(2)}) copy-start(bf16[70,512]{1,0:T(8,128)(2,1)} %copy-done.5) | copy-start | bytes 215044
  24.6 0.7 %copy-start.8 = (f32[4,8,128]{2,1,0:T(8,128)S(1)}, f32[4,8,128]{2,1,0:T(8,128)}, u32[]{:S(2)}) copy-start(f32[4,8,128]{2,1,0:T(8,128)} %copy-done.7) | copy-start | bytes 49156
  29.5 11.2 %collective-permute-start.2 = (bf16[4,16,512]{2,1,0:T(8,128)(2,1)S(1)}, bf16[4,16,512]{2,1,0:T(8,128)(2,1)S(1)}, u32[]{:S(2)}, u32[]{:S(2)}) collective-permute-start(bf16[4,16,512]{2,1,0:T(8,128)(2,1)S(1)} %get-tuple-element.47.fm_ref), channel_id=1, source_target_pairs={{0,1},{1,2},{2,3},{3,4},{4,5},{5,6},{6,7},{7,8},{8,9},{9,10},{10,1... | collective-permute-start | bytes 196616 | tf_op jit(solution)/shard_map/ppermute | solution.py:734
  29.9 10.8 %collective-permute-start.3 = (bf16[4,16,512]{2,1,0:T(8,128)(2,1)S(1)}, bf16[4,16,512]{2,1,0:T(8,128)(2,1)S(1)}, u32[]{:S(2)}, u32[]{:S(2)}) collective-permute-start(bf16[4,16,512]{2,1,0:T(8,128)(2,1)S(1)} %get-tuple-element.47.fm_ref), channel_id=1, source_target_pairs={{0,15},{1,0},{2,1},{3,2},{4,3},{5,4},{6,5},{7,6},{8,7},{9,8},{10,9... | collective-permute-start | bytes 196616 | tf_op jit(solution)/shard_map/ppermute | solution.py:734
  33.9 6.7 %collective-permute-start.4 = (bf16[3,8,512]{2,1,0:T(8,128)(2,1)}, bf16[3,8,512]{2,1,0:T(8,128)(2,1)S(1)}, u32[]{:S(2)}, u32[]{:S(2)}) collective-permute-start(bf16[3,8,512]{2,1,0:T(8,128)(2,1)} %get-tuple-element.48), channel_id=1, source_target_pairs={{0,2},{1,3},{2,4},{3,5},{4,6},{5,7},{6,8},{7,9},{8,10},{9,11},{10,... | collective-permute-start | bytes 73736 | tf_op jit(solution)/shard_map/ppermute | solution.py:734
  33.9 6.7 %collective-permute-start.5 = (bf16[3,8,512]{2,1,0:T(8,128)(2,1)}, bf16[3,8,512]{2,1,0:T(8,128)(2,1)S(1)}, u32[]{:S(2)}, u32[]{:S(2)}) collective-permute-start(bf16[3,8,512]{2,1,0:T(8,128)(2,1)} %get-tuple-element.49), channel_id=1, source_target_pairs={{0,14},{1,15},{2,0},{3,1},{4,2},{5,3},{6,4},{7,5},{8,6},{9,7},{10,... | collective-permute-start | bytes 73736 | tf_op jit(solution)/shard_map/ppermute | solution.py:734
  49.7 14.0 %all-to-all-start.1 = ((bf16[16,27,128]{2,1,0:T(8,128)(2,1)}), bf16[16,27,128]{2,1,0:T(8,128)(2,1)S(1)}, u32[]{:S(2)}, u32[]{:S(2)}) async-start(bf16[16,27,128]{2,1,0:T(8,128)(2,1)} %get-tuple-element.60), calls=%async_computation.1 | async-start | bytes 262144 | tf_op jit(solution)/shard_map/all_to_all | solution.py:812

commit v7 on v6

--- a/solution.py
+++ b/solution.py
@@ -18,7 +18,7 @@
 ENTRIES = tuple((c, i, j) for c in range(2) for i in range(3) for j in range(3))
 SLABROWS = 24
 BLOCKROWS = 64
-LIMIT = 40 * 1024 * 1024
+LIMIT = 8 * 1024 * 1024
 
 
 def lane_iota(rows):
@@ -713,7 +713,7 @@
         offset += width
 
 
-def call(body, outs, scratch, places=None, cost=None):
+def call(body, outs, scratch, places=None, cost=None, limit=LIMIT):
     specs = {}
     if places is not None:
         specs["in_specs"] = [pl.BlockSpec(memory_space=place) for place in places]
@@ -721,7 +721,7 @@
         body,
         out_shape=[jax.ShapeDtypeStruct(shape, dtype) for shape, dtype in outs],
         scratch_shapes=[pltpu.VMEM(*item) if isinstance(item, tuple) else item for item in scratch],
-        compiler_params=pltpu.CompilerParams(vmem_limit_bytes=LIMIT),
+        compiler_params=pltpu.CompilerParams(vmem_limit_bytes=limit),
         cost_estimate=cost,
         **specs,
     )
@@ -801,6 +801,7 @@
             ((3, 8, window), F32), ((8, window), F32), ((H, window), BF16), ((H, window), BF16), ((H, 4 * SITES), BF16),
             ((432, 4 * SITES), BF16), ((72, 4 * SITES), BF16), ((432, LANES), F32),
         ],
+        limit=20 * 1024 * 1024,
     )(fm, below, above, fbelow, fabove, loops, p1, p2, p3, p4, b2, b3, b4)
     if count != 16:
         offset = 0

time: 65.1 us -> 65.1 us (level)
  no operation moved by 1% of the time
where the time goes in v7:
time: 65.1 us; the launch traced here: 64.5 us
  starting transfers between devices  24.5 us (38%)
  Pallas kernels  24.3 us (37%)
  waiting for transfers between devices  7.69 us (12%)
  local copies, waits for them, and re-layouts  7.29 us (11%)
  between operations  0.75 us (1%)
    ppermute x6, starting transfers between devices, send(): lax.ppermute(value, 'tm', [(i, (i + distance) % count) for i in range(cou...  14.7 us
    pallas_call x1, Pallas kernels, on_device(): call(functools.partial(conv_kernel, count == 16), [((4, 8, SITES), F32),...  9.06 us
    unnamed x32, local copies, waits for them, and re-layouts  7.29 us
    all_to_all x1, waiting for transfers between devices, on_device(): grads = lax.all_to_all(grads, 'tm', split_axis=0, concat_axis=0, tiled=True)  6.95 us
    all_to_all x1, starting transfers between devices, on_device(): grads = lax.all_to_all(grads, 'tm', split_axis=0, concat_axis=0, tiled=True)  6.1 us
    pallas_call x1, Pallas kernels, on_device(): call(space_kernel, [field, ((4, 4, 16, LANES), F32), ((4, 9, 2, 8, LANES)...  4.81 us
    pallas_call x1, Pallas kernels, on_device(): call(time_kernel, [((4, 16, SITES), BF16), ((3, 8, SITES), BF16), ((3, 8,...  4.13 us
    all_to_all x1, starting transfers between devices, on_device(): lax.all_to_all(block, 'tm', split_axis=0, concat_axis=0, tiled=True)  3.62 us
  transfers between devices with their start and end apart: 8, of which 2 were waited for; matrix products, arithmetic and copies ran while one was open for 0% of the time, Pallas kernels for 17%

profile of v7, /device:TPU:0, one launch (start us, length us, event | category | flops | bytes accessed | tf_op | source)
XLA Modules:
  0.0 64.5 jit_solution(16818214898195203099)
XLA Ops:
  0.6 1.1 %copy-done = f32[4,2,3,3,1,4,512]{6,5,4,3,2,1,0:T(4,128)S(1)} copy-done((f32[4,2,3,3,1,4,512]{6,5,4,3,2,1,0:T(4,128)S(1)}, f32[4,2,3,3,1,4,512]{6,5,4,3,2,1,0:T(4,128)}, u32[]{:S(2)}) %copy-start) | copy-done | bytes 589848
  1.7 2.4 %shard_map.119 = (bf16[70,512]{1,0:T(8,128)(2,1)S(1)}, bf16[70,512]{1,0:T(8,128)(2,1)S(1)}, f32[4,18,2,8,128]{4,3,2,1,0:T(8,128)S(1)}, f32[3,18,2,8,128]{4,3,2,1...) custom-call(f32[4,2,3,3,1,4,512]{6,5,4,3,2,1,0:T(4,128)S(1)} %copy-done), custom_call_target="tpu_custom_call" | custom-call | tf_op jit(solution)/shard_map/pallas_call | solution.py:741
  4.7 5.1 %collective-permute-start.1 = (bf16[70,512]{1,0:T(8,128)(2,1)S(1)}, bf16[70,512]{1,0:T(8,128)(2,1)S(1)}, u32[]{:S(2)}, u32[]{:S(2)}) collective-permute-start(bf16[70,512]{1,0:T(8,128)(2,1)S(1)} %get-tuple-element.39), channel_id=1, source_target_pairs={{0,15},{1,0},{2,1},{3,2},{4,3},{5,4},{6,5},{7,6},{8,7},{9,8},{10,9... | collective-permute-start | bytes 215048 | tf_op jit(solution)/shard_map/ppermute | solution.py:734
  9.7 0.6 %copy-done.14 = s32[1,4]{1,0:T(1,128)S(1)} copy-done((s32[1,4]{1,0:T(1,128)S(1)}, s32[1,4]{1,0:T(1,128)}, u32[]{:S(2)}) %copy-start.14) | copy-done | bytes 40
  10.4 4.8 %shard_map.120 = (f32[4,18,2,8,128]{4,3,2,1,0:T(8,128)S(1)}, f32[4,4,16,128]{3,2,1,0:T(8,128)S(1)}, f32[4,9,2,8,128]{4,3,2,1,0:T(8,128)S(1)}, f32[3,18,2,8,128]{4,3,2,1,0:T(8,128)S(1)}, f32[4,8,128]{2,1,0:T(8,128)S(1)}) custom-call(s32[1,4]{1,0:T(1,128)S(1)} %copy-done.14, s32[1,4]{1,0:T(1,128)S(1)} %copy-done.15, ...), custom_call_target="tpu_custom_call" | custom-call | flops 4000000000 | bytes 16000000 | tf_op jit(solution)/shard_map/pallas_call | solution.py:748
  15.2 0.8 %copy-done.1 = f32[3,18,2,8,128]{4,3,2,1,0:T(8,128)} copy-done((f32[3,18,2,8,128]{4,3,2,1,0:T(8,128)}, f32[3,18,2,8,128]{4,3,2,1,0:T(8,128)S(1)}, u32[]{:S(2)}) %copy-start.1) | copy-done | bytes 442392
  16.0 0.6 copy-done.7
  16.6 0.6 copy-done.10
  17.3 0.9 %shard_map.122 = bf16[16,64,128]{2,1,0:T(8,128)(2,1)} custom-call(s32[1]{0:T(128)} %bitcast.core_ref, bf16[70,512]{1,0:T(8,128)(2,1)S(1)} %collective-permute-done.up_ref, bf16[70,512]{1,0:T(8,128)(2,1)S(1)} %collective-permute-done.1.down_ref, f32[12,4,128]{2,1,0:T(4,128)S(1)} %get-tuple-element.50.slab, bf16[216]{0:T(256)(128)(2,1)S(1)} %copy-done.11, ...), custom_call_target="tpu_custom_call" | custom-call | tf_op jit(solution)/shard_map/pallas_call | solution.py:756
  18.2 3.6 %all-to-all-start = ((bf16[16,64,128]{2,1,0:T(8,128)(2,1)}), bf16[16,64,128]{2,1,0:T(8,128)(2,1)S(1)}, u32[]{:S(2)}, u32[]{:S(2)}) async-start(bf16[16,64,128]{2,1,0:T(8,128)(2,1)} %shard_map.122), calls=%async_computation | async-start | bytes 524288 | tf_op jit(solution)/shard_map/all_to_all | solution.py:762
  21.8 1.0 %copy-done.2 = f32[3,18,2,8,128]{4,3,2,1,0:T(8,128)S(1)} copy-done((f32[3,18,2,8,128]{4,3,2,1,0:T(8,128)S(1)}, f32[3,18,2,8,128]{4,3,2,1,0:T(8,128)}, u32[]{:S(2)}) %copy-start.2) | copy-done | bytes 442392
  22.8 0.9 %copy-done.4 = bf16[70,512]{1,0:T(8,128)(2,1)S(1)} copy-done((bf16[70,512]{1,0:T(8,128)(2,1)S(1)}, bf16[70,512]{1,0:T(8,128)(2,1)}, u32[]{:S(2)}) %copy-start.4) | copy-done | bytes 71704
  23.7 0.9 %copy-done.6 = bf16[70,512]{1,0:T(8,128)(2,1)S(1)} copy-done((bf16[70,512]{1,0:T(8,128)(2,1)S(1)}, bf16[70,512]{1,0:T(8,128)(2,1)}, u32[]{:S(2)}) %copy-start.6) | copy-done | bytes 71704
  24.6 0.7 %copy-done.8 = f32[4,8,128]{2,1,0:T(8,128)S(1)} copy-done((f32[4,8,128]{2,1,0:T(8,128)S(1)}, f32[4,8,128]{2,1,0:T(8,128)}, u32[]{:S(2)}) %copy-start.8) | copy-done | bytes 16408
  25.3 4.1 %shard_map.121 = (bf16[4,16,512]{2,1,0:T(8,128)(2,1)S(1)}, bf16[3,8,512]{2,1,0:T(8,128)(2,1)}, bf16[3,8,512]{2,1,0:T(8,128)(2,1)}, f32[4,18,2,8,128]{4,3,2,1,0:T(8,128)S(1)}, f32[4,18,2,8,128]{4,3,2,1,0:T(8,128)S(1)}) custom-call(f32[4,18,2,8,128]{4,3,2,1,0:T(8,128)S(1)} %get-tuple-element.35.dense, f32[4,18,2,8,128]{4,3,2,1,0:T(8,128)S(1)} %get-tuple-element.37.cots, ...), custom_call_target="tpu_custom_call" | custom-call | tf_op jit(solution)/shard_map/pallas_call | solution.py:763
  29.9 4.0 %collective-permute-start.3 = (bf16[4,16,512]{2,1,0:T(8,128)(2,1)S(1)}, bf16[4,16,512]{2,1,0:T(8,128)(2,1)S(1)}, u32[]{:S(2)}, u32[]{:S(2)}) collective-permute-start(bf16[4,16,512]{2,1,0:T(8,128)(2,1)S(1)} %get-tuple-element.47.fm_ref), channel_id=1, source_target_pairs={{0,15},{1,0},{2,1},{3,2},{4,3},{5,4},{6,5},{7,6},{8,7},{9,8},{10,9... | collective-permute-start | bytes 196616 | tf_op jit(solution)/shard_map/ppermute | solution.py:734
  33.9 4.7 %collective-permute-start.5 = (bf16[3,8,512]{2,1,0:T(8,128)(2,1)}, bf16[3,8,512]{2,1,0:T(8,128)(2,1)S(1)}, u32[]{:S(2)}, u32[]{:S(2)}) collective-permute-start(bf16[3,8,512]{2,1,0:T(8,128)(2,1)} %get-tuple-element.49), channel_id=1, source_target_pairs={{0,14},{1,15},{2,0},{3,1},{4,2},{5,3},{6,4},{7,5},{8,6},{9,7},{10,... | collective-permute-start | bytes 73736 | tf_op jit(solution)/shard_map/ppermute | solution.py:734
  38.6 1.3 %shard_map.123 = (f32[2,4,128]{2,1,0:T(4,128)S(1)}, bf16[48,72]{1,0:T(8,128)(2,1)S(1)}, bf16[48,432]{1,0:T(8,128)(2,1)S(1)}, bf16[48,432]{1,0:T(8,128)(2,1)S(1)}...) custom-call(bf16[16,64,128]{2,1,0:T(8,128)(2,1)S(1)} %all-to-all-don, ...), custom_call_target="tpu_custom_call" | custom-call | tf_op jit(solution)/shard_map/pallas_call | solution.py:782
  39.9 0.7 %collective-permute-done.4.fbelow_ref = bf16[3,8,512]{2,1,0:T(8,128)(2,1)S(1)} collective-permute-done((bf16[3,8,512]{2,1,0:T(8,128)(2,1)}, bf16[3,8,512]{2,1,0:T(8,128)(2,1)S(1)}, u32[]{:S(2)}, u32[]{:S(2)}) %collective-permute-start.4) | collective-permute-done | bytes 24608 | tf_op jit(solution)/shard_map/ppermute | solution.py:734
  40.7 9.1 %shard_map.124 = (f32[4,8,512]{2,1,0:T(8,128)S(1)}, bf16[16,27,128]{2,1,0:T(8,128)(2,1)}) custom-call(bf16[4,16,512]{2,1,0:T(8,128)(2,1)S(1)} %get-tuple-element.47.fm_ref, bf16[4,16,512]{2,1,0:T(8,128)(2,1)S(1)} %collective-permute-done.2.below_ref, bf16[4,16,512]{2,1,0:T(8,128)(2,1)S(1)} %collective-permute-done.3.above_ref, ...), custom_call_target="tpu_custom_call" | custom-call | tf_op jit(solution)/shard_map/pallas_call | solution.py:796
  49.7 6.1 %all-to-all-start.1 = ((bf16[16,27,128]{2,1,0:T(8,128)(2,1)}), bf16[16,27,128]{2,1,0:T(8,128)(2,1)S(1)}, u32[]{:S(2)}, u32[]{:S(2)}) async-start(bf16[16,27,128]{2,1,0:T(8,128)(2,1)} %get-tuple-element.60), calls=%async_computation.1 | async-start | bytes 262144 | tf_op jit(solution)/shard_map/all_to_all | solution.py:813
  55.8 1.0 %shard_map.125 = f32[4,2,3,3,1,4,512]{6,5,4,3,2,1,0:T(4,128)} custom-call(f32[4,18,2,8,128]{4,3,2,1,0:T(8,128)S(1)} %get-tuple-element.35.dense, f32[4,18,2,8,128]{4,3,2,1,0:T(8,128)S(1)} %get-tuple-element.45.w1_ref, f32[4,18,2,8,128]{4,3,2,1,0:T(8,128)S(1)} %get-tuple-element.46.w2_ref, f32[4,8,512]{2,1,0:T(8,128)S(1)} %get-tuple-element.59.coeff_ref), custom_call_target="tpu_custom_call" | custom-call | tf_op jit(solution)/shard_map/pallas_call | solution.py:814
  56.8 6.9 %all-to-all-done.1.parts_ref = bf16[16,27,128]{2,1,0:T(8,128)(2,1)S(1)} async-done(((bf16[16,27,128]{2,1,0:T(8,128)(2,1)}), bf16[16,27,128]{2,1,0:T(8,128)(2,1)S(1)}, u32[]{:S(2)}, u32[]{:S(2)}) %all-to-all-start.1) | async-done | bytes 110624 | tf_op jit(solution)/shard_map/all_to_all | solution.py:813
  63.8 0.8 %shard_map.126 = (f32[1,216]{1,0:T(1,128)}, f32[1,1296]{1,0:T(1,128)}, f32[1,1296]{1,0:T(1,128)}, f32[1,108]{1,0:T(1,128)}) custom-call(bf16[16,27,128]{2,1,0:T(8,128)(2,1)S(1)} %all-to-all-done.1.parts_ref), custom_call_target="tpu_custom_call" | custom-call | tf_op jit(solution)/shard_map/pallas_call | solution.py:817
  (32 shorter events, 1.1 us)
Async XLA Ops:
  0.6 1.1 %copy-start = (f32[4,2,3,3,1,4,512]{6,5,4,3,2,1,0:T(4,128)S(1)}, f32[4,2,3,3,1,4,512]{6,5,4,3,2,1,0:T(4,128)}, u32[]{:S(2)}) copy-start(f32[4,2,3,3,1,4,512]{6,5,4,3,2,1,0:T(4,128)} %links_ref.1) | copy-start | bytes 1769476
  1.7 8.0 %copy-start.13 = (bf16[4,2,3,3,1,4,512]{6,5,4,3,2,1,0:T(4,128)(2,1)S(1)}, bf16[4,2,3,3,1,4,512]{6,5,4,3,2,1,0:T(4,128)(2,1)}, u32[]{:S(2)}) copy-start(bf16[4,2,3,3,1,4,512]{6,5,4,3,2,1,0:T(4,128)(2,1)} %cot_ref.1) | copy-start | bytes 884740
  4.2 12.4 %collective-permute-start = (bf16[70,512]{1,0:T(8,128)(2,1)S(1)}, bf16[70,512]{1,0:T(8,128)(2,1)S(1)}, u32[]{:S(2)}, u32[]{:S(2)}) collective-permute-start(bf16[70,512]{1,0:T(8,128)(2,1)S(1)} %get-tuple-element.38), channel_id=1, source_target_pairs={{0,1},{1,2},{2,3},{3,4},{4,5},{5,6},{6,7},{7,8},{8,9},{9,10},{10,1... | collective-permute-start | bytes 215048 | tf_op jit(solution)/shard_map/ppermute | solution.py:734
  4.7 11.9 %collective-permute-start.1 = (bf16[70,512]{1,0:T(8,128)(2,1)S(1)}, bf16[70,512]{1,0:T(8,128)(2,1)S(1)}, u32[]{:S(2)}, u32[]{:S(2)}) collective-permute-start(bf16[70,512]{1,0:T(8,128)(2,1)S(1)} %get-tuple-element.39), channel_id=1, source_target_pairs={{0,15},{1,0},{2,1},{3,2},{4,3},{5,4},{6,5},{7,6},{8,7},{9,8},{10,9... | collective-permute-start | bytes 215048 | tf_op jit(solution)/shard_map/ppermute | solution.py:734
  9.7 0.7 %copy-start.14 = (s32[1,4]{1,0:T(1,128)S(1)}, s32[1,4]{1,0:T(1,128)}, u32[]{:S(2)}) copy-start(s32[1,4]{1,0:T(1,128)} %parity_ref.1) | copy-start | bytes 52
  9.7 0.7 %copy-start.15 = (s32[1,4]{1,0:T(1,128)S(1)}, s32[1,4]{1,0:T(1,128)}, u32[]{:S(2)}) copy-start(s32[1,4]{1,0:T(1,128)} %subset_ref.1) | copy-start | bytes 52
  15.2 0.8 %copy-start.1 = (f32[3,18,2,8,128]{4,3,2,1,0:T(8,128)}, f32[3,18,2,8,128]{4,3,2,1,0:T(8,128)S(1)}, u32[]{:S(2)}) copy-start(f32[3,18,2,8,128]{4,3,2,1,0:T(8,128)S(1)} %get-tuple-element.44.sums_ref) | copy-start | bytes 1327108
  16.0 0.6 copy-start.7
  16.6 0.7 %copy-start.10 = (bf16[1296]{0:T(1024)(128)(2,1)S(1)}, bf16[1296]{0:T(1024)(128)(2,1)}, u32[]{:S(2)}) copy-start(bf16[1296]{0:T(1024)(128)(2,1)} %w3_ref.1) | copy-start | bytes 7780
  16.6 0.7 %copy-start.9 = (bf16[1296]{0:T(1024)(128)(2,1)S(1)}, bf16[1296]{0:T(1024)(128)(2,1)}, u32[]{:S(2)}) copy-start(bf16[1296]{0:T(1024)(128)(2,1)} %w2_ref.1) | copy-start | bytes 7780
  16.6 1.6 %copy-start.3 = (bf16[70,512]{1,0:T(8,128)(2,1)}, bf16[70,512]{1,0:T(8,128)(2,1)S(1)}, u32[]{:S(2)}) copy-start(bf16[70,512]{1,0:T(8,128)(2,1)S(1)} %collective-permute-done.up_ref) | copy-start | bytes 215044
  16.6 1.6 %copy-start.5 = (bf16[70,512]{1,0:T(8,128)(2,1)}, bf16[70,512]{1,0:T(8,128)(2,1)S(1)}, u32[]{:S(2)}) copy-start(bf16[70,512]{1,0:T(8,128)(2,1)S(1)} %collective-permute-done.1.down_ref) | copy-start | bytes 215044
  16.6 0.7 %copy-start.11 = (bf16[216]{0:T(256)(128)(2,1)S(1)}, bf16[216]{0:T(256)(128)(2,1)}, u32[]{:S(2)}) copy-start(bf16[216]{0:T(256)(128)(2,1)} %w1_ref.1) | copy-start | bytes 1300
  16.6 0.7 %copy-start.12 = (bf16[108]{0:T(256)(128)(2,1)S(1)}, bf16[108]{0:T(256)(128)(2,1)}, u32[]{:S(2)}) copy-start(bf16[108]{0:T(256)(128)(2,1)} %w4_ref.1) | copy-start | bytes 652
  18.2 20.4 %all-to-all-start = ((bf16[16,64,128]{2,1,0:T(8,128)(2,1)}), bf16[16,64,128]{2,1,0:T(8,128)(2,1)S(1)}, u32[]{:S(2)}, u32[]{:S(2)}) async-start(bf16[16,64,128]{2,1,0:T(8,128)(2,1)} %shard_map.122), calls=%async_computation | async-start | bytes 524288 | tf_op jit(solution)/shard_map/all_to_all | solution.py:762
  21.8 1.0 %copy-start.2 = (f32[3,18,2,8,128]{4,3,2,1,0:T(8,128)S(1)}, f32[3,18,2,8,128]{4,3,2,1,0:T(8,128)}, u32[]{:S(2)}) copy-start(f32[3,18,2,8,128]{4,3,2,1,0:T(8,128)} %copy-done.1) | copy-start | bytes 1327108
  22.8 0.9 %copy-start.4 = (bf16[70,512]{1,0:T(8,128)(2,1)S(1)}, bf16[70,512]{1,0:T(8,128)(2,1)}, u32[]{:S(2)}) copy-start(bf16[70,512]{1,0:T(8,128)(2,1)} %copy-done.3) | copy-start | bytes 215044
  23.7 0.9 %copy-start.6 = (bf16[70,512]{1,0:T(8,128)(2,1)S(1)}, bf16[70,512]{1,0:T(8,128)(2,1)}, u32[]{:S(2)}) copy-start(bf16[70,512]{1,0:T(8,128)(2,1)} %copy-done.5) | copy-start | bytes 215044
  24.6 0.7 %copy-start.8 = (f32[4,8,128]{2,1,0:T(8,128)S(1)}, f32[4,8,128]{2,1,0:T(8,128)}, u32[]{:S(2)}) copy-start(f32[4,8,128]{2,1,0:T(8,128)} %copy-done.7) | copy-start | bytes 49156
  29.5 11.2 %collective-permute-start.2 = (bf16[4,16,512]{2,1,0:T(8,128)(2,1)S(1)}, bf16[4,16,512]{2,1,0:T(8,128)(2,1)S(1)}, u32[]{:S(2)}, u32[]{:S(2)}) collective-permute-start(bf16[4,16,512]{2,1,0:T(8,128)(2,1)S(1)} %get-tuple-element.47.fm_ref), channel_id=1, source_target_pairs={{0,1},{1,2},{2,3},{3,4},{4,5},{5,6},{6,7},{7,8},{8,9},{9,10},{10,1... | collective-permute-start | bytes 196616 | tf_op jit(solution)/shard_map/ppermute | solution.py:734
  29.9 10.8 %collective-permute-start.3 = (bf16[4,16,512]{2,1,0:T(8,128)(2,1)S(1)}, bf16[4,16,512]{2,1,0:T(8,128)(2,1)S(1)}, u32[]{:S(2)}, u32[]{:S(2)}) collective-permute-start(bf16[4,16,512]{2,1,0:T(8,128)(2,1)S(1)} %get-tuple-element.47.fm_ref), channel_id=1, source_target_pairs={{0,15},{1,0},{2,1},{3,2},{4,3},{5,4},{6,5},{7,6},{8,7},{9,8},{10,9... | collective-permute-start | bytes 196616 | tf_op jit(solution)/shard_map/ppermute | solution.py:734
  33.9 6.7 %collective-permute-start.4 = (bf16[3,8,512]{2,1,0:T(8,128)(2,1)}, bf16[3,8,512]{2,1,0:T(8,128)(2,1)S(1)}, u32[]{:S(2)}, u32[]{:S(2)}) collective-permute-start(bf16[3,8,512]{2,1,0:T(8,128)(2,1)} %get-tuple-element.48), channel_id=1, source_target_pairs={{0,2},{1,3},{2,4},{3,5},{4,6},{5,7},{6,8},{7,9},{8,10},{9,11},{10,... | collective-permute-start | bytes 73736 | tf_op jit(solution)/shard_map/ppermute | solution.py:734
  33.9 6.7 %collective-permute-start.5 = (bf16[3,8,512]{2,1,0:T(8,128)(2,1)}, bf16[3,8,512]{2,1,0:T(8,128)(2,1)S(1)}, u32[]{:S(2)}, u32[]{:S(2)}) collective-permute-start(bf16[3,8,512]{2,1,0:T(8,128)(2,1)} %get-tuple-element.49), channel_id=1, source_target_pairs={{0,14},{1,15},{2,0},{3,1},{4,2},{5,3},{6,4},{7,5},{8,6},{9,7},{10,... | collective-permute-start | bytes 73736 | tf_op jit(solution)/shard_map/ppermute | solution.py:734
  49.7 14.0 %all-to-all-start.1 = ((bf16[16,27,128]{2,1,0:T(8,128)(2,1)}), bf16[16,27,128]{2,1,0:T(8,128)(2,1)S(1)}, u32[]{:S(2)}, u32[]{:S(2)}) async-start(bf16[16,27,128]{2,1,0:T(8,128)(2,1)} %get-tuple-element.60), calls=%async_computation.1 | async-start | bytes 262144 | tf_op jit(solution)/shard_map/all_to_all | solution.py:813

commit v8 on v7

--- a/solution.py
+++ b/solution.py
@@ -277,7 +277,7 @@
 
 
 def block_kernel(
-    widths, core_ref, up_ref, down_ref, slab, w1_ref, w2_ref, w3_ref, w4_ref, rows_ref, block_ref, other, block
+    widths, core_ref, up_ref, down_ref, slab, w1_ref, w2_ref, w3_ref, w4_ref, after_ref, block_ref, other, block
 ):
     even = core_ref[0] == 0
     up = up_ref[0:16].astype(F32)
@@ -752,14 +752,6 @@
         places=(smem, smem, vmem, vmem, vmem),
         cost=pl.CostEstimate(flops=4_000_000_000, bytes_accessed=16_000_000, transcendentals=0),
     )(parity, link_subset, dense, cotangent, staples)
-    core = (lax.axis_index("tm") % 2).astype(jnp.int32)[None]
-    (block,) = call(
-        functools.partial(block_kernel, widths),
-        [((count, BLOCKROWS, LANES), BF16)],
-        [((12, 4, LANES), F32), ((BLOCKROWS, LANES), F32)],
-        places=(smem,) + (vmem,) * 8,
-    )(core, up, down, slab, w_first, w_second, w_third, w_last, rows)
-    gathered = lax.all_to_all(block, "tm", split_axis=0, concat_axis=0, tiled=True)
     fm, fup, fdown, applied, twice = call(
         time_kernel,
         [((4, 16, SITES), BF16), ((3, 8, SITES), BF16), ((3, 8, SITES), BF16), field, field],
@@ -768,6 +760,14 @@
             ((4, 9, 2, 8, LANES), F32), ((4, 4, 16, LANES), F32),
         ],
     )(dense, cots, up, down, gates, edges, rows, forces, sums)
+    core = (lax.axis_index("tm") % 2).astype(jnp.int32)[None]
+    (block,) = call(
+        functools.partial(block_kernel, widths),
+        [((count, BLOCKROWS, LANES), BF16)],
+        [((12, 4, LANES), F32), ((BLOCKROWS, LANES), F32)],
+        places=(smem,) + (vmem,) * 8,
+    )(core, up, down, slab, w_first, w_second, w_third, w_last, fdown)
+    gathered = lax.all_to_all(block, "tm", split_axis=0, concat_axis=0, tiled=True)
     below = send(fm, 1)
     above = send(fm, -1)
     fbelow = send(fup, 2)

time: 65.1 us -> 63.3 us (0.972)
  local copies, waits for them, and re-layouts: 7.29 us -> 6.25 us
  starting transfers between devices: 24.5 us -> 23.8 us
    all_to_all x1, waiting for transfers between devices: 0.01 us -> 1.29 us  [on_device(): lax.all_to_all(block, 'tm', split_axis=0, concat_axis=0, tiled=True)]
    unnamed x32 -> x28, local copies, waits for them, and re-layouts: 7.29 us -> 6.25 us
    all_to_all x1, starting transfers between devices: 6.1 us -> 5.3 us  [on_device(): grads = lax.all_to_all(grads, 'tm', split_axis=0, concat_axis=0, tiled=True)]
    ppermute x6, waiting for transfers between devices: 0.74 us -> 0.02 us  [send(): lax.ppermute(value, 'tm', [(i, (i + distance) % count) for i in range(cou...]
  transfers between devices with their start and end apart: 8 -> 8, of which waited for: 2 -> 2; matrix products, arithmetic and copies ran while one was open for 0% -> 0% of each run, Pallas kernels for 17% -> 11%
where the time goes in v8:
time: 63.3 us; the launch traced here: 62.8 us
  starting transfers between devices  23.8 us (38%)
  Pallas kernels  23.7 us (37%)
  waiting for transfers between devices  8.25 us (13%)
  local copies, waits for them, and re-layouts  6.25 us (10%)
  between operations  0.76 us (1%)
    ppermute x6, starting transfers between devices, send(): lax.ppermute(value, 'tm', [(i, (i + distance) % count) for i in range(cou...  14.8 us
    pallas_call x1, Pallas kernels, on_device(): call(functools.partial(conv_kernel, count == 16), [((4, 8, SITES), F32),...  9.06 us
    all_to_all x1, waiting for transfers between devices, on_device(): grads = lax.all_to_all(grads, 'tm', split_axis=0, concat_axis=0, tiled=True)  6.95 us
    unnamed x28, local copies, waits for them, and re-layouts  6.25 us
    all_to_all x1, starting transfers between devices, on_device(): grads = lax.all_to_all(grads, 'tm', split_axis=0, concat_axis=0, tiled=True)  5.3 us
    pallas_call x1, Pallas kernels, on_device(): call(space_kernel, [field, ((4, 4, 16, LANES), F32), ((4, 9, 2, 8, LANES)...  4.81 us
    all_to_all x1, starting transfers between devices, on_device(): lax.all_to_all(block, 'tm', split_axis=0, concat_axis=0, tiled=True)  3.75 us
    pallas_call x1, Pallas kernels, on_device(): call(time_kernel, [((4, 16, SITES), BF16), ((3, 8, SITES), BF16), ((3, 8,...  3.52 us
  transfers between devices with their start and end apart: 8, of which 2 were waited for; matrix products, arithmetic and copies ran while one was open for 0% of the time, Pallas kernels for 11%

profile of v8, /device:TPU:0, one launch (start us, length us, event | category | flops | bytes accessed | tf_op | source)
XLA Modules:
  0.0 62.8 jit_solution(5145765191190156187)
XLA Ops:
  0.6 1.1 %copy-done = f32[4,2,3,3,1,4,512]{6,5,4,3,2,1,0:T(4,128)S(1)} copy-done((f32[4,2,3,3,1,4,512]{6,5,4,3,2,1,0:T(4,128)S(1)}, f32[4,2,3,3,1,4,512]{6,5,4,3,2,1,0:T(4,128)}, u32[]{:S(2)}) %copy-start) | copy-done | bytes 589848
  1.7 2.4 %shard_map.119 = (bf16[70,512]{1,0:T(8,128)(2,1)S(1)}, bf16[70,512]{1,0:T(8,128)(2,1)S(1)}, f32[4,18,2,8,128]{4,3,2,1,0:T(8,128)S(1)}, f32[3,18,2,8,128]{4,3,2,1...) custom-call(f32[4,2,3,3,1,4,512]{6,5,4,3,2,1,0:T(4,128)S(1)} %copy-done), custom_call_target="tpu_custom_call" | custom-call | tf_op jit(solution)/shard_map/pallas_call | solution.py:741
  4.2 0.5 collective-permute-start
  4.7 5.1 %collective-permute-start.1 = (bf16[70,512]{1,0:T(8,128)(2,1)S(1)}, bf16[70,512]{1,0:T(8,128)(2,1)S(1)}, u32[]{:S(2)}, u32[]{:S(2)}) collective-permute-start(bf16[70,512]{1,0:T(8,128)(2,1)S(1)} %get-tuple-element.39), channel_id=1, source_target_pairs={{0,15},{1,0},{2,1},{3,2},{4,3},{5,4},{6,5},{7,6},{8,7},{9,8},{10,9... | collective-permute-start | bytes 215048 | tf_op jit(solution)/shard_map/ppermute | solution.py:734
  9.7 0.6 %copy-done.12 = s32[1,4]{1,0:T(1,128)S(1)} copy-done((s32[1,4]{1,0:T(1,128)S(1)}, s32[1,4]{1,0:T(1,128)}, u32[]{:S(2)}) %copy-start.12) | copy-done | bytes 40
  10.4 4.8 %shard_map.120 = (f32[4,18,2,8,128]{4,3,2,1,0:T(8,128)S(1)}, f32[4,4,16,128]{3,2,1,0:T(8,128)S(1)}, f32[4,9,2,8,128]{4,3,2,1,0:T(8,128)S(1)}, f32[3,18,2,8,128]{4,3,2,1,0:T(8,128)S(1)}, f32[4,8,128]{2,1,0:T(8,128)S(1)}) custom-call(s32[1,4]{1,0:T(1,128)S(1)} %copy-done.12, s32[1,4]{1,0:T(1,128)S(1)} %copy-done.13, ...), custom_call_target="tpu_custom_call" | custom-call | flops 4000000000 | bytes 16000000 | tf_op jit(solution)/shard_map/pallas_call | solution.py:748
  15.2 0.7 %copy-done.1 = f32[4,9,2,8,128]{4,3,2,1,0:T(8,128)} copy-done((f32[4,9,2,8,128]{4,3,2,1,0:T(8,128)}, f32[4,9,2,8,128]{4,3,2,1,0:T(8,128)S(1)}, u32[]{:S(2)}) %copy-start.1) | copy-done | bytes 294936
  15.9 0.6 %copy-done.3 = f32[4,4,16,128]{3,2,1,0:T(8,128)} copy-done((f32[4,4,16,128]{3,2,1,0:T(8,128)}, f32[4,4,16,128]{3,2,1,0:T(8,128)S(1)}, u32[]{:S(2)}) %copy-start.3) | copy-done | bytes 131096
  16.6 1.0 %copy-done.2 = f32[4,9,2,8,128]{4,3,2,1,0:T(8,128)S(1)} copy-done((f32[4,9,2,8,128]{4,3,2,1,0:T(8,128)S(1)}, f32[4,9,2,8,128]{4,3,2,1,0:T(8,128)}, u32[]{:S(2)}) %copy-start.2) | copy-done | bytes 294936
  17.5 0.9 %copy-done.4 = f32[4,4,16,128]{3,2,1,0:T(8,128)S(1)} copy-done((f32[4,4,16,128]{3,2,1,0:T(8,128)S(1)}, f32[4,4,16,128]{3,2,1,0:T(8,128)}, u32[]{:S(2)}) %copy-start.4) | copy-done | bytes 131096
  18.4 3.5 %shard_map.121 = (bf16[4,16,512]{2,1,0:T(8,128)(2,1)S(1)}, bf16[3,8,512]{2,1,0:T(8,128)(2,1)S(1)}, bf16[3,8,512]{2,1,0:T(8,128)(2,1)S(1)}, f32[4,18,2,8,128]{4,3,2,1,0:T(8,128)S(1)}, f32[4,18,2,8,128]{4,3,2,1,0:T(8,128)S(1)}) custom-call(f32[4,18,2,8,128]{4,3,2,1,0:T(8,128)S(1)} %get-tuple-element.35.dense, ...), custom_call_target="tpu_custom_call" | custom-call | tf_op jit(solution)/shard_map/pallas_call | solution.py:755
  22.0 0.6 copy-done.5
  22.6 0.7 %copy-done.7 = bf16[1296]{0:T(1024)(128)(2,1)S(1)} copy-done((bf16[1296]{0:T(1024)(128)(2,1)S(1)}, bf16[1296]{0:T(1024)(128)(2,1)}, u32[]{:S(2)}) %copy-start.7) | copy-done | bytes 2616
  23.3 0.9 %shard_map.122 = bf16[16,64,128]{2,1,0:T(8,128)(2,1)} custom-call(s32[1]{0:T(128)} %bitcast.core_ref, bf16[70,512]{1,0:T(8,128)(2,1)S(1)} %collective-permute-done.up_ref, bf16[70,512]{1,0:T(8,128)(2,1)S(1)} %collective-permute-done.1.down_ref, f32[12,4,128]{2,1,0:T(4,128)S(1)} %get-tuple-element.50.slab, bf16[216]{0:T(256)(128)(2,1)S(1)} %copy-done.9, ...), custom_call_target="tpu_custom_call" | custom-call | tf_op jit(solution)/shard_map/pallas_call | solution.py:764
  24.2 3.8 %all-to-all-start = ((bf16[16,64,128]{2,1,0:T(8,128)(2,1)}), bf16[16,64,128]{2,1,0:T(8,128)(2,1)S(1)}, u32[]{:S(2)}, u32[]{:S(2)}) async-start(bf16[16,64,128]{2,1,0:T(8,128)(2,1)} %shard_map.122), calls=%async_computation | async-start | bytes 524288 | tf_op jit(solution)/shard_map/all_to_all | solution.py:770
  28.4 4.0 %collective-permute-start.3 = (bf16[4,16,512]{2,1,0:T(8,128)(2,1)S(1)}, bf16[4,16,512]{2,1,0:T(8,128)(2,1)S(1)}, u32[]{:S(2)}, u32[]{:S(2)}) collective-permute-start(bf16[4,16,512]{2,1,0:T(8,128)(2,1)S(1)} %copy-done.6), channel_id=1, source_target_pairs={{0,15},{1,0},{2,1},{3,2},{4,3},{5,4},{6,5},{7,6},{8,7},{9,8},{10,9... | collective-permute-start | bytes 196616 | tf_op jit(solution)/shard_map/ppermute | solution.py:734
  32.4 4.7 %collective-permute-start.5 = (bf16[3,8,512]{2,1,0:T(8,128)(2,1)S(1)}, bf16[3,8,512]{2,1,0:T(8,128)(2,1)S(1)}, u32[]{:S(2)}, u32[]{:S(2)}) collective-permute-start(bf16[3,8,512]{2,1,0:T(8,128)(2,1)S(1)} %get-tuple-element.49.after_ref), channel_id=1, source_target_pairs={{0,14},{1,15},{2,0},{3,1},{4,2},{5,3},{6,4},{7,5},{8,6},{9,7},{10,... | collective-permute-start | bytes 73736 | tf_op jit(solution)/shard_map/ppermute | solution.py:734
  37.2 1.3 %all-to-all-done.gathered_ref = bf16[16,64,128]{2,1,0:T(8,128)(2,1)S(1)} async-done(((bf16[16,64,128]{2,1,0:T(8,128)(2,1)}), bf16[16,64,128]{2,1,0:T(8,128)(2,1)S(1)}, u32[]{:S(2)}, u32[]{:S(2)}) %all-to-all-start) | async-done | bytes 262176 | tf_op jit(solution)/shard_map/all_to_all | solution.py:770
  38.4 1.3 %shard_map.123 = (f32[2,4,128]{2,1,0:T(4,128)S(1)}, bf16[48,72]{1,0:T(8,128)(2,1)S(1)}, bf16[48,432]{1,0:T(8,128)(2,1)S(1)}, bf16[48,432]{1,0:T(8,128)(2,1)S(1)}...) custom-call(bf16[16,64,128]{2,1,0:T(8,128)(2,1)S(1)} %all-to-all-don, ...), custom_call_target="tpu_custom_call" | custom-call | tf_op jit(solution)/shard_map/pallas_call | solution.py:782
  39.8 9.1 %shard_map.124 = (f32[4,8,512]{2,1,0:T(8,128)S(1)}, bf16[16,27,128]{2,1,0:T(8,128)(2,1)}) custom-call(bf16[4,16,512]{2,1,0:T(8,128)(2,1)S(1)} %copy-done.6, bf16[4,16,512]{2,1,0:T(8,128)(2,1)S(1)} %collective-permute-done.2.below_ref, bf16[4,16,512]{2,1,0:T(8,128)(2,1)S(1)} %collective-permute-done.3.above_ref, ...), custom_call_target="tpu_custom_call" | custom-call | tf_op jit(solution)/shard_map/pallas_call | solution.py:796
  48.8 5.3 %all-to-all-start.1 = ((bf16[16,27,128]{2,1,0:T(8,128)(2,1)}), bf16[16,27,128]{2,1,0:T(8,128)(2,1)S(1)}, u32[]{:S(2)}, u32[]{:S(2)}) async-start(bf16[16,27,128]{2,1,0:T(8,128)(2,1)} %get-tuple-element.60), calls=%async_computation.1 | async-start | bytes 262144 | tf_op jit(solution)/shard_map/all_to_all | solution.py:813
  54.1 1.0 %shard_map.125 = f32[4,2,3,3,1,4,512]{6,5,4,3,2,1,0:T(4,128)} custom-call(f32[4,18,2,8,128]{4,3,2,1,0:T(8,128)S(1)} %get-tuple-element.35.dense, f32[4,18,2,8,128]{4,3,2,1,0:T(8,128)S(1)} %get-tuple-element.45.w1_ref, f32[4,18,2,8,128]{4,3,2,1,0:T(8,128)S(1)} %get-tuple-element.46.w2_ref, f32[4,8,512]{2,1,0:T(8,128)S(1)} %get-tuple-element.59.coeff_ref), custom_call_target="tpu_custom_call" | custom-call | tf_op jit(solution)/shard_map/pallas_call | solution.py:814
  55.1 6.9 %all-to-all-done.1.parts_ref = bf16[16,27,128]{2,1,0:T(8,128)(2,1)S(1)} async-done(((bf16[16,27,128]{2,1,0:T(8,128)(2,1)}), bf16[16,27,128]{2,1,0:T(8,128)(2,1)S(1)}, u32[]{:S(2)}, u32[]{:S(2)}) %all-to-all-start.1) | async-done | bytes 110624 | tf_op jit(solution)/shard_map/all_to_all | solution.py:813
  62.1 0.8 %shard_map.126 = (f32[1,216]{1,0:T(1,128)}, f32[1,1296]{1,0:T(1,128)}, f32[1,1296]{1,0:T(1,128)}, f32[1,108]{1,0:T(1,128)}) custom-call(bf16[16,27,128]{2,1,0:T(8,128)(2,1)S(1)} %all-to-all-done.1.parts_ref), custom_call_target="tpu_custom_call" | custom-call | tf_op jit(solution)/shard_map/pallas_call | solution.py:817
  (28 shorter events, 0.5 us)
Async XLA Ops:
  0.6 1.1 %copy-start = (f32[4,2,3,3,1,4,512]{6,5,4,3,2,1,0:T(4,128)S(1)}, f32[4,2,3,3,1,4,512]{6,5,4,3,2,1,0:T(4,128)}, u32[]{:S(2)}) copy-start(f32[4,2,3,3,1,4,512]{6,5,4,3,2,1,0:T(4,128)} %links_ref.1) | copy-start | bytes 1769476
  1.7 8.0 %copy-start.11 = (bf16[4,2,3,3,1,4,512]{6,5,4,3,2,1,0:T(4,128)(2,1)S(1)}, bf16[4,2,3,3,1,4,512]{6,5,4,3,2,1,0:T(4,128)(2,1)}, u32[]{:S(2)}) copy-start(bf16[4,2,3,3,1,4,512]{6,5,4,3,2,1,0:T(4,128)(2,1)} %cot_ref.1) | copy-start | bytes 884740
  4.2 12.4 %collective-permute-start = (bf16[70,512]{1,0:T(8,128)(2,1)S(1)}, bf16[70,512]{1,0:T(8,128)(2,1)S(1)}, u32[]{:S(2)}, u32[]{:S(2)}) collective-permute-start(bf16[70,512]{1,0:T(8,128)(2,1)S(1)} %get-tuple-element.38), channel_id=1, source_target_pairs={{0,1},{1,2},{2,3},{3,4},{4,5},{5,6},{6,7},{7,8},{8,9},{9,10},{10,1... | collective-permute-start | bytes 215048 | tf_op jit(solution)/shard_map/ppermute | solution.py:734
  4.7 11.9 %collective-permute-start.1 = (bf16[70,512]{1,0:T(8,128)(2,1)S(1)}, bf16[70,512]{1,0:T(8,128)(2,1)S(1)}, u32[]{:S(2)}, u32[]{:S(2)}) collective-permute-start(bf16[70,512]{1,0:T(8,128)(2,1)S(1)} %get-tuple-element.39), channel_id=1, source_target_pairs={{0,15},{1,0},{2,1},{3,2},{4,3},{5,4},{6,5},{7,6},{8,7},{9,8},{10,9... | collective-permute-start | bytes 215048 | tf_op jit(solution)/shard_map/ppermute | solution.py:734
  9.7 0.7 %copy-start.12 = (s32[1,4]{1,0:T(1,128)S(1)}, s32[1,4]{1,0:T(1,128)}, u32[]{:S(2)}) copy-start(s32[1,4]{1,0:T(1,128)} %parity_ref.1) | copy-start | bytes 52
  9.7 0.7 %copy-start.13 = (s32[1,4]{1,0:T(1,128)S(1)}, s32[1,4]{1,0:T(1,128)}, u32[]{:S(2)}) copy-start(s32[1,4]{1,0:T(1,128)} %subset_ref.1) | copy-start | bytes 52
  15.2 0.7 %copy-start.1 = (f32[4,9,2,8,128]{4,3,2,1,0:T(8,128)}, f32[4,9,2,8,128]{4,3,2,1,0:T(8,128)S(1)}, u32[]{:S(2)}) copy-start(f32[4,9,2,8,128]{4,3,2,1,0:T(8,128)S(1)} %get-tuple-element.43.forces_ref) | copy-start | bytes 884740
  15.9 0.6 %copy-start.3 = (f32[4,4,16,128]{3,2,1,0:T(8,128)}, f32[4,4,16,128]{3,2,1,0:T(8,128)S(1)}, u32[]{:S(2)}) copy-start(f32[4,4,16,128]{3,2,1,0:T(8,128)S(1)} %get-tuple-element.42.rows_ref) | copy-start | bytes 393220
  16.6 1.0 %copy-start.2 = (f32[4,9,2,8,128]{4,3,2,1,0:T(8,128)S(1)}, f32[4,9,2,8,128]{4,3,2,1,0:T(8,128)}, u32[]{:S(2)}) copy-start(f32[4,9,2,8,128]{4,3,2,1,0:T(8,128)} %copy-done.1) | copy-start | bytes 884740
  17.5 0.9 %copy-start.4 = (f32[4,4,16,128]{3,2,1,0:T(8,128)S(1)}, f32[4,4,16,128]{3,2,1,0:T(8,128)}, u32[]{:S(2)}) copy-start(f32[4,4,16,128]{3,2,1,0:T(8,128)} %copy-done.3) | copy-start | bytes 393220
  18.4 4.1 %copy-start.8 = (bf16[1296]{0:T(1024)(128)(2,1)S(1)}, bf16[1296]{0:T(1024)(128)(2,1)}, u32[]{:S(2)}) copy-start(bf16[1296]{0:T(1024)(128)(2,1)} %w3_ref.1) | copy-start | bytes 7780
  22.0 0.6 copy-start.5
  22.6 0.7 %copy-start.7 = (bf16[1296]{0:T(1024)(128)(2,1)S(1)}, bf16[1296]{0:T(1024)(128)(2,1)}, u32[]{:S(2)}) copy-start(bf16[1296]{0:T(1024)(128)(2,1)} %w2_ref.1) | copy-start | bytes 7780
  22.6 0.7 %copy-start.9 = (bf16[216]{0:T(256)(128)(2,1)S(1)}, bf16[216]{0:T(256)(128)(2,1)}, u32[]{:S(2)}) copy-start(bf16[216]{0:T(256)(128)(2,1)} %w1_ref.1) | copy-start | bytes 1300
  22.6 0.7 %copy-start.10 = (bf16[108]{0:T(256)(128)(2,1)S(1)}, bf16[108]{0:T(256)(128)(2,1)}, u32[]{:S(2)}) copy-start(bf16[108]{0:T(256)(128)(2,1)} %w4_ref.1) | copy-start | bytes 652
  24.2 3.8 %copy-start.6 = (bf16[4,16,512]{2,1,0:T(8,128)(2,1)S(1)}, bf16[4,16,512]{2,1,0:T(8,128)(2,1)}, u32[]{:S(2)}) copy-start(bf16[4,16,512]{2,1,0:T(8,128)(2,1)} %copy-done.5) | copy-start | bytes 196612
  24.2 14.3 %all-to-all-start = ((bf16[16,64,128]{2,1,0:T(8,128)(2,1)}), bf16[16,64,128]{2,1,0:T(8,128)(2,1)S(1)}, u32[]{:S(2)}, u32[]{:S(2)}) async-start(bf16[16,64,128]{2,1,0:T(8,128)(2,1)} %shard_map.122), calls=%async_computation | async-start | bytes 524288 | tf_op jit(solution)/shard_map/all_to_all | solution.py:770
  27.9 11.8 %collective-permute-start.2 = (bf16[4,16,512]{2,1,0:T(8,128)(2,1)S(1)}, bf16[4,16,512]{2,1,0:T(8,128)(2,1)S(1)}, u32[]{:S(2)}, u32[]{:S(2)}) collective-permute-start(bf16[4,16,512]{2,1,0:T(8,128)(2,1)S(1)} %copy-done.6), channel_id=1, source_target_pairs={{0,1},{1,2},{2,3},{3,4},{4,5},{5,6},{6,7},{7,8},{8,9},{9,10},{10,1... | collective-permute-start | bytes 196616 | tf_op jit(solution)/shard_map/ppermute | solution.py:734
  28.4 11.4 %collective-permute-start.3 = (bf16[4,16,512]{2,1,0:T(8,128)(2,1)S(1)}, bf16[4,16,512]{2,1,0:T(8,128)(2,1)S(1)}, u32[]{:S(2)}, u32[]{:S(2)}) collective-permute-start(bf16[4,16,512]{2,1,0:T(8,128)(2,1)S(1)} %copy-done.6), channel_id=1, source_target_pairs={{0,15},{1,0},{2,1},{3,2},{4,3},{5,4},{6,5},{7,6},{8,7},{9,8},{10,9... | collective-permute-start | bytes 196616 | tf_op jit(solution)/shard_map/ppermute | solution.py:734
  32.4 7.3 %collective-permute-start.4 = (bf16[3,8,512]{2,1,0:T(8,128)(2,1)S(1)}, bf16[3,8,512]{2,1,0:T(8,128)(2,1)S(1)}, u32[]{:S(2)}, u32[]{:S(2)}) collective-permute-start(bf16[3,8,512]{2,1,0:T(8,128)(2,1)S(1)} %get-tuple-element.48), channel_id=1, source_target_pairs={{0,2},{1,3},{2,4},{3,5},{4,6},{5,7},{6,8},{7,9},{8,10},{9,11},{10,... | collective-permute-start | bytes 73736 | tf_op jit(solution)/shard_map/ppermute | solution.py:734
  32.4 7.3 %collective-permute-start.5 = (bf16[3,8,512]{2,1,0:T(8,128)(2,1)S(1)}, bf16[3,8,512]{2,1,0:T(8,128)(2,1)S(1)}, u32[]{:S(2)}, u32[]{:S(2)}) collective-permute-start(bf16[3,8,512]{2,1,0:T(8,128)(2,1)S(1)} %get-tuple-element.49.after_ref), channel_id=1, source_target_pairs={{0,14},{1,15},{2,0},{3,1},{4,2},{5,3},{6,4},{7,5},{8,6},{9,7},{10,... | collective-permute-start | bytes 73736 | tf_op jit(solution)/shard_map/ppermute | solution.py:734
  48.8 13.2 %all-to-all-start.1 = ((bf16[16,27,128]{2,1,0:T(8,128)(2,1)}), bf16[16,27,128]{2,1,0:T(8,128)(2,1)S(1)}, u32[]{:S(2)}, u32[]{:S(2)}) async-start(bf16[16,27,128]{2,1,0:T(8,128)(2,1)} %get-tuple-element.60), calls=%async_computation.1 | async-start | bytes 262144 | tf_op jit(solution)/shard_map/all_to_all | solution.py:813

commit v9 on v7

--- a/solution.py
+++ b/solution.py
@@ -16,6 +16,10 @@
 PAIRS = ((0, 1), (0, 2), (0, 3), (1, 2), (1, 3), (2, 3))
 SWAP = (0, 2, 1, 4, 3, 6, 5, 8, 7)
 ENTRIES = tuple((c, i, j) for c in range(2) for i in range(3) for j in range(3))
+EDGE = 4
+STAPLE = 7
+PLANE = 180
+GATE = 186
 SLABROWS = 24
 BLOCKROWS = 64
 LIMIT = 8 * 1024 * 1024
@@ -206,7 +210,7 @@
     lax.fori_loop(0, 4, body, 0)
 
 
-def face_kernel(links_ref, up_ref, down_ref, dense, edges, staples, slab, moved, rows):
+def face_kernel(links_ref, up_ref, down_ref, dense, slab, moved, rows):
     pack_links(links_ref, dense)
 
     def shift_body(e, carry):
@@ -227,12 +231,12 @@
         edge = mat_mul(u_mu, load_matrix(lambda e: moved[mu, e, c]))
 
         def write_edge(e, value):
-            edges[mu, e, c] = value
+            dense[EDGE + mu, e, c] = value
 
         store_matrix(edge, write_edge)
 
         def write(e, value):
-            staples[mu, e, c] = value
+            dense[STAPLE + mu, e, c] = value
             rows[16 + mu * 18 + e, pl.ds(c, 1)] = value[3:4]
             rows[16 + mu * 18 + e, pl.ds(2 + c, 1)] = value[7:8]
 
@@ -277,7 +281,7 @@
 
 
 def block_kernel(
-    widths, core_ref, up_ref, down_ref, slab, w1_ref, w2_ref, w3_ref, w4_ref, rows_ref, block_ref, other, block
+    widths, core_ref, up_ref, down_ref, slab, w1_ref, w2_ref, w3_ref, w4_ref, after_ref, block_ref, other, block
 ):
     even = core_ref[0] == 0
     up = up_ref[0:16].astype(F32)
@@ -312,12 +316,28 @@
         rows[t, 2 + c, pl.ds(channel, 1), :] = value[4 + t:5 + t]
 
 
-def space_kernel(
-    parity_ref, subset_ref, dense, cot_ref, time_staples, cots, rows, forces, sums, gates, moved, staples
-):
-    pack_links(cot_ref, cots)
-    rows[...] = jnp.zeros_like(rows)
-    forces[...] = jnp.zeros_like(forces)
+def sum_at(mu, e, c):
+    return (mu * 18 + e) * 2 + c
+
+
+def force_at(mu, e, c):
+    return 108 + (mu * 9 + e) * 2 + c
+
+
+def cot_at(mu, e, c):
+    return 190 + (mu * 18 + e) * 2 + c
+
+
+def space_kernel(parity_ref, subset_ref, dense, cot_ref, state, moved, staples):
+    def cot_body(mu, carry):
+        for e, (part, i, j) in enumerate(ENTRIES):
+            low, high = pack_pair(cot_ref[mu, part, i, j, 0].astype(F32))
+            state[cot_at(mu, e, 0)] = low
+            state[cot_at(mu, e, 1)] = high
+        return carry
+
+    lax.fori_loop(0, 4, cot_body, 0)
+    state[108:180] = jnp.zeros((72, 8, LANES), F32)
     steps = row_iota() % 4
     lanes = lane_iota(8)
     colour = (lanes // 64 + lanes // 8 % 8 + lanes % 8 + steps) % 2
@@ -328,7 +348,7 @@
         subset = jnp.where(steps == t, subset_ref[0, t], subset)
     for mu in range(4):
         active = jnp.logical_and(colour == parity, jnp.right_shift(subset, mu) % 2 == 1)
-        gates[mu] = jnp.where(active, 1.0, 0.0)
+        state[GATE + mu] = jnp.where(active, 1.0, 0.0)
 
     def shift_body(e, carry):
         for nu in range(3):
@@ -352,10 +372,10 @@
         one = mat_mul(u_mu, load_matrix(lambda e: moved[mu, nu, e, c]))
         two = mat_mul(u_nu, load_matrix(lambda e: moved[nu, mu, e, c]))
         loop = mat_mul(one, dagger(two))
-        put_row(rows, jnp.where(plane == 2, 3, plane), c, (loop[0][0][0] + loop[0][1][1] + loop[0][2][2]) / 3.0)
+        state[PLANE + step] = (loop[0][0][0] + loop[0][1][1] + loop[0][2][2]) / 3.0
         for e, part in enumerate(anti_parts(loop)):
-            forces[mu, e, c] += part
-            forces[nu, e, c] -= part
+            state[force_at(mu, e, c)] += part
+            state[force_at(nu, e, c)] -= part
 
         def write_mu(e, value):
             staples[mu, nu, e, c] = value
@@ -371,28 +391,34 @@
 
     def lower_body(e, carry):
         for mu in range(3):
-            acc = [jnp.where(steps == 0, 0.0, pltpu.roll(time_staples[mu, e, c], 1, 0)) for c in range(2)]
+            acc = [jnp.where(steps == 0, 0.0, pltpu.roll(dense[STAPLE + mu, e, c], 1, 0)) for c in range(2)]
             for nu in range(3):
                 if nu != mu:
                     pair = dense_shift([staples[mu, nu, e, 0], staples[mu, nu, e, 1]], nu, -1)
                     acc = [acc[c] + pair[c] for c in range(2)]
-            sums[mu, e, 0] = acc[0]
-            sums[mu, e, 1] = acc[1]
+            state[sum_at(mu, e, 0)] = acc[0]
+            state[sum_at(mu, e, 1)] = acc[1]
         return carry
 
     lax.fori_loop(0, 18, lower_body, 0)
 
 
 def time_kernel(
-    dense, cots, up_ref, down_ref, gates, edges, rows_ref, forces_ref, sums_ref,
+    dense, state, up_ref, down_ref,
     fm_ref, fup_ref, fdown_ref, w1_ref, w2_ref,
     moved, staples, sums, halo_up, halo_down, forces, rows,
 ):
     for q in range(4):
         halo_up[:, q, :] = up_ref[:, q * 128:q * 128 + 128].astype(F32)
         halo_down[:, q, :] = down_ref[:, q * 128:q * 128 + 128].astype(F32)
-    rows[...] = rows_ref[...]
-    forces[...] = forces_ref[...]
+    rows[...] = jnp.zeros_like(rows)
+    for channel, plane in ((0, 0), (1, 1), (3, 2)):
+        for c in range(2):
+            put_row(rows, channel, c, state[PLANE + 2 * plane + c])
+    for mu in range(4):
+        for e in range(9):
+            for c in range(2):
+                forces[mu, e, c] = state[force_at(mu, e, c)]
     steps = row_iota() % 4
 
     def shift_body(e, carry):
@@ -401,7 +427,7 @@
             below = halo_pair(halo_up, 16 + nu * 18 + e)
             for c in range(2):
                 moved[nu, e, c] = jnp.where(steps == 3, halo[c], pltpu.roll(dense[nu, e, c], 7, 0))
-                sums[nu, e, c] = sums_ref[nu, e, c] + jnp.where(steps == 0, below[c], 0.0)
+                sums[nu, e, c] = state[sum_at(nu, e, c)] + jnp.where(steps == 0, below[c], 0.0)
         return carry
 
     lax.fori_loop(0, 18, shift_body, 0)
@@ -409,7 +435,7 @@
     def plane_body(step, carry):
         mu = step // 2
         c = step % 2
-        one = load_matrix(lambda e: edges[mu, e, c])
+        one = load_matrix(lambda e: dense[EDGE + mu, e, c])
         two = mat_mul(load_matrix(lambda e: dense[3, e, c]), load_matrix(lambda e: moved[mu, e, c]))
         loop = mat_mul(one, dagger(two))
         put_row(rows, jnp.where(mu == 0, 2, mu + 3), c, (loop[0][0][0] + loop[0][1][1] + loop[0][2][2]) / 3.0)
@@ -447,11 +473,11 @@
         parts = [part * (1.0 / 12.0) for part in parts]
         applied = anti_mul(parts, current)
         twice = anti_mul(parts, applied)
-        gate = gates[mu]
+        gate = state[GATE + mu]
         slope = jnp.zeros_like(gate)
         curve = jnp.zeros_like(gate)
         for e, (part, i, j) in enumerate(ENTRIES):
-            weight = cots[mu, e, c]
+            weight = state[cot_at(mu, e, c)]
             slope = slope + weight * applied[part][i][j]
             curve = curve + weight * twice[part][i][j]
             w1_ref[mu, e, c] = gate * applied[part][i][j]
@@ -734,31 +760,31 @@
         return lax.ppermute(value, "tm", [(i, (i + distance) % count) for i in range(count)])
 
     widths = (768 // count, 768 // count, 128 // count, 64 // count)
+    vmem, smem = pltpu.VMEM, pltpu.SMEM
     field = ((4, 18, 2, 8, LANES), F32)
     space = ((3, 18, 2, 8, LANES), F32)
     edge_rows = ((70, SITES), BF16)
-    vmem, smem = pltpu.VMEM, pltpu.SMEM
-    up, down, dense, edges, staples, slab = call(
+    up, down, dense, slab = call(
         face_kernel,
-        [edge_rows, edge_rows, field, space, space, ((12, 4, LANES), F32)],
+        [edge_rows, edge_rows, ((10, 18, 2, 8, LANES), F32), ((12, 4, LANES), F32)],
         [space, ((70, 4, LANES), F32)],
     )(links)
     up = send(up, 1)
     down = send(down, -1)
-    cots, rows, forces, sums, gates = call(
+    (state,) = call(
         space_kernel,
-        [field, ((4, 4, 16, LANES), F32), ((4, 9, 2, 8, LANES), F32), space, ((4, 8, LANES), F32)],
+        [((334, 8, LANES), F32)],
         [((3, 3, 18, 2, 8, LANES), F32), ((3, 3, 18, 2, 8, LANES), F32)],
-        places=(smem, smem, vmem, vmem, vmem),
+        places=(smem, smem, vmem, vmem),
         cost=pl.CostEstimate(flops=4_000_000_000, bytes_accessed=16_000_000, transcendentals=0),
-    )(parity, link_subset, dense, cotangent, staples)
+    )(parity, link_subset, dense, cotangent)
     core = (lax.axis_index("tm") % 2).astype(jnp.int32)[None]
     (block,) = call(
         functools.partial(block_kernel, widths),
         [((count, BLOCKROWS, LANES), BF16)],
         [((12, 4, LANES), F32), ((BLOCKROWS, LANES), F32)],
-        places=(smem,) + (vmem,) * 8,
-    )(core, up, down, slab, w_first, w_second, w_third, w_last, rows)
+        places=(smem,) + (vmem,) * 7 + (pl.ANY,),
+    )(core, up, down, slab, w_first, w_second, w_third, w_last, state)
     gathered = lax.all_to_all(block, "tm", split_axis=0, concat_axis=0, tiled=True)
     fm, fup, fdown, applied, twice = call(
         time_kernel,
@@ -767,7 +793,7 @@
             space, space, field, ((70, 4, LANES), F32), ((70, 4, LANES), F32),
             ((4, 9, 2, 8, LANES), F32), ((4, 4, 16, LANES), F32),
         ],
-    )(dense, cots, up, down, gates, edges, rows, forces, sums)
+    )(dense, state, up, down)
     below = send(fm, 1)
     above = send(fm, -1)
     fbelow = send(fup, 2)

time: 65.1 us -> 62 us (0.952)
  waiting for transfers between devices: 7.69 us -> 5.35 us
    all_to_all x1, waiting for transfers between devices: 6.95 us -> 4.82 us  [on_device(): grads = lax.all_to_all(grads, 'tm', split_axis=0, concat_axis=0, tiled=True)]
    unnamed x32 -> x24, local copies, waits for them, and re-layouts: 7.29 us -> 7.13 us
where the time goes in v9:
time: 62 us; the launch traced here: 61.5 us
  starting transfers between devices  24.4 us (39%)
  Pallas kernels  23.8 us (38%)
  local copies, waits for them, and re-layouts  7.13 us (12%)
  waiting for transfers between devices  5.35 us (9%)
  between operations  0.78 us (1%)
    ppermute x6, starting transfers between devices, send(): lax.ppermute(value, 'tm', [(i, (i + distance) % count) for i in range(cou...  14.7 us
    pallas_call x1, Pallas kernels, on_device(): call(functools.partial(conv_kernel, count == 16), [((4, 8, SITES), F32),...  9.06 us
    unnamed x24, local copies, waits for them, and re-layouts  7.13 us
    all_to_all x1, starting transfers between devices, on_device(): grads = lax.all_to_all(grads, 'tm', split_axis=0, concat_axis=0, tiled=True)  6.09 us
    pallas_call x1, Pallas kernels, on_device(): call(space_kernel, [((334, 8, LANES), F32)], [((3, 3, 18, 2, 8, LANES), F...  4.83 us
    all_to_all x1, waiting for transfers between devices, on_device(): grads = lax.all_to_all(grads, 'tm', split_axis=0, concat_axis=0, tiled=True)  4.82 us
    all_to_all x1, starting transfers between devices, on_device(): lax.all_to_all(block, 'tm', split_axis=0, concat_axis=0, tiled=True)  3.62 us
    pallas_call x1, Pallas kernels, on_device(): call(time_kernel, [((4, 16, SITES), BF16), ((3, 8, SITES), BF16), ((3, 8,...  3.54 us
  transfers between devices with their start and end apart: 8, of which 2 were waited for; matrix products, arithmetic and copies ran while one was open for 0% of the time, Pallas kernels for 17%

profile of v9, /device:TPU:0, one launch (start us, length us, event | category | flops | bytes accessed | tf_op | source)
XLA Modules:
  0.0 61.5 jit_solution(670813385377779437)
XLA Ops:
  0.6 1.1 %copy-done.4 = f32[4,2,3,3,1,4,512]{6,5,4,3,2,1,0:T(4,128)S(1)} copy-done((f32[4,2,3,3,1,4,512]{6,5,4,3,2,1,0:T(4,128)S(1)}, f32[4,2,3,3,1,4,512]{6,5,4,3,2,1,0:T(4,128)}, u32[]{:S(2)}) %copy-start.4) | copy-done | bytes 589848
  1.7 2.5 %shard_map.119 = (bf16[70,512]{1,0:T(8,128)(2,1)S(1)}, bf16[70,512]{1,0:T(8,128)(2,1)S(1)}, f32[10,18,2,8,128]{4,3,2,1,0:T(8,128)S(1)}, f32[12,4,128]{2,1,0:T(4,128)S(1)}) custom-call(f32[4,2,3,3,1,4,512]{6,5,4,3,2,1,0:T(4,128)S(1)} %copy-done.4), custom_call_target="tpu_custom_call" | custom-call | tf_op jit(solution)/shard_map/pallas_call | solution.py:767
  4.2 0.5 collective-permute-start
  4.7 5.1 %collective-permute-start.1 = (bf16[70,512]{1,0:T(8,128)(2,1)S(1)}, bf16[70,512]{1,0:T(8,128)(2,1)S(1)}, u32[]{:S(2)}, u32[]{:S(2)}) collective-permute-start(bf16[70,512]{1,0:T(8,128)(2,1)S(1)} %get-tuple-element.30), channel_id=1, source_target_pairs={{0,15},{1,0},{2,1},{3,2},{4,3},{5,4},{6,5},{7,6},{8,7},{9,8},{10,9... | collective-permute-start | bytes 215048 | tf_op jit(solution)/shard_map/ppermute | solution.py:760
  9.7 1.0 %copy-done.9 = bf16[4,2,3,3,1,4,512]{6,5,4,3,2,1,0:T(4,128)(2,1)S(1)} copy-done((bf16[4,2,3,3,1,4,512]{6,5,4,3,2,1,0:T(4,128)(2,1)S(1)}, bf16[4,2,3,3,1,4,512]{6,5,4,3,2,1,0:T(4,128)(2,1)}, u32[]{:S(2)}) %copy-start.9) | copy-done | bytes 294936
  10.7 0.7 %copy-done.10 = s32[1,4]{1,0:T(1,128)S(1)} copy-done((s32[1,4]{1,0:T(1,128)S(1)}, s32[1,4]{1,0:T(1,128)}, u32[]{:S(2)}) %copy-start.10) | copy-done | bytes 40
  11.3 0.7 %copy-done.11 = s32[1,4]{1,0:T(1,128)S(1)} copy-done((s32[1,4]{1,0:T(1,128)S(1)}, s32[1,4]{1,0:T(1,128)}, u32[]{:S(2)}) %copy-start.11) | copy-done | bytes 40
  12.0 4.8 %shard_map.120.state.after_ref = f32[334,8,128]{2,1,0:T(8,128)S(1)} custom-call(s32[1,4]{1,0:T(1,128)S(1)} %copy-done.10, s32[1,4]{1,0:T(1,128)S(1)} %copy-done.11, f32[10,18,2,8,128]{4,3,2,1,0:T(8,128)S(1)} %get-tuple-element.28.dense, bf16[4,2,3,3,1,4,512]{6,5,4,3,2,1,0:T(4,128)(2,1)S(1)} %copy-done.9), custom_call_target="tpu_custom_call" | custom-call | flops 4000000000 | bytes 16000000 | tf_op jit(solution)/shard_map/pallas_call | solution.py:774
  16.9 0.9 %shard_map.122 = bf16[16,64,128]{2,1,0:T(8,128)(2,1)} custom-call(s32[1]{0:T(128)} %bitcast.core_ref, bf16[70,512]{1,0:T(8,128)(2,1)S(1)} %collective-permute-done.up_ref, bf16[70,512]{1,0:T(8,128)(2,1)S(1)} %collective-permute-done.1.down_ref, f32[12,4,128]{2,1,0:T(4,128)S(1)} %get-tuple-element.36.slab, bf16[216]{0:T(256)(128)(2,1)S(1)} %copy-done.7, ...), custom_call_target="tpu_custom_call" | custom-call | tf_op jit(solution)/shard_map/pallas_call | solution.py:782
  17.8 3.6 %all-to-all-start = ((bf16[16,64,128]{2,1,0:T(8,128)(2,1)}), bf16[16,64,128]{2,1,0:T(8,128)(2,1)S(1)}, u32[]{:S(2)}, u32[]{:S(2)}) async-start(bf16[16,64,128]{2,1,0:T(8,128)(2,1)} %shard_map.122), calls=%async_computation | async-start | bytes 524288 | tf_op jit(solution)/shard_map/all_to_all | solution.py:788
  21.4 3.5 %shard_map.121 = (bf16[4,16,512]{2,1,0:T(8,128)(2,1)S(1)}, bf16[3,8,512]{2,1,0:T(8,128)(2,1)S(1)}, bf16[3,8,512]{2,1,0:T(8,128)(2,1)S(1)}, f32[4,18,2,8,128]{4,3,2,1,0:T(8,128)S(1)}, f32[4,18,2,8,128]{4,3,2,1,0:T(8,128)S(1)}) custom-call(f32[10,18,2,8,128]{4,3,2,1,0:T(8,128)S(1)} %get-tuple-element.28.dense, f32[334,8,128]{2,1,0:T(8,128)S(1)} %shard_map.120.state.after_ref, ...), custom_call_target="tpu_custom_call" | custom-call | tf_op jit(solution)/shard_map/pallas_call | solution.py:789
  25.0 0.8 %copy-done = f32[4,18,2,8,128]{4,3,2,1,0:T(8,128)} copy-done((f32[4,18,2,8,128]{4,3,2,1,0:T(8,128)}, f32[4,18,2,8,128]{4,3,2,1,0:T(8,128)S(1)}, u32[]{:S(2)}) %copy-start) | copy-done | bytes 589848
  25.8 0.9 %copy-done.2 = f32[4,18,2,8,128]{4,3,2,1,0:T(8,128)} copy-done((f32[4,18,2,8,128]{4,3,2,1,0:T(8,128)}, f32[4,18,2,8,128]{4,3,2,1,0:T(8,128)S(1)}, u32[]{:S(2)}) %copy-start.2) | copy-done | bytes 589848
  27.1 4.0 %collective-permute-start.3 = (bf16[4,16,512]{2,1,0:T(8,128)(2,1)S(1)}, bf16[4,16,512]{2,1,0:T(8,128)(2,1)S(1)}, u32[]{:S(2)}, u32[]{:S(2)}) collective-permute-start(bf16[4,16,512]{2,1,0:T(8,128)(2,1)S(1)} %get-tuple-element.33.fm_ref), channel_id=1, source_target_pairs={{0,15},{1,0},{2,1},{3,2},{4,3},{5,4},{6,5},{7,6},{8,7},{9,8},{10,9... | collective-permute-start | bytes 196616 | tf_op jit(solution)/shard_map/ppermute | solution.py:760
  31.1 4.7 %collective-permute-start.5 = (bf16[3,8,512]{2,1,0:T(8,128)(2,1)S(1)}, bf16[3,8,512]{2,1,0:T(8,128)(2,1)S(1)}, u32[]{:S(2)}, u32[]{:S(2)}) collective-permute-start(bf16[3,8,512]{2,1,0:T(8,128)(2,1)S(1)} %get-tuple-element.35), channel_id=1, source_target_pairs={{0,14},{1,15},{2,0},{3,1},{4,2},{5,3},{6,4},{7,5},{8,6},{9,7},{10,... | collective-permute-start | bytes 73736 | tf_op jit(solution)/shard_map/ppermute | solution.py:760
  35.8 1.3 %shard_map.123 = (f32[2,4,128]{2,1,0:T(4,128)S(1)}, bf16[48,72]{1,0:T(8,128)(2,1)S(1)}, bf16[48,432]{1,0:T(8,128)(2,1)S(1)}, bf16[48,432]{1,0:T(8,128)(2,1)S(1)}...) custom-call(bf16[16,64,128]{2,1,0:T(8,128)(2,1)S(1)} %all-to-all-don, ...), custom_call_target="tpu_custom_call" | custom-call | tf_op jit(solution)/shard_map/pallas_call | solution.py:808
  37.1 0.5 collective-permute-done.4.fbelow_ref
  37.6 9.1 %shard_map.124 = (f32[4,8,512]{2,1,0:T(8,128)S(1)}, bf16[16,27,128]{2,1,0:T(8,128)(2,1)}) custom-call(bf16[4,16,512]{2,1,0:T(8,128)(2,1)S(1)} %get-tuple-element.33.fm_ref, bf16[4,16,512]{2,1,0:T(8,128)(2,1)S(1)} %collective-permute-done.2.below_ref, bf16[4,16,512]{2,1,0:T(8,128)(2,1)S(1)} %collective-permute-done.3.above_ref, ...), custom_call_target="tpu_custom_call" | custom-call | tf_op jit(solution)/shard_map/pallas_call | solution.py:822
  46.7 6.1 %all-to-all-start.1 = ((bf16[16,27,128]{2,1,0:T(8,128)(2,1)}), bf16[16,27,128]{2,1,0:T(8,128)(2,1)S(1)}, u32[]{:S(2)}, u32[]{:S(2)}) async-start(bf16[16,27,128]{2,1,0:T(8,128)(2,1)} %get-tuple-element.46), calls=%async_computation.1 | async-start | bytes 262144 | tf_op jit(solution)/shard_map/all_to_all | solution.py:839
  52.8 1.1 %copy-done.1 = f32[4,18,2,8,128]{4,3,2,1,0:T(8,128)S(1)} copy-done((f32[4,18,2,8,128]{4,3,2,1,0:T(8,128)S(1)}, f32[4,18,2,8,128]{4,3,2,1,0:T(8,128)}, u32[]{:S(2)}) %copy-start.1) | copy-done | bytes 589848
  53.9 1.1 %copy-done.3 = f32[4,18,2,8,128]{4,3,2,1,0:T(8,128)S(1)} copy-done((f32[4,18,2,8,128]{4,3,2,1,0:T(8,128)S(1)}, f32[4,18,2,8,128]{4,3,2,1,0:T(8,128)}, u32[]{:S(2)}) %copy-start.3) | copy-done | bytes 589848
  54.9 1.0 %shard_map.125 = f32[4,2,3,3,1,4,512]{6,5,4,3,2,1,0:T(4,128)} custom-call(f32[10,18,2,8,128]{4,3,2,1,0:T(8,128)S(1)} %get-tuple-element.28.dense, f32[4,18,2,8,128]{4,3,2,1,0:T(8,128)S(1)} %copy-done.1, f32[4,18,2,8,128]{4,3,2,1,0:T(8,128)S(1)} %copy-done.3, f32[4,8,512]{2,1,0:T(8,128)S(1)} %get-tuple-element.45.coeff_ref), custom_call_target="tpu_custom_call" | custom-call | tf_op jit(solution)/shard_map/pallas_call | solution.py:840
  55.9 4.8 %all-to-all-done.1.parts_ref = bf16[16,27,128]{2,1,0:T(8,128)(2,1)S(1)} async-done(((bf16[16,27,128]{2,1,0:T(8,128)(2,1)}), bf16[16,27,128]{2,1,0:T(8,128)(2,1)S(1)}, u32[]{:S(2)}, u32[]{:S(2)}) %all-to-all-start.1) | async-done | bytes 110624 | tf_op jit(solution)/shard_map/all_to_all | solution.py:839
  60.7 0.8 %shard_map.126 = (f32[1,216]{1,0:T(1,128)}, f32[1,1296]{1,0:T(1,128)}, f32[1,1296]{1,0:T(1,128)}, f32[1,108]{1,0:T(1,128)}) custom-call(bf16[16,27,128]{2,1,0:T(8,128)(2,1)S(1)} %all-to-all-done.1.parts_ref), custom_call_target="tpu_custom_call" | custom-call | tf_op jit(solution)/shard_map/pallas_call | solution.py:843
  (24 shorter events, 0.5 us)
Async XLA Ops:
  0.6 1.1 %copy-start.4 = (f32[4,2,3,3,1,4,512]{6,5,4,3,2,1,0:T(4,128)S(1)}, f32[4,2,3,3,1,4,512]{6,5,4,3,2,1,0:T(4,128)}, u32[]{:S(2)}) copy-start(f32[4,2,3,3,1,4,512]{6,5,4,3,2,1,0:T(4,128)} %links_ref.1) | copy-start | bytes 1769476
  4.2 12.7 %collective-permute-start = (bf16[70,512]{1,0:T(8,128)(2,1)S(1)}, bf16[70,512]{1,0:T(8,128)(2,1)S(1)}, u32[]{:S(2)}, u32[]{:S(2)}) collective-permute-start(bf16[70,512]{1,0:T(8,128)(2,1)S(1)} %get-tuple-element.29), channel_id=1, source_target_pairs={{0,1},{1,2},{2,3},{3,4},{4,5},{5,6},{6,7},{7,8},{8,9},{9,10},{10,1... | collective-permute-start | bytes 215048 | tf_op jit(solution)/shard_map/ppermute | solution.py:760
  4.7 12.2 %collective-permute-start.1 = (bf16[70,512]{1,0:T(8,128)(2,1)S(1)}, bf16[70,512]{1,0:T(8,128)(2,1)S(1)}, u32[]{:S(2)}, u32[]{:S(2)}) collective-permute-start(bf16[70,512]{1,0:T(8,128)(2,1)S(1)} %get-tuple-element.30), channel_id=1, source_target_pairs={{0,15},{1,0},{2,1},{3,2},{4,3},{5,4},{6,5},{7,6},{8,7},{9,8},{10,9... | collective-permute-start | bytes 215048 | tf_op jit(solution)/shard_map/ppermute | solution.py:760
  9.7 1.0 %copy-start.9 = (bf16[4,2,3,3,1,4,512]{6,5,4,3,2,1,0:T(4,128)(2,1)S(1)}, bf16[4,2,3,3,1,4,512]{6,5,4,3,2,1,0:T(4,128)(2,1)}, u32[]{:S(2)}) copy-start(bf16[4,2,3,3,1,4,512]{6,5,4,3,2,1,0:T(4,128)(2,1)} %cot_ref.1) | copy-start | bytes 884740
  10.7 0.7 %copy-start.10 = (s32[1,4]{1,0:T(1,128)S(1)}, s32[1,4]{1,0:T(1,128)}, u32[]{:S(2)}) copy-start(s32[1,4]{1,0:T(1,128)} %parity_ref.1) | copy-start | bytes 52
  11.3 0.7 %copy-start.11 = (s32[1,4]{1,0:T(1,128)S(1)}, s32[1,4]{1,0:T(1,128)}, u32[]{:S(2)}) copy-start(s32[1,4]{1,0:T(1,128)} %subset_ref.1) | copy-start | bytes 52
  12.0 4.9 %copy-start.5 = (bf16[1296]{0:T(1024)(128)(2,1)S(1)}, bf16[1296]{0:T(1024)(128)(2,1)}, u32[]{:S(2)}) copy-start(bf16[1296]{0:T(1024)(128)(2,1)} %w2_ref.1) | copy-start | bytes 7780
  12.0 4.9 %copy-start.6 = (bf16[1296]{0:T(1024)(128)(2,1)S(1)}, bf16[1296]{0:T(1024)(128)(2,1)}, u32[]{:S(2)}) copy-start(bf16[1296]{0:T(1024)(128)(2,1)} %w3_ref.1) | copy-start | bytes 7780
  12.0 4.9 %copy-start.7 = (bf16[216]{0:T(256)(128)(2,1)S(1)}, bf16[216]{0:T(256)(128)(2,1)}, u32[]{:S(2)}) copy-start(bf16[216]{0:T(256)(128)(2,1)} %w1_ref.1) | copy-start | bytes 1300
  12.0 4.9 %copy-start.8 = (bf16[108]{0:T(256)(128)(2,1)S(1)}, bf16[108]{0:T(256)(128)(2,1)}, u32[]{:S(2)}) copy-start(bf16[108]{0:T(256)(128)(2,1)} %w4_ref.1) | copy-start | bytes 652
  17.8 18.0 %all-to-all-start = ((bf16[16,64,128]{2,1,0:T(8,128)(2,1)}), bf16[16,64,128]{2,1,0:T(8,128)(2,1)S(1)}, u32[]{:S(2)}, u32[]{:S(2)}) async-start(bf16[16,64,128]{2,1,0:T(8,128)(2,1)} %shard_map.122), calls=%async_computation | async-start | bytes 524288 | tf_op jit(solution)/shard_map/all_to_all | solution.py:788
  25.0 0.8 %copy-start = (f32[4,18,2,8,128]{4,3,2,1,0:T(8,128)}, f32[4,18,2,8,128]{4,3,2,1,0:T(8,128)S(1)}, u32[]{:S(2)}) copy-start(f32[4,18,2,8,128]{4,3,2,1,0:T(8,128)S(1)} %get-tuple-element.31.w1_ref) | copy-start | bytes 1769476
  25.8 0.9 %copy-start.2 = (f32[4,18,2,8,128]{4,3,2,1,0:T(8,128)}, f32[4,18,2,8,128]{4,3,2,1,0:T(8,128)S(1)}, u32[]{:S(2)}) copy-start(f32[4,18,2,8,128]{4,3,2,1,0:T(8,128)S(1)} %get-tuple-element.32.w2_ref) | copy-start | bytes 1769476
  26.7 11.0 %collective-permute-start.2 = (bf16[4,16,512]{2,1,0:T(8,128)(2,1)S(1)}, bf16[4,16,512]{2,1,0:T(8,128)(2,1)S(1)}, u32[]{:S(2)}, u32[]{:S(2)}) collective-permute-start(bf16[4,16,512]{2,1,0:T(8,128)(2,1)S(1)} %get-tuple-element.33.fm_ref), channel_id=1, source_target_pairs={{0,1},{1,2},{2,3},{3,4},{4,5},{5,6},{6,7},{7,8},{8,9},{9,10},{10,1... | collective-permute-start | bytes 196616 | tf_op jit(solution)/shard_map/ppermute | solution.py:760
  27.1 10.6 %collective-permute-start.3 = (bf16[4,16,512]{2,1,0:T(8,128)(2,1)S(1)}, bf16[4,16,512]{2,1,0:T(8,128)(2,1)S(1)}, u32[]{:S(2)}, u32[]{:S(2)}) collective-permute-start(bf16[4,16,512]{2,1,0:T(8,128)(2,1)S(1)} %get-tuple-element.33.fm_ref), channel_id=1, source_target_pairs={{0,15},{1,0},{2,1},{3,2},{4,3},{5,4},{6,5},{7,6},{8,7},{9,8},{10,9... | collective-permute-start | bytes 196616 | tf_op jit(solution)/shard_map/ppermute | solution.py:760
  31.1 6.5 %collective-permute-start.4 = (bf16[3,8,512]{2,1,0:T(8,128)(2,1)S(1)}, bf16[3,8,512]{2,1,0:T(8,128)(2,1)S(1)}, u32[]{:S(2)}, u32[]{:S(2)}) collective-permute-start(bf16[3,8,512]{2,1,0:T(8,128)(2,1)S(1)} %get-tuple-element.34), channel_id=1, source_target_pairs={{0,2},{1,3},{2,4},{3,5},{4,6},{5,7},{6,8},{7,9},{8,10},{9,11},{10,... | collective-permute-start | bytes 73736 | tf_op jit(solution)/shard_map/ppermute | solution.py:760
  31.1 6.5 %collective-permute-start.5 = (bf16[3,8,512]{2,1,0:T(8,128)(2,1)S(1)}, bf16[3,8,512]{2,1,0:T(8,128)(2,1)S(1)}, u32[]{:S(2)}, u32[]{:S(2)}) collective-permute-start(bf16[3,8,512]{2,1,0:T(8,128)(2,1)S(1)} %get-tuple-element.35), channel_id=1, source_target_pairs={{0,14},{1,15},{2,0},{3,1},{4,2},{5,3},{6,4},{7,5},{8,6},{9,7},{10,... | collective-permute-start | bytes 73736 | tf_op jit(solution)/shard_map/ppermute | solution.py:760
  46.7 14.0 %all-to-all-start.1 = ((bf16[16,27,128]{2,1,0:T(8,128)(2,1)}), bf16[16,27,128]{2,1,0:T(8,128)(2,1)S(1)}, u32[]{:S(2)}, u32[]{:S(2)}) async-start(bf16[16,27,128]{2,1,0:T(8,128)(2,1)} %get-tuple-element.46), calls=%async_computation.1 | async-start | bytes 262144 | tf_op jit(solution)/shard_map/all_to_all | solution.py:839
  52.8 1.1 %copy-start.1 = (f32[4,18,2,8,128]{4,3,2,1,0:T(8,128)S(1)}, f32[4,18,2,8,128]{4,3,2,1,0:T(8,128)}, u32[]{:S(2)}) copy-start(f32[4,18,2,8,128]{4,3,2,1,0:T(8,128)} %copy-done) | copy-start | bytes 1769476
  53.9 1.1 %copy-start.3 = (f32[4,18,2,8,128]{4,3,2,1,0:T(8,128)S(1)}, f32[4,18,2,8,128]{4,3,2,1,0:T(8,128)}, u32[]{:S(2)}) copy-start(f32[4,18,2,8,128]{4,3,2,1,0:T(8,128)} %copy-done.2) | copy-start | bytes 1769476

commit v10 on v9

--- a/solution.py
+++ b/solution.py
@@ -328,7 +328,7 @@
     return 190 + (mu * 18 + e) * 2 + c
 
 
-def space_kernel(parity_ref, subset_ref, dense, cot_ref, state, moved, staples):
+def space_kernel(code_ref, dense, cot_ref, state, moved, staples):
     def cot_body(mu, carry):
         for e, (part, i, j) in enumerate(ENTRIES):
             low, high = pack_pair(cot_ref[mu, part, i, j, 0].astype(F32))
@@ -341,13 +341,11 @@
     steps = row_iota() % 4
     lanes = lane_iota(8)
     colour = (lanes // 64 + lanes // 8 % 8 + lanes % 8 + steps) % 2
-    parity = jnp.zeros_like(steps)
-    subset = jnp.zeros_like(steps)
+    code = jnp.zeros_like(steps)
     for t in range(4):
-        parity = jnp.where(steps == t, parity_ref[0, t], parity)
-        subset = jnp.where(steps == t, subset_ref[0, t], subset)
+        code = jnp.where(steps == t, code_ref[0, t], code)
     for mu in range(4):
-        active = jnp.logical_and(colour == parity, jnp.right_shift(subset, mu) % 2 == 1)
+        active = jnp.logical_and(colour == code % 2, jnp.right_shift(code, mu + 1) % 2 == 1)
         state[GATE + mu] = jnp.where(active, 1.0, 0.0)
 
     def shift_body(e, carry):
@@ -581,6 +579,23 @@
     return [jnp.where(low, rolled[(q + 3) % 4], rolled[q]) for q in range(4)]
 
 
+def all_shifts(chunks):
+    lanes = lane_iota(chunks[0].shape[0])
+    y = lanes // 8 % 8
+    z = lanes % 8
+    low = lanes < 64
+    half = [roll_lanes(chunk, 64) for chunk in chunks]
+    return [
+        chunks,
+        [jnp.where(low, half[q], half[(q + 1) % 4]) for q in range(4)],
+        [jnp.where(low, half[(q + 3) % 4], half[q]) for q in range(4)],
+        [roll_lanes(jnp.where(y == 0, half[q], chunks[q]), -8) for q in range(4)],
+        [roll_lanes(jnp.where(y == 7, half[q], chunks[q]), 8) for q in range(4)],
+        [roll_lanes(jnp.where(z == 0, roll_lanes(chunk, 8), chunk), -1) for chunk in chunks],
+        [roll_lanes(jnp.where(z == 7, roll_lanes(chunk, -8), chunk), 1) for chunk in chunks],
+    ]
+
+
 def span(slice_index, count=1):
     if isinstance(slice_index, int):
         return slice(slice_index * SITES, (slice_index + count) * SITES)
@@ -593,8 +608,7 @@
 
 def stack_wide(source, target, index, slot):
     chunks = chunks_of(source[:, span(index)])
-    for position in range(7):
-        shifted = one_shift(chunks, position)
+    for position, shifted in enumerate(all_shifts(chunks)):
         for q in range(4):
             lanes = slice(slot * SITES + q * 128, slot * SITES + q * 128 + 128)
             target[H * position:H * position + H, lanes] = shifted[q]
@@ -606,7 +620,7 @@
     chunks = chunks_of(source[:, span(index)])
     ahead = chunks_of(source[:, span(index + 1)])
     behind = chunks_of(source[:, span(index - 1)])
-    columns = [one_shift(chunks, position) for position in range(7)] + [ahead, behind]
+    columns = all_shifts(chunks) + [ahead, behind]
     for q in range(4):
         lanes = slice(slot * SITES + q * 128, slot * SITES + q * 128 + 128)
         target[0:72, lanes] = jnp.concatenate([column[q] for column in columns], axis=0).astype(BF16)
@@ -708,7 +722,7 @@
         grads_ref[...] = packed[...].astype(BF16)
 
 
-def update_kernel(dense, w1_ref, w2_ref, coeff_ref, out_ref, factors):
+def update_kernel(links_ref, w1_ref, w2_ref, coeff_ref, out_ref, factors):
     for mu in range(4):
         for t in range(4):
             for c in range(2):
@@ -719,7 +733,8 @@
         factor = [factors[mu, c] for c in range(2)]
         half = [0.5 * value * value for value in factor]
         for e, (part, i, j) in enumerate(ENTRIES):
-            new = [dense[mu, e, c] + factor[c] * w1_ref[mu, e, c] + half[c] * w2_ref[mu, e, c] for c in range(2)]
+            pair = pack_pair(links_ref[mu, part, i, j, 0])
+            new = [pair[c] + factor[c] * w1_ref[mu, e, c] + half[c] * w2_ref[mu, e, c] for c in range(2)]
             out_ref[mu, part, i, j, 0] = jnp.concatenate(
                 [new[0][0:4], new[1][0:4], new[0][4:8], new[1][4:8]], axis=1
             )
@@ -775,9 +790,9 @@
         space_kernel,
         [((334, 8, LANES), F32)],
         [((3, 3, 18, 2, 8, LANES), F32), ((3, 3, 18, 2, 8, LANES), F32)],
-        places=(smem, smem, vmem, vmem),
+        places=(smem, vmem, vmem),
         cost=pl.CostEstimate(flops=4_000_000_000, bytes_accessed=16_000_000, transcendentals=0),
-    )(parity, link_subset, dense, cotangent)
+    )(parity + 2 * link_subset, dense, cotangent)
     core = (lax.axis_index("tm") % 2).astype(jnp.int32)[None]
     (block,) = call(
         functools.partial(block_kernel, widths),
@@ -827,7 +842,7 @@
             ((3, 8, window), F32), ((8, window), F32), ((H, window), BF16), ((H, window), BF16), ((H, 4 * SITES), BF16),
             ((432, 4 * SITES), BF16), ((72, 4 * SITES), BF16), ((432, LANES), F32),
         ],
-        limit=20 * 1024 * 1024,
+        limit=LIMIT,
     )(fm, below, above, fbelow, fabove, loops, p1, p2, p3, p4, b2, b3, b4)
     if count != 16:
         offset = 0
@@ -839,7 +854,7 @@
     grads = lax.all_to_all(grads, "tm", split_axis=0, concat_axis=0, tiled=True)
     (new_links,) = call(
         update_kernel, [(links.shape, F32)], [((4, 2, 8, LANES), F32)]
-    )(dense, applied, twice, coeff)
+    )(links, applied, twice, coeff)
     grad_first, grad_second, grad_third, grad_last = call(
         functools.partial(sum_kernel, widths),
         [((1, 27 * width), F32) for width in (widths[2], widths[0], widths[1], widths[3])],

time: 62 us -> 64.3 us (1.037)
  Pallas kernels: 23.8 us -> 26.2 us
  other arithmetic: 0 us -> 0.67 us
    pallas_call x1, Pallas kernels: 1.27 us -> 2.22 us  [on_device(): call(panel_kernel_plain, panel_outs, panel_scratch)(gathered)]
    pallas_call x1, Pallas kernels: 9.06 us -> 9.88 us  [on_device(): call(functools.partial(conv_kernel, count == 16), [((4, 8, SITES), F32),...]
    add x0 -> x1, other arithmetic: none -> 0.67 us  [on_device(): parity + 2 * link_subset]
    unnamed x24 -> x26, local copies, waits for them, and re-layouts: 7.13 us -> 6.71 us
  transfers between devices with their start and end apart: 8 -> 8, of which waited for: 2 -> 1; matrix products, arithmetic and copies ran while one was open for 0% -> 1% of each run, Pallas kernels for 17% -> 19%
where the time goes in v10:
time: 64.3 us; the launch traced here: 63.8 us
  Pallas kernels  26.2 us (41%)
  starting transfers between devices  24.6 us (38%)
  local copies, waits for them, and re-layouts  6.71 us (10%)
  waiting for transfers between devices  4.78 us (7%)
  between operations  0.82 us (1%)
  other arithmetic  0.67 us (1%)
    ppermute x6, starting transfers between devices, send(): lax.ppermute(value, 'tm', [(i, (i + distance) % count) for i in range(cou...  14.7 us
    pallas_call x1, Pallas kernels, on_device(): call(functools.partial(conv_kernel, count == 16), [((4, 8, SITES), F32),...  9.88 us
    unnamed x26, local copies, waits for them, and re-layouts  6.71 us
    all_to_all x1, starting transfers between devices, on_device(): grads = lax.all_to_all(grads, 'tm', split_axis=0, concat_axis=0, tiled=True)  5.64 us
    pallas_call x1, Pallas kernels, on_device(): call(space_kernel, [((334, 8, LANES), F32)], [((3, 3, 18, 2, 8, LANES), F...  4.83 us
    all_to_all x1, waiting for transfers between devices, on_device(): grads = lax.all_to_all(grads, 'tm', split_axis=0, concat_axis=0, tiled=True)  4.76 us
    all_to_all x1, starting transfers between devices, on_device(): lax.all_to_all(block, 'tm', split_axis=0, concat_axis=0, tiled=True)  4.19 us
    pallas_call x1, Pallas kernels, on_device(): call(time_kernel, [((4, 16, SITES), BF16), ((3, 8, SITES), BF16), ((3, 8,...  4.15 us
  transfers between devices with their start and end apart: 8, of which 1 were waited for; matrix products, arithmetic and copies ran while one was open for 1% of the time, Pallas kernels for 19%

profile of v10, /device:TPU:0, one launch (start us, length us, event | category | flops | bytes accessed | tf_op | source)
XLA Modules:
  0.0 63.8 jit_solution(7090498020402614184)
XLA Ops:
  0.6 1.1 %copy-done = f32[4,2,3,3,1,4,512]{6,5,4,3,2,1,0:T(4,128)S(1)} copy-done((f32[4,2,3,3,1,4,512]{6,5,4,3,2,1,0:T(4,128)S(1)}, f32[4,2,3,3,1,4,512]{6,5,4,3,2,1,0:T(4,128)}, u32[]{:S(2)}) %copy-start) | copy-done | bytes 589848
  1.7 2.5 %shard_map.119 = (bf16[70,512]{1,0:T(8,128)(2,1)S(1)}, bf16[70,512]{1,0:T(8,128)(2,1)S(1)}, f32[10,18,2,8,128]{4,3,2,1,0:T(8,128)S(1)}, f32[12,4,128]{2,1,0:T(4,128)S(1)}) custom-call(f32[4,2,3,3,1,4,512]{6,5,4,3,2,1,0:T(4,128)S(1)} %copy-done), custom_call_target="tpu_custom_call" | custom-call | tf_op jit(solution)/shard_map/pallas_call | solution.py:782
  4.2 0.5 collective-permute-start
  4.7 5.1 %collective-permute-start.1 = (bf16[70,512]{1,0:T(8,128)(2,1)S(1)}, bf16[70,512]{1,0:T(8,128)(2,1)S(1)}, u32[]{:S(2)}, u32[]{:S(2)}) collective-permute-start(bf16[70,512]{1,0:T(8,128)(2,1)S(1)} %get-tuple-element.30), channel_id=1, source_target_pairs={{0,15},{1,0},{2,1},{3,2},{4,3},{5,4},{6,5},{7,6},{8,7},{9,8},{10,9... | collective-permute-start | bytes 215048 | tf_op jit(solution)/shard_map/ppermute | solution.py:775
  9.7 0.7 %multiply_add_fusion.code_ref = s32[1,4]{1,0:T(1,128)S(1)} fusion(s32[1,4]{1,0:T(1,128)} %param.10, s32[1,4]{1,0:T(1,128)} %param.11), kind=kLoop, calls=%fused_computation | loop fusion | flops 8 | bytes 48 | tf_op jit(solution)/shard_map/add | solution.py:795
  10.4 1.0 %copy-done.12 = bf16[4,2,3,3,1,4,512]{6,5,4,3,2,1,0:T(4,128)(2,1)S(1)} copy-done((bf16[4,2,3,3,1,4,512]{6,5,4,3,2,1,0:T(4,128)(2,1)S(1)}, bf16[4,2,3,3,1,4,512]{6,5,4,3,2,1,0:T(4,128)(2,1)}, u32[]{:S(2)}) %copy-start.12) | copy-done | bytes 294936
  11.4 4.8 %shard_map.120.state.after_ref = f32[334,8,128]{2,1,0:T(8,128)S(1)} custom-call(s32[1,4]{1,0:T(1,128)S(1)} %multiply_add_fusion.code_ref, f32[10,18,2,8,128]{4,3,2,1,0:T(8,128)S(1)} %get-tuple-element.28.dense, bf16[4,2,3,3,1,4,512]{6,5,4,3,2,1,0:T(4,128)(2,1)S(1)} %copy-done.12), custom_call_target="tpu_custom_call" | custom-call | flops 4000000000 | bytes 16000000 | tf_op jit(solution)/shard_map/pallas_call | solution.py:789
  16.3 0.9 %shard_map.122 = bf16[16,64,128]{2,1,0:T(8,128)(2,1)} custom-call(s32[1]{0:T(128)} %bitcast.core_ref, bf16[70,512]{1,0:T(8,128)(2,1)S(1)} %collective-permute-done.up_ref, bf16[70,512]{1,0:T(8,128)(2,1)S(1)} %collective-permute-done.1.down_ref, f32[12,4,128]{2,1,0:T(4,128)S(1)} %get-tuple-element.36.slab, bf16[216]{0:T(256)(128)(2,1)S(1)} %copy-done.10, ...), custom_call_target="tpu_custom_call" | custom-call | tf_op jit(solution)/shard_map/pallas_call | solution.py:797
  17.2 4.2 %all-to-all-start = ((bf16[16,64,128]{2,1,0:T(8,128)(2,1)}), bf16[16,64,128]{2,1,0:T(8,128)(2,1)}, u32[]{:S(2)}, u32[]{:S(2)}) async-start(bf16[16,64,128]{2,1,0:T(8,128)(2,1)} %shard_map.122), calls=%async_computation | async-start | bytes 524288 | tf_op jit(solution)/shard_map/all_to_all | solution.py:803
  21.4 0.9 %copy-done.7 = bf16[70,512]{1,0:T(8,128)(2,1)S(1)} copy-done((bf16[70,512]{1,0:T(8,128)(2,1)S(1)}, bf16[70,512]{1,0:T(8,128)(2,1)}, u32[]{:S(2)}) %copy-start.7) | copy-done | bytes 71704
  22.3 4.2 %shard_map.121 = (bf16[4,16,512]{2,1,0:T(8,128)(2,1)}, bf16[3,8,512]{2,1,0:T(8,128)(2,1)S(1)}, bf16[3,8,512]{2,1,0:T(8,128)(2,1)S(1)}, f32[4,18,2,8,128]{4,3,2,1,0:T(8,128)S(1)}, f32[4,18,2,8,128]{4,3,2,1,0:T(8,128)S(1)}) custom-call(f32[10,18,2,8,128]{4,3,2,1,0:T(8,128)S(1)} %get-tuple-element.28.dense, f32[334,8,128]{2,1,0:T(8,128)S(1)} %shard_map.120.state.after_ref, ...), custom_call_target="tpu_custom_call" | custom-call | tf_op jit(solution)/shard_map/pallas_call | solution.py:804
  26.4 0.8 %copy-done.2 = f32[4,18,2,8,128]{4,3,2,1,0:T(8,128)} copy-done((f32[4,18,2,8,128]{4,3,2,1,0:T(8,128)}, f32[4,18,2,8,128]{4,3,2,1,0:T(8,128)S(1)}, u32[]{:S(2)}) %copy-start.2) | copy-done | bytes 589848
  27.3 0.8 %copy-done.4 = f32[4,18,2,8,128]{4,3,2,1,0:T(8,128)} copy-done((f32[4,18,2,8,128]{4,3,2,1,0:T(8,128)}, f32[4,18,2,8,128]{4,3,2,1,0:T(8,128)S(1)}, u32[]{:S(2)}) %copy-start.4) | copy-done | bytes 589848
  28.1 0.2 collective-permute-start.2
  28.3 4.2 %collective-permute-start.3 = (bf16[4,16,512]{2,1,0:T(8,128)(2,1)}, bf16[4,16,512]{2,1,0:T(8,128)(2,1)S(1)}, u32[]{:S(2)}, u32[]{:S(2)}) collective-permute-start(bf16[4,16,512]{2,1,0:T(8,128)(2,1)} %get-tuple-element.33.fm_ref), channel_id=1, source_target_pairs={{0,15},{1,0},{2,1},{3,2},{4,3},{5,4},{6,5},{7,6},{8,7},{9,8},{10,9... | collective-permute-start | bytes 196616 | tf_op jit(solution)/shard_map/ppermute | solution.py:775
  32.5 4.7 %collective-permute-start.5 = (bf16[3,8,512]{2,1,0:T(8,128)(2,1)S(1)}, bf16[3,8,512]{2,1,0:T(8,128)(2,1)S(1)}, u32[]{:S(2)}, u32[]{:S(2)}) collective-permute-start(bf16[3,8,512]{2,1,0:T(8,128)(2,1)S(1)} %get-tuple-element.35), channel_id=1, source_target_pairs={{0,14},{1,15},{2,0},{3,1},{4,2},{5,3},{6,4},{7,5},{8,6},{9,7},{10,... | collective-permute-start | bytes 73736 | tf_op jit(solution)/shard_map/ppermute | solution.py:775
  37.3 2.2 %shard_map.123 = (f32[2,4,128]{2,1,0:T(4,128)S(1)}, bf16[48,72]{1,0:T(8,128)(2,1)S(1)}, bf16[48,432]{1,0:T(8,128)(2,1)S(1)}, bf16[48,432]{1,0:T(8,128)(2,1)S(1)}...) custom-call(bf16[16,64,128]{2,1,0:T(8,128)(2,1)} %all-to-all-done.ga, ...), custom_call_target="tpu_custom_call" | custom-call | tf_op jit(solution)/shard_map/pallas_call | solution.py:823
  39.5 9.9 %shard_map.124 = (f32[4,8,512]{2,1,0:T(8,128)S(1)}, bf16[16,27,128]{2,1,0:T(8,128)(2,1)}) custom-call(bf16[4,16,512]{2,1,0:T(8,128)(2,1)} %get-tuple-element.33.fm_ref, bf16[4,16,512]{2,1,0:T(8,128)(2,1)S(1)} %collective-permute-done.2.below_ref, bf16[4,16,512]{2,1,0:T(8,128)(2,1)S(1)} %collective-permute-done.3.above_ref, ...), custom_call_target="tpu_custom_call" | custom-call | tf_op jit(solution)/shard_map/pallas_call | solution.py:837
  49.4 5.6 %all-to-all-start.1 = ((bf16[16,27,128]{2,1,0:T(8,128)(2,1)}), bf16[16,27,128]{2,1,0:T(8,128)(2,1)S(1)}, u32[]{:S(2)}, u32[]{:S(2)}) async-start(bf16[16,27,128]{2,1,0:T(8,128)(2,1)} %get-tuple-element.46), calls=%async_computation.1 | async-start | bytes 262144 | tf_op jit(solution)/shard_map/all_to_all | solution.py:854
  55.1 1.1 %copy-done.3 = f32[4,18,2,8,128]{4,3,2,1,0:T(8,128)S(1)} copy-done((f32[4,18,2,8,128]{4,3,2,1,0:T(8,128)S(1)}, f32[4,18,2,8,128]{4,3,2,1,0:T(8,128)}, u32[]{:S(2)}) %copy-start.3) | copy-done | bytes 589848
  56.1 1.1 %copy-done.5 = f32[4,18,2,8,128]{4,3,2,1,0:T(8,128)S(1)} copy-done((f32[4,18,2,8,128]{4,3,2,1,0:T(8,128)S(1)}, f32[4,18,2,8,128]{4,3,2,1,0:T(8,128)}, u32[]{:S(2)}) %copy-start.5) | copy-done | bytes 589848
  57.2 1.0 %shard_map.125 = f32[4,2,3,3,1,4,512]{6,5,4,3,2,1,0:T(4,128)} custom-call(f32[4,2,3,3,1,4,512]{6,5,4,3,2,1,0:T(4,128)S(1)} %copy-done.1, f32[4,18,2,8,128]{4,3,2,1,0:T(8,128)S(1)} %copy-done.3, f32[4,18,2,8,128]{4,3,2,1,0:T(8,128)S(1)} %copy-done.5, f32[4,8,512]{2,1,0:T(8,128)S(1)} %get-tuple-element.45.coeff_ref), custom_call_target="tpu_custom_call" | custom-call | tf_op jit(solution)/shard_map/pallas_call | solution.py:855
  58.2 4.8 %all-to-all-done.1.parts_ref = bf16[16,27,128]{2,1,0:T(8,128)(2,1)S(1)} async-done(((bf16[16,27,128]{2,1,0:T(8,128)(2,1)}), bf16[16,27,128]{2,1,0:T(8,128)(2,1)S(1)}, u32[]{:S(2)}, u32[]{:S(2)}) %all-to-all-start.1) | async-done | bytes 110624 | tf_op jit(solution)/shard_map/all_to_all | solution.py:854
  63.0 0.8 %shard_map.126 = (f32[1,216]{1,0:T(1,128)}, f32[1,1296]{1,0:T(1,128)}, f32[1,1296]{1,0:T(1,128)}, f32[1,108]{1,0:T(1,128)}) custom-call(bf16[16,27,128]{2,1,0:T(8,128)(2,1)S(1)} %all-to-all-done.1.parts_ref), custom_call_target="tpu_custom_call" | custom-call | tf_op jit(solution)/shard_map/pallas_call | solution.py:858
  (27 shorter events, 0.1 us)
Async XLA Ops:
  0.6 1.1 %copy-start = (f32[4,2,3,3,1,4,512]{6,5,4,3,2,1,0:T(4,128)S(1)}, f32[4,2,3,3,1,4,512]{6,5,4,3,2,1,0:T(4,128)}, u32[]{:S(2)}) copy-start(f32[4,2,3,3,1,4,512]{6,5,4,3,2,1,0:T(4,128)} %links_ref.3) | copy-start | bytes 1769476
  4.2 12.1 %collective-permute-start = (bf16[70,512]{1,0:T(8,128)(2,1)S(1)}, bf16[70,512]{1,0:T(8,128)(2,1)S(1)}, u32[]{:S(2)}, u32[]{:S(2)}) collective-permute-start(bf16[70,512]{1,0:T(8,128)(2,1)S(1)} %get-tuple-element.29), channel_id=1, source_target_pairs={{0,1},{1,2},{2,3},{3,4},{4,5},{5,6},{6,7},{7,8},{8,9},{9,10},{10,1... | collective-permute-start | bytes 215048 | tf_op jit(solution)/shard_map/ppermute | solution.py:775
  4.7 11.6 %collective-permute-start.1 = (bf16[70,512]{1,0:T(8,128)(2,1)S(1)}, bf16[70,512]{1,0:T(8,128)(2,1)S(1)}, u32[]{:S(2)}, u32[]{:S(2)}) collective-permute-start(bf16[70,512]{1,0:T(8,128)(2,1)S(1)} %get-tuple-element.30), channel_id=1, source_target_pairs={{0,15},{1,0},{2,1},{3,2},{4,3},{5,4},{6,5},{7,6},{8,7},{9,8},{10,9... | collective-permute-start | bytes 215048 | tf_op jit(solution)/shard_map/ppermute | solution.py:775
  10.4 1.0 %copy-start.12 = (bf16[4,2,3,3,1,4,512]{6,5,4,3,2,1,0:T(4,128)(2,1)S(1)}, bf16[4,2,3,3,1,4,512]{6,5,4,3,2,1,0:T(4,128)(2,1)}, u32[]{:S(2)}) copy-start(bf16[4,2,3,3,1,4,512]{6,5,4,3,2,1,0:T(4,128)(2,1)} %cot_ref.1) | copy-start | bytes 884740
  11.4 4.9 %copy-start.8 = (bf16[1296]{0:T(1024)(128)(2,1)S(1)}, bf16[1296]{0:T(1024)(128)(2,1)}, u32[]{:S(2)}) copy-start(bf16[1296]{0:T(1024)(128)(2,1)} %w2_ref.1) | copy-start | bytes 7780
  11.4 4.9 %copy-start.9 = (bf16[1296]{0:T(1024)(128)(2,1)S(1)}, bf16[1296]{0:T(1024)(128)(2,1)}, u32[]{:S(2)}) copy-start(bf16[1296]{0:T(1024)(128)(2,1)} %w3_ref.1) | copy-start | bytes 7780
  11.4 4.9 %copy-start.10 = (bf16[216]{0:T(256)(128)(2,1)S(1)}, bf16[216]{0:T(256)(128)(2,1)}, u32[]{:S(2)}) copy-start(bf16[216]{0:T(256)(128)(2,1)} %w1_ref.1) | copy-start | bytes 1300
  11.4 4.9 %copy-start.11 = (bf16[108]{0:T(256)(128)(2,1)S(1)}, bf16[108]{0:T(256)(128)(2,1)}, u32[]{:S(2)}) copy-start(bf16[108]{0:T(256)(128)(2,1)} %w4_ref.1) | copy-start | bytes 652
  16.2 1.0 %copy-start.6 = (bf16[70,512]{1,0:T(8,128)(2,1)}, bf16[70,512]{1,0:T(8,128)(2,1)S(1)}, u32[]{:S(2)}) copy-start(bf16[70,512]{1,0:T(8,128)(2,1)S(1)} %collective-permute-done.1.down_ref) | copy-start | bytes 215044
  17.2 20.1 %all-to-all-start = ((bf16[16,64,128]{2,1,0:T(8,128)(2,1)}), bf16[16,64,128]{2,1,0:T(8,128)(2,1)}, u32[]{:S(2)}, u32[]{:S(2)}) async-start(bf16[16,64,128]{2,1,0:T(8,128)(2,1)} %shard_map.122), calls=%async_computation | async-start | bytes 524288 | tf_op jit(solution)/shard_map/all_to_all | solution.py:803
  21.4 0.9 %copy-start.7 = (bf16[70,512]{1,0:T(8,128)(2,1)S(1)}, bf16[70,512]{1,0:T(8,128)(2,1)}, u32[]{:S(2)}) copy-start(bf16[70,512]{1,0:T(8,128)(2,1)} %copy-done.6) | copy-start | bytes 215044
  22.3 32.8 %copy-start.1 = (f32[4,2,3,3,1,4,512]{6,5,4,3,2,1,0:T(4,128)S(1)}, f32[4,2,3,3,1,4,512]{6,5,4,3,2,1,0:T(4,128)}, u32[]{:S(2)}) copy-start(f32[4,2,3,3,1,4,512]{6,5,4,3,2,1,0:T(4,128)} %links_ref.3) | copy-start | bytes 1769476
  26.4 0.8 %copy-start.2 = (f32[4,18,2,8,128]{4,3,2,1,0:T(8,128)}, f32[4,18,2,8,128]{4,3,2,1,0:T(8,128)S(1)}, u32[]{:S(2)}) copy-start(f32[4,18,2,8,128]{4,3,2,1,0:T(8,128)S(1)} %get-tuple-element.31.w1_ref) | copy-start | bytes 1769476
  27.3 0.8 %copy-start.4 = (f32[4,18,2,8,128]{4,3,2,1,0:T(8,128)}, f32[4,18,2,8,128]{4,3,2,1,0:T(8,128)S(1)}, u32[]{:S(2)}) copy-start(f32[4,18,2,8,128]{4,3,2,1,0:T(8,128)S(1)} %get-tuple-element.32.w2_ref) | copy-start | bytes 1769476
  28.1 11.4 %collective-permute-start.2 = (bf16[4,16,512]{2,1,0:T(8,128)(2,1)}, bf16[4,16,512]{2,1,0:T(8,128)(2,1)S(1)}, u32[]{:S(2)}, u32[]{:S(2)}) collective-permute-start(bf16[4,16,512]{2,1,0:T(8,128)(2,1)} %get-tuple-element.33.fm_ref), channel_id=1, source_target_pairs={{0,1},{1,2},{2,3},{3,4},{4,5},{5,6},{6,7},{7,8},{8,9},{9,10},{10,1... | collective-permute-start | bytes 196616 | tf_op jit(solution)/shard_map/ppermute | solution.py:775
  28.3 11.2 %collective-permute-start.3 = (bf16[4,16,512]{2,1,0:T(8,128)(2,1)}, bf16[4,16,512]{2,1,0:T(8,128)(2,1)S(1)}, u32[]{:S(2)}, u32[]{:S(2)}) collective-permute-start(bf16[4,16,512]{2,1,0:T(8,128)(2,1)} %get-tuple-element.33.fm_ref), channel_id=1, source_target_pairs={{0,15},{1,0},{2,1},{3,2},{4,3},{5,4},{6,5},{7,6},{8,7},{9,8},{10,9... | collective-permute-start | bytes 196616 | tf_op jit(solution)/shard_map/ppermute | solution.py:775
  32.5 7.0 %collective-permute-start.4 = (bf16[3,8,512]{2,1,0:T(8,128)(2,1)S(1)}, bf16[3,8,512]{2,1,0:T(8,128)(2,1)S(1)}, u32[]{:S(2)}, u32[]{:S(2)}) collective-permute-start(bf16[3,8,512]{2,1,0:T(8,128)(2,1)S(1)} %get-tuple-element.34), channel_id=1, source_target_pairs={{0,2},{1,3},{2,4},{3,5},{4,6},{5,7},{6,8},{7,9},{8,10},{9,11},{10,... | collective-permute-start | bytes 73736 | tf_op jit(solution)/shard_map/ppermute | solution.py:775
  32.5 7.0 %collective-permute-start.5 = (bf16[3,8,512]{2,1,0:T(8,128)(2,1)S(1)}, bf16[3,8,512]{2,1,0:T(8,128)(2,1)S(1)}, u32[]{:S(2)}, u32[]{:S(2)}) collective-permute-start(bf16[3,8,512]{2,1,0:T(8,128)(2,1)S(1)} %get-tuple-element.35), channel_id=1, source_target_pairs={{0,14},{1,15},{2,0},{3,1},{4,2},{5,3},{6,4},{7,5},{8,6},{9,7},{10,... | collective-permute-start | bytes 73736 | tf_op jit(solution)/shard_map/ppermute | solution.py:775
  49.4 13.6 %all-to-all-start.1 = ((bf16[16,27,128]{2,1,0:T(8,128)(2,1)}), bf16[16,27,128]{2,1,0:T(8,128)(2,1)S(1)}, u32[]{:S(2)}, u32[]{:S(2)}) async-start(bf16[16,27,128]{2,1,0:T(8,128)(2,1)} %get-tuple-element.46), calls=%async_computation.1 | async-start | bytes 262144 | tf_op jit(solution)/shard_map/all_to_all | solution.py:854
  55.1 1.1 %copy-start.3 = (f32[4,18,2,8,128]{4,3,2,1,0:T(8,128)S(1)}, f32[4,18,2,8,128]{4,3,2,1,0:T(8,128)}, u32[]{:S(2)}) copy-start(f32[4,18,2,8,128]{4,3,2,1,0:T(8,128)} %copy-done.2) | copy-start | bytes 1769476
  56.1 1.1 %copy-start.5 = (f32[4,18,2,8,128]{4,3,2,1,0:T(8,128)S(1)}, f32[4,18,2,8,128]{4,3,2,1,0:T(8,128)}, u32[]{:S(2)}) copy-start(f32[4,18,2,8,128]{4,3,2,1,0:T(8,128)} %copy-done.4) | copy-start | bytes 1769476

commit v11 on v10

--- a/solution.py
+++ b/solution.py
@@ -722,7 +722,7 @@
         grads_ref[...] = packed[...].astype(BF16)
 
 
-def update_kernel(links_ref, w1_ref, w2_ref, coeff_ref, out_ref, factors):
+def update_kernel(dense, w1_ref, w2_ref, coeff_ref, out_ref, factors):
     for mu in range(4):
         for t in range(4):
             for c in range(2):
@@ -733,8 +733,7 @@
         factor = [factors[mu, c] for c in range(2)]
         half = [0.5 * value * value for value in factor]
         for e, (part, i, j) in enumerate(ENTRIES):
-            pair = pack_pair(links_ref[mu, part, i, j, 0])
-            new = [pair[c] + factor[c] * w1_ref[mu, e, c] + half[c] * w2_ref[mu, e, c] for c in range(2)]
+            new = [dense[mu, e, c] + factor[c] * w1_ref[mu, e, c] + half[c] * w2_ref[mu, e, c] for c in range(2)]
             out_ref[mu, part, i, j, 0] = jnp.concatenate(
                 [new[0][0:4], new[1][0:4], new[0][4:8], new[1][4:8]], axis=1
             )
@@ -842,7 +841,7 @@
             ((3, 8, window), F32), ((8, window), F32), ((H, window), BF16), ((H, window), BF16), ((H, 4 * SITES), BF16),
             ((432, 4 * SITES), BF16), ((72, 4 * SITES), BF16), ((432, LANES), F32),
         ],
-        limit=LIMIT,
+        limit=20 * 1024 * 1024,
     )(fm, below, above, fbelow, fabove, loops, p1, p2, p3, p4, b2, b3, b4)
     if count != 16:
         offset = 0
@@ -854,7 +853,7 @@
     grads = lax.all_to_all(grads, "tm", split_axis=0, concat_axis=0, tiled=True)
     (new_links,) = call(
         update_kernel, [(links.shape, F32)], [((4, 2, 8, LANES), F32)]
-    )(links, applied, twice, coeff)
+    )(dense, applied, twice, coeff)
     grad_first, grad_second, grad_third, grad_last = call(
         functools.partial(sum_kernel, widths),
         [((1, 27 * width), F32) for width in (widths[2], widths[0], widths[1], widths[3])],

time: 64.3 us -> 61.3 us (0.953)
  Pallas kernels: 26.2 us -> 23.8 us
  local copies, waits for them, and re-layouts: 6.71 us -> 5.79 us
    pallas_call x1, Pallas kernels: 2.22 us -> 1.27 us  [on_device(): call(panel_kernel_plain, panel_outs, panel_scratch)(gathered)]
    unnamed x26 -> x20, local copies, waits for them, and re-layouts: 6.71 us -> 5.79 us
    pallas_call x1, Pallas kernels: 9.88 us -> 9.06 us  [on_device(): call(functools.partial(conv_kernel, count == 16), [((4, 8, SITES), F32),...]
  transfers between devices with their start and end apart: 8 -> 8, of which waited for: 1 -> 2; matrix products, arithmetic and copies ran while one was open for 1% -> 1% of each run, Pallas kernels for 19% -> 17%
where the time goes in v11:
time: 61.3 us; the launch traced here: 60.8 us
  starting transfers between devices  24.4 us (40%)
  Pallas kernels  23.8 us (39%)
  local copies, waits for them, and re-layouts  5.79 us (9%)
  waiting for transfers between devices  5.35 us (9%)
  between operations  0.78 us (1%)
  other arithmetic  0.67 us (1%)
    ppermute x6, starting transfers between devices, send(): lax.ppermute(value, 'tm', [(i, (i + distance) % count) for i in range(cou...  14.7 us
    pallas_call x1, Pallas kernels, on_device(): call(functools.partial(conv_kernel, count == 16), [((4, 8, SITES), F32),...  9.06 us
    all_to_all x1, starting transfers between devices, on_device(): grads = lax.all_to_all(grads, 'tm', split_axis=0, concat_axis=0, tiled=True)  6.09 us
    unnamed x20, local copies, waits for them, and re-layouts  5.79 us
    pallas_call x1, Pallas kernels, on_device(): call(space_kernel, [((334, 8, LANES), F32)], [((3, 3, 18, 2, 8, LANES), F...  4.82 us
    all_to_all x1, waiting for transfers between devices, on_device(): grads = lax.all_to_all(grads, 'tm', split_axis=0, concat_axis=0, tiled=True)  4.82 us
    all_to_all x1, starting transfers between devices, on_device(): lax.all_to_all(block, 'tm', split_axis=0, concat_axis=0, tiled=True)  3.62 us
    pallas_call x1, Pallas kernels, on_device(): call(time_kernel, [((4, 16, SITES), BF16), ((3, 8, SITES), BF16), ((3, 8,...  3.54 us
  transfers between devices with their start and end apart: 8, of which 2 were waited for; matrix products, arithmetic and copies ran while one was open for 1% of the time, Pallas kernels for 17%

profile of v11, /device:TPU:0, one launch (start us, length us, event | category | flops | bytes accessed | tf_op | source)
XLA Modules:
  0.0 60.8 jit_solution(7495133857675305973)
XLA Ops:
  0.6 1.1 %copy-done.4 = f32[4,2,3,3,1,4,512]{6,5,4,3,2,1,0:T(4,128)S(1)} copy-done((f32[4,2,3,3,1,4,512]{6,5,4,3,2,1,0:T(4,128)S(1)}, f32[4,2,3,3,1,4,512]{6,5,4,3,2,1,0:T(4,128)}, u32[]{:S(2)}) %copy-start.4) | copy-done | bytes 589848
  1.7 2.5 %shard_map.119 = (bf16[70,512]{1,0:T(8,128)(2,1)S(1)}, bf16[70,512]{1,0:T(8,128)(2,1)S(1)}, f32[10,18,2,8,128]{4,3,2,1,0:T(8,128)S(1)}, f32[12,4,128]{2,1,0:T(4,128)S(1)}) custom-call(f32[4,2,3,3,1,4,512]{6,5,4,3,2,1,0:T(4,128)S(1)} %copy-done.4), custom_call_target="tpu_custom_call" | custom-call | tf_op jit(solution)/shard_map/pallas_call | solution.py:781
  4.2 0.5 collective-permute-start
  4.7 5.1 %collective-permute-start.1 = (bf16[70,512]{1,0:T(8,128)(2,1)S(1)}, bf16[70,512]{1,0:T(8,128)(2,1)S(1)}, u32[]{:S(2)}, u32[]{:S(2)}) collective-permute-start(bf16[70,512]{1,0:T(8,128)(2,1)S(1)} %get-tuple-element.30), channel_id=1, source_target_pairs={{0,15},{1,0},{2,1},{3,2},{4,3},{5,4},{6,5},{7,6},{8,7},{9,8},{10,9... | collective-permute-start | bytes 215048 | tf_op jit(solution)/shard_map/ppermute | solution.py:774
  9.7 0.7 %multiply_add_fusion.code_ref = s32[1,4]{1,0:T(1,128)S(1)} fusion(s32[1,4]{1,0:T(1,128)} %param.10, s32[1,4]{1,0:T(1,128)} %param.11), kind=kLoop, calls=%fused_computation | loop fusion | flops 8 | bytes 48 | tf_op jit(solution)/shard_map/add | solution.py:794
  10.4 1.0 %copy-done.9 = bf16[4,2,3,3,1,4,512]{6,5,4,3,2,1,0:T(4,128)(2,1)S(1)} copy-done((bf16[4,2,3,3,1,4,512]{6,5,4,3,2,1,0:T(4,128)(2,1)S(1)}, bf16[4,2,3,3,1,4,512]{6,5,4,3,2,1,0:T(4,128)(2,1)}, u32[]{:S(2)}) %copy-start.9) | copy-done | bytes 294936
  11.4 4.8 %shard_map.120.state.after_ref = f32[334,8,128]{2,1,0:T(8,128)S(1)} custom-call(s32[1,4]{1,0:T(1,128)S(1)} %multiply_add_fusion.code_ref, f32[10,18,2,8,128]{4,3,2,1,0:T(8,128)S(1)} %get-tuple-element.28.dense, bf16[4,2,3,3,1,4,512]{6,5,4,3,2,1,0:T(4,128)(2,1)S(1)} %copy-done.9), custom_call_target="tpu_custom_call" | custom-call | flops 4000000000 | bytes 16000000 | tf_op jit(solution)/shard_map/pallas_call | solution.py:788
  16.3 0.9 %shard_map.122 = bf16[16,64,128]{2,1,0:T(8,128)(2,1)} custom-call(s32[1]{0:T(128)} %bitcast.core_ref, bf16[70,512]{1,0:T(8,128)(2,1)S(1)} %collective-permute-done.up_ref, bf16[70,512]{1,0:T(8,128)(2,1)S(1)} %collective-permute-done.1.down_ref, f32[12,4,128]{2,1,0:T(4,128)S(1)} %get-tuple-element.36.slab, bf16[216]{0:T(256)(128)(2,1)S(1)} %copy-done.7, ...), custom_call_target="tpu_custom_call" | custom-call | tf_op jit(solution)/shard_map/pallas_call | solution.py:796
  17.2 3.6 %all-to-all-start = ((bf16[16,64,128]{2,1,0:T(8,128)(2,1)}), bf16[16,64,128]{2,1,0:T(8,128)(2,1)S(1)}, u32[]{:S(2)}, u32[]{:S(2)}) async-start(bf16[16,64,128]{2,1,0:T(8,128)(2,1)} %shard_map.122), calls=%async_computation | async-start | bytes 524288 | tf_op jit(solution)/shard_map/all_to_all | solution.py:802
  20.8 3.5 %shard_map.121 = (bf16[4,16,512]{2,1,0:T(8,128)(2,1)S(1)}, bf16[3,8,512]{2,1,0:T(8,128)(2,1)S(1)}, bf16[3,8,512]{2,1,0:T(8,128)(2,1)S(1)}, f32[4,18,2,8,128]{4,3,2,1,0:T(8,128)S(1)}, f32[4,18,2,8,128]{4,3,2,1,0:T(8,128)S(1)}) custom-call(f32[10,18,2,8,128]{4,3,2,1,0:T(8,128)S(1)} %get-tuple-element.28.dense, f32[334,8,128]{2,1,0:T(8,128)S(1)} %shard_map.120.state.after_ref, ...), custom_call_target="tpu_custom_call" | custom-call | tf_op jit(solution)/shard_map/pallas_call | solution.py:803
  24.3 0.8 %copy-done = f32[4,18,2,8,128]{4,3,2,1,0:T(8,128)} copy-done((f32[4,18,2,8,128]{4,3,2,1,0:T(8,128)}, f32[4,18,2,8,128]{4,3,2,1,0:T(8,128)S(1)}, u32[]{:S(2)}) %copy-start) | copy-done | bytes 589848
  25.2 0.8 %copy-done.2 = f32[4,18,2,8,128]{4,3,2,1,0:T(8,128)} copy-done((f32[4,18,2,8,128]{4,3,2,1,0:T(8,128)}, f32[4,18,2,8,128]{4,3,2,1,0:T(8,128)S(1)}, u32[]{:S(2)}) %copy-start.2) | copy-done | bytes 589848
  26.0 0.4 collective-permute-start.2
  26.4 4.0 %collective-permute-start.3 = (bf16[4,16,512]{2,1,0:T(8,128)(2,1)S(1)}, bf16[4,16,512]{2,1,0:T(8,128)(2,1)S(1)}, u32[]{:S(2)}, u32[]{:S(2)}) collective-permute-start(bf16[4,16,512]{2,1,0:T(8,128)(2,1)S(1)} %get-tuple-element.33.fm_ref), channel_id=1, source_target_pairs={{0,15},{1,0},{2,1},{3,2},{4,3},{5,4},{6,5},{7,6},{8,7},{9,8},{10,9... | collective-permute-start | bytes 196616 | tf_op jit(solution)/shard_map/ppermute | solution.py:774
  30.4 4.7 %collective-permute-start.5 = (bf16[3,8,512]{2,1,0:T(8,128)(2,1)S(1)}, bf16[3,8,512]{2,1,0:T(8,128)(2,1)S(1)}, u32[]{:S(2)}, u32[]{:S(2)}) collective-permute-start(bf16[3,8,512]{2,1,0:T(8,128)(2,1)S(1)} %get-tuple-element.35), channel_id=1, source_target_pairs={{0,14},{1,15},{2,0},{3,1},{4,2},{5,3},{6,4},{7,5},{8,6},{9,7},{10,... | collective-permute-start | bytes 73736 | tf_op jit(solution)/shard_map/ppermute | solution.py:774
  35.2 1.3 %shard_map.123 = (f32[2,4,128]{2,1,0:T(4,128)S(1)}, bf16[48,72]{1,0:T(8,128)(2,1)S(1)}, bf16[48,432]{1,0:T(8,128)(2,1)S(1)}, bf16[48,432]{1,0:T(8,128)(2,1)S(1)}...) custom-call(bf16[16,64,128]{2,1,0:T(8,128)(2,1)S(1)} %all-to-all-don, ...), custom_call_target="tpu_custom_call" | custom-call | tf_op jit(solution)/shard_map/pallas_call | solution.py:822
  36.4 0.5 collective-permute-done.4.fbelow_ref
  37.0 9.1 %shard_map.124 = (f32[4,8,512]{2,1,0:T(8,128)S(1)}, bf16[16,27,128]{2,1,0:T(8,128)(2,1)}) custom-call(bf16[4,16,512]{2,1,0:T(8,128)(2,1)S(1)} %get-tuple-element.33.fm_ref, bf16[4,16,512]{2,1,0:T(8,128)(2,1)S(1)} %collective-permute-done.2.below_ref, bf16[4,16,512]{2,1,0:T(8,128)(2,1)S(1)} %collective-permute-done.3.above_ref, ...), custom_call_target="tpu_custom_call" | custom-call | tf_op jit(solution)/shard_map/pallas_call | solution.py:836
  46.0 6.1 %all-to-all-start.1 = ((bf16[16,27,128]{2,1,0:T(8,128)(2,1)}), bf16[16,27,128]{2,1,0:T(8,128)(2,1)S(1)}, u32[]{:S(2)}, u32[]{:S(2)}) async-start(bf16[16,27,128]{2,1,0:T(8,128)(2,1)} %get-tuple-element.46), calls=%async_computation.1 | async-start | bytes 262144 | tf_op jit(solution)/shard_map/all_to_all | solution.py:853
  52.1 1.1 %copy-done.1 = f32[4,18,2,8,128]{4,3,2,1,0:T(8,128)S(1)} copy-done((f32[4,18,2,8,128]{4,3,2,1,0:T(8,128)S(1)}, f32[4,18,2,8,128]{4,3,2,1,0:T(8,128)}, u32[]{:S(2)}) %copy-start.1) | copy-done | bytes 589848
  53.2 1.1 %copy-done.3 = f32[4,18,2,8,128]{4,3,2,1,0:T(8,128)S(1)} copy-done((f32[4,18,2,8,128]{4,3,2,1,0:T(8,128)S(1)}, f32[4,18,2,8,128]{4,3,2,1,0:T(8,128)}, u32[]{:S(2)}) %copy-start.3) | copy-done | bytes 589848
  54.3 1.0 %shard_map.125 = f32[4,2,3,3,1,4,512]{6,5,4,3,2,1,0:T(4,128)} custom-call(f32[10,18,2,8,128]{4,3,2,1,0:T(8,128)S(1)} %get-tuple-element.28.dense, f32[4,18,2,8,128]{4,3,2,1,0:T(8,128)S(1)} %copy-done.1, f32[4,18,2,8,128]{4,3,2,1,0:T(8,128)S(1)} %copy-done.3, f32[4,8,512]{2,1,0:T(8,128)S(1)} %get-tuple-element.45.coeff_ref), custom_call_target="tpu_custom_call" | custom-call | tf_op jit(solution)/shard_map/pallas_call | solution.py:854
  55.2 4.8 %all-to-all-done.1.parts_ref = bf16[16,27,128]{2,1,0:T(8,128)(2,1)S(1)} async-done(((bf16[16,27,128]{2,1,0:T(8,128)(2,1)}), bf16[16,27,128]{2,1,0:T(8,128)(2,1)S(1)}, u32[]{:S(2)}, u32[]{:S(2)}) %all-to-all-start.1) | async-done | bytes 110624 | tf_op jit(solution)/shard_map/all_to_all | solution.py:853
  60.1 0.8 %shard_map.126 = (f32[1,216]{1,0:T(1,128)}, f32[1,1296]{1,0:T(1,128)}, f32[1,1296]{1,0:T(1,128)}, f32[1,108]{1,0:T(1,128)}) custom-call(bf16[16,27,128]{2,1,0:T(8,128)(2,1)S(1)} %all-to-all-done.1.parts_ref), custom_call_target="tpu_custom_call" | custom-call | tf_op jit(solution)/shard_map/pallas_call | solution.py:857
  (21 shorter events, 0.0 us)
Async XLA Ops:
  0.6 1.1 %copy-start.4 = (f32[4,2,3,3,1,4,512]{6,5,4,3,2,1,0:T(4,128)S(1)}, f32[4,2,3,3,1,4,512]{6,5,4,3,2,1,0:T(4,128)}, u32[]{:S(2)}) copy-start(f32[4,2,3,3,1,4,512]{6,5,4,3,2,1,0:T(4,128)} %links_ref.1) | copy-start | bytes 1769476
  4.2 12.1 %collective-permute-start = (bf16[70,512]{1,0:T(8,128)(2,1)S(1)}, bf16[70,512]{1,0:T(8,128)(2,1)S(1)}, u32[]{:S(2)}, u32[]{:S(2)}) collective-permute-start(bf16[70,512]{1,0:T(8,128)(2,1)S(1)} %get-tuple-element.29), channel_id=1, source_target_pairs={{0,1},{1,2},{2,3},{3,4},{4,5},{5,6},{6,7},{7,8},{8,9},{9,10},{10,1... | collective-permute-start | bytes 215048 | tf_op jit(solution)/shard_map/ppermute | solution.py:774
  4.7 11.6 %collective-permute-start.1 = (bf16[70,512]{1,0:T(8,128)(2,1)S(1)}, bf16[70,512]{1,0:T(8,128)(2,1)S(1)}, u32[]{:S(2)}, u32[]{:S(2)}) collective-permute-start(bf16[70,512]{1,0:T(8,128)(2,1)S(1)} %get-tuple-element.30), channel_id=1, source_target_pairs={{0,15},{1,0},{2,1},{3,2},{4,3},{5,4},{6,5},{7,6},{8,7},{9,8},{10,9... | collective-permute-start | bytes 215048 | tf_op jit(solution)/shard_map/ppermute | solution.py:774
  10.4 1.0 %copy-start.9 = (bf16[4,2,3,3,1,4,512]{6,5,4,3,2,1,0:T(4,128)(2,1)S(1)}, bf16[4,2,3,3,1,4,512]{6,5,4,3,2,1,0:T(4,128)(2,1)}, u32[]{:S(2)}) copy-start(bf16[4,2,3,3,1,4,512]{6,5,4,3,2,1,0:T(4,128)(2,1)} %cot_ref.1) | copy-start | bytes 884740
  11.4 4.9 %copy-start.5 = (bf16[1296]{0:T(1024)(128)(2,1)S(1)}, bf16[1296]{0:T(1024)(128)(2,1)}, u32[]{:S(2)}) copy-start(bf16[1296]{0:T(1024)(128)(2,1)} %w2_ref.1) | copy-start | bytes 7780
  11.4 4.9 %copy-start.6 = (bf16[1296]{0:T(1024)(128)(2,1)S(1)}, bf16[1296]{0:T(1024)(128)(2,1)}, u32[]{:S(2)}) copy-start(bf16[1296]{0:T(1024)(128)(2,1)} %w3_ref.1) | copy-start | bytes 7780
  11.4 4.9 %copy-start.7 = (bf16[216]{0:T(256)(128)(2,1)S(1)}, bf16[216]{0:T(256)(128)(2,1)}, u32[]{:S(2)}) copy-start(bf16[216]{0:T(256)(128)(2,1)} %w1_ref.1) | copy-start | bytes 1300
  11.4 4.9 %copy-start.8 = (bf16[108]{0:T(256)(128)(2,1)S(1)}, bf16[108]{0:T(256)(128)(2,1)}, u32[]{:S(2)}) copy-start(bf16[108]{0:T(256)(128)(2,1)} %w4_ref.1) | copy-start | bytes 652
  17.2 18.0 %all-to-all-start = ((bf16[16,64,128]{2,1,0:T(8,128)(2,1)}), bf16[16,64,128]{2,1,0:T(8,128)(2,1)S(1)}, u32[]{:S(2)}, u32[]{:S(2)}) async-start(bf16[16,64,128]{2,1,0:T(8,128)(2,1)} %shard_map.122), calls=%async_computation | async-start | bytes 524288 | tf_op jit(solution)/shard_map/all_to_all | solution.py:802
  24.3 0.8 %copy-start = (f32[4,18,2,8,128]{4,3,2,1,0:T(8,128)}, f32[4,18,2,8,128]{4,3,2,1,0:T(8,128)S(1)}, u32[]{:S(2)}) copy-start(f32[4,18,2,8,128]{4,3,2,1,0:T(8,128)S(1)} %get-tuple-element.31.w1_ref) | copy-start | bytes 1769476
  25.2 0.8 %copy-start.2 = (f32[4,18,2,8,128]{4,3,2,1,0:T(8,128)}, f32[4,18,2,8,128]{4,3,2,1,0:T(8,128)S(1)}, u32[]{:S(2)}) copy-start(f32[4,18,2,8,128]{4,3,2,1,0:T(8,128)S(1)} %get-tuple-element.32.w2_ref) | copy-start | bytes 1769476
  26.0 11.0 %collective-permute-start.2 = (bf16[4,16,512]{2,1,0:T(8,128)(2,1)S(1)}, bf16[4,16,512]{2,1,0:T(8,128)(2,1)S(1)}, u32[]{:S(2)}, u32[]{:S(2)}) collective-permute-start(bf16[4,16,512]{2,1,0:T(8,128)(2,1)S(1)} %get-tuple-element.33.fm_ref), channel_id=1, source_target_pairs={{0,1},{1,2},{2,3},{3,4},{4,5},{5,6},{6,7},{7,8},{8,9},{9,10},{10,1... | collective-permute-start | bytes 196616 | tf_op jit(solution)/shard_map/ppermute | solution.py:774
  26.4 10.6 %collective-permute-start.3 = (bf16[4,16,512]{2,1,0:T(8,128)(2,1)S(1)}, bf16[4,16,512]{2,1,0:T(8,128)(2,1)S(1)}, u32[]{:S(2)}, u32[]{:S(2)}) collective-permute-start(bf16[4,16,512]{2,1,0:T(8,128)(2,1)S(1)} %get-tuple-element.33.fm_ref), channel_id=1, source_target_pairs={{0,15},{1,0},{2,1},{3,2},{4,3},{5,4},{6,5},{7,6},{8,7},{9,8},{10,9... | collective-permute-start | bytes 196616 | tf_op jit(solution)/shard_map/ppermute | solution.py:774
  30.4 6.5 %collective-permute-start.4 = (bf16[3,8,512]{2,1,0:T(8,128)(2,1)S(1)}, bf16[3,8,512]{2,1,0:T(8,128)(2,1)S(1)}, u32[]{:S(2)}, u32[]{:S(2)}) collective-permute-start(bf16[3,8,512]{2,1,0:T(8,128)(2,1)S(1)} %get-tuple-element.34), channel_id=1, source_target_pairs={{0,2},{1,3},{2,4},{3,5},{4,6},{5,7},{6,8},{7,9},{8,10},{9,11},{10,... | collective-permute-start | bytes 73736 | tf_op jit(solution)/shard_map/ppermute | solution.py:774
  30.4 6.5 %collective-permute-start.5 = (bf16[3,8,512]{2,1,0:T(8,128)(2,1)S(1)}, bf16[3,8,512]{2,1,0:T(8,128)(2,1)S(1)}, u32[]{:S(2)}, u32[]{:S(2)}) collective-permute-start(bf16[3,8,512]{2,1,0:T(8,128)(2,1)S(1)} %get-tuple-element.35), channel_id=1, source_target_pairs={{0,14},{1,15},{2,0},{3,1},{4,2},{5,3},{6,4},{7,5},{8,6},{9,7},{10,... | collective-permute-start | bytes 73736 | tf_op jit(solution)/shard_map/ppermute | solution.py:774
  46.0 14.0 %all-to-all-start.1 = ((bf16[16,27,128]{2,1,0:T(8,128)(2,1)}), bf16[16,27,128]{2,1,0:T(8,128)(2,1)S(1)}, u32[]{:S(2)}, u32[]{:S(2)}) async-start(bf16[16,27,128]{2,1,0:T(8,128)(2,1)} %get-tuple-element.46), calls=%async_computation.1 | async-start | bytes 262144 | tf_op jit(solution)/shard_map/all_to_all | solution.py:853
  52.1 1.1 %copy-start.1 = (f32[4,18,2,8,128]{4,3,2,1,0:T(8,128)S(1)}, f32[4,18,2,8,128]{4,3,2,1,0:T(8,128)}, u32[]{:S(2)}) copy-start(f32[4,18,2,8,128]{4,3,2,1,0:T(8,128)} %copy-done) | copy-start | bytes 1769476
  53.2 1.1 %copy-start.3 = (f32[4,18,2,8,128]{4,3,2,1,0:T(8,128)S(1)}, f32[4,18,2,8,128]{4,3,2,1,0:T(8,128)}, u32[]{:S(2)}) copy-start(f32[4,18,2,8,128]{4,3,2,1,0:T(8,128)} %copy-done.2) | copy-start | bytes 1769476

commit v12 on v11

--- a/solution.py
+++ b/solution.py
@@ -16,10 +16,7 @@
 PAIRS = ((0, 1), (0, 2), (0, 3), (1, 2), (1, 3), (2, 3))
 SWAP = (0, 2, 1, 4, 3, 6, 5, 8, 7)
 ENTRIES = tuple((c, i, j) for c in range(2) for i in range(3) for j in range(3))
-EDGE = 4
-STAPLE = 7
 PLANE = 180
-GATE = 186
 SLABROWS = 24
 BLOCKROWS = 64
 LIMIT = 8 * 1024 * 1024
@@ -210,7 +207,7 @@
     lax.fori_loop(0, 4, body, 0)
 
 
-def face_kernel(links_ref, up_ref, down_ref, dense, slab, moved, rows):
+def face_kernel(links_ref, up_ref, down_ref, dense, edges, staples, slab, moved, rows):
     pack_links(links_ref, dense)
 
     def shift_body(e, carry):
@@ -221,7 +218,7 @@
             moved[mu, e, 1] = high
         return carry
 
-    lax.fori_loop(0, 18, shift_body, 0)
+    lax.fori_loop(0, 18, shift_body, 0, unroll=3)
 
     def staple_body(step, carry):
         mu = step // 2
@@ -231,12 +228,12 @@
         edge = mat_mul(u_mu, load_matrix(lambda e: moved[mu, e, c]))
 
         def write_edge(e, value):
-            dense[EDGE + mu, e, c] = value
+            edges[mu, e, c] = value
 
         store_matrix(edge, write_edge)
 
         def write(e, value):
-            dense[STAPLE + mu, e, c] = value
+            staples[mu, e, c] = value
             rows[16 + mu * 18 + e, pl.ds(c, 1)] = value[3:4]
             rows[16 + mu * 18 + e, pl.ds(2 + c, 1)] = value[7:8]
 
@@ -275,7 +272,7 @@
                 rows[16 + mu * 18 + e, 2 + c:3 + c] = value[4:5]
         return carry
 
-    lax.fori_loop(0, 18, down_body, 0)
+    lax.fori_loop(0, 18, down_body, 0, unroll=3)
     for q in range(4):
         down_ref[:, q * 128:q * 128 + 128] = rows[:, q, :].astype(BF16)
 
@@ -324,29 +321,9 @@
     return 108 + (mu * 9 + e) * 2 + c
 
 
-def cot_at(mu, e, c):
-    return 190 + (mu * 18 + e) * 2 + c
-
-
-def space_kernel(code_ref, dense, cot_ref, state, moved, staples):
-    def cot_body(mu, carry):
-        for e, (part, i, j) in enumerate(ENTRIES):
-            low, high = pack_pair(cot_ref[mu, part, i, j, 0].astype(F32))
-            state[cot_at(mu, e, 0)] = low
-            state[cot_at(mu, e, 1)] = high
-        return carry
-
-    lax.fori_loop(0, 4, cot_body, 0)
+def space_kernel(dense, time_staples, state, moved, staples):
     state[108:180] = jnp.zeros((72, 8, LANES), F32)
     steps = row_iota() % 4
-    lanes = lane_iota(8)
-    colour = (lanes // 64 + lanes // 8 % 8 + lanes % 8 + steps) % 2
-    code = jnp.zeros_like(steps)
-    for t in range(4):
-        code = jnp.where(steps == t, code_ref[0, t], code)
-    for mu in range(4):
-        active = jnp.logical_and(colour == code % 2, jnp.right_shift(code, mu + 1) % 2 == 1)
-        state[GATE + mu] = jnp.where(active, 1.0, 0.0)
 
     def shift_body(e, carry):
         for nu in range(3):
@@ -358,7 +335,7 @@
                     moved[mu, nu, e, 1] = high
         return carry
 
-    lax.fori_loop(0, 18, shift_body, 0)
+    lax.fori_loop(0, 18, shift_body, 0, unroll=3)
 
     def plane_body(step, carry):
         plane = step // 2
@@ -389,7 +366,7 @@
 
     def lower_body(e, carry):
         for mu in range(3):
-            acc = [jnp.where(steps == 0, 0.0, pltpu.roll(dense[STAPLE + mu, e, c], 1, 0)) for c in range(2)]
+            acc = [jnp.where(steps == 0, 0.0, pltpu.roll(time_staples[mu, e, c], 1, 0)) for c in range(2)]
             for nu in range(3):
                 if nu != mu:
                     pair = dense_shift([staples[mu, nu, e, 0], staples[mu, nu, e, 1]], nu, -1)
@@ -398,18 +375,28 @@
             state[sum_at(mu, e, 1)] = acc[1]
         return carry
 
-    lax.fori_loop(0, 18, lower_body, 0)
+    lax.fori_loop(0, 18, lower_body, 0, unroll=3)
 
 
 def time_kernel(
-    dense, state, up_ref, down_ref,
-    fm_ref, fup_ref, fdown_ref, w1_ref, w2_ref,
-    moved, staples, sums, halo_up, halo_down, forces, rows,
+    code_ref, dense, edges, state, cot_ref, up_ref, down_ref,
+    fm_ref, fup_ref, fdown_ref, moves_ref,
+    cots, gates, moved, staples, sums, halo_up, halo_down, forces, rows,
 ):
     for q in range(4):
         halo_up[:, q, :] = up_ref[:, q * 128:q * 128 + 128].astype(F32)
         halo_down[:, q, :] = down_ref[:, q * 128:q * 128 + 128].astype(F32)
     rows[...] = jnp.zeros_like(rows)
+    pack_links(cot_ref, cots)
+    lanes = lane_iota(8)
+    site_steps = row_iota() % 4
+    colour = (lanes // 64 + lanes // 8 % 8 + lanes % 8 + site_steps) % 2
+    code = jnp.zeros_like(site_steps)
+    for t in range(4):
+        code = jnp.where(site_steps == t, code_ref[0, t], code)
+    for mu in range(4):
+        active = jnp.logical_and(colour == code % 2, jnp.right_shift(code, mu + 1) % 2 == 1)
+        gates[mu] = jnp.where(active, 1.0, 0.0)
     for channel, plane in ((0, 0), (1, 1), (3, 2)):
         for c in range(2):
             put_row(rows, channel, c, state[PLANE + 2 * plane + c])
@@ -428,12 +415,12 @@
                 sums[nu, e, c] = state[sum_at(nu, e, c)] + jnp.where(steps == 0, below[c], 0.0)
         return carry
 
-    lax.fori_loop(0, 18, shift_body, 0)
+    lax.fori_loop(0, 18, shift_body, 0, unroll=3)
 
     def plane_body(step, carry):
         mu = step // 2
         c = step % 2
-        one = load_matrix(lambda e: dense[EDGE + mu, e, c])
+        one = load_matrix(lambda e: edges[mu, e, c])
         two = mat_mul(load_matrix(lambda e: dense[3, e, c]), load_matrix(lambda e: moved[mu, e, c]))
         loop = mat_mul(one, dagger(two))
         put_row(rows, jnp.where(mu == 0, 2, mu + 3), c, (loop[0][0][0] + loop[0][1][1] + loop[0][2][2]) / 3.0)
@@ -458,7 +445,7 @@
         sums[3, e, 1] = acc[1]
         return carry
 
-    lax.fori_loop(0, 18, lower_body, 0)
+    lax.fori_loop(0, 18, lower_body, 0, unroll=3)
 
     def force_body(step, carry):
         mu = step // 2
@@ -471,15 +458,15 @@
         parts = [part * (1.0 / 12.0) for part in parts]
         applied = anti_mul(parts, current)
         twice = anti_mul(parts, applied)
-        gate = state[GATE + mu]
+        gate = gates[mu]
         slope = jnp.zeros_like(gate)
         curve = jnp.zeros_like(gate)
         for e, (part, i, j) in enumerate(ENTRIES):
-            weight = state[cot_at(mu, e, c)]
+            weight = cots[mu, e, c]
             slope = slope + weight * applied[part][i][j]
             curve = curve + weight * twice[part][i][j]
-            w1_ref[mu, e, c] = gate * applied[part][i][j]
-            w2_ref[mu, e, c] = gate * twice[part][i][j]
+            moves_ref[0, mu, e, c] = (gate * applied[part][i][j]).astype(BF16)
+            moves_ref[1, mu, e, c] = (gate * twice[part][i][j]).astype(BF16)
         put_row(rows, 8 + mu, c, gate * slope)
         put_row(rows, 12 + mu, c, gate * curve)
         return carry
@@ -659,21 +646,38 @@
         stack_thin(source, thin, index, slot)
         return jnp.dot(weights[...], thin[:, slot_of(slot)], preferred_element_type=F32)
 
-    for index in range(1, 17):
-        h1[:, span(index)] = jnp.tanh(thin_dot(feats, p1_ref, index, index % 4)).astype(BF16)
-    for index in range(2, 16):
-        h2[:, span(index)] = jnp.tanh(wide_dot(h1, p2_ref, index, index % 4)).astype(BF16)
-    for index in range(3, 15):
-        out = jnp.tanh(wide_dot(h2, p3_ref, index, index % 4)).astype(BF16)
-        h3[:, span(index)] = out
-        taps = jnp.dot(p4_ref[...], out, preferred_element_type=F32)
-        acc = None
-        for position in range(7):
-            shifted = one_shift(chunks_of(taps[8 * position:8 * position + 8]), position)
-            acc = shifted if acc is None else [a + b for a, b in zip(acc, shifted)]
-        parts[0, :, span(index)] = jnp.concatenate(acc, axis=1)
-        parts[1, :, span(index)] = taps[56:64]
-        parts[2, :, span(index)] = taps[64:72]
+    def layer_one(half, carry):
+        for s in range(8):
+            index = 1 + 8 * half + s
+            h1[:, span(index)] = jnp.tanh(thin_dot(feats, p1_ref, index, s % 4)).astype(BF16)
+        return carry
+
+    lax.fori_loop(0, 2, layer_one, 0)
+
+    def layer_two(half, carry):
+        for s in range(7):
+            index = 2 + 7 * half + s
+            h2[:, span(index)] = jnp.tanh(wide_dot(h1, p2_ref, index, s % 4)).astype(BF16)
+        return carry
+
+    lax.fori_loop(0, 2, layer_two, 0)
+
+    def layer_three(half, carry):
+        for s in range(6):
+            index = 3 + 6 * half + s
+            out = jnp.tanh(wide_dot(h2, p3_ref, index, s % 4)).astype(BF16)
+            h3[:, span(index)] = out
+            taps = jnp.dot(p4_ref[...], out, preferred_element_type=F32)
+            acc = None
+            for position in range(7):
+                shifted = one_shift(chunks_of(taps[8 * position:8 * position + 8]), position)
+                acc = shifted if acc is None else [a + b for a, b in zip(acc, shifted)]
+            parts[0, :, span(index)] = jnp.concatenate(acc, axis=1)
+            parts[1, :, span(index)] = taps[56:64]
+            parts[2, :, span(index)] = taps[64:72]
+        return carry
+
+    lax.fori_loop(0, 2, layer_three, 0)
 
     for index in range(4, 14):
         coeff = jnp.tanh(parts[0, :, span(index)] + parts[1, :, span(index + 1)] + parts[2, :, span(index - 1)])
@@ -722,7 +726,7 @@
         grads_ref[...] = packed[...].astype(BF16)
 
 
-def update_kernel(dense, w1_ref, w2_ref, coeff_ref, out_ref, factors):
+def update_kernel(dense, moves_ref, coeff_ref, out_ref, factors):
     for mu in range(4):
         for t in range(4):
             for c in range(2):
@@ -733,7 +737,12 @@
         factor = [factors[mu, c] for c in range(2)]
         half = [0.5 * value * value for value in factor]
         for e, (part, i, j) in enumerate(ENTRIES):
-            new = [dense[mu, e, c] + factor[c] * w1_ref[mu, e, c] + half[c] * w2_ref[mu, e, c] for c in range(2)]
+            new = [
+                dense[mu, e, c]
+                + factor[c] * moves_ref[0, mu, e, c].astype(F32)
+                + half[c] * moves_ref[1, mu, e, c].astype(F32)
+                for c in range(2)
+            ]
             out_ref[mu, part, i, j, 0] = jnp.concatenate(
                 [new[0][0:4], new[1][0:4], new[0][4:8], new[1][4:8]], axis=1
             )
@@ -778,20 +787,19 @@
     field = ((4, 18, 2, 8, LANES), F32)
     space = ((3, 18, 2, 8, LANES), F32)
     edge_rows = ((70, SITES), BF16)
-    up, down, dense, slab = call(
+    up, down, dense, edges, staples, slab = call(
         face_kernel,
-        [edge_rows, edge_rows, ((10, 18, 2, 8, LANES), F32), ((12, 4, LANES), F32)],
+        [edge_rows, edge_rows, field, space, space, ((12, 4, LANES), F32)],
         [space, ((70, 4, LANES), F32)],
     )(links)
     up = send(up, 1)
     down = send(down, -1)
     (state,) = call(
         space_kernel,
-        [((334, 8, LANES), F32)],
+        [((186, 8, LANES), F32)],
         [((3, 3, 18, 2, 8, LANES), F32), ((3, 3, 18, 2, 8, LANES), F32)],
-        places=(smem, vmem, vmem),
         cost=pl.CostEstimate(flops=4_000_000_000, bytes_accessed=16_000_000, transcendentals=0),
-    )(parity + 2 * link_subset, dense, cotangent)
+    )(dense, staples)
     core = (lax.axis_index("tm") % 2).astype(jnp.int32)[None]
     (block,) = call(
         functools.partial(block_kernel, widths),
@@ -800,14 +808,18 @@
         places=(smem,) + (vmem,) * 7 + (pl.ANY,),
     )(core, up, down, slab, w_first, w_second, w_third, w_last, state)
     gathered = lax.all_to_all(block, "tm", split_axis=0, concat_axis=0, tiled=True)
-    fm, fup, fdown, applied, twice = call(
+    fm, fup, fdown, moves = call(
         time_kernel,
-        [((4, 16, SITES), BF16), ((3, 8, SITES), BF16), ((3, 8, SITES), BF16), field, field],
         [
-            space, space, field, ((70, 4, LANES), F32), ((70, 4, LANES), F32),
+            ((4, 16, SITES), BF16), ((3, 8, SITES), BF16), ((3, 8, SITES), BF16),
+            ((2, 4, 18, 2, 8, LANES), BF16),
+        ],
+        [
+            field, ((4, 8, LANES), F32), space, space, field, ((70, 4, LANES), F32), ((70, 4, LANES), F32),
             ((4, 9, 2, 8, LANES), F32), ((4, 4, 16, LANES), F32),
         ],
-    )(dense, state, up, down)
+        places=(smem,) + (vmem,) * 6,
+    )(parity + 2 * link_subset, dense, edges, state, cotangent, up, down)
     below = send(fm, 1)
     above = send(fm, -1)
     fbelow = send(fup, 2)
@@ -853,7 +865,7 @@
     grads = lax.all_to_all(grads, "tm", split_axis=0, concat_axis=0, tiled=True)
     (new_links,) = call(
         update_kernel, [(links.shape, F32)], [((4, 2, 8, LANES), F32)]
-    )(dense, applied, twice, coeff)
+    )(dense, moves, coeff)
     grad_first, grad_second, grad_third, grad_last = call(
         functools.partial(sum_kernel, widths),
         [((1, 27 * width), F32) for width in (widths[2], widths[0], widths[1], widths[3])],

time: 61.3 us -> 58.9 us (0.961)
  local copies, waits for them, and re-layouts: 5.79 us -> 1.73 us
  waiting for transfers between devices: 5.35 us -> 7.45 us
  starting transfers between devices: 24.4 us -> 26.2 us
  Pallas kernels: 23.8 us -> 22.3 us
  other arithmetic: 0.67 us -> 0.01 us
    unnamed x20 -> x16, local copies, waits for them, and re-layouts: 5.79 us -> 1.73 us
    pallas_call x2, Pallas kernels: 7.28 us -> 4.14 us  [the longest x1 2.59 us: on_device(): call(space_kernel, [((186, 8, LANES), F32)], [((3, 3, 18, 2, 8, LANES), F...]
    all_to_all x1, waiting for transfers between devices: 4.82 us -> 6.91 us  [on_device(): grads = lax.all_to_all(grads, 'tm', split_axis=0, concat_axis=0, tiled=True)]
    pallas_call x1, Pallas kernels: 9.06 us -> 10.9 us  [on_device(): call(functools.partial(conv_kernel, count == 16), [((4, 8, SITES), F32),...]
    all_to_all x1, starting transfers between devices: 3.62 us -> 5.33 us  [on_device(): lax.all_to_all(block, 'tm', split_axis=0, concat_axis=0, tiled=True)]
    add x1, other arithmetic: 0.67 us -> 0.01 us  [on_device(): parity + 2 * link_subset]
  transfers between devices with their start and end apart: 8 -> 8, of which waited for: 2 -> 2; matrix products, arithmetic and copies ran while one was open for 1% -> 0% of each run, Pallas kernels for 17% -> 14%
where the time goes in v12:
time: 58.9 us; the launch traced here: 58.5 us
  starting transfers between devices  26.2 us (44%)
  Pallas kernels  22.3 us (38%)
  waiting for transfers between devices  7.45 us (13%)
  local copies, waits for them, and re-layouts  1.73 us (3%)
  between operations  0.79 us (1%)
    ppermute x6, starting transfers between devices, send(): lax.ppermute(value, 'tm', [(i, (i + distance) % count) for i in range(cou...  14.8 us
    pallas_call x1, Pallas kernels, on_device(): call(functools.partial(conv_kernel, count == 16), [((4, 8, SITES), F32),...  10.9 us
    all_to_all x1, waiting for transfers between devices, on_device(): grads = lax.all_to_all(grads, 'tm', split_axis=0, concat_axis=0, tiled=True)  6.91 us
    all_to_all x1, starting transfers between devices, on_device(): grads = lax.all_to_all(grads, 'tm', split_axis=0, concat_axis=0, tiled=True)  6.1 us
    all_to_all x1, starting transfers between devices, on_device(): lax.all_to_all(block, 'tm', split_axis=0, concat_axis=0, tiled=True)  5.33 us
    pallas_call x1, Pallas kernels, on_device(): call(time_kernel, [((4, 16, SITES), BF16), ((3, 8, SITES), BF16), ((3, 8,...  3.31 us
    pallas_call x1, Pallas kernels, on_device(): call(space_kernel, [((186, 8, LANES), F32)], [((3, 3, 18, 2, 8, LANES), F...  2.59 us
    unnamed x16, local copies, waits for them, and re-layouts  1.73 us
  transfers between devices with their start and end apart: 8, of which 2 were waited for; matrix products, arithmetic and copies ran while one was open for 0% of the time, Pallas kernels for 14%

profile of v12, /device:TPU:0, one launch (start us, length us, event | category | flops | bytes accessed | tf_op | source)
XLA Modules:
  0.0 58.5 jit_solution(14905852286693547918)
XLA Ops:
  0.6 1.1 %copy-done = f32[4,2,3,3,1,4,512]{6,5,4,3,2,1,0:T(4,128)S(1)} copy-done((f32[4,2,3,3,1,4,512]{6,5,4,3,2,1,0:T(4,128)S(1)}, f32[4,2,3,3,1,4,512]{6,5,4,3,2,1,0:T(4,128)}, u32[]{:S(2)}) %copy-start) | copy-done | bytes 589848
  1.7 1.6 %shard_map.119 = (bf16[70,512]{1,0:T(8,128)(2,1)S(1)}, bf16[70,512]{1,0:T(8,128)(2,1)S(1)}, f32[4,18,2,8,128]{4,3,2,1,0:T(8,128)S(1)}, f32[3,18,2,8,128]{4,3,2,1...) custom-call(f32[4,2,3,3,1,4,512]{6,5,4,3,2,1,0:T(4,128)S(1)} %copy-done), custom_call_target="tpu_custom_call" | custom-call | tf_op jit(solution)/shard_map/pallas_call | solution.py:790
  3.3 0.5 collective-permute-start
  3.8 5.1 %collective-permute-start.1 = (bf16[70,512]{1,0:T(8,128)(2,1)S(1)}, bf16[70,512]{1,0:T(8,128)(2,1)S(1)}, u32[]{:S(2)}, u32[]{:S(2)}) collective-permute-start(bf16[70,512]{1,0:T(8,128)(2,1)S(1)} %get-tuple-element.33), channel_id=1, source_target_pairs={{0,15},{1,0},{2,1},{3,2},{4,3},{5,4},{6,5},{7,6},{8,7},{9,8},{10,9... | collective-permute-start | bytes 215048 | tf_op jit(solution)/shard_map/ppermute | solution.py:783
  8.8 2.6 %shard_map.120.state.after_ref = f32[186,8,128]{2,1,0:T(8,128)S(1)} custom-call(f32[4,18,2,8,128]{4,3,2,1,0:T(8,128)S(1)} %get-tuple-element.29.dense, f32[3,18,2,8,128]{4,3,2,1,0:T(8,128)S(1)} %get-tuple-element.31.time_staples), custom_call_target="tpu_custom_call" | custom-call | flops 4000000000 | bytes 16000000 | tf_op jit(solution)/shard_map/pallas_call | solution.py:797
  11.4 0.0 copy-start.3
  11.4 0.0 copy-start.2
  11.5 0.0 copy-start.5
  11.5 0.6 %copy-done.3 = bf16[1296]{0:T(1024)(128)(2,1)S(1)} copy-done((bf16[1296]{0:T(1024)(128)(2,1)S(1)}, bf16[1296]{0:T(1024)(128)(2,1)}, u32[]{:S(2)}) %copy-start.3) | copy-done | bytes 2616
  12.1 0.0 copy-done.2
  12.1 0.0 copy-done.5
  12.1 0.9 %shard_map.122 = bf16[16,64,128]{2,1,0:T(8,128)(2,1)} custom-call(s32[1]{0:T(128)} %bitcast.core_ref, bf16[70,512]{1,0:T(8,128)(2,1)S(1)} %collective-permute-done.up_ref, bf16[70,512]{1,0:T(8,128)(2,1)S(1)} %collective-permute-done.1.down_ref, f32[12,4,128]{2,1,0:T(4,128)S(1)} %get-tuple-element.38.slab, bf16[216]{0:T(256)(128)(2,1)S(1)} %copy-done.4, ...), custom_call_target="tpu_custom_call" | custom-call | tf_op jit(solution)/shard_map/pallas_call | solution.py:804
  13.0 5.3 %all-to-all-start = ((bf16[16,64,128]{2,1,0:T(8,128)(2,1)}), bf16[16,64,128]{2,1,0:T(8,128)(2,1)S(1)}, u32[]{:S(2)}, u32[]{:S(2)}) async-start(bf16[16,64,128]{2,1,0:T(8,128)(2,1)} %shard_map.122), calls=%async_computation | async-start | bytes 524288 | tf_op jit(solution)/shard_map/all_to_all | solution.py:810
  18.4 3.3 %shard_map.121 = (bf16[4,16,512]{2,1,0:T(8,128)(2,1)S(1)}, bf16[3,8,512]{2,1,0:T(8,128)(2,1)S(1)}, bf16[3,8,512]{2,1,0:T(8,128)(2,1)S(1)}, bf16[2,4,18,2,8,128]{5,4,3,2,1,0:T(8,128)(2,1)S(1)}) custom-call(s32[1,4]{1,0:T(1,128)S(1)} %multiply_add_fusion.code_ref, f32[4,18,2,8,128]{4,3,2,1,0:T(8,128)S(1)} %get-tuple-element.29.dense, ...), custom_call_target="tpu_custom_call" | custom-call | tf_op jit(solution)/shard_map/pallas_call | solution.py:811
  21.7 0.5 collective-permute-start.2
  22.2 4.0 %collective-permute-start.3 = (bf16[4,16,512]{2,1,0:T(8,128)(2,1)S(1)}, bf16[4,16,512]{2,1,0:T(8,128)(2,1)S(1)}, u32[]{:S(2)}, u32[]{:S(2)}) collective-permute-start(bf16[4,16,512]{2,1,0:T(8,128)(2,1)S(1)} %get-tuple-element.35.fm_ref), channel_id=1, source_target_pairs={{0,15},{1,0},{2,1},{3,2},{4,3},{5,4},{6,5},{7,6},{8,7},{9,8},{10,9... | collective-permute-start | bytes 196616 | tf_op jit(solution)/shard_map/ppermute | solution.py:783
  26.2 4.7 %collective-permute-start.5 = (bf16[3,8,512]{2,1,0:T(8,128)(2,1)S(1)}, bf16[3,8,512]{2,1,0:T(8,128)(2,1)S(1)}, u32[]{:S(2)}, u32[]{:S(2)}) collective-permute-start(bf16[3,8,512]{2,1,0:T(8,128)(2,1)S(1)} %get-tuple-element.37), channel_id=1, source_target_pairs={{0,14},{1,15},{2,0},{3,1},{4,2},{5,3},{6,4},{7,5},{8,6},{9,7},{10,... | collective-permute-start | bytes 73736 | tf_op jit(solution)/shard_map/ppermute | solution.py:783
  31.0 1.3 %shard_map.123 = (f32[2,4,128]{2,1,0:T(4,128)S(1)}, bf16[48,72]{1,0:T(8,128)(2,1)S(1)}, bf16[48,432]{1,0:T(8,128)(2,1)S(1)}, bf16[48,432]{1,0:T(8,128)(2,1)S(1)}...) custom-call(bf16[16,64,128]{2,1,0:T(8,128)(2,1)S(1)} %all-to-all-don, ...), custom_call_target="tpu_custom_call" | custom-call | tf_op jit(solution)/shard_map/pallas_call | solution.py:834
  32.2 0.5 collective-permute-done.4.fbelow_ref
  32.8 10.9 %shard_map.124 = (f32[4,8,512]{2,1,0:T(8,128)S(1)}, bf16[16,27,128]{2,1,0:T(8,128)(2,1)}) custom-call(bf16[4,16,512]{2,1,0:T(8,128)(2,1)S(1)} %get-tuple-element.35.fm_ref, bf16[4,16,512]{2,1,0:T(8,128)(2,1)S(1)} %collective-permute-done.2.below_ref, bf16[4,16,512]{2,1,0:T(8,128)(2,1)S(1)} %collective-permute-done.3.above_ref, ...), custom_call_target="tpu_custom_call" | custom-call | tf_op jit(solution)/shard_map/pallas_call | solution.py:848
  43.7 6.1 %all-to-all-start.1 = ((bf16[16,27,128]{2,1,0:T(8,128)(2,1)}), bf16[16,27,128]{2,1,0:T(8,128)(2,1)S(1)}, u32[]{:S(2)}, u32[]{:S(2)}) async-start(bf16[16,27,128]{2,1,0:T(8,128)(2,1)} %get-tuple-element.48), calls=%async_computation.1 | async-start | bytes 262144 | tf_op jit(solution)/shard_map/all_to_all | solution.py:865
  49.8 1.0 %shard_map.125 = f32[4,2,3,3,1,4,512]{6,5,4,3,2,1,0:T(4,128)} custom-call(f32[4,18,2,8,128]{4,3,2,1,0:T(8,128)S(1)} %get-tuple-element.29.dense, bf16[2,4,18,2,8,128]{5,4,3,2,1,0:T(8,128)(2,1)S(1)} %get-tuple-element.34.moves_ref, f32[4,8,512]{2,1,0:T(8,128)S(1)} %get-tuple-element.47.coeff_ref), custom_call_target="tpu_custom_call" | custom-call | tf_op jit(solution)/shard_map/pallas_call | solution.py:866
  50.8 6.9 %all-to-all-done.1.parts_ref = bf16[16,27,128]{2,1,0:T(8,128)(2,1)S(1)} async-done(((bf16[16,27,128]{2,1,0:T(8,128)(2,1)}), bf16[16,27,128]{2,1,0:T(8,128)(2,1)S(1)}, u32[]{:S(2)}, u32[]{:S(2)}) %all-to-all-start.1) | async-done | bytes 110624 | tf_op jit(solution)/shard_map/all_to_all | solution.py:865
  57.7 0.8 %shard_map.126 = (f32[1,216]{1,0:T(1,128)}, f32[1,1296]{1,0:T(1,128)}, f32[1,1296]{1,0:T(1,128)}, f32[1,108]{1,0:T(1,128)}) custom-call(bf16[16,27,128]{2,1,0:T(8,128)(2,1)S(1)} %all-to-all-done.1.parts_ref), custom_call_target="tpu_custom_call" | custom-call | tf_op jit(solution)/shard_map/pallas_call | solution.py:869
  (17 shorter events, 0.0 us)
Async XLA Ops:
  0.6 1.1 %copy-start = (f32[4,2,3,3,1,4,512]{6,5,4,3,2,1,0:T(4,128)S(1)}, f32[4,2,3,3,1,4,512]{6,5,4,3,2,1,0:T(4,128)}, u32[]{:S(2)}) copy-start(f32[4,2,3,3,1,4,512]{6,5,4,3,2,1,0:T(4,128)} %links_ref.1) | copy-start | bytes 1769476
  3.3 8.2 %collective-permute-start = (bf16[70,512]{1,0:T(8,128)(2,1)S(1)}, bf16[70,512]{1,0:T(8,128)(2,1)S(1)}, u32[]{:S(2)}, u32[]{:S(2)}) collective-permute-start(bf16[70,512]{1,0:T(8,128)(2,1)S(1)} %get-tuple-element.32), channel_id=1, source_target_pairs={{0,1},{1,2},{2,3},{3,4},{4,5},{5,6},{6,7},{7,8},{8,9},{9,10},{10,1... | collective-permute-start | bytes 215048 | tf_op jit(solution)/shard_map/ppermute | solution.py:783
  3.8 7.7 %collective-permute-start.1 = (bf16[70,512]{1,0:T(8,128)(2,1)S(1)}, bf16[70,512]{1,0:T(8,128)(2,1)S(1)}, u32[]{:S(2)}, u32[]{:S(2)}) collective-permute-start(bf16[70,512]{1,0:T(8,128)(2,1)S(1)} %get-tuple-element.33), channel_id=1, source_target_pairs={{0,15},{1,0},{2,1},{3,2},{4,3},{5,4},{6,5},{7,6},{8,7},{9,8},{10,9... | collective-permute-start | bytes 215048 | tf_op jit(solution)/shard_map/ppermute | solution.py:783
  11.4 0.7 %copy-start.3 = (bf16[1296]{0:T(1024)(128)(2,1)S(1)}, bf16[1296]{0:T(1024)(128)(2,1)}, u32[]{:S(2)}) copy-start(bf16[1296]{0:T(1024)(128)(2,1)} %w3_ref.1) | copy-start | bytes 7780
  11.4 0.7 %copy-start.2 = (bf16[1296]{0:T(1024)(128)(2,1)S(1)}, bf16[1296]{0:T(1024)(128)(2,1)}, u32[]{:S(2)}) copy-start(bf16[1296]{0:T(1024)(128)(2,1)} %w2_ref.1) | copy-start | bytes 7780
  11.5 0.7 %copy-start.4 = (bf16[216]{0:T(256)(128)(2,1)S(1)}, bf16[216]{0:T(256)(128)(2,1)}, u32[]{:S(2)}) copy-start(bf16[216]{0:T(256)(128)(2,1)} %w1_ref.1) | copy-start | bytes 1300
  11.5 0.7 %copy-start.5 = (bf16[108]{0:T(256)(128)(2,1)S(1)}, bf16[108]{0:T(256)(128)(2,1)}, u32[]{:S(2)}) copy-start(bf16[108]{0:T(256)(128)(2,1)} %w4_ref.1) | copy-start | bytes 652
  13.0 5.3 %copy-start.6 = (s32[1,4]{1,0:T(1,128)S(1)}, s32[1,4]{1,0:T(1,128)}, u32[]{:S(2)}) copy-start(s32[1,4]{1,0:T(1,128)} %param.10) | copy-start | bytes 52
  13.0 5.4 %copy-start.7 = (s32[1,4]{1,0:T(1,128)S(1)}, s32[1,4]{1,0:T(1,128)}, u32[]{:S(2)}) copy-start(s32[1,4]{1,0:T(1,128)} %param.11) | copy-start | bytes 52
  13.0 5.4 %copy-start.1 = (bf16[4,2,3,3,1,4,512]{6,5,4,3,2,1,0:T(4,128)(2,1)S(1)}, bf16[4,2,3,3,1,4,512]{6,5,4,3,2,1,0:T(4,128)(2,1)}, u32[]{:S(2)}) copy-start(bf16[4,2,3,3,1,4,512]{6,5,4,3,2,1,0:T(4,128)(2,1)} %cot_ref.1) | copy-start | bytes 884740
  13.0 17.9 %all-to-all-start = ((bf16[16,64,128]{2,1,0:T(8,128)(2,1)}), bf16[16,64,128]{2,1,0:T(8,128)(2,1)S(1)}, u32[]{:S(2)}, u32[]{:S(2)}) async-start(bf16[16,64,128]{2,1,0:T(8,128)(2,1)} %shard_map.122), calls=%async_computation | async-start | bytes 524288 | tf_op jit(solution)/shard_map/all_to_all | solution.py:810
  21.7 11.0 %collective-permute-start.2 = (bf16[4,16,512]{2,1,0:T(8,128)(2,1)S(1)}, bf16[4,16,512]{2,1,0:T(8,128)(2,1)S(1)}, u32[]{:S(2)}, u32[]{:S(2)}) collective-permute-start(bf16[4,16,512]{2,1,0:T(8,128)(2,1)S(1)} %get-tuple-element.35.fm_ref), channel_id=1, source_target_pairs={{0,1},{1,2},{2,3},{3,4},{4,5},{5,6},{6,7},{7,8},{8,9},{9,10},{10,1... | collective-permute-start | bytes 196616 | tf_op jit(solution)/shard_map/ppermute | solution.py:783
  22.2 10.6 %collective-permute-start.3 = (bf16[4,16,512]{2,1,0:T(8,128)(2,1)S(1)}, bf16[4,16,512]{2,1,0:T(8,128)(2,1)S(1)}, u32[]{:S(2)}, u32[]{:S(2)}) collective-permute-start(bf16[4,16,512]{2,1,0:T(8,128)(2,1)S(1)} %get-tuple-element.35.fm_ref), channel_id=1, source_target_pairs={{0,15},{1,0},{2,1},{3,2},{4,3},{5,4},{6,5},{7,6},{8,7},{9,8},{10,9... | collective-permute-start | bytes 196616 | tf_op jit(solution)/shard_map/ppermute | solution.py:783
  26.2 6.5 %collective-permute-start.4 = (bf16[3,8,512]{2,1,0:T(8,128)(2,1)S(1)}, bf16[3,8,512]{2,1,0:T(8,128)(2,1)S(1)}, u32[]{:S(2)}, u32[]{:S(2)}) collective-permute-start(bf16[3,8,512]{2,1,0:T(8,128)(2,1)S(1)} %get-tuple-element.36), channel_id=1, source_target_pairs={{0,2},{1,3},{2,4},{3,5},{4,6},{5,7},{6,8},{7,9},{8,10},{9,11},{10,... | collective-permute-start | bytes 73736 | tf_op jit(solution)/shard_map/ppermute | solution.py:783
  26.2 6.5 %collective-permute-start.5 = (bf16[3,8,512]{2,1,0:T(8,128)(2,1)S(1)}, bf16[3,8,512]{2,1,0:T(8,128)(2,1)S(1)}, u32[]{:S(2)}, u32[]{:S(2)}) collective-permute-start(bf16[3,8,512]{2,1,0:T(8,128)(2,1)S(1)} %get-tuple-element.37), channel_id=1, source_target_pairs={{0,14},{1,15},{2,0},{3,1},{4,2},{5,3},{6,4},{7,5},{8,6},{9,7},{10,... | collective-permute-start | bytes 73736 | tf_op jit(solution)/shard_map/ppermute | solution.py:783
  43.7 14.0 %all-to-all-start.1 = ((bf16[16,27,128]{2,1,0:T(8,128)(2,1)}), bf16[16,27,128]{2,1,0:T(8,128)(2,1)S(1)}, u32[]{:S(2)}, u32[]{:S(2)}) async-start(bf16[16,27,128]{2,1,0:T(8,128)(2,1)} %get-tuple-element.48), calls=%async_computation.1 | async-start | bytes 262144 | tf_op jit(solution)/shard_map/all_to_all | solution.py:865

commit v13 on v12

--- a/solution.py
+++ b/solution.py
@@ -622,7 +622,7 @@
     split, fm_ref, below_ref, above_ref, fbelow_ref, fabove_ref, loops_ref,
     p1_ref, p2_ref, p3_ref, p4_ref, b2_ref, b3_ref, b4_ref,
     coeff_ref, grads_ref,
-    feats, mixed, h1, h2, h3, parts, lasts, g3, g2, g1, wide, thin, packed,
+    feats, mixed, h1, h2, h3, parts, lasts, g3, g2, g1, wide, wide_back, wide_first, thin, thin_back, packed,
 ):
     row8 = lax.broadcasted_iota(jnp.int32, (8, SITES), 0)
     loop_re = jnp.concatenate([loops_ref[0, q:q + 1, :] for q in range(4)], axis=1)
@@ -638,48 +638,35 @@
             feats[:, span(base + j)] = value[0:8] + loops
             mixed[:, span(base + j)] = value[8:16]
 
-    def wide_dot(source, weights, index, slot):
-        stack_wide(source, wide, index, slot)
-        return jnp.dot(weights[...], wide[:, slot_of(slot)], preferred_element_type=F32)
-
-    def thin_dot(source, weights, index, slot):
-        stack_thin(source, thin, index, slot)
-        return jnp.dot(weights[...], thin[:, slot_of(slot)], preferred_element_type=F32)
-
-    def layer_one(half, carry):
-        for s in range(8):
-            index = 1 + 8 * half + s
-            h1[:, span(index)] = jnp.tanh(thin_dot(feats, p1_ref, index, s % 4)).astype(BF16)
-        return carry
-
-    lax.fori_loop(0, 2, layer_one, 0)
-
-    def layer_two(half, carry):
-        for s in range(7):
-            index = 2 + 7 * half + s
-            h2[:, span(index)] = jnp.tanh(wide_dot(h1, p2_ref, index, s % 4)).astype(BF16)
-        return carry
-
-    lax.fori_loop(0, 2, layer_two, 0)
-
-    def layer_three(half, carry):
-        for s in range(6):
-            index = 3 + 6 * half + s
-            out = jnp.tanh(wide_dot(h2, p3_ref, index, s % 4)).astype(BF16)
-            h3[:, span(index)] = out
-            taps = jnp.dot(p4_ref[...], out, preferred_element_type=F32)
-            acc = None
-            for position in range(7):
-                shifted = one_shift(chunks_of(taps[8 * position:8 * position + 8]), position)
-                acc = shifted if acc is None else [a + b for a, b in zip(acc, shifted)]
-            parts[0, :, span(index)] = jnp.concatenate(acc, axis=1)
-            parts[1, :, span(index)] = taps[56:64]
-            parts[2, :, span(index)] = taps[64:72]
-        return carry
-
-    lax.fori_loop(0, 2, layer_three, 0)
-
-    for index in range(4, 14):
+    own = span(7, 4)
+    contract = (((1,), (1,)), ((), ()))
+
+    def own_slot(index, others):
+        return index - 7 if 7 <= index < 11 else 4 + others.index(index)
+
+    def dot(weights, stack, slot):
+        return jnp.dot(weights[...], stack[:, slot_of(slot)], preferred_element_type=F32)
+
+    def first_dot(index):
+        h1[:, span(index)] = jnp.tanh(dot(p1_ref, thin, index % 4)).astype(BF16)
+
+    def second_dot(index):
+        h2[:, span(index)] = jnp.tanh(dot(p2_ref, wide, index % 2)).astype(BF16)
+
+    def third_dot(index):
+        h3[:, span(index)] = jnp.tanh(dot(p3_ref, wide, 2 + index % 2)).astype(BF16)
+
+    def taps_of(index):
+        taps = jnp.dot(p4_ref[...], h3[:, span(index)], preferred_element_type=F32)
+        acc = None
+        for position in range(7):
+            shifted = one_shift(chunks_of(taps[8 * position:8 * position + 8]), position)
+            acc = shifted if acc is None else [a + b for a, b in zip(acc, shifted)]
+        parts[0, :, span(index)] = jnp.concatenate(acc, axis=1)
+        parts[1, :, span(index)] = taps[56:64]
+        parts[2, :, span(index)] = taps[64:72]
+
+    def last_of(index):
         coeff = jnp.tanh(parts[0, :, span(index)] + parts[1, :, span(index + 1)] + parts[2, :, span(index - 1)])
         blend = mixed[:, span(index)]
         value = (blend + coeff * pltpu.roll(blend, 4, 0)) * (1.0 - coeff * coeff)
@@ -687,22 +674,52 @@
         if 7 <= index < 11:
             coeff_ref[index - 7] = coeff
 
-    own = span(7, 4)
-    contract = (((1,), (1,)), ((), ()))
-    for index in (5, 6, 11, 12, 7, 8, 9, 10):
-        out = thin_dot(lasts, b4_ref, index, (index + 1) % 4)
+    halo3, halo2 = (5, 6, 11, 12), (6, 11)
+
+    def back_third(index):
+        out = dot(b4_ref, thin_back, own_slot(index, halo3))
         g3[:, span(index)] = (out * one_minus_square(h3[:, span(index)])).astype(BF16)
-    grad_last = lax.dot_general(thin[...], h3[:, own], contract, preferred_element_type=F32)
-    for index in (6, 11, 7, 8, 9, 10):
-        out = wide_dot(g3, b3_ref, index, (index + 1) % 4)
+
+    def back_second(index):
+        out = dot(b3_ref, wide_back, own_slot(index, halo2))
         g2[:, span(index)] = (out * one_minus_square(h2[:, span(index)])).astype(BF16)
-    grad_third = lax.dot_general(wide[...], h2[:, own], contract, preferred_element_type=F32)
-    for index in (7, 8, 9, 10):
-        out = wide_dot(g2, b2_ref, index, (index + 1) % 4)
+
+    def back_first(index):
+        out = dot(b2_ref, wide_first, index - 7)
         g1[:, slot_of(index - 7)] = (out * one_minus_square(h1[:, span(index)])).astype(BF16)
-    grad_second = lax.dot_general(wide[...], h1[:, own], contract, preferred_element_type=F32)
-    for index in (7, 8, 9, 10):
-        stack_thin(feats, thin, index, index - 7)
+
+    stages = (
+        (0, 1, 17, lambda i: stack_thin(feats, thin, i, i % 4)),
+        (1, 1, 17, first_dot),
+        (3, 2, 16, lambda i: stack_wide(h1, wide, i, i % 2)),
+        (4, 2, 16, second_dot),
+        (6, 3, 15, lambda i: stack_wide(h2, wide, i, 2 + i % 2)),
+        (7, 3, 15, third_dot),
+        (8, 3, 15, taps_of),
+        (10, 4, 14, last_of),
+        (12, 5, 13, lambda i: stack_thin(lasts, thin_back, i, own_slot(i, halo3))),
+        (13, 5, 13, back_third),
+        (15, 6, 12, lambda i: stack_wide(g3, wide_back, i, own_slot(i, halo2))),
+        (16, 6, 12, back_second),
+        (18, 7, 11, lambda i: stack_wide(g2, wide_first, i, i - 7)),
+        (19, 7, 11, back_first),
+    )
+    for step in range(1, 30):
+        for delay, low, high, task in reversed(stages):
+            if low <= step - delay < high:
+                task(step - delay)
+        if step == 18:
+            for index in (7, 8, 9, 10):
+                stack_thin(feats, thin, index, index - 7)
+        if step == 23:
+            grad_last = lax.dot_general(
+                thin_back[:, 0:4 * SITES], h3[:, own], contract, preferred_element_type=F32
+            )
+        if step == 26:
+            grad_third = lax.dot_general(
+                wide_back[:, 0:4 * SITES], h2[:, own], contract, preferred_element_type=F32
+            )
+    grad_second = lax.dot_general(wide_first[...], h1[:, own], contract, preferred_element_type=F32)
     grad_first = lax.dot_general(g1[...], thin[...], contract, preferred_element_type=F32)
 
     spread, keep = selectors()
@@ -851,7 +868,8 @@
         [
             ((8, window), F32), ((8, window), F32), ((H, window), BF16), ((H, window), BF16), ((H, window), BF16),
             ((3, 8, window), F32), ((8, window), F32), ((H, window), BF16), ((H, window), BF16), ((H, 4 * SITES), BF16),
-            ((432, 4 * SITES), BF16), ((72, 4 * SITES), BF16), ((432, LANES), F32),
+            ((432, 4 * SITES), BF16), ((432, 6 * SITES), BF16), ((432, 4 * SITES), BF16),
+            ((72, 4 * SITES), BF16), ((72, 8 * SITES), BF16), ((432, LANES), F32),
         ],
         limit=20 * 1024 * 1024,
     )(fm, below, above, fbelow, fabove, loops, p1, p2, p3, p4, b2, b3, b4)

time: 58.9 us -> 57.4 us (0.975)
  Pallas kernels: 22.3 us -> 20.8 us
    pallas_call x1, Pallas kernels: 10.9 us -> 9.39 us  [on_device(): call(functools.partial(conv_kernel, count == 16), [((4, 8, SITES), F32),...]
where the time goes in v13:
time: 57.4 us; the launch traced here: 57 us
  starting transfers between devices  26.2 us (46%)
  Pallas kernels  20.8 us (36%)
  waiting for transfers between devices  7.45 us (13%)
  local copies, waits for them, and re-layouts  1.73 us (3%)
  between operations  0.79 us (1%)
    ppermute x6, starting transfers between devices, send(): lax.ppermute(value, 'tm', [(i, (i + distance) % count) for i in range(cou...  14.8 us
    pallas_call x1, Pallas kernels, on_device(): call(functools.partial(conv_kernel, count == 16), [((4, 8, SITES), F32),...  9.39 us
    all_to_all x1, waiting for transfers between devices, on_device(): grads = lax.all_to_all(grads, 'tm', split_axis=0, concat_axis=0, tiled=True)  6.91 us
    all_to_all x1, starting transfers between devices, on_device(): grads = lax.all_to_all(grads, 'tm', split_axis=0, concat_axis=0, tiled=True)  6.1 us
    all_to_all x1, starting transfers between devices, on_device(): lax.all_to_all(block, 'tm', split_axis=0, concat_axis=0, tiled=True)  5.33 us
    pallas_call x1, Pallas kernels, on_device(): call(time_kernel, [((4, 16, SITES), BF16), ((3, 8, SITES), BF16), ((3, 8,...  3.31 us
    pallas_call x1, Pallas kernels, on_device(): call(space_kernel, [((186, 8, LANES), F32)], [((3, 3, 18, 2, 8, LANES), F...  2.59 us
    unnamed x16, local copies, waits for them, and re-layouts  1.73 us
  transfers between devices with their start and end apart: 8, of which 2 were waited for; matrix products, arithmetic and copies ran while one was open for 0% of the time, Pallas kernels for 14%

profile of v13, /device:TPU:0, one launch (start us, length us, event | category | flops | bytes accessed | tf_op | source)
XLA Modules:
  0.0 57.0 jit_solution(11340825058921884071)
XLA Ops:
  0.6 1.1 %copy-done = f32[4,2,3,3,1,4,512]{6,5,4,3,2,1,0:T(4,128)S(1)} copy-done((f32[4,2,3,3,1,4,512]{6,5,4,3,2,1,0:T(4,128)S(1)}, f32[4,2,3,3,1,4,512]{6,5,4,3,2,1,0:T(4,128)}, u32[]{:S(2)}) %copy-start) | copy-done | bytes 589848
  1.7 1.6 %shard_map.119 = (bf16[70,512]{1,0:T(8,128)(2,1)S(1)}, bf16[70,512]{1,0:T(8,128)(2,1)S(1)}, f32[4,18,2,8,128]{4,3,2,1,0:T(8,128)S(1)}, f32[3,18,2,8,128]{4,3,2,1...) custom-call(f32[4,2,3,3,1,4,512]{6,5,4,3,2,1,0:T(4,128)S(1)} %copy-done), custom_call_target="tpu_custom_call" | custom-call | tf_op jit(solution)/shard_map/pallas_call | solution.py:807
  3.3 0.5 collective-permute-start
  3.8 5.1 %collective-permute-start.1 = (bf16[70,512]{1,0:T(8,128)(2,1)S(1)}, bf16[70,512]{1,0:T(8,128)(2,1)S(1)}, u32[]{:S(2)}, u32[]{:S(2)}) collective-permute-start(bf16[70,512]{1,0:T(8,128)(2,1)S(1)} %get-tuple-element.33), channel_id=1, source_target_pairs={{0,15},{1,0},{2,1},{3,2},{4,3},{5,4},{6,5},{7,6},{8,7},{9,8},{10,9... | collective-permute-start | bytes 215048 | tf_op jit(solution)/shard_map/ppermute | solution.py:800
  8.8 2.6 %shard_map.120.state.after_ref = f32[186,8,128]{2,1,0:T(8,128)S(1)} custom-call(f32[4,18,2,8,128]{4,3,2,1,0:T(8,128)S(1)} %get-tuple-element.29.dense, f32[3,18,2,8,128]{4,3,2,1,0:T(8,128)S(1)} %get-tuple-element.31.time_staples), custom_call_target="tpu_custom_call" | custom-call | flops 4000000000 | bytes 16000000 | tf_op jit(solution)/shard_map/pallas_call | solution.py:814
  11.4 0.0 copy-start.3
  11.4 0.0 copy-start.2
  11.5 0.0 copy-start.4
  11.5 0.6 %copy-done.3 = bf16[1296]{0:T(1024)(128)(2,1)S(1)} copy-done((bf16[1296]{0:T(1024)(128)(2,1)S(1)}, bf16[1296]{0:T(1024)(128)(2,1)}, u32[]{:S(2)}) %copy-start.3) | copy-done | bytes 2616
  12.1 0.0 copy-done.2
  12.1 0.0 copy-done.5
  12.1 0.9 %shard_map.122 = bf16[16,64,128]{2,1,0:T(8,128)(2,1)} custom-call(s32[1]{0:T(128)} %bitcast.core_ref, bf16[70,512]{1,0:T(8,128)(2,1)S(1)} %collective-permute-done.up_ref, bf16[70,512]{1,0:T(8,128)(2,1)S(1)} %collective-permute-done.1.down_ref, f32[12,4,128]{2,1,0:T(4,128)S(1)} %get-tuple-element.38.slab, bf16[216]{0:T(256)(128)(2,1)S(1)} %copy-done.4, ...), custom_call_target="tpu_custom_call" | custom-call | tf_op jit(solution)/shard_map/pallas_call | solution.py:821
  13.0 5.3 %all-to-all-start = ((bf16[16,64,128]{2,1,0:T(8,128)(2,1)}), bf16[16,64,128]{2,1,0:T(8,128)(2,1)S(1)}, u32[]{:S(2)}, u32[]{:S(2)}) async-start(bf16[16,64,128]{2,1,0:T(8,128)(2,1)} %shard_map.122), calls=%async_computation | async-start | bytes 524288 | tf_op jit(solution)/shard_map/all_to_all | solution.py:827
  18.4 3.3 %shard_map.121 = (bf16[4,16,512]{2,1,0:T(8,128)(2,1)S(1)}, bf16[3,8,512]{2,1,0:T(8,128)(2,1)S(1)}, bf16[3,8,512]{2,1,0:T(8,128)(2,1)S(1)}, bf16[2,4,18,2,8,128]{5,4,3,2,1,0:T(8,128)(2,1)S(1)}) custom-call(s32[1,4]{1,0:T(1,128)S(1)} %multiply_add_fusion.code_ref, f32[4,18,2,8,128]{4,3,2,1,0:T(8,128)S(1)} %get-tuple-element.29.dense, ...), custom_call_target="tpu_custom_call" | custom-call | tf_op jit(solution)/shard_map/pallas_call | solution.py:828
  21.7 0.5 collective-permute-start.2
  22.2 4.0 %collective-permute-start.3 = (bf16[4,16,512]{2,1,0:T(8,128)(2,1)S(1)}, bf16[4,16,512]{2,1,0:T(8,128)(2,1)S(1)}, u32[]{:S(2)}, u32[]{:S(2)}) collective-permute-start(bf16[4,16,512]{2,1,0:T(8,128)(2,1)S(1)} %get-tuple-element.35.fm_ref), channel_id=1, source_target_pairs={{0,15},{1,0},{2,1},{3,2},{4,3},{5,4},{6,5},{7,6},{8,7},{9,8},{10,9... | collective-permute-start | bytes 196616 | tf_op jit(solution)/shard_map/ppermute | solution.py:800
  26.2 4.7 %collective-permute-start.5 = (bf16[3,8,512]{2,1,0:T(8,128)(2,1)S(1)}, bf16[3,8,512]{2,1,0:T(8,128)(2,1)S(1)}, u32[]{:S(2)}, u32[]{:S(2)}) collective-permute-start(bf16[3,8,512]{2,1,0:T(8,128)(2,1)S(1)} %get-tuple-element.37), channel_id=1, source_target_pairs={{0,14},{1,15},{2,0},{3,1},{4,2},{5,3},{6,4},{7,5},{8,6},{9,7},{10,... | collective-permute-start | bytes 73736 | tf_op jit(solution)/shard_map/ppermute | solution.py:800
  31.0 1.3 %shard_map.123 = (f32[2,4,128]{2,1,0:T(4,128)S(1)}, bf16[48,72]{1,0:T(8,128)(2,1)S(1)}, bf16[48,432]{1,0:T(8,128)(2,1)S(1)}, bf16[48,432]{1,0:T(8,128)(2,1)S(1)}...) custom-call(bf16[16,64,128]{2,1,0:T(8,128)(2,1)S(1)} %all-to-all-don, ...), custom_call_target="tpu_custom_call" | custom-call | tf_op jit(solution)/shard_map/pallas_call | solution.py:851
  32.2 0.5 collective-permute-done.4.fbelow_ref
  32.8 9.4 %shard_map.124 = (f32[4,8,512]{2,1,0:T(8,128)S(1)}, bf16[16,27,128]{2,1,0:T(8,128)(2,1)}) custom-call(bf16[4,16,512]{2,1,0:T(8,128)(2,1)S(1)} %get-tuple-element.35.fm_ref, bf16[4,16,512]{2,1,0:T(8,128)(2,1)S(1)} %collective-permute-done.2.below_ref, bf16[4,16,512]{2,1,0:T(8,128)(2,1)S(1)} %collective-permute-done.3.above_ref, ...), custom_call_target="tpu_custom_call" | custom-call | tf_op jit(solution)/shard_map/pallas_call | solution.py:865
  42.2 6.1 %all-to-all-start.1 = ((bf16[16,27,128]{2,1,0:T(8,128)(2,1)}), bf16[16,27,128]{2,1,0:T(8,128)(2,1)S(1)}, u32[]{:S(2)}, u32[]{:S(2)}) async-start(bf16[16,27,128]{2,1,0:T(8,128)(2,1)} %get-tuple-element.48), calls=%async_computation.1 | async-start | bytes 262144 | tf_op jit(solution)/shard_map/all_to_all | solution.py:883
  48.3 1.0 %shard_map.125 = f32[4,2,3,3,1,4,512]{6,5,4,3,2,1,0:T(4,128)} custom-call(f32[4,18,2,8,128]{4,3,2,1,0:T(8,128)S(1)} %get-tuple-element.29.dense, bf16[2,4,18,2,8,128]{5,4,3,2,1,0:T(8,128)(2,1)S(1)} %get-tuple-element.34.moves_ref, f32[4,8,512]{2,1,0:T(8,128)S(1)} %get-tuple-element.47.coeff_ref), custom_call_target="tpu_custom_call" | custom-call | tf_op jit(solution)/shard_map/pallas_call | solution.py:884
  49.3 6.9 %all-to-all-done.1.parts_ref = bf16[16,27,128]{2,1,0:T(8,128)(2,1)S(1)} async-done(((bf16[16,27,128]{2,1,0:T(8,128)(2,1)}), bf16[16,27,128]{2,1,0:T(8,128)(2,1)S(1)}, u32[]{:S(2)}, u32[]{:S(2)}) %all-to-all-start.1) | async-done | bytes 110624 | tf_op jit(solution)/shard_map/all_to_all | solution.py:883
  56.2 0.8 %shard_map.126 = (f32[1,216]{1,0:T(1,128)}, f32[1,1296]{1,0:T(1,128)}, f32[1,1296]{1,0:T(1,128)}, f32[1,108]{1,0:T(1,128)}) custom-call(bf16[16,27,128]{2,1,0:T(8,128)(2,1)S(1)} %all-to-all-done.1.parts_ref), custom_call_target="tpu_custom_call" | custom-call | tf_op jit(solution)/shard_map/pallas_call | solution.py:887
  (17 shorter events, 0.0 us)
Async XLA Ops:
  0.6 1.1 %copy-start = (f32[4,2,3,3,1,4,512]{6,5,4,3,2,1,0:T(4,128)S(1)}, f32[4,2,3,3,1,4,512]{6,5,4,3,2,1,0:T(4,128)}, u32[]{:S(2)}) copy-start(f32[4,2,3,3,1,4,512]{6,5,4,3,2,1,0:T(4,128)} %links_ref.1) | copy-start | bytes 1769476
  3.3 8.2 %collective-permute-start = (bf16[70,512]{1,0:T(8,128)(2,1)S(1)}, bf16[70,512]{1,0:T(8,128)(2,1)S(1)}, u32[]{:S(2)}, u32[]{:S(2)}) collective-permute-start(bf16[70,512]{1,0:T(8,128)(2,1)S(1)} %get-tuple-element.32), channel_id=1, source_target_pairs={{0,1},{1,2},{2,3},{3,4},{4,5},{5,6},{6,7},{7,8},{8,9},{9,10},{10,1... | collective-permute-start | bytes 215048 | tf_op jit(solution)/shard_map/ppermute | solution.py:800
  3.8 7.7 %collective-permute-start.1 = (bf16[70,512]{1,0:T(8,128)(2,1)S(1)}, bf16[70,512]{1,0:T(8,128)(2,1)S(1)}, u32[]{:S(2)}, u32[]{:S(2)}) collective-permute-start(bf16[70,512]{1,0:T(8,128)(2,1)S(1)} %get-tuple-element.33), channel_id=1, source_target_pairs={{0,15},{1,0},{2,1},{3,2},{4,3},{5,4},{6,5},{7,6},{8,7},{9,8},{10,9... | collective-permute-start | bytes 215048 | tf_op jit(solution)/shard_map/ppermute | solution.py:800
  11.4 0.7 %copy-start.3 = (bf16[1296]{0:T(1024)(128)(2,1)S(1)}, bf16[1296]{0:T(1024)(128)(2,1)}, u32[]{:S(2)}) copy-start(bf16[1296]{0:T(1024)(128)(2,1)} %w3_ref.1) | copy-start | bytes 7780
  11.4 0.7 %copy-start.2 = (bf16[1296]{0:T(1024)(128)(2,1)S(1)}, bf16[1296]{0:T(1024)(128)(2,1)}, u32[]{:S(2)}) copy-start(bf16[1296]{0:T(1024)(128)(2,1)} %w2_ref.1) | copy-start | bytes 7780
  11.5 0.7 %copy-start.4 = (bf16[216]{0:T(256)(128)(2,1)S(1)}, bf16[216]{0:T(256)(128)(2,1)}, u32[]{:S(2)}) copy-start(bf16[216]{0:T(256)(128)(2,1)} %w1_ref.1) | copy-start | bytes 1300
  11.5 0.7 %copy-start.5 = (bf16[108]{0:T(256)(128)(2,1)S(1)}, bf16[108]{0:T(256)(128)(2,1)}, u32[]{:S(2)}) copy-start(bf16[108]{0:T(256)(128)(2,1)} %w4_ref.1) | copy-start | bytes 652
  13.0 5.3 %copy-start.6 = (s32[1,4]{1,0:T(1,128)S(1)}, s32[1,4]{1,0:T(1,128)}, u32[]{:S(2)}) copy-start(s32[1,4]{1,0:T(1,128)} %param.10) | copy-start | bytes 52
  13.0 5.4 %copy-start.7 = (s32[1,4]{1,0:T(1,128)S(1)}, s32[1,4]{1,0:T(1,128)}, u32[]{:S(2)}) copy-start(s32[1,4]{1,0:T(1,128)} %param.11) | copy-start | bytes 52
  13.0 5.4 %copy-start.1 = (bf16[4,2,3,3,1,4,512]{6,5,4,3,2,1,0:T(4,128)(2,1)S(1)}, bf16[4,2,3,3,1,4,512]{6,5,4,3,2,1,0:T(4,128)(2,1)}, u32[]{:S(2)}) copy-start(bf16[4,2,3,3,1,4,512]{6,5,4,3,2,1,0:T(4,128)(2,1)} %cot_ref.1) | copy-start | bytes 884740
  13.0 17.9 %all-to-all-start = ((bf16[16,64,128]{2,1,0:T(8,128)(2,1)}), bf16[16,64,128]{2,1,0:T(8,128)(2,1)S(1)}, u32[]{:S(2)}, u32[]{:S(2)}) async-start(bf16[16,64,128]{2,1,0:T(8,128)(2,1)} %shard_map.122), calls=%async_computation | async-start | bytes 524288 | tf_op jit(solution)/shard_map/all_to_all | solution.py:827
  21.7 11.0 %collective-permute-start.2 = (bf16[4,16,512]{2,1,0:T(8,128)(2,1)S(1)}, bf16[4,16,512]{2,1,0:T(8,128)(2,1)S(1)}, u32[]{:S(2)}, u32[]{:S(2)}) collective-permute-start(bf16[4,16,512]{2,1,0:T(8,128)(2,1)S(1)} %get-tuple-element.35.fm_ref), channel_id=1, source_target_pairs={{0,1},{1,2},{2,3},{3,4},{4,5},{5,6},{6,7},{7,8},{8,9},{9,10},{10,1... | collective-permute-start | bytes 196616 | tf_op jit(solution)/shard_map/ppermute | solution.py:800
  22.2 10.6 %collective-permute-start.3 = (bf16[4,16,512]{2,1,0:T(8,128)(2,1)S(1)}, bf16[4,16,512]{2,1,0:T(8,128)(2,1)S(1)}, u32[]{:S(2)}, u32[]{:S(2)}) collective-permute-start(bf16[4,16,512]{2,1,0:T(8,128)(2,1)S(1)} %get-tuple-element.35.fm_ref), channel_id=1, source_target_pairs={{0,15},{1,0},{2,1},{3,2},{4,3},{5,4},{6,5},{7,6},{8,7},{9,8},{10,9... | collective-permute-start | bytes 196616 | tf_op jit(solution)/shard_map/ppermute | solution.py:800
  26.2 6.5 %collective-permute-start.4 = (bf16[3,8,512]{2,1,0:T(8,128)(2,1)S(1)}, bf16[3,8,512]{2,1,0:T(8,128)(2,1)S(1)}, u32[]{:S(2)}, u32[]{:S(2)}) collective-permute-start(bf16[3,8,512]{2,1,0:T(8,128)(2,1)S(1)} %get-tuple-element.36), channel_id=1, source_target_pairs={{0,2},{1,3},{2,4},{3,5},{4,6},{5,7},{6,8},{7,9},{8,10},{9,11},{10,... | collective-permute-start | bytes 73736 | tf_op jit(solution)/shard_map/ppermute | solution.py:800
  26.2 6.5 %collective-permute-start.5 = (bf16[3,8,512]{2,1,0:T(8,128)(2,1)S(1)}, bf16[3,8,512]{2,1,0:T(8,128)(2,1)S(1)}, u32[]{:S(2)}, u32[]{:S(2)}) collective-permute-start(bf16[3,8,512]{2,1,0:T(8,128)(2,1)S(1)} %get-tuple-element.37), channel_id=1, source_target_pairs={{0,14},{1,15},{2,0},{3,1},{4,2},{5,3},{6,4},{7,5},{8,6},{9,7},{10,... | collective-permute-start | bytes 73736 | tf_op jit(solution)/shard_map/ppermute | solution.py:800
  42.2 14.0 %all-to-all-start.1 = ((bf16[16,27,128]{2,1,0:T(8,128)(2,1)}), bf16[16,27,128]{2,1,0:T(8,128)(2,1)S(1)}, u32[]{:S(2)}, u32[]{:S(2)}) async-start(bf16[16,27,128]{2,1,0:T(8,128)(2,1)} %get-tuple-element.48), calls=%async_computation.1 | async-start | bytes 262144 | tf_op jit(solution)/shard_map/all_to_all | solution.py:883

commit v14 on v13

--- a/solution.py
+++ b/solution.py
@@ -583,6 +583,35 @@
     ]
 
 
+def mask_rows(masks):
+    lanes = lane_iota(H)
+    y = lanes // 8 % 8
+    z = lanes % 8
+    for k, chosen in enumerate((lanes < 64, y == 0, y == 7, z == 0, z == 7)):
+        picked = jnp.where(chosen, 1.0, 0.0)
+        masks[2 * k] = picked.astype(BF16)
+        masks[2 * k + 1] = (1.0 - picked).astype(BF16)
+
+
+def masked_shifts(chunks, masks):
+    half = [roll_lanes(chunk, 64) for chunk in chunks]
+    low = [chunk * masks[0] for chunk in half]
+    high = [chunk * masks[1] for chunk in half]
+
+    def blend(k, first, second):
+        return first * masks[2 * k] + second * masks[2 * k + 1]
+
+    return [
+        chunks,
+        [low[q] + high[(q + 1) % 4] for q in range(4)],
+        [low[(q + 3) % 4] + high[q] for q in range(4)],
+        [roll_lanes(blend(1, half[q], chunks[q]), -8) for q in range(4)],
+        [roll_lanes(blend(2, half[q], chunks[q]), 8) for q in range(4)],
+        [roll_lanes(blend(3, roll_lanes(chunk, 8), chunk), -1) for chunk in chunks],
+        [roll_lanes(blend(4, roll_lanes(chunk, -8), chunk), 1) for chunk in chunks],
+    ]
+
+
 def span(slice_index, count=1):
     if isinstance(slice_index, int):
         return slice(slice_index * SITES, (slice_index + count) * SITES)
@@ -593,9 +622,9 @@
     return slice(slot * SITES, (slot + 1) * SITES)
 
 
-def stack_wide(source, target, index, slot):
+def stack_wide(source, target, index, slot, masks):
     chunks = chunks_of(source[:, span(index)])
-    for position, shifted in enumerate(all_shifts(chunks)):
+    for position, shifted in enumerate(masked_shifts(chunks, masks)):
         for q in range(4):
             lanes = slice(slot * SITES + q * 128, slot * SITES + q * 128 + 128)
             target[H * position:H * position + H, lanes] = shifted[q]
@@ -622,8 +651,9 @@
     split, fm_ref, below_ref, above_ref, fbelow_ref, fabove_ref, loops_ref,
     p1_ref, p2_ref, p3_ref, p4_ref, b2_ref, b3_ref, b4_ref,
     coeff_ref, grads_ref,
-    feats, mixed, h1, h2, h3, parts, lasts, g3, g2, g1, wide, wide_back, wide_first, thin, thin_back, packed,
+    feats, mixed, h1, h2, h3, parts, lasts, g3, g2, g1, wide, wide_back, wide_first, thin, thin_back, packed, masks,
 ):
+    mask_rows(masks)
     row8 = lax.broadcasted_iota(jnp.int32, (8, SITES), 0)
     loop_re = jnp.concatenate([loops_ref[0, q:q + 1, :] for q in range(4)], axis=1)
     loop_im = jnp.concatenate([loops_ref[1, q:q + 1, :] for q in range(4)], axis=1)
@@ -691,17 +721,17 @@
     stages = (
         (0, 1, 17, lambda i: stack_thin(feats, thin, i, i % 4)),
         (1, 1, 17, first_dot),
-        (3, 2, 16, lambda i: stack_wide(h1, wide, i, i % 2)),
+        (3, 2, 16, lambda i: stack_wide(h1, wide, i, i % 2, masks)),
         (4, 2, 16, second_dot),
-        (6, 3, 15, lambda i: stack_wide(h2, wide, i, 2 + i % 2)),
+        (6, 3, 15, lambda i: stack_wide(h2, wide, i, 2 + i % 2, masks)),
         (7, 3, 15, third_dot),
         (8, 3, 15, taps_of),
         (10, 4, 14, last_of),
         (12, 5, 13, lambda i: stack_thin(lasts, thin_back, i, own_slot(i, halo3))),
         (13, 5, 13, back_third),
-        (15, 6, 12, lambda i: stack_wide(g3, wide_back, i, own_slot(i, halo2))),
+        (15, 6, 12, lambda i: stack_wide(g3, wide_back, i, own_slot(i, halo2), masks)),
         (16, 6, 12, back_second),
-        (18, 7, 11, lambda i: stack_wide(g2, wide_first, i, i - 7)),
+        (18, 7, 11, lambda i: stack_wide(g2, wide_first, i, i - 7, masks)),
         (19, 7, 11, back_first),
     )
     for step in range(1, 30):
@@ -869,7 +899,7 @@
             ((8, window), F32), ((8, window), F32), ((H, window), BF16), ((H, window), BF16), ((H, window), BF16),
             ((3, 8, window), F32), ((8, window), F32), ((H, window), BF16), ((H, window), BF16), ((H, 4 * SITES), BF16),
             ((432, 4 * SITES), BF16), ((432, 6 * SITES), BF16), ((432, 4 * SITES), BF16),
-            ((72, 4 * SITES), BF16), ((72, 8 * SITES), BF16), ((432, LANES), F32),
+            ((72, 4 * SITES), BF16), ((72, 8 * SITES), BF16), ((432, LANES), F32), ((10, H, LANES), BF16),
         ],
         limit=20 * 1024 * 1024,
     )(fm, below, above, fbelow, fabove, loops, p1, p2, p3, p4, b2, b3, b4)

time: 57.4 us -> 57.7 us (level)
  no operation moved by 1% of the time
where the time goes in v14:
time: 57.7 us; the launch traced here: 57.4 us
  starting transfers between devices  26.2 us (45%)
  Pallas kernels  21.2 us (37%)
  waiting for transfers between devices  7.45 us (13%)
  local copies, waits for them, and re-layouts  1.73 us (3%)
  between operations  0.79 us (1%)
    ppermute x6, starting transfers between devices, send(): lax.ppermute(value, 'tm', [(i, (i + distance) % count) for i in range(cou...  14.8 us
    pallas_call x1, Pallas kernels, on_device(): call(functools.partial(conv_kernel, count == 16), [((4, 8, SITES), F32),...  9.8 us
    all_to_all x1, waiting for transfers between devices, on_device(): grads = lax.all_to_all(grads, 'tm', split_axis=0, concat_axis=0, tiled=True)  6.91 us
    all_to_all x1, starting transfers between devices, on_device(): grads = lax.all_to_all(grads, 'tm', split_axis=0, concat_axis=0, tiled=True)  6.09 us
    all_to_all x1, starting transfers between devices, on_device(): lax.all_to_all(block, 'tm', split_axis=0, concat_axis=0, tiled=True)  5.33 us
    pallas_call x1, Pallas kernels, on_device(): call(time_kernel, [((4, 16, SITES), BF16), ((3, 8, SITES), BF16), ((3, 8,...  3.31 us
    pallas_call x1, Pallas kernels, on_device(): call(space_kernel, [((186, 8, LANES), F32)], [((3, 3, 18, 2, 8, LANES), F...  2.59 us
    unnamed x16, local copies, waits for them, and re-layouts  1.73 us
  transfers between devices with their start and end apart: 8, of which 2 were waited for; matrix products, arithmetic and copies ran while one was open for 0% of the time, Pallas kernels for 14%

profile of v14, /device:TPU:0, one launch (start us, length us, event | category | flops | bytes accessed | tf_op | source)
XLA Modules:
  0.0 57.4 jit_solution(11688467078907328067)
XLA Ops:
  0.6 1.1 %copy-done = f32[4,2,3,3,1,4,512]{6,5,4,3,2,1,0:T(4,128)S(1)} copy-done((f32[4,2,3,3,1,4,512]{6,5,4,3,2,1,0:T(4,128)S(1)}, f32[4,2,3,3,1,4,512]{6,5,4,3,2,1,0:T(4,128)}, u32[]{:S(2)}) %copy-start) | copy-done | bytes 589848
  1.7 1.6 %shard_map.119 = (bf16[70,512]{1,0:T(8,128)(2,1)S(1)}, bf16[70,512]{1,0:T(8,128)(2,1)S(1)}, f32[4,18,2,8,128]{4,3,2,1,0:T(8,128)S(1)}, f32[3,18,2,8,128]{4,3,2,1...) custom-call(f32[4,2,3,3,1,4,512]{6,5,4,3,2,1,0:T(4,128)S(1)} %copy-done), custom_call_target="tpu_custom_call" | custom-call | tf_op jit(solution)/shard_map/pallas_call | solution.py:837
  3.3 0.5 collective-permute-start
  3.8 5.1 %collective-permute-start.1 = (bf16[70,512]{1,0:T(8,128)(2,1)S(1)}, bf16[70,512]{1,0:T(8,128)(2,1)S(1)}, u32[]{:S(2)}, u32[]{:S(2)}) collective-permute-start(bf16[70,512]{1,0:T(8,128)(2,1)S(1)} %get-tuple-element.33), channel_id=1, source_target_pairs={{0,15},{1,0},{2,1},{3,2},{4,3},{5,4},{6,5},{7,6},{8,7},{9,8},{10,9... | collective-permute-start | bytes 215048 | tf_op jit(solution)/shard_map/ppermute | solution.py:830
  8.8 2.6 %shard_map.120.state.after_ref = f32[186,8,128]{2,1,0:T(8,128)S(1)} custom-call(f32[4,18,2,8,128]{4,3,2,1,0:T(8,128)S(1)} %get-tuple-element.29.dense, f32[3,18,2,8,128]{4,3,2,1,0:T(8,128)S(1)} %get-tuple-element.31.time_staples), custom_call_target="tpu_custom_call" | custom-call | flops 4000000000 | bytes 16000000 | tf_op jit(solution)/shard_map/pallas_call | solution.py:844
  11.4 0.0 copy-start.3
  11.5 0.0 copy-start.4
  11.5 0.0 copy-start.5
  11.5 0.6 %copy-done.3 = bf16[1296]{0:T(1024)(128)(2,1)S(1)} copy-done((bf16[1296]{0:T(1024)(128)(2,1)S(1)}, bf16[1296]{0:T(1024)(128)(2,1)}, u32[]{:S(2)}) %copy-start.3) | copy-done | bytes 2616
  12.1 0.0 copy-done.2
  12.1 0.0 copy-done.5
  12.1 0.9 %shard_map.122 = bf16[16,64,128]{2,1,0:T(8,128)(2,1)} custom-call(s32[1]{0:T(128)} %bitcast.core_ref, bf16[70,512]{1,0:T(8,128)(2,1)S(1)} %collective-permute-done.up_ref, bf16[70,512]{1,0:T(8,128)(2,1)S(1)} %collective-permute-done.1.down_ref, f32[12,4,128]{2,1,0:T(4,128)S(1)} %get-tuple-element.38.slab, bf16[216]{0:T(256)(128)(2,1)S(1)} %copy-done.4, ...), custom_call_target="tpu_custom_call" | custom-call | tf_op jit(solution)/shard_map/pallas_call | solution.py:851
  13.0 5.3 %all-to-all-start = ((bf16[16,64,128]{2,1,0:T(8,128)(2,1)}), bf16[16,64,128]{2,1,0:T(8,128)(2,1)S(1)}, u32[]{:S(2)}, u32[]{:S(2)}) async-start(bf16[16,64,128]{2,1,0:T(8,128)(2,1)} %shard_map.122), calls=%async_computation | async-start | bytes 524288 | tf_op jit(solution)/shard_map/all_to_all | solution.py:857
  18.4 3.3 %shard_map.121 = (bf16[4,16,512]{2,1,0:T(8,128)(2,1)S(1)}, bf16[3,8,512]{2,1,0:T(8,128)(2,1)S(1)}, bf16[3,8,512]{2,1,0:T(8,128)(2,1)S(1)}, bf16[2,4,18,2,8,128]{5,4,3,2,1,0:T(8,128)(2,1)S(1)}) custom-call(s32[1,4]{1,0:T(1,128)S(1)} %multiply_add_fusion.code_ref, f32[4,18,2,8,128]{4,3,2,1,0:T(8,128)S(1)} %get-tuple-element.29.dense, ...), custom_call_target="tpu_custom_call" | custom-call | tf_op jit(solution)/shard_map/pallas_call | solution.py:858
  21.7 0.5 collective-permute-start.2
  22.2 4.0 %collective-permute-start.3 = (bf16[4,16,512]{2,1,0:T(8,128)(2,1)S(1)}, bf16[4,16,512]{2,1,0:T(8,128)(2,1)S(1)}, u32[]{:S(2)}, u32[]{:S(2)}) collective-permute-start(bf16[4,16,512]{2,1,0:T(8,128)(2,1)S(1)} %get-tuple-element.35.fm_ref), channel_id=1, source_target_pairs={{0,15},{1,0},{2,1},{3,2},{4,3},{5,4},{6,5},{7,6},{8,7},{9,8},{10,9... | collective-permute-start | bytes 196616 | tf_op jit(solution)/shard_map/ppermute | solution.py:830
  26.2 4.7 %collective-permute-start.5 = (bf16[3,8,512]{2,1,0:T(8,128)(2,1)S(1)}, bf16[3,8,512]{2,1,0:T(8,128)(2,1)S(1)}, u32[]{:S(2)}, u32[]{:S(2)}) collective-permute-start(bf16[3,8,512]{2,1,0:T(8,128)(2,1)S(1)} %get-tuple-element.37), channel_id=1, source_target_pairs={{0,14},{1,15},{2,0},{3,1},{4,2},{5,3},{6,4},{7,5},{8,6},{9,7},{10,... | collective-permute-start | bytes 73736 | tf_op jit(solution)/shard_map/ppermute | solution.py:830
  31.0 1.3 %shard_map.123 = (f32[2,4,128]{2,1,0:T(4,128)S(1)}, bf16[48,72]{1,0:T(8,128)(2,1)S(1)}, bf16[48,432]{1,0:T(8,128)(2,1)S(1)}, bf16[48,432]{1,0:T(8,128)(2,1)S(1)}...) custom-call(bf16[16,64,128]{2,1,0:T(8,128)(2,1)S(1)} %all-to-all-don, ...), custom_call_target="tpu_custom_call" | custom-call | tf_op jit(solution)/shard_map/pallas_call | solution.py:881
  32.2 0.5 collective-permute-done.4.fbelow_ref
  32.8 9.8 %shard_map.124 = (f32[4,8,512]{2,1,0:T(8,128)S(1)}, bf16[16,27,128]{2,1,0:T(8,128)(2,1)}) custom-call(bf16[4,16,512]{2,1,0:T(8,128)(2,1)S(1)} %get-tuple-element.35.fm_ref, bf16[4,16,512]{2,1,0:T(8,128)(2,1)S(1)} %collective-permute-done.2.below_ref, bf16[4,16,512]{2,1,0:T(8,128)(2,1)S(1)} %collective-permute-done.3.above_ref, ...), custom_call_target="tpu_custom_call" | custom-call | tf_op jit(solution)/shard_map/pallas_call | solution.py:895
  42.6 6.1 %all-to-all-start.1 = ((bf16[16,27,128]{2,1,0:T(8,128)(2,1)}), bf16[16,27,128]{2,1,0:T(8,128)(2,1)S(1)}, u32[]{:S(2)}, u32[]{:S(2)}) async-start(bf16[16,27,128]{2,1,0:T(8,128)(2,1)} %get-tuple-element.48), calls=%async_computation.1 | async-start | bytes 262144 | tf_op jit(solution)/shard_map/all_to_all | solution.py:913
  48.7 1.0 %shard_map.125 = f32[4,2,3,3,1,4,512]{6,5,4,3,2,1,0:T(4,128)} custom-call(f32[4,18,2,8,128]{4,3,2,1,0:T(8,128)S(1)} %get-tuple-element.29.dense, bf16[2,4,18,2,8,128]{5,4,3,2,1,0:T(8,128)(2,1)S(1)} %get-tuple-element.34.moves_ref, f32[4,8,512]{2,1,0:T(8,128)S(1)} %get-tuple-element.47.coeff_ref), custom_call_target="tpu_custom_call" | custom-call | tf_op jit(solution)/shard_map/pallas_call | solution.py:914
  49.7 6.9 %all-to-all-done.1.parts_ref = bf16[16,27,128]{2,1,0:T(8,128)(2,1)S(1)} async-done(((bf16[16,27,128]{2,1,0:T(8,128)(2,1)}), bf16[16,27,128]{2,1,0:T(8,128)(2,1)S(1)}, u32[]{:S(2)}, u32[]{:S(2)}) %all-to-all-start.1) | async-done | bytes 110624 | tf_op jit(solution)/shard_map/all_to_all | solution.py:913
  56.6 0.8 %shard_map.126 = (f32[1,216]{1,0:T(1,128)}, f32[1,1296]{1,0:T(1,128)}, f32[1,1296]{1,0:T(1,128)}, f32[1,108]{1,0:T(1,128)}) custom-call(bf16[16,27,128]{2,1,0:T(8,128)(2,1)S(1)} %all-to-all-done.1.parts_ref), custom_call_target="tpu_custom_call" | custom-call | tf_op jit(solution)/shard_map/pallas_call | solution.py:917
  (17 shorter events, 0.0 us)
Async XLA Ops:
  0.6 1.1 %copy-start = (f32[4,2,3,3,1,4,512]{6,5,4,3,2,1,0:T(4,128)S(1)}, f32[4,2,3,3,1,4,512]{6,5,4,3,2,1,0:T(4,128)}, u32[]{:S(2)}) copy-start(f32[4,2,3,3,1,4,512]{6,5,4,3,2,1,0:T(4,128)} %links_ref.1) | copy-start | bytes 1769476
  3.3 8.2 %collective-permute-start = (bf16[70,512]{1,0:T(8,128)(2,1)S(1)}, bf16[70,512]{1,0:T(8,128)(2,1)S(1)}, u32[]{:S(2)}, u32[]{:S(2)}) collective-permute-start(bf16[70,512]{1,0:T(8,128)(2,1)S(1)} %get-tuple-element.32), channel_id=1, source_target_pairs={{0,1},{1,2},{2,3},{3,4},{4,5},{5,6},{6,7},{7,8},{8,9},{9,10},{10,1... | collective-permute-start | bytes 215048 | tf_op jit(solution)/shard_map/ppermute | solution.py:830
  3.8 7.7 %collective-permute-start.1 = (bf16[70,512]{1,0:T(8,128)(2,1)S(1)}, bf16[70,512]{1,0:T(8,128)(2,1)S(1)}, u32[]{:S(2)}, u32[]{:S(2)}) collective-permute-start(bf16[70,512]{1,0:T(8,128)(2,1)S(1)} %get-tuple-element.33), channel_id=1, source_target_pairs={{0,15},{1,0},{2,1},{3,2},{4,3},{5,4},{6,5},{7,6},{8,7},{9,8},{10,9... | collective-permute-start | bytes 215048 | tf_op jit(solution)/shard_map/ppermute | solution.py:830
  11.4 0.7 %copy-start.3 = (bf16[1296]{0:T(1024)(128)(2,1)S(1)}, bf16[1296]{0:T(1024)(128)(2,1)}, u32[]{:S(2)}) copy-start(bf16[1296]{0:T(1024)(128)(2,1)} %w3_ref.1) | copy-start | bytes 7780
  11.4 0.7 %copy-start.2 = (bf16[1296]{0:T(1024)(128)(2,1)S(1)}, bf16[1296]{0:T(1024)(128)(2,1)}, u32[]{:S(2)}) copy-start(bf16[1296]{0:T(1024)(128)(2,1)} %w2_ref.1) | copy-start | bytes 7780
  11.5 0.7 %copy-start.4 = (bf16[216]{0:T(256)(128)(2,1)S(1)}, bf16[216]{0:T(256)(128)(2,1)}, u32[]{:S(2)}) copy-start(bf16[216]{0:T(256)(128)(2,1)} %w1_ref.1) | copy-start | bytes 1300
  11.5 0.7 %copy-start.5 = (bf16[108]{0:T(256)(128)(2,1)S(1)}, bf16[108]{0:T(256)(128)(2,1)}, u32[]{:S(2)}) copy-start(bf16[108]{0:T(256)(128)(2,1)} %w4_ref.1) | copy-start | bytes 652
  13.0 5.3 %copy-start.6 = (s32[1,4]{1,0:T(1,128)S(1)}, s32[1,4]{1,0:T(1,128)}, u32[]{:S(2)}) copy-start(s32[1,4]{1,0:T(1,128)} %param.10) | copy-start | bytes 52
  13.0 5.4 %copy-start.7 = (s32[1,4]{1,0:T(1,128)S(1)}, s32[1,4]{1,0:T(1,128)}, u32[]{:S(2)}) copy-start(s32[1,4]{1,0:T(1,128)} %param.11) | copy-start | bytes 52
  13.0 5.4 %copy-start.1 = (bf16[4,2,3,3,1,4,512]{6,5,4,3,2,1,0:T(4,128)(2,1)S(1)}, bf16[4,2,3,3,1,4,512]{6,5,4,3,2,1,0:T(4,128)(2,1)}, u32[]{:S(2)}) copy-start(bf16[4,2,3,3,1,4,512]{6,5,4,3,2,1,0:T(4,128)(2,1)} %cot_ref.1) | copy-start | bytes 884740
  13.0 17.9 %all-to-all-start = ((bf16[16,64,128]{2,1,0:T(8,128)(2,1)}), bf16[16,64,128]{2,1,0:T(8,128)(2,1)S(1)}, u32[]{:S(2)}, u32[]{:S(2)}) async-start(bf16[16,64,128]{2,1,0:T(8,128)(2,1)} %shard_map.122), calls=%async_computation | async-start | bytes 524288 | tf_op jit(solution)/shard_map/all_to_all | solution.py:857
  21.7 11.0 %collective-permute-start.2 = (bf16[4,16,512]{2,1,0:T(8,128)(2,1)S(1)}, bf16[4,16,512]{2,1,0:T(8,128)(2,1)S(1)}, u32[]{:S(2)}, u32[]{:S(2)}) collective-permute-start(bf16[4,16,512]{2,1,0:T(8,128)(2,1)S(1)} %get-tuple-element.35.fm_ref), channel_id=1, source_target_pairs={{0,1},{1,2},{2,3},{3,4},{4,5},{5,6},{6,7},{7,8},{8,9},{9,10},{10,1... | collective-permute-start | bytes 196616 | tf_op jit(solution)/shard_map/ppermute | solution.py:830
  22.2 10.6 %collective-permute-start.3 = (bf16[4,16,512]{2,1,0:T(8,128)(2,1)S(1)}, bf16[4,16,512]{2,1,0:T(8,128)(2,1)S(1)}, u32[]{:S(2)}, u32[]{:S(2)}) collective-permute-start(bf16[4,16,512]{2,1,0:T(8,128)(2,1)S(1)} %get-tuple-element.35.fm_ref), channel_id=1, source_target_pairs={{0,15},{1,0},{2,1},{3,2},{4,3},{5,4},{6,5},{7,6},{8,7},{9,8},{10,9... | collective-permute-start | bytes 196616 | tf_op jit(solution)/shard_map/ppermute | solution.py:830
  26.2 6.5 %collective-permute-start.4 = (bf16[3,8,512]{2,1,0:T(8,128)(2,1)S(1)}, bf16[3,8,512]{2,1,0:T(8,128)(2,1)S(1)}, u32[]{:S(2)}, u32[]{:S(2)}) collective-permute-start(bf16[3,8,512]{2,1,0:T(8,128)(2,1)S(1)} %get-tuple-element.36), channel_id=1, source_target_pairs={{0,2},{1,3},{2,4},{3,5},{4,6},{5,7},{6,8},{7,9},{8,10},{9,11},{10,... | collective-permute-start | bytes 73736 | tf_op jit(solution)/shard_map/ppermute | solution.py:830
  26.2 6.5 %collective-permute-start.5 = (bf16[3,8,512]{2,1,0:T(8,128)(2,1)S(1)}, bf16[3,8,512]{2,1,0:T(8,128)(2,1)S(1)}, u32[]{:S(2)}, u32[]{:S(2)}) collective-permute-start(bf16[3,8,512]{2,1,0:T(8,128)(2,1)S(1)} %get-tuple-element.37), channel_id=1, source_target_pairs={{0,14},{1,15},{2,0},{3,1},{4,2},{5,3},{6,4},{7,5},{8,6},{9,7},{10,... | collective-permute-start | bytes 73736 | tf_op jit(solution)/shard_map/ppermute | solution.py:830
  42.6 14.0 %all-to-all-start.1 = ((bf16[16,27,128]{2,1,0:T(8,128)(2,1)}), bf16[16,27,128]{2,1,0:T(8,128)(2,1)S(1)}, u32[]{:S(2)}, u32[]{:S(2)}) async-start(bf16[16,27,128]{2,1,0:T(8,128)(2,1)} %get-tuple-element.48), calls=%async_computation.1 | async-start | bytes 262144 | tf_op jit(solution)/shard_map/all_to_all | solution.py:913

commit v15 on v13

--- a/solution.py
+++ b/solution.py
@@ -278,9 +278,9 @@
 
 
 def block_kernel(
-    widths, core_ref, up_ref, down_ref, slab, w1_ref, w2_ref, w3_ref, w4_ref, after_ref, block_ref, other, block
+    widths, place_ref, up_ref, down_ref, slab, w1_ref, w2_ref, w3_ref, w4_ref, after_ref, block_ref, other, block
 ):
-    even = core_ref[0] == 0
+    even = place_ref[0] % 2 == 0
     up = up_ref[0:16].astype(F32)
     down = down_ref[0:16].astype(F32)
     for q in range(4):
@@ -380,7 +380,7 @@
 
 def time_kernel(
     code_ref, dense, edges, state, cot_ref, up_ref, down_ref,
-    fm_ref, fup_ref, fdown_ref, moves_ref,
+    fm_ref, planes_ref, moves_ref,
     cots, gates, moved, staples, sums, halo_up, halo_down, forces, rows,
 ):
     for q in range(4):
@@ -476,10 +476,7 @@
         for q in range(4):
             value = rows[t, q]
             fm_ref[t, :, q * 128:q * 128 + 128] = value.astype(BF16)
-            if t > 0:
-                fup_ref[t - 1, :, q * 128:q * 128 + 128] = value[0:8].astype(BF16)
-            if t < 3:
-                fdown_ref[t, :, q * 128:q * 128 + 128] = value[0:8].astype(BF16)
+            planes_ref[t, :, q * 128:q * 128 + 128] = value[0:8].astype(BF16)
 
 
 def selectors():
@@ -619,7 +616,7 @@
 
 
 def conv_kernel(
-    split, fm_ref, below_ref, above_ref, fbelow_ref, fabove_ref, loops_ref,
+    split, place_ref, fm_ref, near_ref, far_ref, near_chip_ref, far_chip_ref, loops_ref,
     p1_ref, p2_ref, p3_ref, p4_ref, b2_ref, b3_ref, b4_ref,
     coeff_ref, grads_ref,
     feats, mixed, h1, h2, h3, parts, lasts, g3, g2, g1, wide, wide_back, wide_first, thin, thin_back, packed,
@@ -629,12 +626,17 @@
     loop_im = jnp.concatenate([loops_ref[1, q:q + 1, :] for q in range(4)], axis=1)
     loops = jnp.where(row8 == 6, loop_re, jnp.where(row8 == 7, loop_im, 0.0))
     loops = loops.astype(BF16).astype(F32)
-    for j in range(3):
-        feats[:, span(j)] = fbelow_ref[j].astype(F32) + loops
-        feats[:, span(15 + j)] = fabove_ref[j].astype(F32) + loops
-    for base, ref in ((3, below_ref), (7, fm_ref), (11, above_ref)):
-        for j in range(4):
-            value = ref[j].astype(F32)
+    first_core = place_ref[0] % 2 == 0
+    first_chip = place_ref[0] // 2 % 2 == 0
+    for j in range(4):
+        near, far = near_chip_ref[j].astype(F32), far_chip_ref[j].astype(F32)
+        if j > 0:
+            feats[:, span(j - 1)] = jnp.where(first_chip, far, near) + loops
+        if j < 3:
+            feats[:, span(15 + j)] = jnp.where(first_chip, near, far) + loops
+        near, far = near_ref[j].astype(F32), far_ref[j].astype(F32)
+        below, above = jnp.where(first_core, far, near), jnp.where(first_core, near, far)
+        for base, value in ((3, below), (7, fm_ref[j].astype(F32)), (11, above)):
             feats[:, span(base + j)] = value[0:8] + loops
             mixed[:, span(base + j)] = value[8:16]
 
@@ -799,6 +801,10 @@
     def send(value, distance):
         return lax.ppermute(value, "tm", [(i, (i + distance) % count) for i in range(count)])
 
+    def swap(value, pairs):
+        return lax.ppermute(value, "tm", pairs + [(target, source) for source, target in pairs])
+
+    chips = count // 2
     widths = (768 // count, 768 // count, 128 // count, 64 // count)
     vmem, smem = pltpu.VMEM, pltpu.SMEM
     field = ((4, 18, 2, 8, LANES), F32)
@@ -817,18 +823,18 @@
         [((3, 3, 18, 2, 8, LANES), F32), ((3, 3, 18, 2, 8, LANES), F32)],
         cost=pl.CostEstimate(flops=4_000_000_000, bytes_accessed=16_000_000, transcendentals=0),
     )(dense, staples)
-    core = (lax.axis_index("tm") % 2).astype(jnp.int32)[None]
+    place = lax.axis_index("tm").astype(jnp.int32)[None]
     (block,) = call(
         functools.partial(block_kernel, widths),
         [((count, BLOCKROWS, LANES), BF16)],
         [((12, 4, LANES), F32), ((BLOCKROWS, LANES), F32)],
         places=(smem,) + (vmem,) * 7 + (pl.ANY,),
-    )(core, up, down, slab, w_first, w_second, w_third, w_last, state)
+    )(place, up, down, slab, w_first, w_second, w_third, w_last, state)
     gathered = lax.all_to_all(block, "tm", split_axis=0, concat_axis=0, tiled=True)
-    fm, fup, fdown, moves = call(
+    fm, planes, moves = call(
         time_kernel,
         [
-            ((4, 16, SITES), BF16), ((3, 8, SITES), BF16), ((3, 8, SITES), BF16),
+            ((4, 16, SITES), BF16), ((4, 8, SITES), BF16),
             ((2, 4, 18, 2, 8, LANES), BF16),
         ],
         [
@@ -837,10 +843,10 @@
         ],
         places=(smem,) + (vmem,) * 6,
     )(parity + 2 * link_subset, dense, edges, state, cotangent, up, down)
-    below = send(fm, 1)
-    above = send(fm, -1)
-    fbelow = send(fup, 2)
-    fabove = send(fdown, -2)
+    far_chip = swap(planes, [(2 * c + k, (2 * c + 2 + k) % count) for c in range(1, chips, 2) for k in range(2)])
+    far_core = swap(fm, [(i, (i + 1) % count) for i in range(1, count, 2)])
+    near_chip = swap(planes, [(2 * c + k, 2 * c + 2 + k) for c in range(0, chips, 2) for k in range(2)])
+    near_core = swap(fm, [(i, i + 1) for i in range(0, count, 2)])
 
     panel_outs = [
         ((2, 4, LANES), F32), ((H, 72), BF16), ((H, 432), BF16), ((H, 432), BF16), ((72, H), BF16),
@@ -872,7 +878,8 @@
             ((72, 4 * SITES), BF16), ((72, 8 * SITES), BF16), ((432, LANES), F32),
         ],
         limit=20 * 1024 * 1024,
-    )(fm, below, above, fbelow, fabove, loops, p1, p2, p3, p4, b2, b3, b4)
+        places=(smem,) + (vmem,) * 13,
+    )(place, fm, near_core, far_core, near_chip, far_chip, loops, p1, p2, p3, p4, b2, b3, b4)
     if count != 16:
         offset = 0
         pieces = []

time: 57.4 us -> 55 us (0.958)
  starting transfers between devices: 26.2 us -> 21.2 us
  waiting for transfers between devices: 7.45 us -> 10.2 us
    ppermute x6 -> x2, starting transfers between devices: 14.8 us -> 5.56 us  [send(): lax.ppermute(value, 'tm', [(i, (i + distance) % count) for i in range(cou...]
    ppermute x0 -> x4, starting transfers between devices: none -> 6.83 us  [swap(): lax.ppermute(value, 'tm', pairs + [(target, source) for source, target in...]
    ppermute x0 -> x4, waiting for transfers between devices: none -> 2.98 us  [swap(): lax.ppermute(value, 'tm', pairs + [(target, source) for source, target in...]
    all_to_all x1, starting transfers between devices: 6.1 us -> 3.51 us  [on_device(): grads = lax.all_to_all(grads, 'tm', split_axis=0, concat_axis=0, tiled=True)]
  transfers between devices with their start and end apart: 8 -> 8, of which waited for: 2 -> 4; matrix products, arithmetic and copies ran while one was open for 0% -> 0% of each run, Pallas kernels for 14% -> 15%
where the time goes in v15:
time: 55 us; the launch traced here: 54.6 us
  starting transfers between devices  21.2 us (39%)
  Pallas kernels  20.7 us (38%)
  waiting for transfers between devices  10.2 us (19%)
  local copies, waits for them, and re-layouts  1.73 us (3%)
  between operations  0.78 us (1%)
    pallas_call x1, Pallas kernels, on_device(): call(functools.partial(conv_kernel, count == 16), [((4, 8, SITES), F32),...  9.29 us
    all_to_all x1, waiting for transfers between devices, on_device(): grads = lax.all_to_all(grads, 'tm', split_axis=0, concat_axis=0, tiled=True)  6.88 us
    ppermute x4, starting transfers between devices, swap(): lax.ppermute(value, 'tm', pairs + [(target, source) for source, target in...  6.83 us
    ppermute x2, starting transfers between devices, send(): lax.ppermute(value, 'tm', [(i, (i + distance) % count) for i in range(cou...  5.56 us
    all_to_all x1, starting transfers between devices, on_device(): lax.all_to_all(block, 'tm', split_axis=0, concat_axis=0, tiled=True)  5.34 us
    all_to_all x1, starting transfers between devices, on_device(): grads = lax.all_to_all(grads, 'tm', split_axis=0, concat_axis=0, tiled=True)  3.51 us
    pallas_call x1, Pallas kernels, on_device(): call(time_kernel, [((4, 16, SITES), BF16), ((4, 8, SITES), BF16), ((2, 4,...  3.31 us
    ppermute x4, waiting for transfers between devices, swap(): lax.ppermute(value, 'tm', pairs + [(target, source) for source, target in...  2.98 us
  transfers between devices with their start and end apart: 8, of which 4 were waited for; matrix products, arithmetic and copies ran while one was open for 0% of the time, Pallas kernels for 15%

profile of v15, /device:TPU:0, one launch (start us, length us, event | category | flops | bytes accessed | tf_op | source)
XLA Modules:
  0.0 54.6 jit_solution(5675661746802635862)
XLA Ops:
  0.6 1.1 %copy-done = f32[4,2,3,3,1,4,512]{6,5,4,3,2,1,0:T(4,128)S(1)} copy-done((f32[4,2,3,3,1,4,512]{6,5,4,3,2,1,0:T(4,128)S(1)}, f32[4,2,3,3,1,4,512]{6,5,4,3,2,1,0:T(4,128)}, u32[]{:S(2)}) %copy-start) | copy-done | bytes 589848
  1.7 1.6 %shard_map.119 = (bf16[70,512]{1,0:T(8,128)(2,1)S(1)}, bf16[70,512]{1,0:T(8,128)(2,1)S(1)}, f32[4,18,2,8,128]{4,3,2,1,0:T(8,128)S(1)}, f32[3,18,2,8,128]{4,3,2,1...) custom-call(f32[4,2,3,3,1,4,512]{6,5,4,3,2,1,0:T(4,128)S(1)} %copy-done), custom_call_target="tpu_custom_call" | custom-call | tf_op jit(solution)/shard_map/pallas_call | solution.py:813
  3.3 0.5 collective-permute-start
  3.8 5.1 %collective-permute-start.1 = (bf16[70,512]{1,0:T(8,128)(2,1)S(1)}, bf16[70,512]{1,0:T(8,128)(2,1)S(1)}, u32[]{:S(2)}, u32[]{:S(2)}) collective-permute-start(bf16[70,512]{1,0:T(8,128)(2,1)S(1)} %get-tuple-element.32), channel_id=1, source_target_pairs={{0,15},{1,0},{2,1},{3,2},{4,3},{5,4},{6,5},{7,6},{8,7},{9,8},{10,9... | collective-permute-start | bytes 215048 | tf_op jit(solution)/shard_map/ppermute | solution.py:802
  8.8 2.6 %shard_map.120.state.after_ref = f32[186,8,128]{2,1,0:T(8,128)S(1)} custom-call(f32[4,18,2,8,128]{4,3,2,1,0:T(8,128)S(1)} %get-tuple-element.28.dense, f32[3,18,2,8,128]{4,3,2,1,0:T(8,128)S(1)} %get-tuple-element.30.time_staples), custom_call_target="tpu_custom_call" | custom-call | flops 4000000000 | bytes 16000000 | tf_op jit(solution)/shard_map/pallas_call | solution.py:820
  11.4 0.0 copy-start.2
  11.5 0.6 %copy-done.3 = bf16[1296]{0:T(1024)(128)(2,1)S(1)} copy-done((bf16[1296]{0:T(1024)(128)(2,1)S(1)}, bf16[1296]{0:T(1024)(128)(2,1)}, u32[]{:S(2)}) %copy-start.3) | copy-done | bytes 2616
  12.1 0.0 copy-done.2
  12.1 0.0 copy-done.5
  12.1 0.9 %shard_map.122 = bf16[16,64,128]{2,1,0:T(8,128)(2,1)} custom-call(s32[1]{0:T(128)} %bitcast.place_ref, bf16[70,512]{1,0:T(8,128)(2,1)S(1)} %collective-permute-done.up_ref, bf16[70,512]{1,0:T(8,128)(2,1)S(1)} %collective-permute-done.1.down_ref, f32[12,4,128]{2,1,0:T(4,128)S(1)} %get-tuple-element.36.slab, bf16[216]{0:T(256)(128)(2,1)S(1)} %copy-done.4, ...), custom_call_target="tpu_custom_call" | custom-call | tf_op jit(solution)/shard_map/pallas_call | solution.py:827
  13.0 5.3 %all-to-all-start = ((bf16[16,64,128]{2,1,0:T(8,128)(2,1)}), bf16[16,64,128]{2,1,0:T(8,128)(2,1)S(1)}, u32[]{:S(2)}, u32[]{:S(2)}) async-start(bf16[16,64,128]{2,1,0:T(8,128)(2,1)} %shard_map.122), calls=%async_computation | async-start | bytes 524288 | tf_op jit(solution)/shard_map/all_to_all | solution.py:833
  18.4 3.3 %shard_map.121 = (bf16[4,16,512]{2,1,0:T(8,128)(2,1)S(1)}, bf16[4,8,512]{2,1,0:T(8,128)(2,1)S(1)}, bf16[2,4,18,2,8,128]{5,4,3,2,1,0:T(8,128)(2,1)S(1)}) custom-call(s32[1,4]{1,0:T(1,128)S(1)} %multiply_add_fusion.code_ref, f32[4,18,2,8,128]{4,3,2,1,0:T(8,128)S(1)} %get-tuple-element.28.dense, f32[3,18,2,8,128]{4,3,2,1,0:T(8,128)S(1)} %get-tuple-element.29.edges, ...), custom_call_target="tpu_custom_call" | custom-call | tf_op jit(solution)/shard_map/pallas_call | solution.py:834
  21.7 0.5 collective-permute-start.2
  22.2 4.3 %collective-permute-start.3 = (bf16[4,16,512]{2,1,0:T(8,128)(2,1)S(1)}, bf16[4,16,512]{2,1,0:T(8,128)(2,1)S(1)}, u32[]{:S(2)}, u32[]{:S(2)}) collective-permute-start(bf16[4,16,512]{2,1,0:T(8,128)(2,1)S(1)} %get-tuple-element.34.fm_ref), channel_id=1, source_target_pairs={{1,2},{3,4},{5,6},{7,8},{9,10},{11,12},{13,14},{15,0},{2,1},{4,3},... | collective-permute-start | bytes 196616 | tf_op jit(solution)/shard_map/ppermute | solution.py:805
  26.5 2.0 %collective-permute-start.5 = (bf16[4,8,512]{2,1,0:T(8,128)(2,1)S(1)}, bf16[4,8,512]{2,1,0:T(8,128)(2,1)S(1)}, u32[]{:S(2)}, u32[]{:S(2)}) collective-permute-start(bf16[4,8,512]{2,1,0:T(8,128)(2,1)S(1)} %get-tuple-element.35), channel_id=1, source_target_pairs={{2,4},{3,5},{6,8},{7,9},{10,12},{11,13},{14,0},{15,1},{4,2},{5,3},... | collective-permute-start | bytes 98312 | tf_op jit(solution)/shard_map/ppermute | solution.py:805
  28.6 0.3 all-to-all-done.gathered_ref
  28.9 1.3 %shard_map.123 = (f32[2,4,128]{2,1,0:T(4,128)S(1)}, bf16[48,72]{1,0:T(8,128)(2,1)S(1)}, bf16[48,432]{1,0:T(8,128)(2,1)S(1)}, bf16[48,432]{1,0:T(8,128)(2,1)S(1)}...) custom-call(bf16[16,64,128]{2,1,0:T(8,128)(2,1)S(1)} %all-to-all-don, ...), custom_call_target="tpu_custom_call" | custom-call | tf_op jit(solution)/shard_map/pallas_call | solution.py:857
  30.2 0.3 collective-permute-done.4.near_chip_ref
  30.5 2.7 %collective-permute-done.5.far_chip_ref = bf16[4,8,512]{2,1,0:T(8,128)(2,1)S(1)} collective-permute-done((bf16[4,8,512]{2,1,0:T(8,128)(2,1)S(1)}, bf16[4,8,512]{2,1,0:T(8,128)(2,1)S(1)}, u32[]{:S(2)}, u32[]{:S(2)}) %collective-permute-start.5) | collective-permute-done | bytes 32800 | tf_op jit(solution)/shard_map/ppermute | solution.py:805
  33.2 9.3 %shard_map.124 = (f32[4,8,512]{2,1,0:T(8,128)S(1)}, bf16[16,27,128]{2,1,0:T(8,128)(2,1)}) custom-call(s32[1]{0:T(128)} %bitcast.place_ref, bf16[4,16,512]{2,1,0:T(8,128)(2,1)S(1)} %get-tuple-element.34.fm_ref, bf16[4,16,512]{2,1,0:T(8,128)(2,1)S(1)} %collective-permute-done.2.near_ref, bf16[4,16,512]{2,1,0:T(8,128)(2,1)S(1)} %collective-permute-done.3.far_ref, ...), custom_call_target="tpu_custom_call" | custom-call | tf_op jit(solution)/shard_map/pallas_call | solution.py:871
  42.4 3.5 %all-to-all-start.1 = ((bf16[16,27,128]{2,1,0:T(8,128)(2,1)}), bf16[16,27,128]{2,1,0:T(8,128)(2,1)S(1)}, u32[]{:S(2)}, u32[]{:S(2)}) async-start(bf16[16,27,128]{2,1,0:T(8,128)(2,1)} %get-tuple-element.46), calls=%async_computation.1 | async-start | bytes 262144 | tf_op jit(solution)/shard_map/all_to_all | solution.py:890
  46.0 1.0 %shard_map.125 = f32[4,2,3,3,1,4,512]{6,5,4,3,2,1,0:T(4,128)} custom-call(f32[4,18,2,8,128]{4,3,2,1,0:T(8,128)S(1)} %get-tuple-element.28.dense, bf16[2,4,18,2,8,128]{5,4,3,2,1,0:T(8,128)(2,1)S(1)} %get-tuple-element.33.moves_ref, f32[4,8,512]{2,1,0:T(8,128)S(1)} %get-tuple-element.45.coeff_ref), custom_call_target="tpu_custom_call" | custom-call | tf_op jit(solution)/shard_map/pallas_call | solution.py:891
  47.0 6.9 %all-to-all-done.1.parts_ref = bf16[16,27,128]{2,1,0:T(8,128)(2,1)S(1)} async-done(((bf16[16,27,128]{2,1,0:T(8,128)(2,1)}), bf16[16,27,128]{2,1,0:T(8,128)(2,1)S(1)}, u32[]{:S(2)}, u32[]{:S(2)}) %all-to-all-start.1) | async-done | bytes 110624 | tf_op jit(solution)/shard_map/all_to_all | solution.py:890
  53.9 0.8 %shard_map.126 = (f32[1,216]{1,0:T(1,128)}, f32[1,1296]{1,0:T(1,128)}, f32[1,1296]{1,0:T(1,128)}, f32[1,108]{1,0:T(1,128)}) custom-call(bf16[16,27,128]{2,1,0:T(8,128)(2,1)S(1)} %all-to-all-done.1.parts_ref), custom_call_target="tpu_custom_call" | custom-call | tf_op jit(solution)/shard_map/pallas_call | solution.py:894
  (17 shorter events, 0.0 us)
Async XLA Ops:
  0.6 1.1 %copy-start = (f32[4,2,3,3,1,4,512]{6,5,4,3,2,1,0:T(4,128)S(1)}, f32[4,2,3,3,1,4,512]{6,5,4,3,2,1,0:T(4,128)}, u32[]{:S(2)}) copy-start(f32[4,2,3,3,1,4,512]{6,5,4,3,2,1,0:T(4,128)} %links_ref.1) | copy-start | bytes 1769476
  3.3 8.2 %collective-permute-start = (bf16[70,512]{1,0:T(8,128)(2,1)S(1)}, bf16[70,512]{1,0:T(8,128)(2,1)S(1)}, u32[]{:S(2)}, u32[]{:S(2)}) collective-permute-start(bf16[70,512]{1,0:T(8,128)(2,1)S(1)} %get-tuple-element.31), channel_id=1, source_target_pairs={{0,1},{1,2},{2,3},{3,4},{4,5},{5,6},{6,7},{7,8},{8,9},{9,10},{10,1... | collective-permute-start | bytes 215048 | tf_op jit(solution)/shard_map/ppermute | solution.py:802
  3.8 7.7 %collective-permute-start.1 = (bf16[70,512]{1,0:T(8,128)(2,1)S(1)}, bf16[70,512]{1,0:T(8,128)(2,1)S(1)}, u32[]{:S(2)}, u32[]{:S(2)}) collective-permute-start(bf16[70,512]{1,0:T(8,128)(2,1)S(1)} %get-tuple-element.32), channel_id=1, source_target_pairs={{0,15},{1,0},{2,1},{3,2},{4,3},{5,4},{6,5},{7,6},{8,7},{9,8},{10,9... | collective-permute-start | bytes 215048 | tf_op jit(solution)/shard_map/ppermute | solution.py:802
  11.4 0.7 %copy-start.3 = (bf16[1296]{0:T(1024)(128)(2,1)S(1)}, bf16[1296]{0:T(1024)(128)(2,1)}, u32[]{:S(2)}) copy-start(bf16[1296]{0:T(1024)(128)(2,1)} %w3_ref.1) | copy-start | bytes 7780
  11.4 0.7 %copy-start.2 = (bf16[1296]{0:T(1024)(128)(2,1)S(1)}, bf16[1296]{0:T(1024)(128)(2,1)}, u32[]{:S(2)}) copy-start(bf16[1296]{0:T(1024)(128)(2,1)} %w2_ref.1) | copy-start | bytes 7780
  11.5 0.7 %copy-start.4 = (bf16[216]{0:T(256)(128)(2,1)S(1)}, bf16[216]{0:T(256)(128)(2,1)}, u32[]{:S(2)}) copy-start(bf16[216]{0:T(256)(128)(2,1)} %w1_ref.1) | copy-start | bytes 1300
  11.5 0.7 %copy-start.5 = (bf16[108]{0:T(256)(128)(2,1)S(1)}, bf16[108]{0:T(256)(128)(2,1)}, u32[]{:S(2)}) copy-start(bf16[108]{0:T(256)(128)(2,1)} %w4_ref.1) | copy-start | bytes 652
  13.0 5.4 %copy-start.6 = (s32[1,4]{1,0:T(1,128)S(1)}, s32[1,4]{1,0:T(1,128)}, u32[]{:S(2)}) copy-start(s32[1,4]{1,0:T(1,128)} %param.10) | copy-start | bytes 52
  13.0 5.4 %copy-start.7 = (s32[1,4]{1,0:T(1,128)S(1)}, s32[1,4]{1,0:T(1,128)}, u32[]{:S(2)}) copy-start(s32[1,4]{1,0:T(1,128)} %param.11) | copy-start | bytes 52
  13.0 5.4 %copy-start.1 = (bf16[4,2,3,3,1,4,512]{6,5,4,3,2,1,0:T(4,128)(2,1)S(1)}, bf16[4,2,3,3,1,4,512]{6,5,4,3,2,1,0:T(4,128)(2,1)}, u32[]{:S(2)}) copy-start(bf16[4,2,3,3,1,4,512]{6,5,4,3,2,1,0:T(4,128)(2,1)} %cot_ref.1) | copy-start | bytes 884740
  13.0 15.9 %all-to-all-start = ((bf16[16,64,128]{2,1,0:T(8,128)(2,1)}), bf16[16,64,128]{2,1,0:T(8,128)(2,1)S(1)}, u32[]{:S(2)}, u32[]{:S(2)}) async-start(bf16[16,64,128]{2,1,0:T(8,128)(2,1)} %shard_map.122), calls=%async_computation | async-start | bytes 524288 | tf_op jit(solution)/shard_map/all_to_all | solution.py:833
  21.7 11.4 %collective-permute-start.2 = (bf16[4,16,512]{2,1,0:T(8,128)(2,1)S(1)}, bf16[4,16,512]{2,1,0:T(8,128)(2,1)S(1)}, u32[]{:S(2)}, u32[]{:S(2)}) collective-permute-start(bf16[4,16,512]{2,1,0:T(8,128)(2,1)S(1)} %get-tuple-element.34.fm_ref), channel_id=1, source_target_pairs={{0,1},{2,3},{4,5},{6,7},{8,9},{10,11},{12,13},{14,15},{1,0},{3,2},... | collective-permute-start | bytes 196616 | tf_op jit(solution)/shard_map/ppermute | solution.py:805
  22.2 11.0 %collective-permute-start.3 = (bf16[4,16,512]{2,1,0:T(8,128)(2,1)S(1)}, bf16[4,16,512]{2,1,0:T(8,128)(2,1)S(1)}, u32[]{:S(2)}, u32[]{:S(2)}) collective-permute-start(bf16[4,16,512]{2,1,0:T(8,128)(2,1)S(1)} %get-tuple-element.34.fm_ref), channel_id=1, source_target_pairs={{1,2},{3,4},{5,6},{7,8},{9,10},{11,12},{13,14},{15,0},{2,1},{4,3},... | collective-permute-start | bytes 196616 | tf_op jit(solution)/shard_map/ppermute | solution.py:805
  26.5 3.9 %collective-permute-start.4 = (bf16[4,8,512]{2,1,0:T(8,128)(2,1)S(1)}, bf16[4,8,512]{2,1,0:T(8,128)(2,1)S(1)}, u32[]{:S(2)}, u32[]{:S(2)}) collective-permute-start(bf16[4,8,512]{2,1,0:T(8,128)(2,1)S(1)} %get-tuple-element.35), channel_id=1, source_target_pairs={{0,2},{1,3},{4,6},{5,7},{8,10},{9,11},{12,14},{13,15},{2,0},{3,1},... | collective-permute-start | bytes 98312 | tf_op jit(solution)/shard_map/ppermute | solution.py:805
  26.5 6.6 %collective-permute-start.5 = (bf16[4,8,512]{2,1,0:T(8,128)(2,1)S(1)}, bf16[4,8,512]{2,1,0:T(8,128)(2,1)S(1)}, u32[]{:S(2)}, u32[]{:S(2)}) collective-permute-start(bf16[4,8,512]{2,1,0:T(8,128)(2,1)S(1)} %get-tuple-element.35), channel_id=1, source_target_pairs={{2,4},{3,5},{6,8},{7,9},{10,12},{11,13},{14,0},{15,1},{4,2},{5,3},... | collective-permute-start | bytes 98312 | tf_op jit(solution)/shard_map/ppermute | solution.py:805
  42.4 11.4 %all-to-all-start.1 = ((bf16[16,27,128]{2,1,0:T(8,128)(2,1)}), bf16[16,27,128]{2,1,0:T(8,128)(2,1)S(1)}, u32[]{:S(2)}, u32[]{:S(2)}) async-start(bf16[16,27,128]{2,1,0:T(8,128)(2,1)} %get-tuple-element.46), calls=%async_computation.1 | async-start | bytes 262144 | tf_op jit(solution)/shard_map/all_to_all | solution.py:890

commit v16 on v15

--- a/solution.py
+++ b/solution.py
@@ -218,7 +218,7 @@
             moved[mu, e, 1] = high
         return carry
 
-    lax.fori_loop(0, 18, shift_body, 0, unroll=3)
+    lax.fori_loop(0, 18, shift_body, 0, unroll=6)
 
     def staple_body(step, carry):
         mu = step // 2
@@ -240,7 +240,7 @@
         store_matrix(mat_mul(dagger(edge), u_t), write)
         return carry
 
-    lax.fori_loop(0, 6, staple_body, 0)
+    lax.fori_loop(0, 6, staple_body, 0, unroll=2)
 
     def slab_body(c, carry):
         u_t = load_matrix(lambda e: dense[3, e, c])
@@ -272,7 +272,7 @@
                 rows[16 + mu * 18 + e, 2 + c:3 + c] = value[4:5]
         return carry
 
-    lax.fori_loop(0, 18, down_body, 0, unroll=3)
+    lax.fori_loop(0, 18, down_body, 0, unroll=6)
     for q in range(4):
         down_ref[:, q * 128:q * 128 + 128] = rows[:, q, :].astype(BF16)
 
@@ -335,7 +335,7 @@
                     moved[mu, nu, e, 1] = high
         return carry
 
-    lax.fori_loop(0, 18, shift_body, 0, unroll=3)
+    lax.fori_loop(0, 18, shift_body, 0, unroll=6)
 
     def plane_body(step, carry):
         plane = step // 2
@@ -362,7 +362,7 @@
         store_matrix(mat_mul(dagger(two), u_mu), write_nu)
         return carry
 
-    lax.fori_loop(0, 6, plane_body, 0)
+    lax.fori_loop(0, 6, plane_body, 0, unroll=2)
 
     def lower_body(e, carry):
         for mu in range(3):
@@ -375,7 +375,7 @@
             state[sum_at(mu, e, 1)] = acc[1]
         return carry
 
-    lax.fori_loop(0, 18, lower_body, 0, unroll=3)
+    lax.fori_loop(0, 18, lower_body, 0, unroll=6)
 
 
 def time_kernel(
@@ -415,7 +415,7 @@
                 sums[nu, e, c] = state[sum_at(nu, e, c)] + jnp.where(steps == 0, below[c], 0.0)
         return carry
 
-    lax.fori_loop(0, 18, shift_body, 0, unroll=3)
+    lax.fori_loop(0, 18, shift_body, 0, unroll=6)
 
     def plane_body(step, carry):
         mu = step // 2
@@ -434,7 +434,7 @@
         store_matrix(mat_mul(dagger(two), load_matrix(lambda e: dense[mu, e, c])), write)
         return carry
 
-    lax.fori_loop(0, 6, plane_body, 0)
+    lax.fori_loop(0, 6, plane_body, 0, unroll=2)
 
     def lower_body(e, carry):
         acc = None
@@ -445,7 +445,7 @@
         sums[3, e, 1] = acc[1]
         return carry
 
-    lax.fori_loop(0, 18, lower_body, 0, unroll=3)
+    lax.fori_loop(0, 18, lower_body, 0, unroll=6)
 
     def force_body(step, carry):
         mu = step // 2
@@ -471,7 +471,7 @@
         put_row(rows, 12 + mu, c, gate * curve)
         return carry
 
-    lax.fori_loop(0, 8, force_body, 0)
+    lax.fori_loop(0, 8, force_body, 0, unroll=2)
     for t in range(4):
         for q in range(4):
             value = rows[t, q]
@@ -717,26 +717,28 @@
             grad_last = lax.dot_general(
                 thin_back[:, 0:4 * SITES], h3[:, own], contract, preferred_element_type=F32
             )
+            spread, keep = selectors()
+            ordered = jnp.concatenate([grad_last[8 * SWAP[k]:8 * SWAP[k] + 8] for k in range(TAPS)], axis=0)
+            broad = jnp.dot(spread, ordered.astype(BF16), preferred_element_type=F32)
+        if step == 24:
+            broad = jnp.where(keep, broad, 0.0).astype(BF16)
+            place = (
+                lax.broadcasted_iota(jnp.int32, (H, LANES), 1)
+                == 104 + lax.broadcasted_iota(jnp.int32, (H, LANES), 0) % 4
+            ).astype(F32).astype(BF16)
+            packed[...] = jnp.dot(broad, place, preferred_element_type=F32)
         if step == 26:
             grad_third = lax.dot_general(
                 wide_back[:, 0:4 * SITES], h2[:, own], contract, preferred_element_type=F32
             )
+        if step == 27:
+            for k in range(TAPS):
+                packed[H * k:H * k + H, 48:96] = grad_third[H * SWAP[k]:H * SWAP[k] + H]
     grad_second = lax.dot_general(wide_first[...], h1[:, own], contract, preferred_element_type=F32)
     grad_first = lax.dot_general(g1[...], thin[...], contract, preferred_element_type=F32)
-
-    spread, keep = selectors()
-    ordered = jnp.concatenate([grad_last[8 * SWAP[k]:8 * SWAP[k] + 8] for k in range(TAPS)], axis=0)
-    broad = jnp.dot(spread, ordered.astype(BF16), preferred_element_type=F32)
-    broad = jnp.where(keep, broad, 0.0).astype(BF16)
-    place = (
-        lax.broadcasted_iota(jnp.int32, (H, LANES), 1) == 104 + lax.broadcasted_iota(jnp.int32, (H, LANES), 0) % 4
-    ).astype(F32).astype(BF16)
-    packed[...] = jnp.dot(broad, place, preferred_element_type=F32)
     for k in range(TAPS):
         rows = slice(H * k, H * k + H)
-        back = slice(H * SWAP[k], H * SWAP[k] + H)
-        packed[rows, 0:48] = grad_second[back]
-        packed[rows, 48:96] = grad_third[back]
+        packed[rows, 0:48] = grad_second[H * SWAP[k]:H * SWAP[k] + H]
         packed[rows, 96:104] = grad_first[:, 8 * k:8 * k + 8]
     if split:
         for d in range(16):

time: 55 us -> 54.5 us (level)
  Pallas kernels: 20.7 us -> 19.7 us
  transfers between devices with their start and end apart: 8 -> 8, of which waited for: 4 -> 3; matrix products, arithmetic and copies ran while one was open for 0% -> 0% of each run, Pallas kernels for 15% -> 14%
where the time goes in v16:
time: 54.5 us; the launch traced here: 54.1 us
  starting transfers between devices  21.7 us (40%)
  Pallas kernels  19.7 us (36%)
  waiting for transfers between devices  10.2 us (19%)
  local copies, waits for them, and re-layouts  1.73 us (3%)
  between operations  0.77 us (1%)
    pallas_call x1, Pallas kernels, on_device(): call(functools.partial(conv_kernel, count == 16), [((4, 8, SITES), F32),...  9.31 us
    all_to_all x1, waiting for transfers between devices, on_device(): grads = lax.all_to_all(grads, 'tm', split_axis=0, concat_axis=0, tiled=True)  6.88 us
    ppermute x4, starting transfers between devices, swap(): lax.ppermute(value, 'tm', pairs + [(target, source) for source, target in...  6.83 us
    all_to_all x1, starting transfers between devices, on_device(): lax.all_to_all(block, 'tm', split_axis=0, concat_axis=0, tiled=True)  5.8 us
    ppermute x2, starting transfers between devices, send(): lax.ppermute(value, 'tm', [(i, (i + distance) % count) for i in range(cou...  5.56 us
    all_to_all x1, starting transfers between devices, on_device(): grads = lax.all_to_all(grads, 'tm', split_axis=0, concat_axis=0, tiled=True)  3.51 us
    pallas_call x1, Pallas kernels, on_device(): call(time_kernel, [((4, 16, SITES), BF16), ((4, 8, SITES), BF16), ((2, 4,...  3.04 us
    ppermute x4, waiting for transfers between devices, swap(): lax.ppermute(value, 'tm', pairs + [(target, source) for source, target in...  2.72 us
  transfers between devices with their start and end apart: 8, of which 3 were waited for; matrix products, arithmetic and copies ran while one was open for 0% of the time, Pallas kernels for 14%

profile of v16, /device:TPU:0, one launch (start us, length us, event | category | flops | bytes accessed | tf_op | source)
XLA Modules:
  0.0 54.1 jit_solution(3010977877653612273)
XLA Ops:
  0.6 1.1 %copy-done = f32[4,2,3,3,1,4,512]{6,5,4,3,2,1,0:T(4,128)S(1)} copy-done((f32[4,2,3,3,1,4,512]{6,5,4,3,2,1,0:T(4,128)S(1)}, f32[4,2,3,3,1,4,512]{6,5,4,3,2,1,0:T(4,128)}, u32[]{:S(2)}) %copy-start) | copy-done | bytes 589848
  1.7 1.3 %shard_map.119 = (bf16[70,512]{1,0:T(8,128)(2,1)S(1)}, bf16[70,512]{1,0:T(8,128)(2,1)S(1)}, f32[4,18,2,8,128]{4,3,2,1,0:T(8,128)S(1)}, f32[3,18,2,8,128]{4,3,2,1...) custom-call(f32[4,2,3,3,1,4,512]{6,5,4,3,2,1,0:T(4,128)S(1)} %copy-done), custom_call_target="tpu_custom_call" | custom-call | tf_op jit(solution)/shard_map/pallas_call | solution.py:815
  3.0 0.5 collective-permute-start
  3.5 5.1 %collective-permute-start.1 = (bf16[70,512]{1,0:T(8,128)(2,1)S(1)}, bf16[70,512]{1,0:T(8,128)(2,1)S(1)}, u32[]{:S(2)}, u32[]{:S(2)}) collective-permute-start(bf16[70,512]{1,0:T(8,128)(2,1)S(1)} %get-tuple-element.32), channel_id=1, source_target_pairs={{0,15},{1,0},{2,1},{3,2},{4,3},{5,4},{6,5},{7,6},{8,7},{9,8},{10,9... | collective-permute-start | bytes 215048 | tf_op jit(solution)/shard_map/ppermute | solution.py:804
  8.6 2.1 %shard_map.120.state.after_ref = f32[186,8,128]{2,1,0:T(8,128)S(1)} custom-call(f32[4,18,2,8,128]{4,3,2,1,0:T(8,128)S(1)} %get-tuple-element.28.dense, f32[3,18,2,8,128]{4,3,2,1,0:T(8,128)S(1)} %get-tuple-element.30.time_staples), custom_call_target="tpu_custom_call" | custom-call | flops 4000000000 | bytes 16000000 | tf_op jit(solution)/shard_map/pallas_call | solution.py:822
  10.7 0.0 copy-start.3
  10.8 0.6 %copy-done.3 = bf16[1296]{0:T(1024)(128)(2,1)S(1)} copy-done((bf16[1296]{0:T(1024)(128)(2,1)S(1)}, bf16[1296]{0:T(1024)(128)(2,1)}, u32[]{:S(2)}) %copy-start.3) | copy-done | bytes 2616
  11.4 0.0 copy-done.2
  11.4 0.0 copy-done.5
  11.4 0.9 %shard_map.122 = bf16[16,64,128]{2,1,0:T(8,128)(2,1)} custom-call(s32[1]{0:T(128)} %bitcast.place_ref, bf16[70,512]{1,0:T(8,128)(2,1)S(1)} %collective-permute-done.up_ref, bf16[70,512]{1,0:T(8,128)(2,1)S(1)} %collective-permute-done.1.down_ref, f32[12,4,128]{2,1,0:T(4,128)S(1)} %get-tuple-element.36.slab, bf16[216]{0:T(256)(128)(2,1)S(1)} %copy-done.4, ...), custom_call_target="tpu_custom_call" | custom-call | tf_op jit(solution)/shard_map/pallas_call | solution.py:829
  12.3 5.8 %all-to-all-start = ((bf16[16,64,128]{2,1,0:T(8,128)(2,1)}), bf16[16,64,128]{2,1,0:T(8,128)(2,1)S(1)}, u32[]{:S(2)}, u32[]{:S(2)}) async-start(bf16[16,64,128]{2,1,0:T(8,128)(2,1)} %shard_map.122), calls=%async_computation | async-start | bytes 524288 | tf_op jit(solution)/shard_map/all_to_all | solution.py:835
  18.2 3.0 %shard_map.121 = (bf16[4,16,512]{2,1,0:T(8,128)(2,1)S(1)}, bf16[4,8,512]{2,1,0:T(8,128)(2,1)S(1)}, bf16[2,4,18,2,8,128]{5,4,3,2,1,0:T(8,128)(2,1)S(1)}) custom-call(s32[1,4]{1,0:T(1,128)S(1)} %multiply_add_fusion.code_ref, f32[4,18,2,8,128]{4,3,2,1,0:T(8,128)S(1)} %get-tuple-element.28.dense, f32[3,18,2,8,128]{4,3,2,1,0:T(8,128)S(1)} %get-tuple-element.29.edges, ...), custom_call_target="tpu_custom_call" | custom-call | tf_op jit(solution)/shard_map/pallas_call | solution.py:836
  21.2 0.5 collective-permute-start.2
  21.7 4.3 %collective-permute-start.3 = (bf16[4,16,512]{2,1,0:T(8,128)(2,1)S(1)}, bf16[4,16,512]{2,1,0:T(8,128)(2,1)S(1)}, u32[]{:S(2)}, u32[]{:S(2)}) collective-permute-start(bf16[4,16,512]{2,1,0:T(8,128)(2,1)S(1)} %get-tuple-element.34.fm_ref), channel_id=1, source_target_pairs={{1,2},{3,4},{5,6},{7,8},{9,10},{11,12},{13,14},{15,0},{2,1},{4,3},... | collective-permute-start | bytes 196616 | tf_op jit(solution)/shard_map/ppermute | solution.py:807
  26.0 2.0 %collective-permute-start.5 = (bf16[4,8,512]{2,1,0:T(8,128)(2,1)S(1)}, bf16[4,8,512]{2,1,0:T(8,128)(2,1)S(1)}, u32[]{:S(2)}, u32[]{:S(2)}) collective-permute-start(bf16[4,8,512]{2,1,0:T(8,128)(2,1)S(1)} %get-tuple-element.35), channel_id=1, source_target_pairs={{2,4},{3,5},{6,8},{7,9},{10,12},{11,13},{14,0},{15,1},{4,2},{5,3},... | collective-permute-start | bytes 98312 | tf_op jit(solution)/shard_map/ppermute | solution.py:807
  28.0 0.6 %all-to-all-done.gathered_ref = bf16[16,64,128]{2,1,0:T(8,128)(2,1)S(1)} async-done(((bf16[16,64,128]{2,1,0:T(8,128)(2,1)}), bf16[16,64,128]{2,1,0:T(8,128)(2,1)S(1)}, u32[]{:S(2)}, u32[]{:S(2)}) %all-to-all-start) | async-done | bytes 262176 | tf_op jit(solution)/shard_map/all_to_all | solution.py:835
  28.6 1.3 %shard_map.123 = (f32[2,4,128]{2,1,0:T(4,128)S(1)}, bf16[48,72]{1,0:T(8,128)(2,1)S(1)}, bf16[48,432]{1,0:T(8,128)(2,1)S(1)}, bf16[48,432]{1,0:T(8,128)(2,1)S(1)}...) custom-call(bf16[16,64,128]{2,1,0:T(8,128)(2,1)S(1)} %all-to-all-don, ...), custom_call_target="tpu_custom_call" | custom-call | tf_op jit(solution)/shard_map/pallas_call | solution.py:859
  29.9 0.0 collective-permute-done.4.near_chip_ref
  29.9 2.7 %collective-permute-done.5.far_chip_ref = bf16[4,8,512]{2,1,0:T(8,128)(2,1)S(1)} collective-permute-done((bf16[4,8,512]{2,1,0:T(8,128)(2,1)S(1)}, bf16[4,8,512]{2,1,0:T(8,128)(2,1)S(1)}, u32[]{:S(2)}, u32[]{:S(2)}) %collective-permute-start.5) | collective-permute-done | bytes 32800 | tf_op jit(solution)/shard_map/ppermute | solution.py:807
  32.6 9.3 %shard_map.124 = (f32[4,8,512]{2,1,0:T(8,128)S(1)}, bf16[16,27,128]{2,1,0:T(8,128)(2,1)}) custom-call(s32[1]{0:T(128)} %bitcast.place_ref, bf16[4,16,512]{2,1,0:T(8,128)(2,1)S(1)} %get-tuple-element.34.fm_ref, bf16[4,16,512]{2,1,0:T(8,128)(2,1)S(1)} %collective-permute-done.2.near_ref, bf16[4,16,512]{2,1,0:T(8,128)(2,1)S(1)} %collective-permute-done.3.far_ref, ...), custom_call_target="tpu_custom_call" | custom-call | tf_op jit(solution)/shard_map/pallas_call | solution.py:873
  41.9 3.5 %all-to-all-start.1 = ((bf16[16,27,128]{2,1,0:T(8,128)(2,1)}), bf16[16,27,128]{2,1,0:T(8,128)(2,1)S(1)}, u32[]{:S(2)}, u32[]{:S(2)}) async-start(bf16[16,27,128]{2,1,0:T(8,128)(2,1)} %get-tuple-element.46), calls=%async_computation.1 | async-start | bytes 262144 | tf_op jit(solution)/shard_map/all_to_all | solution.py:892
  45.5 1.0 %shard_map.125 = f32[4,2,3,3,1,4,512]{6,5,4,3,2,1,0:T(4,128)} custom-call(f32[4,18,2,8,128]{4,3,2,1,0:T(8,128)S(1)} %get-tuple-element.28.dense, bf16[2,4,18,2,8,128]{5,4,3,2,1,0:T(8,128)(2,1)S(1)} %get-tuple-element.33.moves_ref, f32[4,8,512]{2,1,0:T(8,128)S(1)} %get-tuple-element.45.coeff_ref), custom_call_target="tpu_custom_call" | custom-call | tf_op jit(solution)/shard_map/pallas_call | solution.py:893
  46.5 6.9 %all-to-all-done.1.parts_ref = bf16[16,27,128]{2,1,0:T(8,128)(2,1)S(1)} async-done(((bf16[16,27,128]{2,1,0:T(8,128)(2,1)}), bf16[16,27,128]{2,1,0:T(8,128)(2,1)S(1)}, u32[]{:S(2)}, u32[]{:S(2)}) %all-to-all-start.1) | async-done | bytes 110624 | tf_op jit(solution)/shard_map/all_to_all | solution.py:892
  53.3 0.8 %shard_map.126 = (f32[1,216]{1,0:T(1,128)}, f32[1,1296]{1,0:T(1,128)}, f32[1,1296]{1,0:T(1,128)}, f32[1,108]{1,0:T(1,128)}) custom-call(bf16[16,27,128]{2,1,0:T(8,128)(2,1)S(1)} %all-to-all-done.1.parts_ref), custom_call_target="tpu_custom_call" | custom-call | tf_op jit(solution)/shard_map/pallas_call | solution.py:896
  (17 shorter events, 0.0 us)
Async XLA Ops:
  0.6 1.1 %copy-start = (f32[4,2,3,3,1,4,512]{6,5,4,3,2,1,0:T(4,128)S(1)}, f32[4,2,3,3,1,4,512]{6,5,4,3,2,1,0:T(4,128)}, u32[]{:S(2)}) copy-start(f32[4,2,3,3,1,4,512]{6,5,4,3,2,1,0:T(4,128)} %links_ref.1) | copy-start | bytes 1769476
  3.0 7.7 %collective-permute-start = (bf16[70,512]{1,0:T(8,128)(2,1)S(1)}, bf16[70,512]{1,0:T(8,128)(2,1)S(1)}, u32[]{:S(2)}, u32[]{:S(2)}) collective-permute-start(bf16[70,512]{1,0:T(8,128)(2,1)S(1)} %get-tuple-element.31), channel_id=1, source_target_pairs={{0,1},{1,2},{2,3},{3,4},{4,5},{5,6},{6,7},{7,8},{8,9},{9,10},{10,1... | collective-permute-start | bytes 215048 | tf_op jit(solution)/shard_map/ppermute | solution.py:804
  3.5 7.2 %collective-permute-start.1 = (bf16[70,512]{1,0:T(8,128)(2,1)S(1)}, bf16[70,512]{1,0:T(8,128)(2,1)S(1)}, u32[]{:S(2)}, u32[]{:S(2)}) collective-permute-start(bf16[70,512]{1,0:T(8,128)(2,1)S(1)} %get-tuple-element.32), channel_id=1, source_target_pairs={{0,15},{1,0},{2,1},{3,2},{4,3},{5,4},{6,5},{7,6},{8,7},{9,8},{10,9... | collective-permute-start | bytes 215048 | tf_op jit(solution)/shard_map/ppermute | solution.py:804
  10.7 0.7 %copy-start.3 = (bf16[1296]{0:T(1024)(128)(2,1)S(1)}, bf16[1296]{0:T(1024)(128)(2,1)}, u32[]{:S(2)}) copy-start(bf16[1296]{0:T(1024)(128)(2,1)} %w3_ref.1) | copy-start | bytes 7780
  10.7 0.7 %copy-start.2 = (bf16[1296]{0:T(1024)(128)(2,1)S(1)}, bf16[1296]{0:T(1024)(128)(2,1)}, u32[]{:S(2)}) copy-start(bf16[1296]{0:T(1024)(128)(2,1)} %w2_ref.1) | copy-start | bytes 7780
  10.7 0.7 %copy-start.4 = (bf16[216]{0:T(256)(128)(2,1)S(1)}, bf16[216]{0:T(256)(128)(2,1)}, u32[]{:S(2)}) copy-start(bf16[216]{0:T(256)(128)(2,1)} %w1_ref.1) | copy-start | bytes 1300
  10.8 0.7 %copy-start.5 = (bf16[108]{0:T(256)(128)(2,1)S(1)}, bf16[108]{0:T(256)(128)(2,1)}, u32[]{:S(2)}) copy-start(bf16[108]{0:T(256)(128)(2,1)} %w4_ref.1) | copy-start | bytes 652
  12.3 5.8 %copy-start.6 = (s32[1,4]{1,0:T(1,128)S(1)}, s32[1,4]{1,0:T(1,128)}, u32[]{:S(2)}) copy-start(s32[1,4]{1,0:T(1,128)} %param.10) | copy-start | bytes 52
  12.3 5.8 %copy-start.7 = (s32[1,4]{1,0:T(1,128)S(1)}, s32[1,4]{1,0:T(1,128)}, u32[]{:S(2)}) copy-start(s32[1,4]{1,0:T(1,128)} %param.11) | copy-start | bytes 52
  12.3 5.8 %copy-start.1 = (bf16[4,2,3,3,1,4,512]{6,5,4,3,2,1,0:T(4,128)(2,1)S(1)}, bf16[4,2,3,3,1,4,512]{6,5,4,3,2,1,0:T(4,128)(2,1)}, u32[]{:S(2)}) copy-start(bf16[4,2,3,3,1,4,512]{6,5,4,3,2,1,0:T(4,128)(2,1)} %cot_ref.1) | copy-start | bytes 884740
  12.3 16.3 %all-to-all-start = ((bf16[16,64,128]{2,1,0:T(8,128)(2,1)}), bf16[16,64,128]{2,1,0:T(8,128)(2,1)S(1)}, u32[]{:S(2)}, u32[]{:S(2)}) async-start(bf16[16,64,128]{2,1,0:T(8,128)(2,1)} %shard_map.122), calls=%async_computation | async-start | bytes 524288 | tf_op jit(solution)/shard_map/all_to_all | solution.py:835
  21.2 11.4 %collective-permute-start.2 = (bf16[4,16,512]{2,1,0:T(8,128)(2,1)S(1)}, bf16[4,16,512]{2,1,0:T(8,128)(2,1)S(1)}, u32[]{:S(2)}, u32[]{:S(2)}) collective-permute-start(bf16[4,16,512]{2,1,0:T(8,128)(2,1)S(1)} %get-tuple-element.34.fm_ref), channel_id=1, source_target_pairs={{0,1},{2,3},{4,5},{6,7},{8,9},{10,11},{12,13},{14,15},{1,0},{3,2},... | collective-permute-start | bytes 196616 | tf_op jit(solution)/shard_map/ppermute | solution.py:807
  21.7 11.0 %collective-permute-start.3 = (bf16[4,16,512]{2,1,0:T(8,128)(2,1)S(1)}, bf16[4,16,512]{2,1,0:T(8,128)(2,1)S(1)}, u32[]{:S(2)}, u32[]{:S(2)}) collective-permute-start(bf16[4,16,512]{2,1,0:T(8,128)(2,1)S(1)} %get-tuple-element.34.fm_ref), channel_id=1, source_target_pairs={{1,2},{3,4},{5,6},{7,8},{9,10},{11,12},{13,14},{15,0},{2,1},{4,3},... | collective-permute-start | bytes 196616 | tf_op jit(solution)/shard_map/ppermute | solution.py:807
  26.0 3.9 %collective-permute-start.4 = (bf16[4,8,512]{2,1,0:T(8,128)(2,1)S(1)}, bf16[4,8,512]{2,1,0:T(8,128)(2,1)S(1)}, u32[]{:S(2)}, u32[]{:S(2)}) collective-permute-start(bf16[4,8,512]{2,1,0:T(8,128)(2,1)S(1)} %get-tuple-element.35), channel_id=1, source_target_pairs={{0,2},{1,3},{4,6},{5,7},{8,10},{9,11},{12,14},{13,15},{2,0},{3,1},... | collective-permute-start | bytes 98312 | tf_op jit(solution)/shard_map/ppermute | solution.py:807
  26.0 6.6 %collective-permute-start.5 = (bf16[4,8,512]{2,1,0:T(8,128)(2,1)S(1)}, bf16[4,8,512]{2,1,0:T(8,128)(2,1)S(1)}, u32[]{:S(2)}, u32[]{:S(2)}) collective-permute-start(bf16[4,8,512]{2,1,0:T(8,128)(2,1)S(1)} %get-tuple-element.35), channel_id=1, source_target_pairs={{2,4},{3,5},{6,8},{7,9},{10,12},{11,13},{14,0},{15,1},{4,2},{5,3},... | collective-permute-start | bytes 98312 | tf_op jit(solution)/shard_map/ppermute | solution.py:807
  41.9 11.4 %all-to-all-start.1 = ((bf16[16,27,128]{2,1,0:T(8,128)(2,1)}), bf16[16,27,128]{2,1,0:T(8,128)(2,1)S(1)}, u32[]{:S(2)}, u32[]{:S(2)}) async-start(bf16[16,27,128]{2,1,0:T(8,128)(2,1)} %get-tuple-element.46), calls=%async_computation.1 | async-start | bytes 262144 | tf_op jit(solution)/shard_map/all_to_all | solution.py:892

commit v17 on v16

--- a/solution.py
+++ b/solution.py
@@ -590,24 +590,27 @@
     return slice(slot * SITES, (slot + 1) * SITES)
 
 
-def stack_wide(source, target, index, slot):
-    chunks = chunks_of(source[:, span(index)])
-    for position, shifted in enumerate(all_shifts(chunks)):
-        for q in range(4):
-            lanes = slice(slot * SITES + q * 128, slot * SITES + q * 128 + 128)
-            target[H * position:H * position + H, lanes] = shifted[q]
-    target[7 * H:8 * H, slot_of(slot)] = source[:, span(index + 1)]
-    target[8 * H:9 * H, slot_of(slot)] = source[:, span(index - 1)]
-
-
-def stack_thin(source, target, index, slot):
-    chunks = chunks_of(source[:, span(index)])
+def wide_dot(weights, source, index, kept=None, slot=0):
+    shifts = all_shifts(chunks_of(source[:, span(index)]))
+    ahead, behind = source[:, span(index + 1)], source[:, span(index - 1)]
+    outs = []
+    for half in range(2):
+        lanes = slice(256 * half, 256 * half + 256)
+        columns = [jnp.concatenate(shifted[2 * half:2 * half + 2], axis=1) for shifted in shifts]
+        stack = jnp.concatenate(columns + [ahead[:, lanes], behind[:, lanes]], axis=0)
+        if kept is not None:
+            kept[:, slot * SITES + 256 * half:slot * SITES + 256 * half + 256] = stack
+        outs.append(jnp.dot(weights[...], stack, preferred_element_type=F32))
+    return jnp.concatenate(outs, axis=1)
+
+
+def thin_stack(source, index):
     ahead = chunks_of(source[:, span(index + 1)])
     behind = chunks_of(source[:, span(index - 1)])
-    columns = all_shifts(chunks) + [ahead, behind]
-    for q in range(4):
-        lanes = slice(slot * SITES + q * 128, slot * SITES + q * 128 + 128)
-        target[0:72, lanes] = jnp.concatenate([column[q] for column in columns], axis=0).astype(BF16)
+    columns = all_shifts(chunks_of(source[:, span(index)])) + [ahead, behind]
+    return jnp.concatenate(
+        [jnp.concatenate([column[q] for column in columns], axis=0).astype(BF16) for q in range(4)], axis=1
+    )
 
 
 def one_minus_square(value):
@@ -619,7 +622,7 @@
     split, place_ref, fm_ref, near_ref, far_ref, near_chip_ref, far_chip_ref, loops_ref,
     p1_ref, p2_ref, p3_ref, p4_ref, b2_ref, b3_ref, b4_ref,
     coeff_ref, grads_ref,
-    feats, mixed, h1, h2, h3, parts, lasts, g3, g2, g1, wide, wide_back, wide_first, thin, thin_back, packed,
+    feats, mixed, h1, h2, h3, parts, lasts, g3, g2, g1, wide_back, wide_first, thin, thin_back, packed,
 ):
     row8 = lax.broadcasted_iota(jnp.int32, (8, SITES), 0)
     loop_re = jnp.concatenate([loops_ref[0, q:q + 1, :] for q in range(4)], axis=1)
@@ -643,20 +646,21 @@
     own = span(7, 4)
     contract = (((1,), (1,)), ((), ()))
 
-    def own_slot(index, others):
-        return index - 7 if 7 <= index < 11 else 4 + others.index(index)
-
-    def dot(weights, stack, slot):
-        return jnp.dot(weights[...], stack[:, slot_of(slot)], preferred_element_type=F32)
-
-    def first_dot(index):
-        h1[:, span(index)] = jnp.tanh(dot(p1_ref, thin, index % 4)).astype(BF16)
-
-    def second_dot(index):
-        h2[:, span(index)] = jnp.tanh(dot(p2_ref, wide, index % 2)).astype(BF16)
-
-    def third_dot(index):
-        h3[:, span(index)] = jnp.tanh(dot(p3_ref, wide, 2 + index % 2)).astype(BF16)
+    def kept_slot(index):
+        return index - 7 if 7 <= index < 11 else None
+
+    def first_layer(index):
+        stack = thin_stack(feats, index)
+        if kept_slot(index) is not None:
+            thin[:, slot_of(index - 7)] = stack
+        out = jnp.dot(p1_ref[...], stack, preferred_element_type=F32)
+        h1[:, span(index)] = jnp.tanh(out).astype(BF16)
+
+    def second_layer(index):
+        h2[:, span(index)] = jnp.tanh(wide_dot(p2_ref, h1, index)).astype(BF16)
+
+    def third_layer(index):
+        h3[:, span(index)] = jnp.tanh(wide_dot(p3_ref, h2, index)).astype(BF16)
 
     def taps_of(index):
         taps = jnp.dot(p4_ref[...], h3[:, span(index)], preferred_element_type=F32)
@@ -676,62 +680,55 @@
         if 7 <= index < 11:
             coeff_ref[index - 7] = coeff
 
-    halo3, halo2 = (5, 6, 11, 12), (6, 11)
-
     def back_third(index):
-        out = dot(b4_ref, thin_back, own_slot(index, halo3))
+        stack = thin_stack(lasts, index)
+        if kept_slot(index) is not None:
+            thin_back[:, slot_of(index - 7)] = stack
+        out = jnp.dot(b4_ref[...], stack, preferred_element_type=F32)
         g3[:, span(index)] = (out * one_minus_square(h3[:, span(index)])).astype(BF16)
 
     def back_second(index):
-        out = dot(b3_ref, wide_back, own_slot(index, halo2))
+        slot = kept_slot(index)
+        out = wide_dot(b3_ref, g3, index, None if slot is None else wide_back, slot or 0)
         g2[:, span(index)] = (out * one_minus_square(h2[:, span(index)])).astype(BF16)
 
     def back_first(index):
-        out = dot(b2_ref, wide_first, index - 7)
+        out = wide_dot(b2_ref, g2, index, wide_first, index - 7)
         g1[:, slot_of(index - 7)] = (out * one_minus_square(h1[:, span(index)])).astype(BF16)
 
     stages = (
-        (0, 1, 17, lambda i: stack_thin(feats, thin, i, i % 4)),
-        (1, 1, 17, first_dot),
-        (3, 2, 16, lambda i: stack_wide(h1, wide, i, i % 2)),
-        (4, 2, 16, second_dot),
-        (6, 3, 15, lambda i: stack_wide(h2, wide, i, 2 + i % 2)),
-        (7, 3, 15, third_dot),
-        (8, 3, 15, taps_of),
-        (10, 4, 14, last_of),
-        (12, 5, 13, lambda i: stack_thin(lasts, thin_back, i, own_slot(i, halo3))),
-        (13, 5, 13, back_third),
-        (15, 6, 12, lambda i: stack_wide(g3, wide_back, i, own_slot(i, halo2))),
-        (16, 6, 12, back_second),
-        (18, 7, 11, lambda i: stack_wide(g2, wide_first, i, i - 7)),
-        (19, 7, 11, back_first),
+        (0, 1, 17, first_layer),
+        (2, 2, 16, second_layer),
+        (4, 3, 15, third_layer),
+        (5, 3, 15, taps_of),
+        (7, 4, 14, last_of),
+        (9, 5, 13, back_third),
+        (11, 6, 12, back_second),
+        (13, 7, 11, back_first),
     )
-    for step in range(1, 30):
+    for step in range(1, 24):
         for delay, low, high, task in reversed(stages):
             if low <= step - delay < high:
                 task(step - delay)
-        if step == 18:
-            for index in (7, 8, 9, 10):
-                stack_thin(feats, thin, index, index - 7)
-        if step == 23:
+        if step == 19:
             grad_last = lax.dot_general(
-                thin_back[:, 0:4 * SITES], h3[:, own], contract, preferred_element_type=F32
+                thin_back[...], h3[:, own], contract, preferred_element_type=F32
             )
             spread, keep = selectors()
             ordered = jnp.concatenate([grad_last[8 * SWAP[k]:8 * SWAP[k] + 8] for k in range(TAPS)], axis=0)
             broad = jnp.dot(spread, ordered.astype(BF16), preferred_element_type=F32)
-        if step == 24:
+        if step == 20:
             broad = jnp.where(keep, broad, 0.0).astype(BF16)
             place = (
                 lax.broadcasted_iota(jnp.int32, (H, LANES), 1)
                 == 104 + lax.broadcasted_iota(jnp.int32, (H, LANES), 0) % 4
             ).astype(F32).astype(BF16)
             packed[...] = jnp.dot(broad, place, preferred_element_type=F32)
-        if step == 26:
+        if step == 21:
             grad_third = lax.dot_general(
-                wide_back[:, 0:4 * SITES], h2[:, own], contract, preferred_element_type=F32
+                wide_back[...], h2[:, own], contract, preferred_element_type=F32
             )
-        if step == 27:
+        if step == 22:
             for k in range(TAPS):
                 packed[H * k:H * k + H, 48:96] = grad_third[H * SWAP[k]:H * SWAP[k] + H]
     grad_second = lax.dot_general(wide_first[...], h1[:, own], contract, preferred_element_type=F32)
@@ -876,8 +873,8 @@
         [
             ((8, window), F32), ((8, window), F32), ((H, window), BF16), ((H, window), BF16), ((H, window), BF16),
             ((3, 8, window), F32), ((8, window), F32), ((H, window), BF16), ((H, window), BF16), ((H, 4 * SITES), BF16),
-            ((432, 4 * SITES), BF16), ((432, 6 * SITES), BF16), ((432, 4 * SITES), BF16),
-            ((72, 4 * SITES), BF16), ((72, 8 * SITES), BF16), ((432, LANES), F32),
+            ((432, 4 * SITES), BF16), ((432, 4 * SITES), BF16), ((72, 4 * SITES), BF16), ((72, 4 * SITES), BF16),
+            ((432, LANES), F32),
         ],
         limit=20 * 1024 * 1024,
         places=(smem,) + (vmem,) * 13,

time: 54.5 us -> 54.2 us (level)
  no operation moved by 1% of the time
where the time goes in v17:
time: 54.2 us; the launch traced here: 53.7 us
  starting transfers between devices  21.7 us (40%)
  Pallas kernels  19.3 us (36%)
  waiting for transfers between devices  10.2 us (19%)
  local copies, waits for them, and re-layouts  1.73 us (3%)
  between operations  0.77 us (1%)
    pallas_call x1, Pallas kernels, on_device(): call(functools.partial(conv_kernel, count == 16), [((4, 8, SITES), F32),...  8.95 us
    all_to_all x1, waiting for transfers between devices, on_device(): grads = lax.all_to_all(grads, 'tm', split_axis=0, concat_axis=0, tiled=True)  6.88 us
    ppermute x4, starting transfers between devices, swap(): lax.ppermute(value, 'tm', pairs + [(target, source) for source, target in...  6.83 us
    all_to_all x1, starting transfers between devices, on_device(): lax.all_to_all(block, 'tm', split_axis=0, concat_axis=0, tiled=True)  5.8 us
    ppermute x2, starting transfers between devices, send(): lax.ppermute(value, 'tm', [(i, (i + distance) % count) for i in range(cou...  5.56 us
    all_to_all x1, starting transfers between devices, on_device(): grads = lax.all_to_all(grads, 'tm', split_axis=0, concat_axis=0, tiled=True)  3.51 us
    pallas_call x1, Pallas kernels, on_device(): call(time_kernel, [((4, 16, SITES), BF16), ((4, 8, SITES), BF16), ((2, 4,...  3.04 us
    ppermute x4, waiting for transfers between devices, swap(): lax.ppermute(value, 'tm', pairs + [(target, source) for source, target in...  2.72 us
  transfers between devices with their start and end apart: 8, of which 3 were waited for; matrix products, arithmetic and copies ran while one was open for 0% of the time, Pallas kernels for 14%

profile of v17, /device:TPU:0, one launch (start us, length us, event | category | flops | bytes accessed | tf_op | source)
XLA Modules:
  0.0 53.7 jit_solution(4898498621687276155)
XLA Ops:
  0.6 1.1 %copy-done = f32[4,2,3,3,1,4,512]{6,5,4,3,2,1,0:T(4,128)S(1)} copy-done((f32[4,2,3,3,1,4,512]{6,5,4,3,2,1,0:T(4,128)S(1)}, f32[4,2,3,3,1,4,512]{6,5,4,3,2,1,0:T(4,128)}, u32[]{:S(2)}) %copy-start) | copy-done | bytes 589848
  1.7 1.3 %shard_map.119 = (bf16[70,512]{1,0:T(8,128)(2,1)S(1)}, bf16[70,512]{1,0:T(8,128)(2,1)S(1)}, f32[4,18,2,8,128]{4,3,2,1,0:T(8,128)S(1)}, f32[3,18,2,8,128]{4,3,2,1...) custom-call(f32[4,2,3,3,1,4,512]{6,5,4,3,2,1,0:T(4,128)S(1)} %copy-done), custom_call_target="tpu_custom_call" | custom-call | tf_op jit(solution)/shard_map/pallas_call | solution.py:812
  3.0 0.5 collective-permute-start
  3.5 5.1 %collective-permute-start.1 = (bf16[70,512]{1,0:T(8,128)(2,1)S(1)}, bf16[70,512]{1,0:T(8,128)(2,1)S(1)}, u32[]{:S(2)}, u32[]{:S(2)}) collective-permute-start(bf16[70,512]{1,0:T(8,128)(2,1)S(1)} %get-tuple-element.32), channel_id=1, source_target_pairs={{0,15},{1,0},{2,1},{3,2},{4,3},{5,4},{6,5},{7,6},{8,7},{9,8},{10,9... | collective-permute-start | bytes 215048 | tf_op jit(solution)/shard_map/ppermute | solution.py:801
  8.6 2.1 %shard_map.120.state.after_ref = f32[186,8,128]{2,1,0:T(8,128)S(1)} custom-call(f32[4,18,2,8,128]{4,3,2,1,0:T(8,128)S(1)} %get-tuple-element.28.dense, f32[3,18,2,8,128]{4,3,2,1,0:T(8,128)S(1)} %get-tuple-element.30.time_staples), custom_call_target="tpu_custom_call" | custom-call | flops 4000000000 | bytes 16000000 | tf_op jit(solution)/shard_map/pallas_call | solution.py:819
  10.7 0.0 copy-start.3
  10.8 0.6 %copy-done.3 = bf16[1296]{0:T(1024)(128)(2,1)S(1)} copy-done((bf16[1296]{0:T(1024)(128)(2,1)S(1)}, bf16[1296]{0:T(1024)(128)(2,1)}, u32[]{:S(2)}) %copy-start.3) | copy-done | bytes 2616
  11.4 0.0 copy-done.2
  11.4 0.0 copy-done.5
  11.4 0.9 %shard_map.122 = bf16[16,64,128]{2,1,0:T(8,128)(2,1)} custom-call(s32[1]{0:T(128)} %bitcast.place_ref, bf16[70,512]{1,0:T(8,128)(2,1)S(1)} %collective-permute-done.up_ref, bf16[70,512]{1,0:T(8,128)(2,1)S(1)} %collective-permute-done.1.down_ref, f32[12,4,128]{2,1,0:T(4,128)S(1)} %get-tuple-element.36.slab, bf16[216]{0:T(256)(128)(2,1)S(1)} %copy-done.4, ...), custom_call_target="tpu_custom_call" | custom-call | tf_op jit(solution)/shard_map/pallas_call | solution.py:826
  12.3 5.8 %all-to-all-start = ((bf16[16,64,128]{2,1,0:T(8,128)(2,1)}), bf16[16,64,128]{2,1,0:T(8,128)(2,1)S(1)}, u32[]{:S(2)}, u32[]{:S(2)}) async-start(bf16[16,64,128]{2,1,0:T(8,128)(2,1)} %shard_map.122), calls=%async_computation | async-start | bytes 524288 | tf_op jit(solution)/shard_map/all_to_all | solution.py:832
  18.2 3.0 %shard_map.121 = (bf16[4,16,512]{2,1,0:T(8,128)(2,1)S(1)}, bf16[4,8,512]{2,1,0:T(8,128)(2,1)S(1)}, bf16[2,4,18,2,8,128]{5,4,3,2,1,0:T(8,128)(2,1)S(1)}) custom-call(s32[1,4]{1,0:T(1,128)S(1)} %multiply_add_fusion.code_ref, f32[4,18,2,8,128]{4,3,2,1,0:T(8,128)S(1)} %get-tuple-element.28.dense, f32[3,18,2,8,128]{4,3,2,1,0:T(8,128)S(1)} %get-tuple-element.29.edges, ...), custom_call_target="tpu_custom_call" | custom-call | tf_op jit(solution)/shard_map/pallas_call | solution.py:833
  21.2 0.5 collective-permute-start.2
  21.7 4.3 %collective-permute-start.3 = (bf16[4,16,512]{2,1,0:T(8,128)(2,1)S(1)}, bf16[4,16,512]{2,1,0:T(8,128)(2,1)S(1)}, u32[]{:S(2)}, u32[]{:S(2)}) collective-permute-start(bf16[4,16,512]{2,1,0:T(8,128)(2,1)S(1)} %get-tuple-element.34.fm_ref), channel_id=1, source_target_pairs={{1,2},{3,4},{5,6},{7,8},{9,10},{11,12},{13,14},{15,0},{2,1},{4,3},... | collective-permute-start | bytes 196616 | tf_op jit(solution)/shard_map/ppermute | solution.py:804
  26.0 2.0 %collective-permute-start.5 = (bf16[4,8,512]{2,1,0:T(8,128)(2,1)S(1)}, bf16[4,8,512]{2,1,0:T(8,128)(2,1)S(1)}, u32[]{:S(2)}, u32[]{:S(2)}) collective-permute-start(bf16[4,8,512]{2,1,0:T(8,128)(2,1)S(1)} %get-tuple-element.35), channel_id=1, source_target_pairs={{2,4},{3,5},{6,8},{7,9},{10,12},{11,13},{14,0},{15,1},{4,2},{5,3},... | collective-permute-start | bytes 98312 | tf_op jit(solution)/shard_map/ppermute | solution.py:804
  28.0 0.6 %all-to-all-done.gathered_ref = bf16[16,64,128]{2,1,0:T(8,128)(2,1)S(1)} async-done(((bf16[16,64,128]{2,1,0:T(8,128)(2,1)}), bf16[16,64,128]{2,1,0:T(8,128)(2,1)S(1)}, u32[]{:S(2)}, u32[]{:S(2)}) %all-to-all-start) | async-done | bytes 262176 | tf_op jit(solution)/shard_map/all_to_all | solution.py:832
  28.6 1.3 %shard_map.123 = (f32[2,4,128]{2,1,0:T(4,128)S(1)}, bf16[48,72]{1,0:T(8,128)(2,1)S(1)}, bf16[48,432]{1,0:T(8,128)(2,1)S(1)}, bf16[48,432]{1,0:T(8,128)(2,1)S(1)}...) custom-call(bf16[16,64,128]{2,1,0:T(8,128)(2,1)S(1)} %all-to-all-don, ...), custom_call_target="tpu_custom_call" | custom-call | tf_op jit(solution)/shard_map/pallas_call | solution.py:856
  29.9 0.0 collective-permute-done.4.near_chip_ref
  29.9 2.7 %collective-permute-done.5.far_chip_ref = bf16[4,8,512]{2,1,0:T(8,128)(2,1)S(1)} collective-permute-done((bf16[4,8,512]{2,1,0:T(8,128)(2,1)S(1)}, bf16[4,8,512]{2,1,0:T(8,128)(2,1)S(1)}, u32[]{:S(2)}, u32[]{:S(2)}) %collective-permute-start.5) | collective-permute-done | bytes 32800 | tf_op jit(solution)/shard_map/ppermute | solution.py:804
  32.6 8.9 %shard_map.124 = (f32[4,8,512]{2,1,0:T(8,128)S(1)}, bf16[16,27,128]{2,1,0:T(8,128)(2,1)}) custom-call(s32[1]{0:T(128)} %bitcast.place_ref, bf16[4,16,512]{2,1,0:T(8,128)(2,1)S(1)} %get-tuple-element.34.fm_ref, bf16[4,16,512]{2,1,0:T(8,128)(2,1)S(1)} %collective-permute-done.2.near_ref, bf16[4,16,512]{2,1,0:T(8,128)(2,1)S(1)} %collective-permute-done.3.far_ref, ...), custom_call_target="tpu_custom_call" | custom-call | tf_op jit(solution)/shard_map/pallas_call | solution.py:870
  41.6 3.5 %all-to-all-start.1 = ((bf16[16,27,128]{2,1,0:T(8,128)(2,1)}), bf16[16,27,128]{2,1,0:T(8,128)(2,1)S(1)}, u32[]{:S(2)}, u32[]{:S(2)}) async-start(bf16[16,27,128]{2,1,0:T(8,128)(2,1)} %get-tuple-element.46), calls=%async_computation.1 | async-start | bytes 262144 | tf_op jit(solution)/shard_map/all_to_all | solution.py:889
  45.1 1.0 %shard_map.125 = f32[4,2,3,3,1,4,512]{6,5,4,3,2,1,0:T(4,128)} custom-call(f32[4,18,2,8,128]{4,3,2,1,0:T(8,128)S(1)} %get-tuple-element.28.dense, bf16[2,4,18,2,8,128]{5,4,3,2,1,0:T(8,128)(2,1)S(1)} %get-tuple-element.33.moves_ref, f32[4,8,512]{2,1,0:T(8,128)S(1)} %get-tuple-element.45.coeff_ref), custom_call_target="tpu_custom_call" | custom-call | tf_op jit(solution)/shard_map/pallas_call | solution.py:890
  46.1 6.9 %all-to-all-done.1.parts_ref = bf16[16,27,128]{2,1,0:T(8,128)(2,1)S(1)} async-done(((bf16[16,27,128]{2,1,0:T(8,128)(2,1)}), bf16[16,27,128]{2,1,0:T(8,128)(2,1)S(1)}, u32[]{:S(2)}, u32[]{:S(2)}) %all-to-all-start.1) | async-done | bytes 110624 | tf_op jit(solution)/shard_map/all_to_all | solution.py:889
  53.0 0.8 %shard_map.126 = (f32[1,216]{1,0:T(1,128)}, f32[1,1296]{1,0:T(1,128)}, f32[1,1296]{1,0:T(1,128)}, f32[1,108]{1,0:T(1,128)}) custom-call(bf16[16,27,128]{2,1,0:T(8,128)(2,1)S(1)} %all-to-all-done.1.parts_ref), custom_call_target="tpu_custom_call" | custom-call | tf_op jit(solution)/shard_map/pallas_call | solution.py:893
  (17 shorter events, 0.0 us)
Async XLA Ops:
  0.6 1.1 %copy-start = (f32[4,2,3,3,1,4,512]{6,5,4,3,2,1,0:T(4,128)S(1)}, f32[4,2,3,3,1,4,512]{6,5,4,3,2,1,0:T(4,128)}, u32[]{:S(2)}) copy-start(f32[4,2,3,3,1,4,512]{6,5,4,3,2,1,0:T(4,128)} %links_ref.1) | copy-start | bytes 1769476
  3.0 7.7 %collective-permute-start = (bf16[70,512]{1,0:T(8,128)(2,1)S(1)}, bf16[70,512]{1,0:T(8,128)(2,1)S(1)}, u32[]{:S(2)}, u32[]{:S(2)}) collective-permute-start(bf16[70,512]{1,0:T(8,128)(2,1)S(1)} %get-tuple-element.31), channel_id=1, source_target_pairs={{0,1},{1,2},{2,3},{3,4},{4,5},{5,6},{6,7},{7,8},{8,9},{9,10},{10,1... | collective-permute-start | bytes 215048 | tf_op jit(solution)/shard_map/ppermute | solution.py:801
  3.5 7.2 %collective-permute-start.1 = (bf16[70,512]{1,0:T(8,128)(2,1)S(1)}, bf16[70,512]{1,0:T(8,128)(2,1)S(1)}, u32[]{:S(2)}, u32[]{:S(2)}) collective-permute-start(bf16[70,512]{1,0:T(8,128)(2,1)S(1)} %get-tuple-element.32), channel_id=1, source_target_pairs={{0,15},{1,0},{2,1},{3,2},{4,3},{5,4},{6,5},{7,6},{8,7},{9,8},{10,9... | collective-permute-start | bytes 215048 | tf_op jit(solution)/shard_map/ppermute | solution.py:801
  10.7 0.7 %copy-start.3 = (bf16[1296]{0:T(1024)(128)(2,1)S(1)}, bf16[1296]{0:T(1024)(128)(2,1)}, u32[]{:S(2)}) copy-start(bf16[1296]{0:T(1024)(128)(2,1)} %w3_ref.1) | copy-start | bytes 7780
  10.7 0.7 %copy-start.2 = (bf16[1296]{0:T(1024)(128)(2,1)S(1)}, bf16[1296]{0:T(1024)(128)(2,1)}, u32[]{:S(2)}) copy-start(bf16[1296]{0:T(1024)(128)(2,1)} %w2_ref.1) | copy-start | bytes 7780
  10.7 0.7 %copy-start.4 = (bf16[216]{0:T(256)(128)(2,1)S(1)}, bf16[216]{0:T(256)(128)(2,1)}, u32[]{:S(2)}) copy-start(bf16[216]{0:T(256)(128)(2,1)} %w1_ref.1) | copy-start | bytes 1300
  10.8 0.7 %copy-start.5 = (bf16[108]{0:T(256)(128)(2,1)S(1)}, bf16[108]{0:T(256)(128)(2,1)}, u32[]{:S(2)}) copy-start(bf16[108]{0:T(256)(128)(2,1)} %w4_ref.1) | copy-start | bytes 652
  12.3 5.8 %copy-start.6 = (s32[1,4]{1,0:T(1,128)S(1)}, s32[1,4]{1,0:T(1,128)}, u32[]{:S(2)}) copy-start(s32[1,4]{1,0:T(1,128)} %param.10) | copy-start | bytes 52
  12.3 5.8 %copy-start.7 = (s32[1,4]{1,0:T(1,128)S(1)}, s32[1,4]{1,0:T(1,128)}, u32[]{:S(2)}) copy-start(s32[1,4]{1,0:T(1,128)} %param.11) | copy-start | bytes 52
  12.3 5.8 %copy-start.1 = (bf16[4,2,3,3,1,4,512]{6,5,4,3,2,1,0:T(4,128)(2,1)S(1)}, bf16[4,2,3,3,1,4,512]{6,5,4,3,2,1,0:T(4,128)(2,1)}, u32[]{:S(2)}) copy-start(bf16[4,2,3,3,1,4,512]{6,5,4,3,2,1,0:T(4,128)(2,1)} %cot_ref.1) | copy-start | bytes 884740
  12.3 16.3 %all-to-all-start = ((bf16[16,64,128]{2,1,0:T(8,128)(2,1)}), bf16[16,64,128]{2,1,0:T(8,128)(2,1)S(1)}, u32[]{:S(2)}, u32[]{:S(2)}) async-start(bf16[16,64,128]{2,1,0:T(8,128)(2,1)} %shard_map.122), calls=%async_computation | async-start | bytes 524288 | tf_op jit(solution)/shard_map/all_to_all | solution.py:832
  21.2 11.4 %collective-permute-start.2 = (bf16[4,16,512]{2,1,0:T(8,128)(2,1)S(1)}, bf16[4,16,512]{2,1,0:T(8,128)(2,1)S(1)}, u32[]{:S(2)}, u32[]{:S(2)}) collective-permute-start(bf16[4,16,512]{2,1,0:T(8,128)(2,1)S(1)} %get-tuple-element.34.fm_ref), channel_id=1, source_target_pairs={{0,1},{2,3},{4,5},{6,7},{8,9},{10,11},{12,13},{14,15},{1,0},{3,2},... | collective-permute-start | bytes 196616 | tf_op jit(solution)/shard_map/ppermute | solution.py:804
  21.7 11.0 %collective-permute-start.3 = (bf16[4,16,512]{2,1,0:T(8,128)(2,1)S(1)}, bf16[4,16,512]{2,1,0:T(8,128)(2,1)S(1)}, u32[]{:S(2)}, u32[]{:S(2)}) collective-permute-start(bf16[4,16,512]{2,1,0:T(8,128)(2,1)S(1)} %get-tuple-element.34.fm_ref), channel_id=1, source_target_pairs={{1,2},{3,4},{5,6},{7,8},{9,10},{11,12},{13,14},{15,0},{2,1},{4,3},... | collective-permute-start | bytes 196616 | tf_op jit(solution)/shard_map/ppermute | solution.py:804
  26.0 3.9 %collective-permute-start.4 = (bf16[4,8,512]{2,1,0:T(8,128)(2,1)S(1)}, bf16[4,8,512]{2,1,0:T(8,128)(2,1)S(1)}, u32[]{:S(2)}, u32[]{:S(2)}) collective-permute-start(bf16[4,8,512]{2,1,0:T(8,128)(2,1)S(1)} %get-tuple-element.35), channel_id=1, source_target_pairs={{0,2},{1,3},{4,6},{5,7},{8,10},{9,11},{12,14},{13,15},{2,0},{3,1},... | collective-permute-start | bytes 98312 | tf_op jit(solution)/shard_map/ppermute | solution.py:804
  26.0 6.6 %collective-permute-start.5 = (bf16[4,8,512]{2,1,0:T(8,128)(2,1)S(1)}, bf16[4,8,512]{2,1,0:T(8,128)(2,1)S(1)}, u32[]{:S(2)}, u32[]{:S(2)}) collective-permute-start(bf16[4,8,512]{2,1,0:T(8,128)(2,1)S(1)} %get-tuple-element.35), channel_id=1, source_target_pairs={{2,4},{3,5},{6,8},{7,9},{10,12},{11,13},{14,0},{15,1},{4,2},{5,3},... | collective-permute-start | bytes 98312 | tf_op jit(solution)/shard_map/ppermute | solution.py:804
  41.6 11.4 %all-to-all-start.1 = ((bf16[16,27,128]{2,1,0:T(8,128)(2,1)}), bf16[16,27,128]{2,1,0:T(8,128)(2,1)S(1)}, u32[]{:S(2)}, u32[]{:S(2)}) async-start(bf16[16,27,128]{2,1,0:T(8,128)(2,1)} %get-tuple-element.46), calls=%async_computation.1 | async-start | bytes 262144 | tf_op jit(solution)/shard_map/all_to_all | solution.py:889

commit v18 on v17

--- a/solution.py
+++ b/solution.py
@@ -14,6 +14,8 @@
 LANES = 128
 SITES = 512
 PAIRS = ((0, 1), (0, 2), (0, 3), (1, 2), (1, 3), (2, 3))
+STACKED = (2, 3, 4, 5, 6)
+AFTER = (0, 1, 7, 8)
 SWAP = (0, 2, 1, 4, 3, 6, 5, 8, 7)
 ENTRIES = tuple((c, i, j) for c in range(2) for i in range(3) for j in range(3))
 PLANE = 180
@@ -490,7 +492,10 @@
     return spread, keep
 
 
-def panel_kernel(gathered_ref, weights_ref, loops_ref, p1_ref, p2_ref, p3_ref, p4_ref, b2_ref, b3_ref, b4_ref, weights):
+def panel_kernel(
+    gathered_ref, weights_ref, loops_ref, p1_ref, p4_ref, b4_ref,
+    s2_ref, s3_ref, t2_ref, t3_ref, a2_ref, a3_ref, c2_ref, c3_ref, weights,
+):
     count = gathered_ref.shape[0]
 
     def read(chip):
@@ -521,12 +526,17 @@
     for k in range(TAPS):
         rows = slice(H * k, H * k + H)
         back = slice(H * SWAP[k], H * SWAP[k] + H)
-        p2_ref[:, rows] = weights[rows, 0:48].astype(BF16)
-        p3_ref[:, rows] = weights[rows, 48:96].astype(BF16)
         p1_ref[:, 8 * k:8 * k + 8] = weights[rows, 96:104].astype(BF16)
         turned = weights[back, :].T
-        b2_ref[:, rows] = turned[0:48].astype(BF16)
-        b3_ref[:, rows] = turned[48:96].astype(BF16)
+        pieces = (weights[rows, 0:48], weights[rows, 48:96], turned[0:48], turned[48:96])
+        if k in STACKED:
+            place = slice(H * STACKED.index(k), H * STACKED.index(k) + H)
+            for ref, piece in zip((s2_ref, s3_ref, t2_ref, t3_ref), pieces):
+                ref[:, place] = piece.astype(BF16)
+        else:
+            place = slice(H * AFTER.index(k), H * AFTER.index(k) + H)
+            for ref, piece in zip((a2_ref, a3_ref, c2_ref, c3_ref), pieces):
+                ref[place, :] = piece.astype(BF16)
     spread, keep = selectors()
     place = (
         lax.broadcasted_iota(jnp.int32, (LANES, H), 0) == 104 + lax.broadcasted_iota(jnp.int32, (LANES, H), 1) % 4
@@ -590,18 +600,36 @@
     return slice(slot * SITES, (slot + 1) * SITES)
 
 
-def wide_dot(weights, source, index, kept=None, slot=0):
+def wide_mix(stacked, after, source, index, low, high, mixes, kept=None):
+    slot = slot_of(index % 4)
+    if index == low - 1:
+        mixes[2, :, slot] = jnp.dot(after[144:192, :], source[:, span(index)], preferred_element_type=F32)
+        return
+    if index == high:
+        mixes[1, :, slot] = jnp.dot(after[96:144, :], source[:, span(index)], preferred_element_type=F32)
+        return
     shifts = all_shifts(chunks_of(source[:, span(index)]))
-    ahead, behind = source[:, span(index + 1)], source[:, span(index - 1)]
     outs = []
     for half in range(2):
-        lanes = slice(256 * half, 256 * half + 256)
         columns = [jnp.concatenate(shifted[2 * half:2 * half + 2], axis=1) for shifted in shifts]
-        stack = jnp.concatenate(columns + [ahead[:, lanes], behind[:, lanes]], axis=0)
+        stack = jnp.concatenate([columns[k] for k in STACKED], axis=0)
         if kept is not None:
-            kept[:, slot * SITES + 256 * half:slot * SITES + 256 * half + 256] = stack
-        outs.append(jnp.dot(weights[...], stack, preferred_element_type=F32))
-    return jnp.concatenate(outs, axis=1)
+            lanes = slice((index - 7) * SITES + 256 * half, (index - 7) * SITES + 256 * half + 256)
+            kept[0:7 * H, lanes] = jnp.concatenate(columns, axis=0)
+        outs.append(jnp.dot(stacked[...], stack, preferred_element_type=F32))
+    terms = jnp.dot(after[...], source[:, span(index)], preferred_element_type=F32)
+    moved = jnp.concatenate(one_shift(chunks_of(terms[48:96]), 1), axis=1)
+    mixes[0, :, slot] = jnp.concatenate(outs, axis=1) + terms[0:48] + moved
+    mixes[1, :, slot] = terms[96:144]
+    mixes[2, :, slot] = terms[144:192]
+
+
+def wide_sum(mixes, index):
+    return (
+        mixes[0, :, slot_of(index % 4)]
+        + mixes[1, :, slot_of((index + 1) % 4)]
+        + mixes[2, :, slot_of((index - 1) % 4)]
+    )
 
 
 def thin_stack(source, index):
@@ -620,9 +648,9 @@
 
 def conv_kernel(
     split, place_ref, fm_ref, near_ref, far_ref, near_chip_ref, far_chip_ref, loops_ref,
-    p1_ref, p2_ref, p3_ref, p4_ref, b2_ref, b3_ref, b4_ref,
+    p1_ref, p4_ref, b4_ref, s2_ref, s3_ref, t2_ref, t3_ref, a2_ref, a3_ref, c2_ref, c3_ref,
     coeff_ref, grads_ref,
-    feats, mixed, h1, h2, h3, parts, lasts, g3, g2, g1, wide_back, wide_first, thin, thin_back, packed,
+    feats, mixed, h1, h2, h3, parts, lasts, g3, g2, g1, wide_back, wide_first, thin, thin_back, packed, mixes,
 ):
     row8 = lax.broadcasted_iota(jnp.int32, (8, SITES), 0)
     loop_re = jnp.concatenate([loops_ref[0, q:q + 1, :] for q in range(4)], axis=1)
@@ -656,11 +684,17 @@
         out = jnp.dot(p1_ref[...], stack, preferred_element_type=F32)
         h1[:, span(index)] = jnp.tanh(out).astype(BF16)
 
+    def second_mix(index):
+        wide_mix(s2_ref, a2_ref, h1, index, 2, 16, mixes.at[0])
+
     def second_layer(index):
-        h2[:, span(index)] = jnp.tanh(wide_dot(p2_ref, h1, index)).astype(BF16)
+        h2[:, span(index)] = jnp.tanh(wide_sum(mixes.at[0], index)).astype(BF16)
+
+    def third_mix(index):
+        wide_mix(s3_ref, a3_ref, h2, index, 3, 15, mixes.at[1])
 
     def third_layer(index):
-        h3[:, span(index)] = jnp.tanh(wide_dot(p3_ref, h2, index)).astype(BF16)
+        h3[:, span(index)] = jnp.tanh(wide_sum(mixes.at[1], index)).astype(BF16)
 
     def taps_of(index):
         taps = jnp.dot(p4_ref[...], h3[:, span(index)], preferred_element_type=F32)
@@ -687,48 +721,64 @@
         out = jnp.dot(b4_ref[...], stack, preferred_element_type=F32)
         g3[:, span(index)] = (out * one_minus_square(h3[:, span(index)])).astype(BF16)
 
+    def keep_times(source, kept, index):
+        kept[7 * H:8 * H, slot_of(index - 7)] = source[:, span(index + 1)]
+        kept[8 * H:9 * H, slot_of(index - 7)] = source[:, span(index - 1)]
+
+    def back_second_mix(index):
+        wide_mix(t3_ref, c3_ref, g3, index, 6, 12, mixes.at[2], wide_back if 7 <= index < 11 else None)
+
     def back_second(index):
-        slot = kept_slot(index)
-        out = wide_dot(b3_ref, g3, index, None if slot is None else wide_back, slot or 0)
+        if 7 <= index < 11:
+            keep_times(g3, wide_back, index)
+        out = wide_sum(mixes.at[2], index)
         g2[:, span(index)] = (out * one_minus_square(h2[:, span(index)])).astype(BF16)
 
+    def back_first_mix(index):
+        wide_mix(t2_ref, c2_ref, g2, index, 7, 11, mixes.at[3], wide_first if 7 <= index < 11 else None)
+
     def back_first(index):
-        out = wide_dot(b2_ref, g2, index, wide_first, index - 7)
+        keep_times(g2, wide_first, index)
+        out = wide_sum(mixes.at[3], index)
         g1[:, slot_of(index - 7)] = (out * one_minus_square(h1[:, span(index)])).astype(BF16)
 
     stages = (
         (0, 1, 17, first_layer),
-        (2, 2, 16, second_layer),
-        (4, 3, 15, third_layer),
-        (5, 3, 15, taps_of),
-        (7, 4, 14, last_of),
-        (9, 5, 13, back_third),
-        (11, 6, 12, back_second),
-        (13, 7, 11, back_first),
+        (1, 1, 17, second_mix),
+        (3, 2, 16, second_layer),
+        (4, 2, 16, third_mix),
+        (6, 3, 15, third_layer),
+        (7, 3, 15, taps_of),
+        (9, 4, 14, last_of),
+        (11, 5, 13, back_third),
+        (12, 5, 13, back_second_mix),
+        (14, 6, 12, back_second),
+        (15, 6, 12, back_first_mix),
+        (17, 7, 11, back_first),
     )
-    for step in range(1, 24):
+    for step in range(1, 28):
         for delay, low, high, task in reversed(stages):
             if low <= step - delay < high:
                 task(step - delay)
-        if step == 19:
+        if step == 21:
             grad_last = lax.dot_general(
                 thin_back[...], h3[:, own], contract, preferred_element_type=F32
             )
             spread, keep = selectors()
             ordered = jnp.concatenate([grad_last[8 * SWAP[k]:8 * SWAP[k] + 8] for k in range(TAPS)], axis=0)
             broad = jnp.dot(spread, ordered.astype(BF16), preferred_element_type=F32)
-        if step == 20:
+        if step == 22:
             broad = jnp.where(keep, broad, 0.0).astype(BF16)
             place = (
                 lax.broadcasted_iota(jnp.int32, (H, LANES), 1)
                 == 104 + lax.broadcasted_iota(jnp.int32, (H, LANES), 0) % 4
             ).astype(F32).astype(BF16)
             packed[...] = jnp.dot(broad, place, preferred_element_type=F32)
-        if step == 21:
+        if step == 24:
             grad_third = lax.dot_general(
                 wide_back[...], h2[:, own], contract, preferred_element_type=F32
             )
-        if step == 22:
+        if step == 25:
             for k in range(TAPS):
                 packed[H * k:H * k + H, 48:96] = grad_third[H * SWAP[k]:H * SWAP[k] + H]
     grad_second = lax.dot_general(wide_first[...], h1[:, own], contract, preferred_element_type=F32)
@@ -848,12 +898,11 @@
     near_core = swap(fm, [(i, i + 1) for i in range(0, count, 2)])
 
     panel_outs = [
-        ((2, 4, LANES), F32), ((H, 72), BF16), ((H, 432), BF16), ((H, 432), BF16), ((72, H), BF16),
-        ((H, 432), BF16), ((H, 432), BF16), ((H, 72), BF16),
-    ]
+        ((2, 4, LANES), F32), ((H, 72), BF16), ((72, H), BF16), ((H, 72), BF16),
+    ] + [((H, 240), BF16)] * 4 + [((192, H), BF16)] * 4
     panel_scratch = [((432, LANES), F32)]
     if count == 16:
-        loops, p1, p2, p3, p4, b2, b3, b4 = call(panel_kernel_plain, panel_outs, panel_scratch)(gathered)
+        loops, *panels = call(panel_kernel_plain, panel_outs, panel_scratch)(gathered)
     else:
         pieces = []
         offset = 0
@@ -862,7 +911,7 @@
             pieces.append(piece.reshape(432, full))
             offset += width
         pieces.append(jnp.zeros((432, 20), BF16))
-        loops, p1, p2, p3, p4, b2, b3, b4 = call(panel_kernel, panel_outs, panel_scratch)(
+        loops, *panels = call(panel_kernel, panel_outs, panel_scratch)(
             gathered, jnp.concatenate(pieces, axis=1)
         )
 
@@ -874,11 +923,11 @@
             ((8, window), F32), ((8, window), F32), ((H, window), BF16), ((H, window), BF16), ((H, window), BF16),
             ((3, 8, window), F32), ((8, window), F32), ((H, window), BF16), ((H, window), BF16), ((H, 4 * SITES), BF16),
             ((432, 4 * SITES), BF16), ((432, 4 * SITES), BF16), ((72, 4 * SITES), BF16), ((72, 4 * SITES), BF16),
-            ((432, LANES), F32),
+            ((432, LANES), F32), ((4, 3, H, 4 * SITES), F32),
         ],
         limit=20 * 1024 * 1024,
-        places=(smem,) + (vmem,) * 13,
-    )(place, fm, near_core, far_core, near_chip, far_chip, loops, p1, p2, p3, p4, b2, b3, b4)
+        places=(smem,) + (vmem,) * 17,
+    )(place, fm, near_core, far_core, near_chip, far_chip, loops, *panels)
     if count != 16:
         offset = 0
         pieces = []

time: 54.2 us -> 57.3 us (1.057)
  Pallas kernels: 19.3 us -> 22.5 us
    pallas_call x1, Pallas kernels: 8.95 us -> 12.1 us  [on_device(): call(functools.partial(conv_kernel, count == 16), [((4, 8, SITES), F32),...]
  transfers between devices with their start and end apart: 8 -> 8, of which waited for: 3 -> 3; matrix products, arithmetic and copies ran while one was open for 0% -> 0% of each run, Pallas kernels for 14% -> 13%
where the time goes in v18:
time: 57.3 us; the launch traced here: 56.9 us
  Pallas kernels  22.5 us (39%)
  starting transfers between devices  21.7 us (38%)
  waiting for transfers between devices  10.1 us (18%)
  local copies, waits for them, and re-layouts  1.73 us (3%)
  between operations  0.78 us (1%)
    pallas_call x1, Pallas kernels, on_device(): call(functools.partial(conv_kernel, count == 16), [((4, 8, SITES), F32),...  12.1 us
    all_to_all x1, waiting for transfers between devices, on_device(): grads = lax.all_to_all(grads, 'tm', split_axis=0, concat_axis=0, tiled=True)  6.88 us
    ppermute x4, starting transfers between devices, swap(): lax.ppermute(value, 'tm', pairs + [(target, source) for source, target in...  6.83 us
    all_to_all x1, starting transfers between devices, on_device(): lax.all_to_all(block, 'tm', split_axis=0, concat_axis=0, tiled=True)  5.8 us
    ppermute x2, starting transfers between devices, send(): lax.ppermute(value, 'tm', [(i, (i + distance) % count) for i in range(cou...  5.56 us
    all_to_all x1, starting transfers between devices, on_device(): grads = lax.all_to_all(grads, 'tm', split_axis=0, concat_axis=0, tiled=True)  3.51 us
    pallas_call x1, Pallas kernels, on_device(): call(time_kernel, [((4, 16, SITES), BF16), ((4, 8, SITES), BF16), ((2, 4,...  3.04 us
    ppermute x4, waiting for transfers between devices, swap(): lax.ppermute(value, 'tm', pairs + [(target, source) for source, target in...  2.65 us
  transfers between devices with their start and end apart: 8, of which 3 were waited for; matrix products, arithmetic and copies ran while one was open for 0% of the time, Pallas kernels for 13%

profile of v18, /device:TPU:0, one launch (start us, length us, event | category | flops | bytes accessed | tf_op | source)
XLA Modules:
  0.0 56.9 jit_solution(11142201486032983514)
XLA Ops:
  0.6 1.1 %copy-done = f32[4,2,3,3,1,4,512]{6,5,4,3,2,1,0:T(4,128)S(1)} copy-done((f32[4,2,3,3,1,4,512]{6,5,4,3,2,1,0:T(4,128)S(1)}, f32[4,2,3,3,1,4,512]{6,5,4,3,2,1,0:T(4,128)}, u32[]{:S(2)}) %copy-start) | copy-done | bytes 589848
  1.7 1.3 %shard_map.119 = (bf16[70,512]{1,0:T(8,128)(2,1)S(1)}, bf16[70,512]{1,0:T(8,128)(2,1)S(1)}, f32[4,18,2,8,128]{4,3,2,1,0:T(8,128)S(1)}, f32[3,18,2,8,128]{4,3,2,1...) custom-call(f32[4,2,3,3,1,4,512]{6,5,4,3,2,1,0:T(4,128)S(1)} %copy-done), custom_call_target="tpu_custom_call" | custom-call | tf_op jit(solution)/shard_map/pallas_call | solution.py:862
  3.0 0.5 collective-permute-start
  3.5 5.1 %collective-permute-start.1 = (bf16[70,512]{1,0:T(8,128)(2,1)S(1)}, bf16[70,512]{1,0:T(8,128)(2,1)S(1)}, u32[]{:S(2)}, u32[]{:S(2)}) collective-permute-start(bf16[70,512]{1,0:T(8,128)(2,1)S(1)} %get-tuple-element.36), channel_id=1, source_target_pairs={{0,15},{1,0},{2,1},{3,2},{4,3},{5,4},{6,5},{7,6},{8,7},{9,8},{10,9... | collective-permute-start | bytes 215048 | tf_op jit(solution)/shard_map/ppermute | solution.py:851
  8.6 2.1 %shard_map.120.state.after_ref = f32[186,8,128]{2,1,0:T(8,128)S(1)} custom-call(f32[4,18,2,8,128]{4,3,2,1,0:T(8,128)S(1)} %get-tuple-element.32.dense, f32[3,18,2,8,128]{4,3,2,1,0:T(8,128)S(1)} %get-tuple-element.34.time_staples), custom_call_target="tpu_custom_call" | custom-call | flops 4000000000 | bytes 16000000 | tf_op jit(solution)/shard_map/pallas_call | solution.py:869
  10.7 0.0 copy-start.2
  10.8 0.0 copy-start.5
  10.8 0.6 %copy-done.3 = bf16[1296]{0:T(1024)(128)(2,1)S(1)} copy-done((bf16[1296]{0:T(1024)(128)(2,1)S(1)}, bf16[1296]{0:T(1024)(128)(2,1)}, u32[]{:S(2)}) %copy-start.3) | copy-done | bytes 2616
  11.4 0.0 copy-done.2
  11.4 0.0 copy-done.5
  11.4 0.9 %shard_map.122 = bf16[16,64,128]{2,1,0:T(8,128)(2,1)} custom-call(s32[1]{0:T(128)} %bitcast.place_ref, bf16[70,512]{1,0:T(8,128)(2,1)S(1)} %collective-permute-done.up_ref, bf16[70,512]{1,0:T(8,128)(2,1)S(1)} %collective-permute-done.1.down_ref, f32[12,4,128]{2,1,0:T(4,128)S(1)} %get-tuple-element.40.slab, bf16[216]{0:T(256)(128)(2,1)S(1)} %copy-done.4, ...), custom_call_target="tpu_custom_call" | custom-call | tf_op jit(solution)/shard_map/pallas_call | solution.py:876
  12.3 5.8 %all-to-all-start = ((bf16[16,64,128]{2,1,0:T(8,128)(2,1)}), bf16[16,64,128]{2,1,0:T(8,128)(2,1)S(1)}, u32[]{:S(2)}, u32[]{:S(2)}) async-start(bf16[16,64,128]{2,1,0:T(8,128)(2,1)} %shard_map.122), calls=%async_computation | async-start | bytes 524288 | tf_op jit(solution)/shard_map/all_to_all | solution.py:882
  18.2 3.0 %shard_map.121 = (bf16[4,16,512]{2,1,0:T(8,128)(2,1)S(1)}, bf16[4,8,512]{2,1,0:T(8,128)(2,1)S(1)}, bf16[2,4,18,2,8,128]{5,4,3,2,1,0:T(8,128)(2,1)S(1)}) custom-call(s32[1,4]{1,0:T(1,128)S(1)} %multiply_add_fusion.code_ref, f32[4,18,2,8,128]{4,3,2,1,0:T(8,128)S(1)} %get-tuple-element.32.dense, f32[3,18,2,8,128]{4,3,2,1,0:T(8,128)S(1)} %get-tuple-element.33.edges, ...), custom_call_target="tpu_custom_call" | custom-call | tf_op jit(solution)/shard_map/pallas_call | solution.py:883
  21.2 0.5 collective-permute-start.2
  21.7 4.3 %collective-permute-start.3 = (bf16[4,16,512]{2,1,0:T(8,128)(2,1)S(1)}, bf16[4,16,512]{2,1,0:T(8,128)(2,1)S(1)}, u32[]{:S(2)}, u32[]{:S(2)}) collective-permute-start(bf16[4,16,512]{2,1,0:T(8,128)(2,1)S(1)} %get-tuple-element.38.fm_ref), channel_id=1, source_target_pairs={{1,2},{3,4},{5,6},{7,8},{9,10},{11,12},{13,14},{15,0},{2,1},{4,3},... | collective-permute-start | bytes 196616 | tf_op jit(solution)/shard_map/ppermute | solution.py:854
  26.0 2.0 %collective-permute-start.5 = (bf16[4,8,512]{2,1,0:T(8,128)(2,1)S(1)}, bf16[4,8,512]{2,1,0:T(8,128)(2,1)S(1)}, u32[]{:S(2)}, u32[]{:S(2)}) collective-permute-start(bf16[4,8,512]{2,1,0:T(8,128)(2,1)S(1)} %get-tuple-element.39), channel_id=1, source_target_pairs={{2,4},{3,5},{6,8},{7,9},{10,12},{11,13},{14,0},{15,1},{4,2},{5,3},... | collective-permute-start | bytes 98312 | tf_op jit(solution)/shard_map/ppermute | solution.py:854
  28.0 0.6 %all-to-all-done.gathered_ref = bf16[16,64,128]{2,1,0:T(8,128)(2,1)S(1)} async-done(((bf16[16,64,128]{2,1,0:T(8,128)(2,1)}), bf16[16,64,128]{2,1,0:T(8,128)(2,1)S(1)}, u32[]{:S(2)}, u32[]{:S(2)}) %all-to-all-start) | async-done | bytes 262176 | tf_op jit(solution)/shard_map/all_to_all | solution.py:882
  28.6 1.3 %shard_map.123 = (f32[2,4,128]{2,1,0:T(4,128)S(1)}, bf16[48,72]{1,0:T(8,128)(2,1)S(1)}, bf16[72,48]{1,0:T(8,128)(2,1)S(1)}, bf16[48,72]{1,0:T(8,128)(2,1)S(1)}, ...) custom-call(bf16[16,64,128]{2,1,0:T(8,128)(2,1)S(1)} %all-to-all-don, ...), custom_call_target="tpu_custom_call" | custom-call | tf_op jit(solution)/shard_map/pallas_call | solution.py:905
  30.0 2.6 %collective-permute-done.5.far_chip_ref = bf16[4,8,512]{2,1,0:T(8,128)(2,1)S(1)} collective-permute-done((bf16[4,8,512]{2,1,0:T(8,128)(2,1)S(1)}, bf16[4,8,512]{2,1,0:T(8,128)(2,1)S(1)}, u32[]{:S(2)}, u32[]{:S(2)}) %collective-permute-start.5) | collective-permute-done | bytes 32800 | tf_op jit(solution)/shard_map/ppermute | solution.py:854
  32.6 12.1 %shard_map.124 = (f32[4,8,512]{2,1,0:T(8,128)S(1)}, bf16[16,27,128]{2,1,0:T(8,128)(2,1)}) custom-call(s32[1]{0:T(128)} %bitcast.place_ref, bf16[4,16,512]{2,1,0:T(8,128)(2,1)S(1)} %get-tuple-element.38.fm_ref, bf16[4,16,512]{2,1,0:T(8,128)(2,1)S(1)} %collective-permute-done.2.near_ref, bf16[4,16,512]{2,1,0:T(8,128)(2,1)S(1)} %collective-permute-done.3.far_ref, ...), custom_call_target="tpu_custom_call" | custom-call | tf_op jit(solution)/shard_map/pallas_call | solution.py:919
  44.7 3.5 %all-to-all-start.1 = ((bf16[16,27,128]{2,1,0:T(8,128)(2,1)}), bf16[16,27,128]{2,1,0:T(8,128)(2,1)S(1)}, u32[]{:S(2)}, u32[]{:S(2)}) async-start(bf16[16,27,128]{2,1,0:T(8,128)(2,1)} %get-tuple-element.54), calls=%async_computation.1 | async-start | bytes 262144 | tf_op jit(solution)/shard_map/all_to_all | solution.py:938
  48.2 1.0 %shard_map.125 = f32[4,2,3,3,1,4,512]{6,5,4,3,2,1,0:T(4,128)} custom-call(f32[4,18,2,8,128]{4,3,2,1,0:T(8,128)S(1)} %get-tuple-element.32.dense, bf16[2,4,18,2,8,128]{5,4,3,2,1,0:T(8,128)(2,1)S(1)} %get-tuple-element.37.moves_ref, f32[4,8,512]{2,1,0:T(8,128)S(1)} %get-tuple-element.53.coeff_ref), custom_call_target="tpu_custom_call" | custom-call | tf_op jit(solution)/shard_map/pallas_call | solution.py:939
  49.2 6.9 %all-to-all-done.1.parts_ref = bf16[16,27,128]{2,1,0:T(8,128)(2,1)S(1)} async-done(((bf16[16,27,128]{2,1,0:T(8,128)(2,1)}), bf16[16,27,128]{2,1,0:T(8,128)(2,1)S(1)}, u32[]{:S(2)}, u32[]{:S(2)}) %all-to-all-start.1) | async-done | bytes 110624 | tf_op jit(solution)/shard_map/all_to_all | solution.py:938
  56.1 0.8 %shard_map.126 = (f32[1,216]{1,0:T(1,128)}, f32[1,1296]{1,0:T(1,128)}, f32[1,1296]{1,0:T(1,128)}, f32[1,108]{1,0:T(1,128)}) custom-call(bf16[16,27,128]{2,1,0:T(8,128)(2,1)S(1)} %all-to-all-done.1.parts_ref), custom_call_target="tpu_custom_call" | custom-call | tf_op jit(solution)/shard_map/pallas_call | solution.py:942
  (17 shorter events, 0.0 us)
Async XLA Ops:
  0.6 1.1 %copy-start = (f32[4,2,3,3,1,4,512]{6,5,4,3,2,1,0:T(4,128)S(1)}, f32[4,2,3,3,1,4,512]{6,5,4,3,2,1,0:T(4,128)}, u32[]{:S(2)}) copy-start(f32[4,2,3,3,1,4,512]{6,5,4,3,2,1,0:T(4,128)} %links_ref.1) | copy-start | bytes 1769476
  3.0 7.7 %collective-permute-start = (bf16[70,512]{1,0:T(8,128)(2,1)S(1)}, bf16[70,512]{1,0:T(8,128)(2,1)S(1)}, u32[]{:S(2)}, u32[]{:S(2)}) collective-permute-start(bf16[70,512]{1,0:T(8,128)(2,1)S(1)} %get-tuple-element.35), channel_id=1, source_target_pairs={{0,1},{1,2},{2,3},{3,4},{4,5},{5,6},{6,7},{7,8},{8,9},{9,10},{10,1... | collective-permute-start | bytes 215048 | tf_op jit(solution)/shard_map/ppermute | solution.py:851
  3.5 7.2 %collective-permute-start.1 = (bf16[70,512]{1,0:T(8,128)(2,1)S(1)}, bf16[70,512]{1,0:T(8,128)(2,1)S(1)}, u32[]{:S(2)}, u32[]{:S(2)}) collective-permute-start(bf16[70,512]{1,0:T(8,128)(2,1)S(1)} %get-tuple-element.36), channel_id=1, source_target_pairs={{0,15},{1,0},{2,1},{3,2},{4,3},{5,4},{6,5},{7,6},{8,7},{9,8},{10,9... | collective-permute-start | bytes 215048 | tf_op jit(solution)/shard_map/ppermute | solution.py:851
  10.7 0.7 %copy-start.3 = (bf16[1296]{0:T(1024)(128)(2,1)S(1)}, bf16[1296]{0:T(1024)(128)(2,1)}, u32[]{:S(2)}) copy-start(bf16[1296]{0:T(1024)(128)(2,1)} %w3_ref.1) | copy-start | bytes 7780
  10.7 0.7 %copy-start.2 = (bf16[1296]{0:T(1024)(128)(2,1)S(1)}, bf16[1296]{0:T(1024)(128)(2,1)}, u32[]{:S(2)}) copy-start(bf16[1296]{0:T(1024)(128)(2,1)} %w2_ref.1) | copy-start | bytes 7780
  10.7 0.7 %copy-start.4 = (bf16[216]{0:T(256)(128)(2,1)S(1)}, bf16[216]{0:T(256)(128)(2,1)}, u32[]{:S(2)}) copy-start(bf16[216]{0:T(256)(128)(2,1)} %w1_ref.1) | copy-start | bytes 1300
  10.8 0.7 %copy-start.5 = (bf16[108]{0:T(256)(128)(2,1)S(1)}, bf16[108]{0:T(256)(128)(2,1)}, u32[]{:S(2)}) copy-start(bf16[108]{0:T(256)(128)(2,1)} %w4_ref.1) | copy-start | bytes 652
  12.3 5.8 %copy-start.6 = (s32[1,4]{1,0:T(1,128)S(1)}, s32[1,4]{1,0:T(1,128)}, u32[]{:S(2)}) copy-start(s32[1,4]{1,0:T(1,128)} %param.10) | copy-start | bytes 52
  12.3 5.8 %copy-start.7 = (s32[1,4]{1,0:T(1,128)S(1)}, s32[1,4]{1,0:T(1,128)}, u32[]{:S(2)}) copy-start(s32[1,4]{1,0:T(1,128)} %param.11) | copy-start | bytes 52
  12.3 5.8 %copy-start.1 = (bf16[4,2,3,3,1,4,512]{6,5,4,3,2,1,0:T(4,128)(2,1)S(1)}, bf16[4,2,3,3,1,4,512]{6,5,4,3,2,1,0:T(4,128)(2,1)}, u32[]{:S(2)}) copy-start(bf16[4,2,3,3,1,4,512]{6,5,4,3,2,1,0:T(4,128)(2,1)} %cot_ref.1) | copy-start | bytes 884740
  12.3 16.3 %all-to-all-start = ((bf16[16,64,128]{2,1,0:T(8,128)(2,1)}), bf16[16,64,128]{2,1,0:T(8,128)(2,1)S(1)}, u32[]{:S(2)}, u32[]{:S(2)}) async-start(bf16[16,64,128]{2,1,0:T(8,128)(2,1)} %shard_map.122), calls=%async_computation | async-start | bytes 524288 | tf_op jit(solution)/shard_map/all_to_all | solution.py:882
  21.2 11.4 %collective-permute-start.2 = (bf16[4,16,512]{2,1,0:T(8,128)(2,1)S(1)}, bf16[4,16,512]{2,1,0:T(8,128)(2,1)S(1)}, u32[]{:S(2)}, u32[]{:S(2)}) collective-permute-start(bf16[4,16,512]{2,1,0:T(8,128)(2,1)S(1)} %get-tuple-element.38.fm_ref), channel_id=1, source_target_pairs={{0,1},{2,3},{4,5},{6,7},{8,9},{10,11},{12,13},{14,15},{1,0},{3,2},... | collective-permute-start | bytes 196616 | tf_op jit(solution)/shard_map/ppermute | solution.py:854
  21.7 11.0 %collective-permute-start.3 = (bf16[4,16,512]{2,1,0:T(8,128)(2,1)S(1)}, bf16[4,16,512]{2,1,0:T(8,128)(2,1)S(1)}, u32[]{:S(2)}, u32[]{:S(2)}) collective-permute-start(bf16[4,16,512]{2,1,0:T(8,128)(2,1)S(1)} %get-tuple-element.38.fm_ref), channel_id=1, source_target_pairs={{1,2},{3,4},{5,6},{7,8},{9,10},{11,12},{13,14},{15,0},{2,1},{4,3},... | collective-permute-start | bytes 196616 | tf_op jit(solution)/shard_map/ppermute | solution.py:854
  26.0 4.0 %collective-permute-start.4 = (bf16[4,8,512]{2,1,0:T(8,128)(2,1)S(1)}, bf16[4,8,512]{2,1,0:T(8,128)(2,1)S(1)}, u32[]{:S(2)}, u32[]{:S(2)}) collective-permute-start(bf16[4,8,512]{2,1,0:T(8,128)(2,1)S(1)} %get-tuple-element.39), channel_id=1, source_target_pairs={{0,2},{1,3},{4,6},{5,7},{8,10},{9,11},{12,14},{13,15},{2,0},{3,1},... | collective-permute-start | bytes 98312 | tf_op jit(solution)/shard_map/ppermute | solution.py:854
  26.0 6.6 %collective-permute-start.5 = (bf16[4,8,512]{2,1,0:T(8,128)(2,1)S(1)}, bf16[4,8,512]{2,1,0:T(8,128)(2,1)S(1)}, u32[]{:S(2)}, u32[]{:S(2)}) collective-permute-start(bf16[4,8,512]{2,1,0:T(8,128)(2,1)S(1)} %get-tuple-element.39), channel_id=1, source_target_pairs={{2,4},{3,5},{6,8},{7,9},{10,12},{11,13},{14,0},{15,1},{4,2},{5,3},... | collective-permute-start | bytes 98312 | tf_op jit(solution)/shard_map/ppermute | solution.py:854
  44.7 11.4 %all-to-all-start.1 = ((bf16[16,27,128]{2,1,0:T(8,128)(2,1)}), bf16[16,27,128]{2,1,0:T(8,128)(2,1)S(1)}, u32[]{:S(2)}, u32[]{:S(2)}) async-start(bf16[16,27,128]{2,1,0:T(8,128)(2,1)} %get-tuple-element.54), calls=%async_computation.1 | async-start | bytes 262144 | tf_op jit(solution)/shard_map/all_to_all | solution.py:938

commit v19 on v17

--- a/solution.py
+++ b/solution.py
@@ -599,9 +599,13 @@
         columns = [jnp.concatenate(shifted[2 * half:2 * half + 2], axis=1) for shifted in shifts]
         stack = jnp.concatenate(columns + [ahead[:, lanes], behind[:, lanes]], axis=0)
         if kept is not None:
-            kept[:, slot * SITES + 256 * half:slot * SITES + 256 * half + 256] = stack
+            kept[0:432, slot * SITES + 256 * half:slot * SITES + 256 * half + 256] = stack
         outs.append(jnp.dot(weights[...], stack, preferred_element_type=F32))
     return jnp.concatenate(outs, axis=1)
+
+
+def turned_back(value):
+    return jnp.concatenate([value[:, 128 * q:128 * q + 128].T for q in range(4)], axis=0)
 
 
 def thin_stack(source, index):
@@ -624,6 +628,8 @@
     coeff_ref, grads_ref,
     feats, mixed, h1, h2, h3, parts, lasts, g3, g2, g1, wide_back, wide_first, thin, thin_back, packed,
 ):
+    wide_back[432:512, :] = jnp.zeros((80, 4 * SITES), BF16)
+    wide_first[432:512, :] = jnp.zeros((80, 4 * SITES), BF16)
     row8 = lax.broadcasted_iota(jnp.int32, (8, SITES), 0)
     loop_re = jnp.concatenate([loops_ref[0, q:q + 1, :] for q in range(4)], axis=1)
     loop_im = jnp.concatenate([loops_ref[1, q:q + 1, :] for q in range(4)], axis=1)
@@ -725,13 +731,15 @@
             ).astype(F32).astype(BF16)
             packed[...] = jnp.dot(broad, place, preferred_element_type=F32)
         if step == 21:
-            grad_third = lax.dot_general(
-                wide_back[...], h2[:, own], contract, preferred_element_type=F32
+            grad_third = turned_back(
+                lax.dot_general(h2[:, own], wide_back[...], contract, preferred_element_type=F32)
             )
         if step == 22:
             for k in range(TAPS):
                 packed[H * k:H * k + H, 48:96] = grad_third[H * SWAP[k]:H * SWAP[k] + H]
-    grad_second = lax.dot_general(wide_first[...], h1[:, own], contract, preferred_element_type=F32)
+    grad_second = turned_back(
+        lax.dot_general(h1[:, own], wide_first[...], contract, preferred_element_type=F32)
+    )
     grad_first = lax.dot_general(g1[...], thin[...], contract, preferred_element_type=F32)
     for k in range(TAPS):
         rows = slice(H * k, H * k + H)
@@ -873,7 +881,7 @@
         [
             ((8, window), F32), ((8, window), F32), ((H, window), BF16), ((H, window), BF16), ((H, window), BF16),
             ((3, 8, window), F32), ((8, window), F32), ((H, window), BF16), ((H, window), BF16), ((H, 4 * SITES), BF16),
-            ((432, 4 * SITES), BF16), ((432, 4 * SITES), BF16), ((72, 4 * SITES), BF16), ((72, 4 * SITES), BF16),
+            ((512, 4 * SITES), BF16), ((512, 4 * SITES), BF16), ((72, 4 * SITES), BF16), ((72, 4 * SITES), BF16),
             ((432, LANES), F32),
         ],
         limit=20 * 1024 * 1024,

time: 54.2 us -> 54.2 us (level)
  no operation moved by 1% of the time
where the time goes in v19:
time: 54.2 us; the launch traced here: 53.8 us
  starting transfers between devices  21.7 us (40%)
  Pallas kernels  19.4 us (36%)
  waiting for transfers between devices  10.2 us (19%)
  local copies, waits for them, and re-layouts  1.73 us (3%)
  between operations  0.77 us (1%)
    pallas_call x1, Pallas kernels, on_device(): call(functools.partial(conv_kernel, count == 16), [((4, 8, SITES), F32),...  9.05 us
    all_to_all x1, waiting for transfers between devices, on_device(): grads = lax.all_to_all(grads, 'tm', split_axis=0, concat_axis=0, tiled=True)  6.88 us
    ppermute x4, starting transfers between devices, swap(): lax.ppermute(value, 'tm', pairs + [(target, source) for source, target in...  6.83 us
    all_to_all x1, starting transfers between devices, on_device(): lax.all_to_all(block, 'tm', split_axis=0, concat_axis=0, tiled=True)  5.8 us
    ppermute x2, starting transfers between devices, send(): lax.ppermute(value, 'tm', [(i, (i + distance) % count) for i in range(cou...  5.56 us
    all_to_all x1, starting transfers between devices, on_device(): grads = lax.all_to_all(grads, 'tm', split_axis=0, concat_axis=0, tiled=True)  3.51 us
    pallas_call x1, Pallas kernels, on_device(): call(time_kernel, [((4, 16, SITES), BF16), ((4, 8, SITES), BF16), ((2, 4,...  3.04 us
    ppermute x4, waiting for transfers between devices, swap(): lax.ppermute(value, 'tm', pairs + [(target, source) for source, target in...  2.72 us
  transfers between devices with their start and end apart: 8, of which 3 were waited for; matrix products, arithmetic and copies ran while one was open for 0% of the time, Pallas kernels for 14%

profile of v19, /device:TPU:0, one launch (start us, length us, event | category | flops | bytes accessed | tf_op | source)
XLA Modules:
  0.0 53.8 jit_solution(834294427238544954)
XLA Ops:
  0.6 1.1 %copy-done = f32[4,2,3,3,1,4,512]{6,5,4,3,2,1,0:T(4,128)S(1)} copy-done((f32[4,2,3,3,1,4,512]{6,5,4,3,2,1,0:T(4,128)S(1)}, f32[4,2,3,3,1,4,512]{6,5,4,3,2,1,0:T(4,128)}, u32[]{:S(2)}) %copy-start) | copy-done | bytes 589848
  1.7 1.3 %shard_map.119 = (bf16[70,512]{1,0:T(8,128)(2,1)S(1)}, bf16[70,512]{1,0:T(8,128)(2,1)S(1)}, f32[4,18,2,8,128]{4,3,2,1,0:T(8,128)S(1)}, f32[3,18,2,8,128]{4,3,2,1...) custom-call(f32[4,2,3,3,1,4,512]{6,5,4,3,2,1,0:T(4,128)S(1)} %copy-done), custom_call_target="tpu_custom_call" | custom-call | tf_op jit(solution)/shard_map/pallas_call | solution.py:820
  3.0 0.5 collective-permute-start
  3.5 5.1 %collective-permute-start.1 = (bf16[70,512]{1,0:T(8,128)(2,1)S(1)}, bf16[70,512]{1,0:T(8,128)(2,1)S(1)}, u32[]{:S(2)}, u32[]{:S(2)}) collective-permute-start(bf16[70,512]{1,0:T(8,128)(2,1)S(1)} %get-tuple-element.32), channel_id=1, source_target_pairs={{0,15},{1,0},{2,1},{3,2},{4,3},{5,4},{6,5},{7,6},{8,7},{9,8},{10,9... | collective-permute-start | bytes 215048 | tf_op jit(solution)/shard_map/ppermute | solution.py:809
  8.6 2.1 %shard_map.120.state.after_ref = f32[186,8,128]{2,1,0:T(8,128)S(1)} custom-call(f32[4,18,2,8,128]{4,3,2,1,0:T(8,128)S(1)} %get-tuple-element.28.dense, f32[3,18,2,8,128]{4,3,2,1,0:T(8,128)S(1)} %get-tuple-element.30.time_staples), custom_call_target="tpu_custom_call" | custom-call | flops 4000000000 | bytes 16000000 | tf_op jit(solution)/shard_map/pallas_call | solution.py:827
  10.7 0.0 copy-start.3
  10.8 0.6 %copy-done.3 = bf16[1296]{0:T(1024)(128)(2,1)S(1)} copy-done((bf16[1296]{0:T(1024)(128)(2,1)S(1)}, bf16[1296]{0:T(1024)(128)(2,1)}, u32[]{:S(2)}) %copy-start.3) | copy-done | bytes 2616
  11.4 0.0 copy-done.2
  11.4 0.0 copy-done.5
  11.4 0.9 %shard_map.122 = bf16[16,64,128]{2,1,0:T(8,128)(2,1)} custom-call(s32[1]{0:T(128)} %bitcast.place_ref, bf16[70,512]{1,0:T(8,128)(2,1)S(1)} %collective-permute-done.up_ref, bf16[70,512]{1,0:T(8,128)(2,1)S(1)} %collective-permute-done.1.down_ref, f32[12,4,128]{2,1,0:T(4,128)S(1)} %get-tuple-element.36.slab, bf16[216]{0:T(256)(128)(2,1)S(1)} %copy-done.4, ...), custom_call_target="tpu_custom_call" | custom-call | tf_op jit(solution)/shard_map/pallas_call | solution.py:834
  12.3 5.8 %all-to-all-start = ((bf16[16,64,128]{2,1,0:T(8,128)(2,1)}), bf16[16,64,128]{2,1,0:T(8,128)(2,1)S(1)}, u32[]{:S(2)}, u32[]{:S(2)}) async-start(bf16[16,64,128]{2,1,0:T(8,128)(2,1)} %shard_map.122), calls=%async_computation | async-start | bytes 524288 | tf_op jit(solution)/shard_map/all_to_all | solution.py:840
  18.2 3.0 %shard_map.121 = (bf16[4,16,512]{2,1,0:T(8,128)(2,1)S(1)}, bf16[4,8,512]{2,1,0:T(8,128)(2,1)S(1)}, bf16[2,4,18,2,8,128]{5,4,3,2,1,0:T(8,128)(2,1)S(1)}) custom-call(s32[1,4]{1,0:T(1,128)S(1)} %multiply_add_fusion.code_ref, f32[4,18,2,8,128]{4,3,2,1,0:T(8,128)S(1)} %get-tuple-element.28.dense, f32[3,18,2,8,128]{4,3,2,1,0:T(8,128)S(1)} %get-tuple-element.29.edges, ...), custom_call_target="tpu_custom_call" | custom-call | tf_op jit(solution)/shard_map/pallas_call | solution.py:841
  21.2 0.5 collective-permute-start.2
  21.7 4.3 %collective-permute-start.3 = (bf16[4,16,512]{2,1,0:T(8,128)(2,1)S(1)}, bf16[4,16,512]{2,1,0:T(8,128)(2,1)S(1)}, u32[]{:S(2)}, u32[]{:S(2)}) collective-permute-start(bf16[4,16,512]{2,1,0:T(8,128)(2,1)S(1)} %get-tuple-element.34.fm_ref), channel_id=1, source_target_pairs={{1,2},{3,4},{5,6},{7,8},{9,10},{11,12},{13,14},{15,0},{2,1},{4,3},... | collective-permute-start | bytes 196616 | tf_op jit(solution)/shard_map/ppermute | solution.py:812
  26.0 2.0 %collective-permute-start.5 = (bf16[4,8,512]{2,1,0:T(8,128)(2,1)S(1)}, bf16[4,8,512]{2,1,0:T(8,128)(2,1)S(1)}, u32[]{:S(2)}, u32[]{:S(2)}) collective-permute-start(bf16[4,8,512]{2,1,0:T(8,128)(2,1)S(1)} %get-tuple-element.35), channel_id=1, source_target_pairs={{2,4},{3,5},{6,8},{7,9},{10,12},{11,13},{14,0},{15,1},{4,2},{5,3},... | collective-permute-start | bytes 98312 | tf_op jit(solution)/shard_map/ppermute | solution.py:812
  28.0 0.6 %all-to-all-done.gathered_ref = bf16[16,64,128]{2,1,0:T(8,128)(2,1)S(1)} async-done(((bf16[16,64,128]{2,1,0:T(8,128)(2,1)}), bf16[16,64,128]{2,1,0:T(8,128)(2,1)S(1)}, u32[]{:S(2)}, u32[]{:S(2)}) %all-to-all-start) | async-done | bytes 262176 | tf_op jit(solution)/shard_map/all_to_all | solution.py:840
  28.6 1.3 %shard_map.123 = (f32[2,4,128]{2,1,0:T(4,128)S(1)}, bf16[48,72]{1,0:T(8,128)(2,1)S(1)}, bf16[48,432]{1,0:T(8,128)(2,1)S(1)}, bf16[48,432]{1,0:T(8,128)(2,1)S(1)}...) custom-call(bf16[16,64,128]{2,1,0:T(8,128)(2,1)S(1)} %all-to-all-don, ...), custom_call_target="tpu_custom_call" | custom-call | tf_op jit(solution)/shard_map/pallas_call | solution.py:864
  29.9 0.0 collective-permute-done.4.near_chip_ref
  29.9 2.7 %collective-permute-done.5.far_chip_ref = bf16[4,8,512]{2,1,0:T(8,128)(2,1)S(1)} collective-permute-done((bf16[4,8,512]{2,1,0:T(8,128)(2,1)S(1)}, bf16[4,8,512]{2,1,0:T(8,128)(2,1)S(1)}, u32[]{:S(2)}, u32[]{:S(2)}) %collective-permute-start.5) | collective-permute-done | bytes 32800 | tf_op jit(solution)/shard_map/ppermute | solution.py:812
  32.6 9.0 %shard_map.124 = (f32[4,8,512]{2,1,0:T(8,128)S(1)}, bf16[16,27,128]{2,1,0:T(8,128)(2,1)}) custom-call(s32[1]{0:T(128)} %bitcast.place_ref, bf16[4,16,512]{2,1,0:T(8,128)(2,1)S(1)} %get-tuple-element.34.fm_ref, bf16[4,16,512]{2,1,0:T(8,128)(2,1)S(1)} %collective-permute-done.2.near_ref, bf16[4,16,512]{2,1,0:T(8,128)(2,1)S(1)} %collective-permute-done.3.far_ref, ...), custom_call_target="tpu_custom_call" | custom-call | tf_op jit(solution)/shard_map/pallas_call | solution.py:878
  41.7 3.5 %all-to-all-start.1 = ((bf16[16,27,128]{2,1,0:T(8,128)(2,1)}), bf16[16,27,128]{2,1,0:T(8,128)(2,1)S(1)}, u32[]{:S(2)}, u32[]{:S(2)}) async-start(bf16[16,27,128]{2,1,0:T(8,128)(2,1)} %get-tuple-element.46), calls=%async_computation.1 | async-start | bytes 262144 | tf_op jit(solution)/shard_map/all_to_all | solution.py:897
  45.2 1.0 %shard_map.125 = f32[4,2,3,3,1,4,512]{6,5,4,3,2,1,0:T(4,128)} custom-call(f32[4,18,2,8,128]{4,3,2,1,0:T(8,128)S(1)} %get-tuple-element.28.dense, bf16[2,4,18,2,8,128]{5,4,3,2,1,0:T(8,128)(2,1)S(1)} %get-tuple-element.33.moves_ref, f32[4,8,512]{2,1,0:T(8,128)S(1)} %get-tuple-element.45.coeff_ref), custom_call_target="tpu_custom_call" | custom-call | tf_op jit(solution)/shard_map/pallas_call | solution.py:898
  46.2 6.9 %all-to-all-done.1.parts_ref = bf16[16,27,128]{2,1,0:T(8,128)(2,1)S(1)} async-done(((bf16[16,27,128]{2,1,0:T(8,128)(2,1)}), bf16[16,27,128]{2,1,0:T(8,128)(2,1)S(1)}, u32[]{:S(2)}, u32[]{:S(2)}) %all-to-all-start.1) | async-done | bytes 110624 | tf_op jit(solution)/shard_map/all_to_all | solution.py:897
  53.1 0.8 %shard_map.126 = (f32[1,216]{1,0:T(1,128)}, f32[1,1296]{1,0:T(1,128)}, f32[1,1296]{1,0:T(1,128)}, f32[1,108]{1,0:T(1,128)}) custom-call(bf16[16,27,128]{2,1,0:T(8,128)(2,1)S(1)} %all-to-all-done.1.parts_ref), custom_call_target="tpu_custom_call" | custom-call | tf_op jit(solution)/shard_map/pallas_call | solution.py:901
  (17 shorter events, 0.0 us)
Async XLA Ops:
  0.6 1.1 %copy-start = (f32[4,2,3,3,1,4,512]{6,5,4,3,2,1,0:T(4,128)S(1)}, f32[4,2,3,3,1,4,512]{6,5,4,3,2,1,0:T(4,128)}, u32[]{:S(2)}) copy-start(f32[4,2,3,3,1,4,512]{6,5,4,3,2,1,0:T(4,128)} %links_ref.1) | copy-start | bytes 1769476
  3.0 7.7 %collective-permute-start = (bf16[70,512]{1,0:T(8,128)(2,1)S(1)}, bf16[70,512]{1,0:T(8,128)(2,1)S(1)}, u32[]{:S(2)}, u32[]{:S(2)}) collective-permute-start(bf16[70,512]{1,0:T(8,128)(2,1)S(1)} %get-tuple-element.31), channel_id=1, source_target_pairs={{0,1},{1,2},{2,3},{3,4},{4,5},{5,6},{6,7},{7,8},{8,9},{9,10},{10,1... | collective-permute-start | bytes 215048 | tf_op jit(solution)/shard_map/ppermute | solution.py:809
  3.5 7.2 %collective-permute-start.1 = (bf16[70,512]{1,0:T(8,128)(2,1)S(1)}, bf16[70,512]{1,0:T(8,128)(2,1)S(1)}, u32[]{:S(2)}, u32[]{:S(2)}) collective-permute-start(bf16[70,512]{1,0:T(8,128)(2,1)S(1)} %get-tuple-element.32), channel_id=1, source_target_pairs={{0,15},{1,0},{2,1},{3,2},{4,3},{5,4},{6,5},{7,6},{8,7},{9,8},{10,9... | collective-permute-start | bytes 215048 | tf_op jit(solution)/shard_map/ppermute | solution.py:809
  10.7 0.7 %copy-start.3 = (bf16[1296]{0:T(1024)(128)(2,1)S(1)}, bf16[1296]{0:T(1024)(128)(2,1)}, u32[]{:S(2)}) copy-start(bf16[1296]{0:T(1024)(128)(2,1)} %w3_ref.1) | copy-start | bytes 7780
  10.7 0.7 %copy-start.2 = (bf16[1296]{0:T(1024)(128)(2,1)S(1)}, bf16[1296]{0:T(1024)(128)(2,1)}, u32[]{:S(2)}) copy-start(bf16[1296]{0:T(1024)(128)(2,1)} %w2_ref.1) | copy-start | bytes 7780
  10.7 0.7 %copy-start.4 = (bf16[216]{0:T(256)(128)(2,1)S(1)}, bf16[216]{0:T(256)(128)(2,1)}, u32[]{:S(2)}) copy-start(bf16[216]{0:T(256)(128)(2,1)} %w1_ref.1) | copy-start | bytes 1300
  10.8 0.7 %copy-start.5 = (bf16[108]{0:T(256)(128)(2,1)S(1)}, bf16[108]{0:T(256)(128)(2,1)}, u32[]{:S(2)}) copy-start(bf16[108]{0:T(256)(128)(2,1)} %w4_ref.1) | copy-start | bytes 652
  12.3 5.8 %copy-start.6 = (s32[1,4]{1,0:T(1,128)S(1)}, s32[1,4]{1,0:T(1,128)}, u32[]{:S(2)}) copy-start(s32[1,4]{1,0:T(1,128)} %param.10) | copy-start | bytes 52
  12.3 5.8 %copy-start.7 = (s32[1,4]{1,0:T(1,128)S(1)}, s32[1,4]{1,0:T(1,128)}, u32[]{:S(2)}) copy-start(s32[1,4]{1,0:T(1,128)} %param.11) | copy-start | bytes 52
  12.3 5.8 %copy-start.1 = (bf16[4,2,3,3,1,4,512]{6,5,4,3,2,1,0:T(4,128)(2,1)S(1)}, bf16[4,2,3,3,1,4,512]{6,5,4,3,2,1,0:T(4,128)(2,1)}, u32[]{:S(2)}) copy-start(bf16[4,2,3,3,1,4,512]{6,5,4,3,2,1,0:T(4,128)(2,1)} %cot_ref.1) | copy-start | bytes 884740
  12.3 16.3 %all-to-all-start = ((bf16[16,64,128]{2,1,0:T(8,128)(2,1)}), bf16[16,64,128]{2,1,0:T(8,128)(2,1)S(1)}, u32[]{:S(2)}, u32[]{:S(2)}) async-start(bf16[16,64,128]{2,1,0:T(8,128)(2,1)} %shard_map.122), calls=%async_computation | async-start | bytes 524288 | tf_op jit(solution)/shard_map/all_to_all | solution.py:840
  21.2 11.4 %collective-permute-start.2 = (bf16[4,16,512]{2,1,0:T(8,128)(2,1)S(1)}, bf16[4,16,512]{2,1,0:T(8,128)(2,1)S(1)}, u32[]{:S(2)}, u32[]{:S(2)}) collective-permute-start(bf16[4,16,512]{2,1,0:T(8,128)(2,1)S(1)} %get-tuple-element.34.fm_ref), channel_id=1, source_target_pairs={{0,1},{2,3},{4,5},{6,7},{8,9},{10,11},{12,13},{14,15},{1,0},{3,2},... | collective-permute-start | bytes 196616 | tf_op jit(solution)/shard_map/ppermute | solution.py:812
  21.7 11.0 %collective-permute-start.3 = (bf16[4,16,512]{2,1,0:T(8,128)(2,1)S(1)}, bf16[4,16,512]{2,1,0:T(8,128)(2,1)S(1)}, u32[]{:S(2)}, u32[]{:S(2)}) collective-permute-start(bf16[4,16,512]{2,1,0:T(8,128)(2,1)S(1)} %get-tuple-element.34.fm_ref), channel_id=1, source_target_pairs={{1,2},{3,4},{5,6},{7,8},{9,10},{11,12},{13,14},{15,0},{2,1},{4,3},... | collective-permute-start | bytes 196616 | tf_op jit(solution)/shard_map/ppermute | solution.py:812
  26.0 3.9 %collective-permute-start.4 = (bf16[4,8,512]{2,1,0:T(8,128)(2,1)S(1)}, bf16[4,8,512]{2,1,0:T(8,128)(2,1)S(1)}, u32[]{:S(2)}, u32[]{:S(2)}) collective-permute-start(bf16[4,8,512]{2,1,0:T(8,128)(2,1)S(1)} %get-tuple-element.35), channel_id=1, source_target_pairs={{0,2},{1,3},{4,6},{5,7},{8,10},{9,11},{12,14},{13,15},{2,0},{3,1},... | collective-permute-start | bytes 98312 | tf_op jit(solution)/shard_map/ppermute | solution.py:812
  26.0 6.6 %collective-permute-start.5 = (bf16[4,8,512]{2,1,0:T(8,128)(2,1)S(1)}, bf16[4,8,512]{2,1,0:T(8,128)(2,1)S(1)}, u32[]{:S(2)}, u32[]{:S(2)}) collective-permute-start(bf16[4,8,512]{2,1,0:T(8,128)(2,1)S(1)} %get-tuple-element.35), channel_id=1, source_target_pairs={{2,4},{3,5},{6,8},{7,9},{10,12},{11,13},{14,0},{15,1},{4,2},{5,3},... | collective-permute-start | bytes 98312 | tf_op jit(solution)/shard_map/ppermute | solution.py:812
  41.7 11.4 %all-to-all-start.1 = ((bf16[16,27,128]{2,1,0:T(8,128)(2,1)}), bf16[16,27,128]{2,1,0:T(8,128)(2,1)S(1)}, u32[]{:S(2)}, u32[]{:S(2)}) async-start(bf16[16,27,128]{2,1,0:T(8,128)(2,1)} %get-tuple-element.46), calls=%async_computation.1 | async-start | bytes 262144 | tf_op jit(solution)/shard_map/all_to_all | solution.py:897

commit v20 on v17

--- a/solution.py
+++ b/solution.py
@@ -218,7 +218,7 @@
             moved[mu, e, 1] = high
         return carry
 
-    lax.fori_loop(0, 18, shift_body, 0, unroll=6)
+    lax.fori_loop(0, 18, shift_body, 0, unroll=9)
 
     def staple_body(step, carry):
         mu = step // 2
@@ -240,7 +240,7 @@
         store_matrix(mat_mul(dagger(edge), u_t), write)
         return carry
 
-    lax.fori_loop(0, 6, staple_body, 0, unroll=2)
+    lax.fori_loop(0, 6, staple_body, 0, unroll=3)
 
     def slab_body(c, carry):
         u_t = load_matrix(lambda e: dense[3, e, c])
@@ -272,7 +272,7 @@
                 rows[16 + mu * 18 + e, 2 + c:3 + c] = value[4:5]
         return carry
 
-    lax.fori_loop(0, 18, down_body, 0, unroll=6)
+    lax.fori_loop(0, 18, down_body, 0, unroll=9)
     for q in range(4):
         down_ref[:, q * 128:q * 128 + 128] = rows[:, q, :].astype(BF16)
 
@@ -335,7 +335,7 @@
                     moved[mu, nu, e, 1] = high
         return carry
 
-    lax.fori_loop(0, 18, shift_body, 0, unroll=6)
+    lax.fori_loop(0, 18, shift_body, 0, unroll=9)
 
     def plane_body(step, carry):
         plane = step // 2
@@ -362,7 +362,7 @@
         store_matrix(mat_mul(dagger(two), u_mu), write_nu)
         return carry
 
-    lax.fori_loop(0, 6, plane_body, 0, unroll=2)
+    lax.fori_loop(0, 6, plane_body, 0, unroll=3)
 
     def lower_body(e, carry):
         for mu in range(3):
@@ -375,7 +375,7 @@
             state[sum_at(mu, e, 1)] = acc[1]
         return carry
 
-    lax.fori_loop(0, 18, lower_body, 0, unroll=6)
+    lax.fori_loop(0, 18, lower_body, 0, unroll=9)
 
 
 def time_kernel(
@@ -415,7 +415,7 @@
                 sums[nu, e, c] = state[sum_at(nu, e, c)] + jnp.where(steps == 0, below[c], 0.0)
         return carry
 
-    lax.fori_loop(0, 18, shift_body, 0, unroll=6)
+    lax.fori_loop(0, 18, shift_body, 0, unroll=9)
 
     def plane_body(step, carry):
         mu = step // 2
@@ -434,7 +434,7 @@
         store_matrix(mat_mul(dagger(two), load_matrix(lambda e: dense[mu, e, c])), write)
         return carry
 
-    lax.fori_loop(0, 6, plane_body, 0, unroll=2)
+    lax.fori_loop(0, 6, plane_body, 0, unroll=3)
 
     def lower_body(e, carry):
         acc = None
@@ -445,7 +445,7 @@
         sums[3, e, 1] = acc[1]
         return carry
 
-    lax.fori_loop(0, 18, lower_body, 0, unroll=6)
+    lax.fori_loop(0, 18, lower_body, 0, unroll=9)
 
     def force_body(step, carry):
         mu = step // 2
@@ -471,7 +471,7 @@
         put_row(rows, 12 + mu, c, gate * curve)
         return carry
 
-    lax.fori_loop(0, 8, force_body, 0, unroll=2)
+    lax.fori_loop(0, 8, force_body, 0, unroll=4)
     for t in range(4):
         for q in range(4):
             value = rows[t, q]

time: 54.2 us -> 54 us (level)
  transfers between devices with their start and end apart: 8 -> 8, of which waited for: 3 -> 4; matrix products, arithmetic and copies ran while one was open for 0% -> 0% of each run, Pallas kernels for 14% -> 13%
where the time goes in v20:
time: 54 us; the launch traced here: 53.6 us
  starting transfers between devices  21.8 us (40%)
  Pallas kernels  19 us (35%)
  waiting for transfers between devices  10.3 us (19%)
  local copies, waits for them, and re-layouts  1.75 us (3%)
  between operations  0.75 us (1%)
    pallas_call x1, Pallas kernels, on_device(): call(functools.partial(conv_kernel, count == 16), [((4, 8, SITES), F32),...  8.95 us
    all_to_all x1, waiting for transfers between devices, on_device(): grads = lax.all_to_all(grads, 'tm', split_axis=0, concat_axis=0, tiled=True)  6.88 us
    ppermute x4, starting transfers between devices, swap(): lax.ppermute(value, 'tm', pairs + [(target, source) for source, target in...  6.83 us
    all_to_all x1, starting transfers between devices, on_device(): lax.all_to_all(block, 'tm', split_axis=0, concat_axis=0, tiled=True)  5.9 us
    ppermute x2, starting transfers between devices, send(): lax.ppermute(value, 'tm', [(i, (i + distance) % count) for i in range(cou...  5.56 us
    all_to_all x1, starting transfers between devices, on_device(): grads = lax.all_to_all(grads, 'tm', split_axis=0, concat_axis=0, tiled=True)  3.51 us
    pallas_call x1, Pallas kernels, on_device(): call(time_kernel, [((4, 16, SITES), BF16), ((4, 8, SITES), BF16), ((2, 4,...  2.93 us
    ppermute x4, waiting for transfers between devices, swap(): lax.ppermute(value, 'tm', pairs + [(target, source) for source, target in...  2.6 us
  transfers between devices with their start and end apart: 8, of which 4 were waited for; matrix products, arithmetic and copies ran while one was open for 0% of the time, Pallas kernels for 13%

profile of v20, /device:TPU:0, one launch (start us, length us, event | category | flops | bytes accessed | tf_op | source)
XLA Modules:
  0.0 53.6 jit_solution(16110228317772589542)
XLA Ops:
  0.6 1.1 %copy-done = f32[4,2,3,3,1,4,512]{6,5,4,3,2,1,0:T(4,128)S(1)} copy-done((f32[4,2,3,3,1,4,512]{6,5,4,3,2,1,0:T(4,128)S(1)}, f32[4,2,3,3,1,4,512]{6,5,4,3,2,1,0:T(4,128)}, u32[]{:S(2)}) %copy-start) | copy-done | bytes 589848
  1.7 1.2 %shard_map.119 = (bf16[70,512]{1,0:T(8,128)(2,1)S(1)}, bf16[70,512]{1,0:T(8,128)(2,1)S(1)}, f32[4,18,2,8,128]{4,3,2,1,0:T(8,128)S(1)}, f32[3,18,2,8,128]{4,3,2,1...) custom-call(f32[4,2,3,3,1,4,512]{6,5,4,3,2,1,0:T(4,128)S(1)} %copy-done), custom_call_target="tpu_custom_call" | custom-call | tf_op jit(solution)/shard_map/pallas_call | solution.py:812
  2.9 0.5 collective-permute-start
  3.4 5.1 %collective-permute-start.1 = (bf16[70,512]{1,0:T(8,128)(2,1)S(1)}, bf16[70,512]{1,0:T(8,128)(2,1)S(1)}, u32[]{:S(2)}, u32[]{:S(2)}) collective-permute-start(bf16[70,512]{1,0:T(8,128)(2,1)S(1)} %get-tuple-element.32), channel_id=1, source_target_pairs={{0,15},{1,0},{2,1},{3,2},{4,3},{5,4},{6,5},{7,6},{8,7},{9,8},{10,9... | collective-permute-start | bytes 215048 | tf_op jit(solution)/shard_map/ppermute | solution.py:801
  8.5 2.0 %shard_map.120.state.after_ref = f32[186,8,128]{2,1,0:T(8,128)S(1)} custom-call(f32[4,18,2,8,128]{4,3,2,1,0:T(8,128)S(1)} %get-tuple-element.28.dense, f32[3,18,2,8,128]{4,3,2,1,0:T(8,128)S(1)} %get-tuple-element.30.time_staples), custom_call_target="tpu_custom_call" | custom-call | flops 4000000000 | bytes 16000000 | tf_op jit(solution)/shard_map/pallas_call | solution.py:819
  10.5 0.1 collective-permute-done.up_ref
  10.6 0.6 %copy-done.3 = bf16[1296]{0:T(1024)(128)(2,1)S(1)} copy-done((bf16[1296]{0:T(1024)(128)(2,1)S(1)}, bf16[1296]{0:T(1024)(128)(2,1)}, u32[]{:S(2)}) %copy-start.3) | copy-done | bytes 2616
  11.2 0.0 copy-done.2
  11.2 0.1 copy-done.4
  11.2 0.0 copy-done.5
  11.3 0.9 %shard_map.122 = bf16[16,64,128]{2,1,0:T(8,128)(2,1)} custom-call(s32[1]{0:T(128)} %bitcast.place_ref, bf16[70,512]{1,0:T(8,128)(2,1)S(1)} %collective-permute-done.up_ref, bf16[70,512]{1,0:T(8,128)(2,1)S(1)} %collective-permute-done.1.down_ref, f32[12,4,128]{2,1,0:T(4,128)S(1)} %get-tuple-element.36.slab, bf16[216]{0:T(256)(128)(2,1)S(1)} %copy-done.4, ...), custom_call_target="tpu_custom_call" | custom-call | tf_op jit(solution)/shard_map/pallas_call | solution.py:826
  12.1 5.9 %all-to-all-start = ((bf16[16,64,128]{2,1,0:T(8,128)(2,1)}), bf16[16,64,128]{2,1,0:T(8,128)(2,1)S(1)}, u32[]{:S(2)}, u32[]{:S(2)}) async-start(bf16[16,64,128]{2,1,0:T(8,128)(2,1)} %shard_map.122), calls=%async_computation | async-start | bytes 524288 | tf_op jit(solution)/shard_map/all_to_all | solution.py:832
  18.1 2.9 %shard_map.121 = (bf16[4,16,512]{2,1,0:T(8,128)(2,1)S(1)}, bf16[4,8,512]{2,1,0:T(8,128)(2,1)S(1)}, bf16[2,4,18,2,8,128]{5,4,3,2,1,0:T(8,128)(2,1)S(1)}) custom-call(s32[1,4]{1,0:T(1,128)S(1)} %multiply_add_fusion.code_ref, f32[4,18,2,8,128]{4,3,2,1,0:T(8,128)S(1)} %get-tuple-element.28.dense, f32[3,18,2,8,128]{4,3,2,1,0:T(8,128)S(1)} %get-tuple-element.29.edges, ...), custom_call_target="tpu_custom_call" | custom-call | tf_op jit(solution)/shard_map/pallas_call | solution.py:833
  21.0 0.5 collective-permute-start.2
  21.5 4.3 %collective-permute-start.3 = (bf16[4,16,512]{2,1,0:T(8,128)(2,1)S(1)}, bf16[4,16,512]{2,1,0:T(8,128)(2,1)S(1)}, u32[]{:S(2)}, u32[]{:S(2)}) collective-permute-start(bf16[4,16,512]{2,1,0:T(8,128)(2,1)S(1)} %get-tuple-element.34.fm_ref), channel_id=1, source_target_pairs={{1,2},{3,4},{5,6},{7,8},{9,10},{11,12},{13,14},{15,0},{2,1},{4,3},... | collective-permute-start | bytes 196616 | tf_op jit(solution)/shard_map/ppermute | solution.py:804
  25.8 2.0 %collective-permute-start.5 = (bf16[4,8,512]{2,1,0:T(8,128)(2,1)S(1)}, bf16[4,8,512]{2,1,0:T(8,128)(2,1)S(1)}, u32[]{:S(2)}, u32[]{:S(2)}) collective-permute-start(bf16[4,8,512]{2,1,0:T(8,128)(2,1)S(1)} %get-tuple-element.35), channel_id=1, source_target_pairs={{2,4},{3,5},{6,8},{7,9},{10,12},{11,13},{14,0},{15,1},{4,2},{5,3},... | collective-permute-start | bytes 98312 | tf_op jit(solution)/shard_map/ppermute | solution.py:804
  27.9 0.7 %all-to-all-done.gathered_ref = bf16[16,64,128]{2,1,0:T(8,128)(2,1)S(1)} async-done(((bf16[16,64,128]{2,1,0:T(8,128)(2,1)}), bf16[16,64,128]{2,1,0:T(8,128)(2,1)S(1)}, u32[]{:S(2)}, u32[]{:S(2)}) %all-to-all-start) | async-done | bytes 262176 | tf_op jit(solution)/shard_map/all_to_all | solution.py:832
  28.6 1.3 %shard_map.123 = (f32[2,4,128]{2,1,0:T(4,128)S(1)}, bf16[48,72]{1,0:T(8,128)(2,1)S(1)}, bf16[48,432]{1,0:T(8,128)(2,1)S(1)}, bf16[48,432]{1,0:T(8,128)(2,1)S(1)}...) custom-call(bf16[16,64,128]{2,1,0:T(8,128)(2,1)S(1)} %all-to-all-don, ...), custom_call_target="tpu_custom_call" | custom-call | tf_op jit(solution)/shard_map/pallas_call | solution.py:856
  29.9 2.6 %collective-permute-done.5.far_chip_ref = bf16[4,8,512]{2,1,0:T(8,128)(2,1)S(1)} collective-permute-done((bf16[4,8,512]{2,1,0:T(8,128)(2,1)S(1)}, bf16[4,8,512]{2,1,0:T(8,128)(2,1)S(1)}, u32[]{:S(2)}, u32[]{:S(2)}) %collective-permute-start.5) | collective-permute-done | bytes 32800 | tf_op jit(solution)/shard_map/ppermute | solution.py:804
  32.5 8.9 %shard_map.124 = (f32[4,8,512]{2,1,0:T(8,128)S(1)}, bf16[16,27,128]{2,1,0:T(8,128)(2,1)}) custom-call(s32[1]{0:T(128)} %bitcast.place_ref, bf16[4,16,512]{2,1,0:T(8,128)(2,1)S(1)} %get-tuple-element.34.fm_ref, bf16[4,16,512]{2,1,0:T(8,128)(2,1)S(1)} %collective-permute-done.2.near_ref, bf16[4,16,512]{2,1,0:T(8,128)(2,1)S(1)} %collective-permute-done.3.far_ref, ...), custom_call_target="tpu_custom_call" | custom-call | tf_op jit(solution)/shard_map/pallas_call | solution.py:870
  41.4 3.5 %all-to-all-start.1 = ((bf16[16,27,128]{2,1,0:T(8,128)(2,1)}), bf16[16,27,128]{2,1,0:T(8,128)(2,1)S(1)}, u32[]{:S(2)}, u32[]{:S(2)}) async-start(bf16[16,27,128]{2,1,0:T(8,128)(2,1)} %get-tuple-element.46), calls=%async_computation.1 | async-start | bytes 262144 | tf_op jit(solution)/shard_map/all_to_all | solution.py:889
  44.9 1.0 %shard_map.125 = f32[4,2,3,3,1,4,512]{6,5,4,3,2,1,0:T(4,128)} custom-call(f32[4,18,2,8,128]{4,3,2,1,0:T(8,128)S(1)} %get-tuple-element.28.dense, bf16[2,4,18,2,8,128]{5,4,3,2,1,0:T(8,128)(2,1)S(1)} %get-tuple-element.33.moves_ref, f32[4,8,512]{2,1,0:T(8,128)S(1)} %get-tuple-element.45.coeff_ref), custom_call_target="tpu_custom_call" | custom-call | tf_op jit(solution)/shard_map/pallas_call | solution.py:890
  45.9 6.9 %all-to-all-done.1.parts_ref = bf16[16,27,128]{2,1,0:T(8,128)(2,1)S(1)} async-done(((bf16[16,27,128]{2,1,0:T(8,128)(2,1)}), bf16[16,27,128]{2,1,0:T(8,128)(2,1)S(1)}, u32[]{:S(2)}, u32[]{:S(2)}) %all-to-all-start.1) | async-done | bytes 110624 | tf_op jit(solution)/shard_map/all_to_all | solution.py:889
  52.8 0.8 %shard_map.126 = (f32[1,216]{1,0:T(1,128)}, f32[1,1296]{1,0:T(1,128)}, f32[1,1296]{1,0:T(1,128)}, f32[1,108]{1,0:T(1,128)}) custom-call(bf16[16,27,128]{2,1,0:T(8,128)(2,1)S(1)} %all-to-all-done.1.parts_ref), custom_call_target="tpu_custom_call" | custom-call | tf_op jit(solution)/shard_map/pallas_call | solution.py:893
  (17 shorter events, 0.0 us)
Async XLA Ops:
  0.6 1.1 %copy-start = (f32[4,2,3,3,1,4,512]{6,5,4,3,2,1,0:T(4,128)S(1)}, f32[4,2,3,3,1,4,512]{6,5,4,3,2,1,0:T(4,128)}, u32[]{:S(2)}) copy-start(f32[4,2,3,3,1,4,512]{6,5,4,3,2,1,0:T(4,128)} %links_ref.1) | copy-start | bytes 1769476
  2.9 7.6 %collective-permute-start = (bf16[70,512]{1,0:T(8,128)(2,1)S(1)}, bf16[70,512]{1,0:T(8,128)(2,1)S(1)}, u32[]{:S(2)}, u32[]{:S(2)}) collective-permute-start(bf16[70,512]{1,0:T(8,128)(2,1)S(1)} %get-tuple-element.31), channel_id=1, source_target_pairs={{0,1},{1,2},{2,3},{3,4},{4,5},{5,6},{6,7},{7,8},{8,9},{9,10},{10,1... | collective-permute-start | bytes 215048 | tf_op jit(solution)/shard_map/ppermute | solution.py:801
  3.4 7.1 %collective-permute-start.1 = (bf16[70,512]{1,0:T(8,128)(2,1)S(1)}, bf16[70,512]{1,0:T(8,128)(2,1)S(1)}, u32[]{:S(2)}, u32[]{:S(2)}) collective-permute-start(bf16[70,512]{1,0:T(8,128)(2,1)S(1)} %get-tuple-element.32), channel_id=1, source_target_pairs={{0,15},{1,0},{2,1},{3,2},{4,3},{5,4},{6,5},{7,6},{8,7},{9,8},{10,9... | collective-permute-start | bytes 215048 | tf_op jit(solution)/shard_map/ppermute | solution.py:801
  10.5 0.7 %copy-start.3 = (bf16[1296]{0:T(1024)(128)(2,1)S(1)}, bf16[1296]{0:T(1024)(128)(2,1)}, u32[]{:S(2)}) copy-start(bf16[1296]{0:T(1024)(128)(2,1)} %w3_ref.1) | copy-start | bytes 7780
  10.5 0.7 %copy-start.2 = (bf16[1296]{0:T(1024)(128)(2,1)S(1)}, bf16[1296]{0:T(1024)(128)(2,1)}, u32[]{:S(2)}) copy-start(bf16[1296]{0:T(1024)(128)(2,1)} %w2_ref.1) | copy-start | bytes 7780
  10.6 0.7 %copy-start.4 = (bf16[216]{0:T(256)(128)(2,1)S(1)}, bf16[216]{0:T(256)(128)(2,1)}, u32[]{:S(2)}) copy-start(bf16[216]{0:T(256)(128)(2,1)} %w1_ref.1) | copy-start | bytes 1300
  10.6 0.7 %copy-start.5 = (bf16[108]{0:T(256)(128)(2,1)S(1)}, bf16[108]{0:T(256)(128)(2,1)}, u32[]{:S(2)}) copy-start(bf16[108]{0:T(256)(128)(2,1)} %w4_ref.1) | copy-start | bytes 652
  12.1 5.9 %copy-start.6 = (s32[1,4]{1,0:T(1,128)S(1)}, s32[1,4]{1,0:T(1,128)}, u32[]{:S(2)}) copy-start(s32[1,4]{1,0:T(1,128)} %param.10) | copy-start | bytes 52
  12.1 5.9 %copy-start.7 = (s32[1,4]{1,0:T(1,128)S(1)}, s32[1,4]{1,0:T(1,128)}, u32[]{:S(2)}) copy-start(s32[1,4]{1,0:T(1,128)} %param.11) | copy-start | bytes 52
  12.1 5.9 %copy-start.1 = (bf16[4,2,3,3,1,4,512]{6,5,4,3,2,1,0:T(4,128)(2,1)S(1)}, bf16[4,2,3,3,1,4,512]{6,5,4,3,2,1,0:T(4,128)(2,1)}, u32[]{:S(2)}) copy-start(bf16[4,2,3,3,1,4,512]{6,5,4,3,2,1,0:T(4,128)(2,1)} %cot_ref.1) | copy-start | bytes 884740
  12.1 16.4 %all-to-all-start = ((bf16[16,64,128]{2,1,0:T(8,128)(2,1)}), bf16[16,64,128]{2,1,0:T(8,128)(2,1)S(1)}, u32[]{:S(2)}, u32[]{:S(2)}) async-start(bf16[16,64,128]{2,1,0:T(8,128)(2,1)} %shard_map.122), calls=%async_computation | async-start | bytes 524288 | tf_op jit(solution)/shard_map/all_to_all | solution.py:832
  21.0 11.4 %collective-permute-start.2 = (bf16[4,16,512]{2,1,0:T(8,128)(2,1)S(1)}, bf16[4,16,512]{2,1,0:T(8,128)(2,1)S(1)}, u32[]{:S(2)}, u32[]{:S(2)}) collective-permute-start(bf16[4,16,512]{2,1,0:T(8,128)(2,1)S(1)} %get-tuple-element.34.fm_ref), channel_id=1, source_target_pairs={{0,1},{2,3},{4,5},{6,7},{8,9},{10,11},{12,13},{14,15},{1,0},{3,2},... | collective-permute-start | bytes 196616 | tf_op jit(solution)/shard_map/ppermute | solution.py:804
  21.5 11.0 %collective-permute-start.3 = (bf16[4,16,512]{2,1,0:T(8,128)(2,1)S(1)}, bf16[4,16,512]{2,1,0:T(8,128)(2,1)S(1)}, u32[]{:S(2)}, u32[]{:S(2)}) collective-permute-start(bf16[4,16,512]{2,1,0:T(8,128)(2,1)S(1)} %get-tuple-element.34.fm_ref), channel_id=1, source_target_pairs={{1,2},{3,4},{5,6},{7,8},{9,10},{11,12},{13,14},{15,0},{2,1},{4,3},... | collective-permute-start | bytes 196616 | tf_op jit(solution)/shard_map/ppermute | solution.py:804
  25.8 4.0 %collective-permute-start.4 = (bf16[4,8,512]{2,1,0:T(8,128)(2,1)S(1)}, bf16[4,8,512]{2,1,0:T(8,128)(2,1)S(1)}, u32[]{:S(2)}, u32[]{:S(2)}) collective-permute-start(bf16[4,8,512]{2,1,0:T(8,128)(2,1)S(1)} %get-tuple-element.35), channel_id=1, source_target_pairs={{0,2},{1,3},{4,6},{5,7},{8,10},{9,11},{12,14},{13,15},{2,0},{3,1},... | collective-permute-start | bytes 98312 | tf_op jit(solution)/shard_map/ppermute | solution.py:804
  25.8 6.6 %collective-permute-start.5 = (bf16[4,8,512]{2,1,0:T(8,128)(2,1)S(1)}, bf16[4,8,512]{2,1,0:T(8,128)(2,1)S(1)}, u32[]{:S(2)}, u32[]{:S(2)}) collective-permute-start(bf16[4,8,512]{2,1,0:T(8,128)(2,1)S(1)} %get-tuple-element.35), channel_id=1, source_target_pairs={{2,4},{3,5},{6,8},{7,9},{10,12},{11,13},{14,0},{15,1},{4,2},{5,3},... | collective-permute-start | bytes 98312 | tf_op jit(solution)/shard_map/ppermute | solution.py:804
  41.4 11.4 %all-to-all-start.1 = ((bf16[16,27,128]{2,1,0:T(8,128)(2,1)}), bf16[16,27,128]{2,1,0:T(8,128)(2,1)S(1)}, u32[]{:S(2)}, u32[]{:S(2)}) async-start(bf16[16,27,128]{2,1,0:T(8,128)(2,1)} %get-tuple-element.46), calls=%async_computation.1 | async-start | bytes 262144 | tf_op jit(solution)/shard_map/all_to_all | solution.py:889
